TPU v7x, 32 devices: a whole 2x2x4 slice. The times are simulated.
32 devices in a mesh: dp: 2 (over y), row: 4 (over z), col: 4 (over x, core).
Axes of the slice: x: 2, y: 2, z: 4, core: 2. Of those that a mesh axis runs over, the one named last changes fastest.
Arguments:
- first_view: bfloat16 [2048, 8192], P('dp', ('row', 'col')), may hold values from -6 to 6
- second_view: bfloat16 [2048, 8192], P('dp', ('row', 'col')), may hold values from -6 to 6
Outputs:
- loss: float32 [], replicated
- grad_first: float32 [2048, 8192], P('dp', ('row', 'col'))
- grad_second: float32 [2048, 8192], P('dp', ('row', 'col'))
All inputs are finite; a program needn't handle non-finite values.
Results may differ from a plain program's by a relative error of at most 0.00085.
Values may be sent and summed in bfloat16 or wider, within the bound.
No kernel may reach another device: no remote copies, remote signals or barrier semaphores. Data moves between devices by JAX's collectives and lax.ppermute only.
A program may use at most 192 MiB of HBM per device.

v0:
```python
import jax
import jax.numpy as jnp
from jax import lax
from jax.sharding import PartitionSpec as P

inv_weight = 25.0
var_weight = 25.0
cov_weight = 1.0
eps_var = 0.0001


def gram(left, right):
    return lax.dot_general(
        left, right, (((0,), (0,)), ((), ())), preferred_element_type=jnp.float32
    )


def diagonal_mask(row_count, row_start, piece_width, col_count, col_index, set_width):
    row_ids = row_start + jnp.arange(row_count, dtype=jnp.int32)
    column_ids = jnp.arange(set_width, dtype=jnp.int32)
    global_cols = (
        column_ids // piece_width * col_count + col_index
    ) * piece_width + column_ids % piece_width
    return row_ids[:, None] == global_cols[None, :]


def on_device(first_view, second_view):
    dp_count = lax.axis_size("dp")
    row_count = lax.axis_size("row")
    col_count = lax.axis_size("col")
    rows_dev, piece_width = first_view.shape
    total = rows_dev * dp_count
    feat = piece_width * row_count * col_count
    block_width = piece_width * col_count
    set_width = piece_width * row_count
    row_index = lax.axis_index("row")
    col_index = lax.axis_index("col")
    dp_index = lax.axis_index("dp")
    first = first_view.astype(jnp.float32)
    second = second_view.astype(jnp.float32)
    sum_first, sum_second = lax.psum((jnp.sum(first, axis=0), jnp.sum(second, axis=0)), "dp")
    cen_first = first - sum_first / total
    cen_second = second - sum_second / total
    sq_first, sq_second = lax.psum(
        (jnp.sum(cen_first * cen_first, axis=0), jnp.sum(cen_second * cen_second, axis=0)), "dp"
    )
    spr_first = jnp.sqrt(sq_first / (total - 1) + eps_var)
    spr_second = jnp.sqrt(sq_second / (total - 1) + eps_var)
    hinge_sum = jnp.sum(jnp.maximum(1.0 - spr_first, 0.0)) + jnp.sum(
        jnp.maximum(1.0 - spr_second, 0.0)
    )
    rnd_first = cen_first.astype(jnp.bfloat16)
    rnd_second = cen_second.astype(jnp.bfloat16)
    wide_first, wide_second = (
        lax.all_gather(rnd_first, "dp", axis=0, tiled=True),
        lax.all_gather(rnd_second, "dp", axis=0, tiled=True),
    )
    blocks_first, blocks_second = (
        lax.all_gather(wide_first, "col", axis=1, tiled=True),
        lax.all_gather(wide_second, "col", axis=1, tiled=True),
    )
    sets_first, sets_second = (
        lax.all_gather(wide_first, "row", axis=1, tiled=True),
        lax.all_gather(wide_second, "row", axis=1, tiled=True),
    )
    mask = diagonal_mask(
        block_width, row_index * block_width, piece_width, col_count, col_index, set_width
    )
    offd_first = jnp.where(mask, jnp.float32(0.0), gram(blocks_first, sets_first) / (total - 1))
    offd_second = jnp.where(mask, jnp.float32(0.0), gram(blocks_second, sets_second) / (total - 1))
    cov_part = (
        (jnp.sum(offd_first * offd_first) + jnp.sum(offd_second * offd_second)) / feat / dp_count
    )
    tile_first = offd_first.astype(jnp.bfloat16)
    tile_second = offd_second.astype(jnp.bfloat16)
    local_first = lax.dynamic_slice_in_dim(sets_first, dp_index * rows_dev, rows_dev, 0)
    local_second = lax.dynamic_slice_in_dim(sets_second, dp_index * rows_dev, rows_dev, 0)
    part_first = lax.dot_general(
        local_first, tile_first, (((1,), (1,)), ((), ())), preferred_element_type=jnp.float32
    )
    part_second = lax.dot_general(
        local_second, tile_second, (((1,), (1,)), ((), ())), preferred_element_type=jnp.float32
    )
    prod_first, prod_second = (
        lax.psum_scatter(part_first, "col", scatter_dimension=1, tiled=True),
        lax.psum_scatter(part_second, "col", scatter_dimension=1, tiled=True),
    )
    differ = first - second
    local_loss = (
        inv_weight * jnp.sum(differ * differ) / (total * feat)
        + var_weight * hinge_sum / feat / dp_count
        + cov_weight * cov_part
    )
    loss = lax.psum(local_loss, ("dp", "row", "col"))
    scale = total * feat / 64.0

    def gradient(sign, centred, spread, product):
        invariant = sign * 2.0 * inv_weight * differ / (total * feat)
        active = jnp.where(spread < 1.0, jnp.float32(1.0), jnp.float32(0.0))
        varterm = -var_weight * centred * active / (feat * spread * (total - 1))
        covterm = 4.0 * cov_weight * product / (feat * (total - 1))
        return scale * (invariant + varterm + covterm)

    return (
        loss,
        gradient(1.0, cen_first, spr_first, prod_first),
        gradient(-1.0, cen_second, spr_second, prod_second),
    )


def solution(mesh):
    return jax.shard_map(
        on_device,
        mesh=mesh,
        in_specs=(P("dp", ("row", "col")), P("dp", ("row", "col"))),
        out_specs=(P(), P("dp", ("row", "col")), P("dp", ("row", "col"))),
        check_vma=False,
    )
```

profile of v0, /device:TPU:0, one launch (start us, length us, event | category | flops | bytes accessed | tf_op | source)
XLA Modules:
  0.0 714.9 jit_solution(7609177890281320216)
XLA Ops:
  7.2 0.0 all-gather.7.cloned.1.call-start
  7.2 1.4 convert_reduce_fusion.1
  8.6 1.4 convert_reduce_fusion
  10.1 5.9 all-reduce.1
  15.9 4.3 fusion.22
  20.2 0.0 all-gather.7.cloned.1.call-update
  20.2 0.0 all-gather.13.cloned.1.call-start
  20.3 0.7 all-gather.13.cloned.1.call-update
  21.0 0.0 all-gather.9.cloned.1.call-start
  21.0 34.3 %all-gather.7.cloned.1.call-done = bf16[2048,512]{1,0:T(8,128)(2,1)} async-done(((bf16[1024,512]{1,0:T(8,128)(2,1)}), bf16[2048,512]{1,0:T(8,128)(2,1)}) %all-gather.7.cloned.1.call-update) | async-done | bytes 2097168 | tf_op jit(solution)/shard_map/all_gather | solution.py:55
  55.3 0.0 all-gather.9.cloned.1.call-update
  55.3 0.0 all-gather.11.cloned.1.call-start
  55.4 0.5 all-gather.11.cloned.1.call-update
  55.9 0.0 all-gather.15.cloned.1.call-start
  55.9 34.6 %all-gather.13.cloned.1.call-done = bf16[2048,512]{1,0:T(8,128)(2,1)} async-done(((bf16[1024,512]{1,0:T(8,128)(2,1)}), bf16[2048,512]{1,0:T(8,128)(2,1)}) %all-gather.13.cloned.1.call-update) | async-done | bytes 2097168 | tf_op jit(solution)/shard_map/all_gather | solution.py:56
  90.6 0.0 all-gather.15.cloned.1.call-update
  90.6 0.0 all-gather.17.cloned.1.call-start
  90.6 0.5 all-gather.17.cloned.1.call-update
  91.2 0.0 reduce-scatter.5.cloned.1.call-start
  91.2 59.2 %all-gather.9.cloned.1.call-done = bf16[2048,2048]{1,0:T(8,128)(2,1)} async-done(((bf16[2048,512]{1,0:T(8,128)(2,1)}), bf16[2048,2048]{1,0:T(8,128)(2,1)}) %all-gather.9.cloned.1.call-update) | async-done | bytes 8388624 | tf_op jit(solution)/shard_map/all_gather | solution.py:59
  150.5 151.1 %all-gather.11.cloned.1.call-done = bf16[2048,2048]{1,0:T(8,128)(2,1)} async-done(((bf16[2048,512]{1,0:T(8,128)(2,1)}), bf16[2048,2048]{1,0:T(8,128)(2,1)}) %all-gather.11.cloned.1.call-update) | async-done | bytes 8388624 | tf_op jit(solution)/shard_map/all_gather | solution.py:63
  301.6 24.3 %fusion.49 = f32[2048,2048]{1,0:T(8,128)} fusion(bf16[2048,2048]{1,0:T(8,128)(2,1)} %all-gather.9.cloned.1.call-done, bf16[2048,2048]{1,0:T(8,128)(2,1)} %all-gather.11.cloned.1.call-done), kind=kOutput, calls=%fused_computation.72 | convolution fusion | flops 17179869184 | bytes 33554432 | tf_op jit(solution)/shard_map/dot_general | solution.py:13
  325.8 33.7 %all-gather.15.cloned.1.call-done = bf16[2048,2048]{1,0:T(8,128)(2,1)} async-done(((bf16[2048,512]{1,0:T(8,128)(2,1)}), bf16[2048,2048]{1,0:T(8,128)(2,1)}) %all-gather.15.cloned.1.call-update) | async-done | bytes 8388624 | tf_op jit(solution)/shard_map/all_gather | solution.py:60
  359.5 151.1 %all-gather.17.cloned.1.call-done = bf16[2048,2048]{1,0:T(8,128)(2,1)} async-done(((bf16[2048,512]{1,0:T(8,128)(2,1)}), bf16[2048,2048]{1,0:T(8,128)(2,1)}) %all-gather.17.cloned.1.call-update) | async-done | bytes 8388624 | tf_op jit(solution)/shard_map/all_gather | solution.py:64
  510.6 0.0 copy-start.2
  510.6 31.4 %multiply_reduce_fusion = (f32[]{:T(128)}, f32[]{:T(128)}, f32[2048,2048]{1,0:T(8,128)}) fusion(s32[2048]{0:T(1024)S(1)} %get-tuple-element.25, s32[2048]{0:T(1024)S(1)} %get-tuple-element.26, f32[2048,2048]{1,0:T(8,128)} %fusion.49, bf16[2048,2048]{1,0:T(8,128)(2,1)} %all-gather.15.cloned.1.call-done, bf16[2048,2048]{1,0:T(8,128)(2,1)} %all-gather.17.cloned.1.call-done), kind=kOutput, calls=%fused_computation.2 | convolution fusion | flops 17217617920 | bytes 50348040 | tf_op jit(solution)/shard_map/dot_general | solution.py:13
  541.9 0.0 copy-done.2
  542.0 14.5 %fusion.2 = f32[1024,2048]{1,0:T(8,128)} fusion(f32[2048,2048]{1,0:T(8,128)} %get-tuple-element.22, s32[2048]{0:T(1024)S(1)} %get-tuple-element.25, s32[2048]{0:T(1024)S(1)} %get-tuple-element.26, bf16[2048,2048]{1,0:T(8,128)(2,1)S(1)} %copy-done.2, s32[]{:T(128)S(6)} %select_n.43), kind=kOutput, calls=%fused_computation.6 | convolution fusion | flops 8606711808 | bytes 29376516 | tf_op jit(solution)/shard_map/dot_general | solution.py:81
  556.5 0.0 reduce-scatter.5.cloned.1.call-update
  556.5 0.0 reduce-scatter.3.cloned.1.call-start
  556.6 16.5 %fusion.4 = f32[1024,2048]{1,0:T(8,128)} fusion(f32[2048,2048]{1,0:T(8,128)} %fusion.49, s32[2048]{0:T(1024)S(1)} %get-tuple-element.25, s32[2048]{0:T(1024)S(1)} %get-tuple-element.26, bf16[2048,2048]{1,0:T(8,128)(2,1)} %all-gather.11.cloned.1.call-done, s32[]{:T(128)S(6)} %select_n.43), kind=kOutput, calls=%fused_computation.7 | convolution fusion | flops 8606711808 | bytes 29376516 | tf_op jit(solution)/shard_map/dot_general | solution.py:78
  573.0 0.0 copy-start
  573.0 0.0 copy-start.1
  573.0 0.0 reduce-scatter.3.cloned.1.call-update
  573.8 4.9 all-reduce
  578.8 0.6 select_multiply_fusion.1
  579.4 0.6 select_multiply_fusion
  582.6 38.3 %psum.39 = f32[]{:T(128)} all-reduce(f32[]{:T(128)S(6)} %add.101), channel_id=1, replica_groups=mesh['dp'=2,'row'=4,'col'=4] {'dp','row','col'}, use_global_device_ids=true, to_apply=%region_13.14 | all-reduce | flops 1 | bytes 8 | tf_op jit(solution)/shard_map/psum | solution.py:94
  621.0 7.0 reduce-scatter.5.cloned.1.call-done
  628.0 74.5 %reduce-scatter.3.cloned.1.call-done = f32[1024,512]{1,0:T(8,128)} async-done(((f32[1024,2048]{1,0:T(8,128)}), f32[1024,512]{1,0:T(8,128)}) %reduce-scatter.3.cloned.1.call-update) | async-done | bytes 2097168 | tf_op jit(solution)/shard_map/reduce_scatter | solution.py:85
  702.5 0.0 copy-done
  702.5 0.0 copy-done.1
  702.5 5.5 fusion.26
  (2 shorter events, 0.0 us)
Async XLA Ops:
  7.2 48.1 %all-gather.7.cloned.1.call-start = ((), (), s32[]{:S(2)}) async-start(), calls=%async_computation.2 | async-start | bytes 3145728 | tf_op jit(solution)/shard_map/all_gather | solution.py:55
  20.2 70.3 %all-gather.13.cloned.1.call-start = ((), (), s32[]{:S(2)}) async-start(), calls=%async_computation.5 | async-start | bytes 3145728 | tf_op jit(solution)/shard_map/all_gather | solution.py:56
  21.0 129.5 %all-gather.9.cloned.1.call-start = ((), (), s32[]{:S(2)}) async-start(), calls=%async_computation.3 | async-start | bytes 10485760 | tf_op jit(solution)/shard_map/all_gather | solution.py:59
  55.3 246.2 %all-gather.11.cloned.1.call-start = ((), (), s32[]{:S(2)}) async-start(), calls=%async_computation.4 | async-start | bytes 10485760 | tf_op jit(solution)/shard_map/all_gather | solution.py:63
  55.9 303.6 %all-gather.15.cloned.1.call-start = ((), (), s32[]{:S(2)}) async-start(), calls=%async_computation.6 | async-start | bytes 10485760 | tf_op jit(solution)/shard_map/all_gather | solution.py:60
  90.6 420.0 %all-gather.17.cloned.1.call-start = ((), (), s32[]{:S(2)}) async-start(), calls=%async_computation.7 | async-start | bytes 10485760 | tf_op jit(solution)/shard_map/all_gather | solution.py:64
  91.2 536.8 %reduce-scatter.5.cloned.1.call-start = ((), (), s32[]{:S(2)}) async-start(), calls=%async_computation.9 | async-start | bytes 10485760 | tf_op jit(solution)/shard_map/reduce_scatter | solution.py:86
  510.6 31.4 %copy-start.2 = (bf16[2048,2048]{1,0:T(8,128)(2,1)S(1)}, bf16[2048,2048]{1,0:T(8,128)(2,1)}, u32[]{:S(2)}) copy-start(bf16[2048,2048]{1,0:T(8,128)(2,1)} %all-gather.17.cloned.1.call-done) | copy-start | bytes 25165828
  556.5 146.0 %reduce-scatter.3.cloned.1.call-start = ((), (), s32[]{:S(2)}) async-start(), calls=%async_computation.8 | async-start | bytes 10485760 | tf_op jit(solution)/shard_map/reduce_scatter | solution.py:85
  573.0 129.5 %copy-start = (bf16[1024,512]{1,0:T(8,128)(2,1)S(1)}, bf16[1024,512]{1,0:T(8,128)(2,1)}, u32[]{:S(2)}) copy-start(bf16[1024,512]{1,0:T(8,128)(2,1)} %param.3) | copy-start | bytes 3145732
  573.0 129.5 %copy-start.1 = (bf16[1024,512]{1,0:T(8,128)(2,1)S(1)}, bf16[1024,512]{1,0:T(8,128)(2,1)}, u32[]{:S(2)}) copy-start(bf16[1024,512]{1,0:T(8,128)(2,1)} %param.2) | copy-start | bytes 3145732
Sparse Core Ops, SparseCore 0:
  20.4 34.8 all-gather.6
  57.4 33.1 all-gather.12
  92.1 58.2 all-gather.8
  151.9 149.6 all-gather.10
  303.0 56.4 all-gather.14
  360.9 149.6 all-gather.16
  556.6 71.2 reduce-scatter.4
  630.7 71.6 reduce-scatter.2
where the time goes:
time: 715 us
  waiting for transfers between devices  547 us (77%)
  matrix products  86.6 us (12%)
  blocking collectives  49.1 us (7%)
  between operations  17.6 us (2%)
  other arithmetic  13.9 us (2%)
    all_gather x1, waiting for transfers between devices, on_device(): lax.all_gather(wide_first, 'row', axis=1, tiled=True)  151 us
    all_gather x1, waiting for transfers between devices, on_device(): lax.all_gather(wide_second, 'row', axis=1, tiled=True)  151 us
    reduce_scatter x1, waiting for transfers between devices, on_device(): lax.psum_scatter(part_first, 'col', scatter_dimension=1, tiled=True)  74.5 us
    all_gather x1, waiting for transfers between devices, on_device(): lax.all_gather(wide_first, 'col', axis=1, tiled=True)  59.2 us
    dot_general x2, matrix products, gram(): lax.dot_general(left, right, (((0,), (0,)), ((), ())), preferred_element_...  55.6 us
    psum x1, blocking collectives, on_device(): loss = lax.psum(local_loss, ('dp', 'row', 'col'))  38.3 us
    all_gather x1, waiting for transfers between devices, on_device(): lax.all_gather(rnd_second, 'dp', axis=0, tiled=True)  34.6 us
    all_gather x1, waiting for transfers between devices, on_device(): lax.all_gather(rnd_first, 'dp', axis=0, tiled=True)  34.3 us
  transfers between devices with their start and end apart: 8, of which 8 were waited for; matrix products, arithmetic and copies ran while one was open for 6% of the time, Pallas kernels for 0%

commit v1 on v0

v1 whole, which is shorter than its diff:
```python
import jax
import jax.numpy as jnp
from jax import lax
from jax.sharding import PartitionSpec as P

inv_weight = 25.0
var_weight = 25.0
cov_weight = 1.0
eps_var = 0.0001


def shift(value, axis, count, step, inner):
    pairs = [
        (index, (index // inner + step) % count * inner + index % inner)
        for index in range(count * inner)
    ]
    return lax.ppermute(value, axis, pairs)


def core_swap(value):
    return lax.ppermute(value, "col", [(index, index ^ 1) for index in range(lax.axis_size("col"))])


def part(value, index, count):
    size = value.shape[0] // count
    return lax.dynamic_slice_in_dim(value, index * size, size, 0)


def scatter_sum(value, axis, count, inner, place):
    total = part(value, place, count).astype(jnp.float32)
    for step in range(1, count):
        sent = part(value, (place + step) % count, count).astype(jnp.bfloat16)
        total = total + shift(sent, axis, count, step, inner).astype(jnp.float32)
    return total


def collect(value, axis, count, inner, place):
    size = value.shape[0]
    whole = jnp.zeros((count * size,) + value.shape[1:], value.dtype)
    whole = lax.dynamic_update_slice_in_dim(whole, value, place * size, 0)
    for step in range(1, count):
        got = shift(value, axis, count, step, inner)
        whole = lax.dynamic_update_slice_in_dim(whole, got, (place - step) % count * size, 0)
    return whole


def outer(left, right):
    return lax.dot_general(
        left, right, (((1,), (1,)), ((), ())), preferred_element_type=jnp.float32
    )


def matmul(left, right, dim):
    return lax.dot_general(
        left, right, (((dim,), (0,)), ((), ())), preferred_element_type=jnp.float32
    )


def on_device(first_view, second_view):
    dp_count = lax.axis_size("dp")
    row_count = lax.axis_size("row")
    col_count = lax.axis_size("col")
    rows, width = first_view.shape
    total = rows * dp_count
    feat = width * row_count * col_count
    half, quarter = rows // 2, rows // 4
    x_count = col_count // 2
    x_place = lax.axis_index("col") // 2
    core = lax.axis_index("col") % 2
    z_place = lax.axis_index("row")

    views = (first_view, second_view)
    values = [view.astype(jnp.float32) for view in views]
    sums = jnp.stack([jnp.sum(value, axis=0) for value in values])
    sums = sums + shift(sums, "dp", dp_count, 1, 1)
    others = [shift(view, "dp", dp_count, 1, 1) for view in views]
    means = [sums[index] / total for index in range(2)]
    centred = [value - mean for value, mean in zip(values, means)]
    rounded = [cen.astype(jnp.bfloat16) for cen in centred]
    partner = [core_swap(rnd) for rnd in rounded]

    def reduce_piece(piece):
        piece = scatter_sum(piece, "col", x_count, 2, x_place)
        return scatter_sum(piece, "row", row_count, 1, z_place)

    def gather_piece(chunk):
        piece = collect(chunk, "row", row_count, 1, z_place)
        piece = collect(piece, "col", x_count, 2, x_place)
        return piece, core_swap(piece)

    def weighted_squares(chunk, doubled_from, piece_rows):
        size = chunk.shape[0]
        ids = (x_place * row_count + z_place) * size + jnp.arange(size, dtype=jnp.int32)
        weight = jnp.where(ids < doubled_from, jnp.float32(1.0), jnp.float32(2.0))
        return jnp.sum(chunk * chunk * weight[:, None])

    eye = jnp.eye(half, dtype=jnp.bool_)
    near = []
    lengths = []
    squares = jnp.float32(0.0)
    for index in range(2):
        both = jnp.concatenate([rounded[index], partner[index]], axis=1)
        wide = both.astype(jnp.float32)
        lengths.append(jnp.sum(wide * wide, axis=1))
        block = part(both, core, 2)
        diagonal = jnp.where(eye, jnp.float32(0.0), outer(block, block))
        cross = outer(part(both[:half], core, 2), both[half:])
        chunk = reduce_piece(jnp.concatenate([diagonal, cross], axis=0))
        squares = squares + weighted_squares(chunk, half, half + quarter)
        near.append(gather_piece(chunk.astype(jnp.bfloat16)))
    lengths = jnp.stack(lengths)
    for axis, count, inner in (("col", x_count, 2), ("row", row_count, 1)):
        lengths = lengths + sum(shift(lengths, axis, count, step, inner) for step in range(1, count))

    far = []
    cen_others, rnd_others = [], []
    for index in range(2):
        cen_other = others[index].astype(jnp.float32) - means[index]
        rnd_other = cen_other.astype(jnp.bfloat16)
        cen_others.append(cen_other)
        rnd_others.append(rnd_other)
        both = jnp.concatenate([rounded[index], partner[index]], axis=1)
        both_other = jnp.concatenate([rnd_other, core_swap(rnd_other)], axis=1)
        block = part(both, core, 2)
        piece = jnp.concatenate(
            [outer(block, both_other[:half]), outer(block, both_other[half:])], axis=0
        )
        chunk = reduce_piece(piece)
        squares = squares + jnp.sum(chunk * chunk)
        far.append(gather_piece(chunk.astype(jnp.bfloat16)))

    differ = values[0] - values[1]
    scale = total * feat / 64.0
    hinge_sum = jnp.float32(0.0)
    norm_sum = jnp.float32(0.0)
    grads = []
    for index in range(2):
        sq_own = jnp.sum(centred[index] * centred[index], axis=0)
        sq_other = jnp.sum(cen_others[index] * cen_others[index], axis=0)
        spread = jnp.sqrt((sq_own + sq_other) / (total - 1) + eps_var)
        hinge_sum = hinge_sum + jnp.sum(jnp.maximum(1.0 - spread, 0.0))
        rnd, rnd_other = rounded[index], rnd_others[index]
        norms = jnp.sum(jnp.square(rnd.astype(jnp.float32)), axis=0) + jnp.sum(
            jnp.square(rnd_other.astype(jnp.float32)), axis=0
        )
        norm_sum = norm_sum + jnp.sum(jnp.square(norms / (total - 1)))
        mine, theirs = near[index]
        low = jnp.where(core == 0, mine, theirs)
        high = jnp.where(core == 0, theirs, mine)
        cross = jnp.concatenate([low[half:], high[half:]], axis=0)
        far_low = jnp.where(core == 0, far[index][0], far[index][1])
        far_high = jnp.where(core == 0, far[index][1], far[index][0])
        top = (
            matmul(low[:half], rnd[:half], 1)
            + matmul(cross, rnd[half:], 1)
            + matmul(far_low[:half], rnd_other[:half], 1)
            + matmul(far_low[half:], rnd_other[half:], 1)
        )
        bottom = (
            matmul(high[:half], rnd[half:], 1)
            + matmul(cross, rnd[:half], 0)
            + matmul(far_high[:half], rnd_other[:half], 1)
            + matmul(far_high[half:], rnd_other[half:], 1)
        )
        product = jnp.concatenate([top, bottom], axis=0)
        product = (
            product + (lengths[index][:, None] - norms[None, :]) * rnd.astype(jnp.float32)
        ) / (total - 1)
        sign = 1.0 - 2.0 * index
        invariant = sign * 2.0 * inv_weight * differ / (total * feat)
        active = jnp.where(spread < 1.0, jnp.float32(1.0), jnp.float32(0.0))
        varterm = -var_weight * centred[index] * active / (feat * spread * (total - 1))
        covterm = 4.0 * cov_weight * product / (feat * (total - 1))
        grads.append(scale * (invariant + varterm + covterm))

    length_sum = jnp.sum(jnp.square(lengths / (total - 1)))
    cov_part = (
        squares / (total - 1) / (total - 1)
        + length_sum / (row_count * col_count)
        - norm_sum / dp_count
    ) / feat
    local_loss = (
        inv_weight * jnp.sum(differ * differ) / (total * feat)
        + var_weight * hinge_sum / feat / dp_count
        + cov_weight * cov_part
    )
    loss = lax.psum(local_loss, ("dp", "row", "col"))
    return loss, grads[0], grads[1]


def solution(mesh):
    return jax.shard_map(
        on_device,
        mesh=mesh,
        in_specs=(P("dp", ("row", "col")), P("dp", ("row", "col"))),
        out_specs=(P(), P("dp", ("row", "col")), P("dp", ("row", "col"))),
        check_vma=False,
    )
```

time: 715 us -> 261 us (0.37)
  waiting for transfers between devices: 547 us -> 66.1 us
  matrix products: 86.6 us -> 20.7 us
  starting transfers between devices: 0.31 us -> 55.8 us
  local copies, waits for them, and re-layouts: 0.01 us -> 25 us
  other arithmetic: 13.9 us -> 38 us
  between operations: 17.6 us -> 8.11 us
    all_gather x6 -> x0, waiting for transfers between devices: 464 us -> none  [the longest x1 151 us: on_device(): lax.all_gather(wide_first, 'row', axis=1, tiled=True)]
    reduce_scatter x2 -> x0, waiting for transfers between devices: 81.5 us -> none  [the longest x1 74.5 us: on_device(): lax.psum_scatter(part_first, 'col', scatter_dimension=1, tiled=True)]
    ppermute x0 -> x47, waiting for transfers between devices: none -> 66.1 us  [the longest x39 66 us: shift(): return lax.ppermute(value, axis, pairs)]
    dot_general x4 -> x24, matrix products: 86.6 us -> 20.7 us  [the longest x8 13.4 us: outer(): lax.dot_general(left, right, (((1,), (1,)), ((), ())), preferred_element_...]
    ppermute x0 -> x47, starting transfers between devices: none -> 55.8 us  [the longest x39 54.1 us: shift(): return lax.ppermute(value, axis, pairs)]
    dynamic_update_slice x0 -> x20, local copies, waits for them, and re-layouts: none -> 19.1 us  [the longest x16 17.2 us: collect(): lax.dynamic_update_slice_in_dim(whole, got, (place - step) % count * size...]
    psum x2 -> x0, blocking collectives: 10.8 us -> none  [the longest x1 5.86 us: on_device(): lax.psum((jnp.sum(first, axis=0), jnp.sum(second, axis=0)), 'dp')]
  transfers between devices with their start and end apart: 8 -> 47, of which waited for: 8 -> 7; matrix products, arithmetic and copies ran while one was open for 6% -> 27% of each run, Pallas kernels for 0% -> 0%
where the time goes in v1:
time: 261 us; the launch traced here: 259 us
  waiting for transfers between devices  66.1 us (25%)
  starting transfers between devices  55.8 us (21%)
  blocking collectives  45.4 us (17%)
  other arithmetic  38 us (15%)
  local copies, waits for them, and re-layouts  25 us (10%)
  matrix products  20.7 us (8%)
  between operations  8.11 us (3%)
    ppermute x39, waiting for transfers between devices, shift(): return lax.ppermute(value, axis, pairs)  66 us
    ppermute x39, starting transfers between devices, shift(): return lax.ppermute(value, axis, pairs)  54.1 us
    psum x1, blocking collectives, on_device(): loss = lax.psum(local_loss, ('dp', 'row', 'col'))  45.4 us
    dynamic_update_slice x16, local copies, waits for them, and re-layouts, collect(): lax.dynamic_update_slice_in_dim(whole, got, (place - step) % count * size...  17.2 us
    dot_general x8, matrix products, outer(): lax.dot_general(left, right, (((1,), (1,)), ((), ())), preferred_element_...  13.4 us
    dot_general x16, matrix products, matmul(): lax.dot_general(left, right, (((dim,), (0,)), ((), ())), preferred_elemen...  7.29 us
    add x4, other arithmetic, scatter_sum(): total = total + shift(sent, axis, count, step, inner).astype(jnp.float32)  6.06 us
  transfers between devices with their start and end apart: 47, of which 7 were waited for; matrix products, arithmetic and copies ran while one was open for 27% of the time, Pallas kernels for 0%

profile of v1, /device:TPU:0, one launch (start us, length us, event | category | flops | bytes accessed | tf_op | source)
XLA Modules:
  0.0 259.1 jit_solution(2513593914379358609)
XLA Ops:
  0.7 3.0 %collective-permute-start.2 = (bf16[1024,512]{1,0:T(8,128)(2,1)}, bf16[1024,512]{1,0:T(8,128)(2,1)S(1)}, u32[]{:S(2)}, u32[]{:S(2)}) collective-permute-start(bf16[1024,512]{1,0:T(8,128)(2,1)} %param.3), channel_id=1, source_target_pairs={{0,16},{16,0},{1,17},{17,1},{2,18},{18,2},{3,19},{19,3},{4,20},{20... | collective-permute-start | bytes 3145736 | tf_op jit(solution)/shard_map/ppermute | solution.py:17
  3.8 1.4 convert_reduce_fusion
  5.2 1.4 convert_reduce_fusion.1
  6.6 2.0 collective-permute-start
  8.6 41.0 %collective-permute-done = f32[2,512]{1,0:T(2,128)S(1)} collective-permute-done((f32[2,512]{1,0:T(2,128)S(1)}, f32[2,512]{1,0:T(2,128)S(1)}, u32[]{:S(2)}, u32[]{:S(2)}) %collective-permute-start) | collective-permute-done | bytes 4128 | tf_op jit(solution)/shard_map/ppermute | solution.py:17
  49.7 2.9 %multiply_reduce_fusion.2 = (f32[512]{0:T(512)S(1)}, bf16[1024,512]{1,0:T(8,128)(2,1)}, f32[512]{0:T(512)S(1)}, f32[512]{0:T(512)S(1)}, f32[512]{0:T(512)S(1)}, ...) fusion(f32[512]{0:T(512)S(1)} %bitcast.28, ...), kind=kLoop, calls=%fused_computation.59 | loop fusion | flops 18345984 | bytes 8409092 | tf_op jit(solution)/shard_map/reduce_sum | solution.py:143
  54.1 1.3 select_multiply_fusion
  57.4 1.2 multiply_reduce_fusion.12
  59.9 1.6 pad_slice_fusion.7
  61.4 1.6 fusion.48
  63.8 1.1 fusion.59
  64.9 1.7 collective-permute-start.9
  66.6 1.6 pad_slice_fusion.3
  69.0 1.9 fusion.52
  72.1 1.7 multiply_reduce_fusion
  73.8 1.7 multiply_reduce_fusion.1
  75.5 1.8 collective-permute-start.23
  77.3 1.8 fusion.36
  79.1 2.2 fusion.56
  81.4 2.2 fusion.33
  83.6 2.2 fusion.54
  85.8 1.2 fusion.43
  87.0 3.6 %collective-permute-start.26 = (f32[2,1024]{1,0:T(2,128)S(1)}, f32[2,1024]{1,0:T(2,128)S(1)}, u32[]{:S(2)}, u32[]{:S(2)}) collective-permute-start(f32[2,1024]{1,0:T(2,128)S(1)} %fusion.125), channel_id=1, source_target_pairs={{0,12},{4,0},{8,4},{12,8},{1,13},{5,1},{9,5},{13,9},{2,14},{6,2},{... | collective-permute-start | bytes 24584 | tf_op jit(solution)/shard_map/ppermute | solution.py:17
  90.7 1.0 collective-permute-start.25
  91.7 1.2 fusion.39
  93.5 2.7 %collective-permute-done.24 = f32[2,1024]{1,0:T(2,128)S(1)} collective-permute-done((f32[2,1024]{1,0:T(2,128)S(1)}, f32[2,1024]{1,0:T(2,128)S(1)}, u32[]{:S(2)}, u32[]{:S(2)}) %collective-permute-start.24) | collective-permute-done | bytes 8224 | tf_op jit(solution)/shard_map/ppermute | solution.py:17
  98.0 1.6 fusion.61
  99.6 2.4 collective-permute-start.12
  102.9 1.2 fusion.65
  104.2 3.2 %collective-permute-done.12 = bf16[96,512]{1,0:T(8,128)(2,1)S(1)} collective-permute-done((bf16[96,512]{1,0:T(8,128)(2,1)S(1)}, bf16[96,512]{1,0:T(8,128)(2,1)S(1)}, u32[]{:S(2)}, u32[]{:S(2)}) %collective-permute-start.12) | collective-permute-done | bytes 98336 | tf_op jit(solution)/shard_map/ppermute | solution.py:17
  107.3 1.3 collective-permute-start.7
  108.7 5.9 %collective-permute-done.11 = bf16[96,512]{1,0:T(8,128)(2,1)S(1)} collective-permute-done((bf16[96,512]{1,0:T(8,128)(2,1)S(1)}, bf16[96,512]{1,0:T(8,128)(2,1)S(1)}, u32[]{:S(2)}, u32[]{:S(2)}) %collective-permute-start.11) | collective-permute-done | bytes 98336 | tf_op jit(solution)/shard_map/ppermute | solution.py:17
  116.1 3.5 %collective-permute-start.37 = (bf16[96,512]{1,0:T(8,128)(2,1)}, bf16[96,512]{1,0:T(8,128)(2,1)}, u32[]{:S(2)}, u32[]{:S(2)}) collective-permute-start(bf16[96,512]{1,0:T(8,128)(2,1)} %get-tuple-element.15), channel_id=1, source_target_pairs={{0,4},{4,8},{8,12},{12,0},{1,5},{5,9},{9,13},{13,1},{2,6},{6,10},{... | collective-permute-start | bytes 294920 | tf_op jit(solution)/shard_map/ppermute | solution.py:17
  119.6 5.8 %collective-permute-done.6 = bf16[96,512]{1,0:T(8,128)(2,1)S(1)} collective-permute-done((bf16[96,512]{1,0:T(8,128)(2,1)S(1)}, bf16[96,512]{1,0:T(8,128)(2,1)S(1)}, u32[]{:S(2)}, u32[]{:S(2)}) %collective-permute-start.6) | collective-permute-done | bytes 98336 | tf_op jit(solution)/shard_map/ppermute | solution.py:17
  127.9 1.1 constant_dynamic-update-slice_fusion.23
  129.1 2.1 collective-permute-start.27
  131.1 1.7 fusion.45
  132.9 2.7 %collective-permute-start.28 = (bf16[96,512]{1,0:T(8,128)(2,1)S(1)}, bf16[96,512]{1,0:T(8,128)(2,1)S(1)}, u32[]{:S(2)}, u32[]{:S(2)}) collective-permute-start(bf16[96,512]{1,0:T(8,128)(2,1)S(1)} %get-tuple-element.19), channel_id=1, source_target_pairs={{0,8},{4,12},{8,0},{12,4},{1,9},{5,13},{9,1},{13,5},{2,10},{6,14},... | collective-permute-start | bytes 294920 | tf_op jit(solution)/shard_map/ppermute | solution.py:17
  135.7 1.5 fusion.41
  138.2 1.5 constant_dynamic-update-slice_fusion.10
  140.6 1.8 collective-permute-start.16
  142.4 1.5 constant_dynamic-update-slice_fusion.9
  144.9 2.7 %collective-permute-start.22 = (bf16[128,512]{1,0:T(8,128)(2,1)S(1)}, bf16[128,512]{1,0:T(8,128)(2,1)S(1)}, u32[]{:S(2)}, u32[]{:S(2)}) collective-permute-start(bf16[128,512]{1,0:T(8,128)(2,1)S(1)} %get-tuple-element.54), channel_id=1, source_target_pairs={{0,12},{4,0},{8,4},{12,8},{1,13},{5,1},{9,5},{13,9},{2,14},{6,2},{... | collective-permute-start | bytes 393224 | tf_op jit(solution)/shard_map/ppermute | solution.py:17
  147.7 1.5 constant_dynamic-update-slice_fusion.8
  149.9 1.0 constant_dynamic-update-slice_fusion.7
  150.9 5.8 %collective-permute-start.15 = (bf16[128,512]{1,0:T(8,128)(2,1)S(1)}, bf16[128,512]{1,0:T(8,128)(2,1)S(1)}, u32[]{:S(2)}, u32[]{:S(2)}) collective-permute-start(bf16[128,512]{1,0:T(8,128)(2,1)S(1)} %get-tuple-element.56), channel_id=1, source_target_pairs={{0,4},{4,8},{8,12},{12,0},{1,5},{5,9},{9,13},{13,1},{2,6},{6,10},{... | collective-permute-start | bytes 393224 | tf_op jit(solution)/shard_map/ppermute | solution.py:17
  156.7 6.5 %collective-permute-done.21 = bf16[128,512]{1,0:T(8,128)(2,1)S(1)} collective-permute-done((bf16[128,512]{1,0:T(8,128)(2,1)S(1)}, bf16[128,512]{1,0:T(8,128)(2,1)S(1)}, u32[]{:S(2)}, u32[]{:S(2)}) %collective-permute-start.21) | collective-permute-done | bytes 131104 | tf_op jit(solution)/shard_map/ppermute | solution.py:17
  164.0 1.2 collective-permute-start.30
  166.0 3.8 %collective-permute-start.44 = (bf16[128,512]{1,0:T(8,128)(2,1)}, bf16[128,512]{1,0:T(8,128)(2,1)}, u32[]{:S(2)}, u32[]{:S(2)}) collective-permute-start(bf16[128,512]{1,0:T(8,128)(2,1)} %get-tuple-element.17), channel_id=1, source_target_pairs={{0,12},{4,0},{8,4},{12,8},{1,13},{5,1},{9,5},{13,9},{2,14},{6,2},{... | collective-permute-start | bytes 393224 | tf_op jit(solution)/shard_map/ppermute | solution.py:17
  175.1 1.6 constant_dynamic-update-slice_fusion.4
  176.6 2.1 collective-permute-start.33
  178.7 1.6 constant_dynamic-update-slice_fusion.3
  180.3 2.9 %collective-permute-start.34 = (bf16[128,512]{1,0:T(8,128)(2,1)}, bf16[128,512]{1,0:T(8,128)(2,1)S(1)}, u32[]{:S(2)}, u32[]{:S(2)}) collective-permute-start(bf16[128,512]{1,0:T(8,128)(2,1)} %get-tuple-element.21), channel_id=1, source_target_pairs={{0,12},{4,0},{8,4},{12,8},{1,13},{5,1},{9,5},{13,9},{2,14},{6,2},{... | collective-permute-start | bytes 393224 | tf_op jit(solution)/shard_map/ppermute | solution.py:17
  183.2 1.6 constant_dynamic-update-slice_fusion.2
  187.0 1.8 constant_dynamic-update-slice_fusion.6
  189.4 1.1 collective-permute-start.35
  192.3 45.4 %psum.7 = f32[]{:T(128)} all-reduce(f32[]{:T(128)S(6)} %add.452), channel_id=1, replica_groups=mesh['dp'=2,'row'=4,'col'=4] {'dp','row','col'}, use_global_device_ids=true, to_apply=%region_22.23 | all-reduce | flops 1 | bytes 8 | tf_op jit(solution)/shard_map/psum | solution.py:187
  237.8 1.9 constant_dynamic-update-slice_fusion.18
  239.9 1.2 constant_dynamic-update-slice_fusion
  241.6 1.1 constant_dynamic-update-slice_fusion.12
  242.8 1.2 broadcast_select_fusion.5
  244.1 1.2 broadcast_select_fusion.7
  247.4 1.1 copy-done.1
  255.2 3.8 %fusion.15 = (f32[1024,512]{1,0:T(8,128)}, f32[1024,512]{1,0:T(8,128)}) fusion(bf16[1024,512]{1,0:T(8,128)(2,1)S(1)} %copy-done.6, f32[512,512]{1,0:T(8,128)S(1)} %fusion.25, f32[512,512]{1,0:T(8,128)S(1)} %fusion.27, bf16[1024,512]{1,0:T(8,128)(2,1)S(1)} %copy-done.8, f32[512]{0:T(512)S(1)} %copy-done.32, f32[1024]{0:T(1024)S(1)} %bitcast.30, ...), kind=kLoop, calls=%fused_computation.48 | loop fusion | flops 16252928 | bytes 10510336 | tf_op jit(solution)/shard_map/mul | solution.py:174
  (198 shorter events, 33.0 us)
Async XLA Ops:
  0.6 49.0 %copy-start.5 = (bf16[1024,512]{1,0:T(8,128)(2,1)S(1)}, bf16[1024,512]{1,0:T(8,128)(2,1)}, u32[]{:S(2)}) copy-start(bf16[1024,512]{1,0:T(8,128)(2,1)} %param.3) | copy-start | bytes 3145732
  0.6 49.0 %copy-start.7 = (bf16[1024,512]{1,0:T(8,128)(2,1)S(1)}, bf16[1024,512]{1,0:T(8,128)(2,1)}, u32[]{:S(2)}) copy-start(bf16[1024,512]{1,0:T(8,128)(2,1)} %param.2) | copy-start | bytes 3145732
  0.7 49.0 %collective-permute-start.2 = (bf16[1024,512]{1,0:T(8,128)(2,1)}, bf16[1024,512]{1,0:T(8,128)(2,1)S(1)}, u32[]{:S(2)}, u32[]{:S(2)}) collective-permute-start(bf16[1024,512]{1,0:T(8,128)(2,1)} %param.3), channel_id=1, source_target_pairs={{0,16},{16,0},{1,17},{17,1},{2,18},{18,2},{3,19},{19,3},{4,20},{20... | collective-permute-start | bytes 3145736 | tf_op jit(solution)/shard_map/ppermute | solution.py:17
  3.7 46.0 %collective-permute-start.1 = (bf16[1024,512]{1,0:T(8,128)(2,1)}, bf16[1024,512]{1,0:T(8,128)(2,1)S(1)}, u32[]{:S(2)}, u32[]{:S(2)}) collective-permute-start(bf16[1024,512]{1,0:T(8,128)(2,1)} %param.2), channel_id=1, source_target_pairs={{0,16},{16,0},{1,17},{17,1},{2,18},{18,2},{3,19},{19,3},{4,20},{20... | collective-permute-start | bytes 3145736 | tf_op jit(solution)/shard_map/ppermute | solution.py:17
  6.6 43.0 %collective-permute-start = (f32[2,512]{1,0:T(2,128)S(1)}, f32[2,512]{1,0:T(2,128)S(1)}, u32[]{:S(2)}, u32[]{:S(2)}) collective-permute-start(f32[2,512]{1,0:T(2,128)S(1)} %pad_maximum_fusion.13), channel_id=1, source_target_pairs={{0,16},{16,0},{1,17},{17,1},{2,18},{18,2},{3,19},{19,3},{4,20},{20... | collective-permute-start | bytes 12296 | tf_op jit(solution)/shard_map/ppermute | solution.py:17
  52.6 7.3 %collective-permute-start.8 = (bf16[1024,512]{1,0:T(8,128)(2,1)S(1)}, bf16[1024,512]{1,0:T(8,128)(2,1)}, u32[]{:S(2)}, u32[]{:S(2)}) collective-permute-start(bf16[1024,512]{1,0:T(8,128)(2,1)S(1)} %get-tuple-element.51), channel_id=1, source_target_pairs={{0,1},{1,0},{2,3},{3,2},{4,5},{5,4},{6,7},{7,6},{8,9},{9,8},{10,11... | collective-permute-start | bytes 3145736 | tf_op jit(solution)/shard_map/ppermute | solution.py:21
  53.1 13.5 %collective-permute-start.3 = (bf16[1024,512]{1,0:T(8,128)(2,1)S(1)}, bf16[1024,512]{1,0:T(8,128)(2,1)}, u32[]{:S(2)}, u32[]{:S(2)}) collective-permute-start(bf16[1024,512]{1,0:T(8,128)(2,1)S(1)} %get-tuple-element.52), channel_id=1, source_target_pairs={{0,1},{1,0},{2,3},{3,2},{4,5},{5,4},{6,7},{7,6},{8,9},{9,8},{10,11... | collective-permute-start | bytes 3145736 | tf_op jit(solution)/shard_map/ppermute | solution.py:21
  53.6 23.7 %collective-permute-start.13 = (bf16[1024,512]{1,0:T(8,128)(2,1)S(1)}, bf16[1024,512]{1,0:T(8,128)(2,1)}, u32[]{:S(2)}, u32[]{:S(2)}) collective-permute-start(bf16[1024,512]{1,0:T(8,128)(2,1)S(1)} %get-tuple-element.50), channel_id=1, source_target_pairs={{0,1},{1,0},{2,3},{3,2},{4,5},{5,4},{6,7},{7,6},{8,9},{9,8},{10,11... | collective-permute-start | bytes 3145736 | tf_op jit(solution)/shard_map/ppermute | solution.py:21
  53.6 27.7 %collective-permute-start.18 = (bf16[1024,512]{1,0:T(8,128)(2,1)}, bf16[1024,512]{1,0:T(8,128)(2,1)}, u32[]{:S(2)}, u32[]{:S(2)}) collective-permute-start(bf16[1024,512]{1,0:T(8,128)(2,1)} %get-tuple-element.25), channel_id=1, source_target_pairs={{0,1},{1,0},{2,3},{3,2},{4,5},{5,4},{6,7},{7,6},{8,9},{9,8},{10,11... | collective-permute-start | bytes 3145736 | tf_op jit(solution)/shard_map/ppermute | solution.py:21
  63.8 2.8 %copy-start.11 = (f32[512,512]{1,0:T(8,128)}, f32[512,512]{1,0:T(8,128)S(1)}, u32[]{:S(2)}) copy-start(f32[512,512]{1,0:T(8,128)S(1)} %convolution_select_fusion) | copy-start | bytes 3145732
  64.9 33.1 %collective-permute-start.9 = (bf16[384,512]{1,0:T(8,128)(2,1)}, bf16[384,512]{1,0:T(8,128)(2,1)}, u32[]{:S(2)}, u32[]{:S(2)}) collective-permute-start(bf16[384,512]{1,0:T(8,128)(2,1)} %fusion.59), channel_id=1, source_target_pairs={{0,2},{1,3},{2,0},{3,1},{4,6},{5,7},{6,4},{7,5},{8,10},{9,11},{10,... | collective-permute-start | bytes 1179656 | tf_op jit(solution)/shard_map/ppermute | solution.py:17
  71.8 31.0 %collective-permute-start.4 = (bf16[384,512]{1,0:T(8,128)(2,1)S(1)}, bf16[384,512]{1,0:T(8,128)(2,1)}, u32[]{:S(2)}, u32[]{:S(2)}) collective-permute-start(bf16[384,512]{1,0:T(8,128)(2,1)S(1)} %fusion.63), channel_id=1, source_target_pairs={{0,2},{1,3},{2,0},{3,1},{4,6},{5,7},{6,4},{7,5},{8,10},{9,11},{10,... | collective-permute-start | bytes 1179656 | tf_op jit(solution)/shard_map/ppermute | solution.py:17
  75.5 11.5 %collective-permute-start.23 = (f32[2,1024]{1,0:T(2,128)S(1)}, f32[2,1024]{1,0:T(2,128)S(1)}, u32[]{:S(2)}, u32[]{:S(2)}) collective-permute-start(f32[2,1024]{1,0:T(2,128)S(1)} %pad_maximum_fusion.12), channel_id=1, source_target_pairs={{0,2},{1,3},{2,0},{3,1},{4,6},{5,7},{6,4},{7,5},{8,10},{9,11},{10,... | collective-permute-start | bytes 24584 | tf_op jit(solution)/shard_map/ppermute | solution.py:17
  79.1 6.6 %copy-start.14 = (f32[512,512]{1,0:T(8,128)}, f32[512,512]{1,0:T(8,128)S(1)}, u32[]{:S(2)}) copy-start(f32[512,512]{1,0:T(8,128)S(1)} %fusion.36) | copy-start | bytes 3145732
  81.3 4.4 %copy-start.4 = (f32[512,512]{1,0:T(8,128)}, f32[512,512]{1,0:T(8,128)S(1)}, u32[]{:S(2)}) copy-start(f32[512,512]{1,0:T(8,128)S(1)} %fusion.56) | copy-start | bytes 3145732
  83.6 8.1 %copy-start.12 = (f32[512,512]{1,0:T(8,128)}, f32[512,512]{1,0:T(8,128)S(1)}, u32[]{:S(2)}) copy-start(f32[512,512]{1,0:T(8,128)S(1)} %fusion.33) | copy-start | bytes 3145732
  85.8 7.1 %copy-start.2 = (f32[512,512]{1,0:T(8,128)}, f32[512,512]{1,0:T(8,128)S(1)}, u32[]{:S(2)}) copy-start(f32[512,512]{1,0:T(8,128)S(1)} %fusion.54) | copy-start | bytes 3145732
  87.0 5.9 %collective-permute-start.26 = (f32[2,1024]{1,0:T(2,128)S(1)}, f32[2,1024]{1,0:T(2,128)S(1)}, u32[]{:S(2)}, u32[]{:S(2)}) collective-permute-start(f32[2,1024]{1,0:T(2,128)S(1)} %fusion.125), channel_id=1, source_target_pairs={{0,12},{4,0},{8,4},{12,8},{1,13},{5,1},{9,5},{13,9},{2,14},{6,2},{... | collective-permute-start | bytes 24584 | tf_op jit(solution)/shard_map/ppermute | solution.py:17
  90.7 5.4 %collective-permute-start.24 = (f32[2,1024]{1,0:T(2,128)S(1)}, f32[2,1024]{1,0:T(2,128)S(1)}, u32[]{:S(2)}, u32[]{:S(2)}) collective-permute-start(f32[2,1024]{1,0:T(2,128)S(1)} %fusion.125), channel_id=1, source_target_pairs={{0,4},{4,8},{8,12},{12,0},{1,5},{5,9},{9,13},{13,1},{2,6},{6,10},{... | collective-permute-start | bytes 24584 | tf_op jit(solution)/shard_map/ppermute | solution.py:17
  90.7 6.0 %collective-permute-start.25 = (f32[2,1024]{1,0:T(2,128)S(1)}, f32[2,1024]{1,0:T(2,128)S(1)}, u32[]{:S(2)}, u32[]{:S(2)}) collective-permute-start(f32[2,1024]{1,0:T(2,128)S(1)} %fusion.125), channel_id=1, source_target_pairs={{0,8},{4,12},{8,0},{12,4},{1,9},{5,13},{9,1},{13,5},{2,10},{6,14},... | collective-permute-start | bytes 24584 | tf_op jit(solution)/shard_map/ppermute | solution.py:17
  92.9 36.1 %collective-permute-start.14 = (bf16[512,512]{1,0:T(8,128)(2,1)}, bf16[512,512]{1,0:T(8,128)(2,1)}, u32[]{:S(2)}, u32[]{:S(2)}) collective-permute-start(bf16[512,512]{1,0:T(8,128)(2,1)} %fusion.43), channel_id=1, source_target_pairs={{0,2},{1,3},{2,0},{3,1},{4,6},{5,7},{6,4},{7,5},{8,10},{9,11},{10,... | collective-permute-start | bytes 1572872 | tf_op jit(solution)/shard_map/ppermute | solution.py:17
  96.1 36.8 %collective-permute-start.19 = (bf16[512,512]{1,0:T(8,128)(2,1)}, bf16[512,512]{1,0:T(8,128)(2,1)}, u32[]{:S(2)}, u32[]{:S(2)}) collective-permute-start(bf16[512,512]{1,0:T(8,128)(2,1)} %fusion.39), channel_id=1, source_target_pairs={{0,2},{1,3},{2,0},{3,1},{4,6},{5,7},{6,4},{7,5},{8,10},{9,11},{10,... | collective-permute-start | bytes 1572872 | tf_op jit(solution)/shard_map/ppermute | solution.py:17
  97.9 4.9 %copy-start.10 = (f32[512,512]{1,0:T(8,128)S(1)}, f32[512,512]{1,0:T(8,128)}, u32[]{:S(2)}) copy-start(f32[512,512]{1,0:T(8,128)} %copy-done.9) | copy-start | bytes 3145732
  97.9 4.9 %copy-start.19 = (f32[256,512]{1,0:T(8,128)S(1)}, f32[256,512]{1,0:T(8,128)}, u32[]{:S(2)}) copy-start(f32[256,512]{1,0:T(8,128)} %copy-done.18) | copy-start | bytes 1572868
  99.6 7.7 %collective-permute-start.12 = (bf16[96,512]{1,0:T(8,128)(2,1)S(1)}, bf16[96,512]{1,0:T(8,128)(2,1)S(1)}, u32[]{:S(2)}, u32[]{:S(2)}) collective-permute-start(bf16[96,512]{1,0:T(8,128)(2,1)S(1)} %get-tuple-element.69), channel_id=1, source_target_pairs={{0,12},{4,0},{8,4},{12,8},{1,13},{5,1},{9,5},{13,9},{2,14},{6,2},{... | collective-permute-start | bytes 294920 | tf_op jit(solution)/shard_map/ppermute | solution.py:17
  102.1 12.5 %collective-permute-start.11 = (bf16[96,512]{1,0:T(8,128)(2,1)S(1)}, bf16[96,512]{1,0:T(8,128)(2,1)S(1)}, u32[]{:S(2)}, u32[]{:S(2)}) collective-permute-start(bf16[96,512]{1,0:T(8,128)(2,1)S(1)} %get-tuple-element.70), channel_id=1, source_target_pairs={{0,8},{4,12},{8,0},{12,4},{1,9},{5,13},{9,1},{13,5},{2,10},{6,14},... | collective-permute-start | bytes 294920 | tf_op jit(solution)/shard_map/ppermute | solution.py:17
  102.8 22.9 %copy-start.34 = (f32[96]{0:T(128)S(1)}, f32[96]{0:T(128)}, u32[]{:S(2)}) copy-start(f32[96]{0:T(128)} %compare_select_fusion) | copy-start | bytes 1156
  102.8 11.8 %collective-permute-start.10 = (bf16[96,512]{1,0:T(8,128)(2,1)S(1)}, bf16[96,512]{1,0:T(8,128)(2,1)S(1)}, u32[]{:S(2)}, u32[]{:S(2)}) collective-permute-start(bf16[96,512]{1,0:T(8,128)(2,1)S(1)} %get-tuple-element.68), channel_id=1, source_target_pairs={{0,4},{4,8},{8,12},{12,0},{1,5},{5,9},{9,13},{13,1},{2,6},{6,10},{... | collective-permute-start | bytes 294920 | tf_op jit(solution)/shard_map/ppermute | solution.py:17
  104.1 22.4 %copy-start.17 = (f32[384,512]{1,0:T(8,128)}, f32[384,512]{1,0:T(8,128)S(1)}, u32[]{:S(2)}) copy-start(f32[384,512]{1,0:T(8,128)S(1)} %fusion.65) | copy-start | bytes 2359300
  107.3 8.8 %collective-permute-start.7 = (bf16[96,512]{1,0:T(8,128)(2,1)S(1)}, bf16[96,512]{1,0:T(8,128)(2,1)S(1)}, u32[]{:S(2)}, u32[]{:S(2)}) collective-permute-start(bf16[96,512]{1,0:T(8,128)(2,1)S(1)} %get-tuple-element.66), channel_id=1, source_target_pairs={{0,12},{4,0},{8,4},{12,8},{1,13},{5,1},{9,5},{13,9},{2,14},{6,2},{... | collective-permute-start | bytes 294920 | tf_op jit(solution)/shard_map/ppermute | solution.py:17
  114.6 10.8 %collective-permute-start.6 = (bf16[96,512]{1,0:T(8,128)(2,1)S(1)}, bf16[96,512]{1,0:T(8,128)(2,1)S(1)}, u32[]{:S(2)}, u32[]{:S(2)}) collective-permute-start(bf16[96,512]{1,0:T(8,128)(2,1)S(1)} %get-tuple-element.67), channel_id=1, source_target_pairs={{0,8},{4,12},{8,0},{12,4},{1,9},{5,13},{9,1},{13,5},{2,10},{6,14},... | collective-permute-start | bytes 294920 | tf_op jit(solution)/shard_map/ppermute | solution.py:17
  114.6 10.8 %collective-permute-start.5 = (bf16[96,512]{1,0:T(8,128)(2,1)S(1)}, bf16[96,512]{1,0:T(8,128)(2,1)S(1)}, u32[]{:S(2)}, u32[]{:S(2)}) collective-permute-start(bf16[96,512]{1,0:T(8,128)(2,1)S(1)} %get-tuple-element.65), channel_id=1, source_target_pairs={{0,4},{4,8},{8,12},{12,0},{1,5},{5,9},{9,13},{13,1},{2,6},{6,10},{... | collective-permute-start | bytes 294920 | tf_op jit(solution)/shard_map/ppermute | solution.py:17
  116.1 10.4 %copy-start.25 = (bf16[96,512]{1,0:T(8,128)(2,1)}, bf16[96,512]{1,0:T(8,128)(2,1)S(1)}, u32[]{:S(2)}) copy-start(bf16[96,512]{1,0:T(8,128)(2,1)S(1)} %collective-permute-done.7) | copy-start | bytes 294916
  116.1 21.1 %collective-permute-start.37 = (bf16[96,512]{1,0:T(8,128)(2,1)}, bf16[96,512]{1,0:T(8,128)(2,1)}, u32[]{:S(2)}, u32[]{:S(2)}) collective-permute-start(bf16[96,512]{1,0:T(8,128)(2,1)} %get-tuple-element.15), channel_id=1, source_target_pairs={{0,4},{4,8},{8,12},{12,0},{1,5},{5,9},{9,13},{13,1},{2,6},{6,10},{... | collective-permute-start | bytes 294920 | tf_op jit(solution)/shard_map/ppermute | solution.py:17
  125.4 15.1 %collective-permute-start.38 = (bf16[96,512]{1,0:T(8,128)(2,1)}, bf16[96,512]{1,0:T(8,128)(2,1)}, u32[]{:S(2)}, u32[]{:S(2)}) collective-permute-start(bf16[96,512]{1,0:T(8,128)(2,1)} %get-tuple-element.15), channel_id=1, source_target_pairs={{0,8},{4,12},{8,0},{12,4},{1,9},{5,13},{9,1},{13,5},{2,10},{6,14},... | collective-permute-start | bytes 294920 | tf_op jit(solution)/shard_map/ppermute | solution.py:17
  125.4 22.2 %collective-permute-start.39 = (bf16[96,512]{1,0:T(8,128)(2,1)}, bf16[96,512]{1,0:T(8,128)(2,1)}, u32[]{:S(2)}, u32[]{:S(2)}) collective-permute-start(bf16[96,512]{1,0:T(8,128)(2,1)} %get-tuple-element.15), channel_id=1, source_target_pairs={{0,12},{4,0},{8,4},{12,8},{1,13},{5,1},{9,5},{13,9},{2,14},{6,2},{... | collective-permute-start | bytes 294920 | tf_op jit(solution)/shard_map/ppermute | solution.py:17
  129.0 6.6 %copy-start.3 = (f32[512,512]{1,0:T(8,128)S(1)}, f32[512,512]{1,0:T(8,128)}, u32[]{:S(2)}) copy-start(f32[512,512]{1,0:T(8,128)} %copy-done.2) | copy-start | bytes 3145732
  129.1 6.6 %copy-start.13 = (f32[512,512]{1,0:T(8,128)S(1)}, f32[512,512]{1,0:T(8,128)}, u32[]{:S(2)}) copy-start(f32[512,512]{1,0:T(8,128)} %copy-done.12) | copy-start | bytes 3145732
  129.1 10.7 %collective-permute-start.27 = (bf16[96,512]{1,0:T(8,128)(2,1)S(1)}, bf16[96,512]{1,0:T(8,128)(2,1)S(1)}, u32[]{:S(2)}, u32[]{:S(2)}) collective-permute-start(bf16[96,512]{1,0:T(8,128)(2,1)S(1)} %get-tuple-element.19), channel_id=1, source_target_pairs={{0,4},{4,8},{8,12},{12,0},{1,5},{5,9},{9,13},{13,1},{2,6},{6,10},{... | collective-permute-start | bytes 294920 | tf_op jit(solution)/shard_map/ppermute | solution.py:17
  132.9 12.0 %collective-permute-start.28 = (bf16[96,512]{1,0:T(8,128)(2,1)S(1)}, bf16[96,512]{1,0:T(8,128)(2,1)S(1)}, u32[]{:S(2)}, u32[]{:S(2)}) collective-permute-start(bf16[96,512]{1,0:T(8,128)(2,1)S(1)} %get-tuple-element.19), channel_id=1, source_target_pairs={{0,8},{4,12},{8,0},{12,4},{1,9},{5,13},{9,1},{13,5},{2,10},{6,14},... | collective-permute-start | bytes 294920 | tf_op jit(solution)/shard_map/ppermute | solution.py:17
  137.2 12.0 %collective-permute-start.29 = (bf16[96,512]{1,0:T(8,128)(2,1)S(1)}, bf16[96,512]{1,0:T(8,128)(2,1)S(1)}, u32[]{:S(2)}, u32[]{:S(2)}) collective-permute-start(bf16[96,512]{1,0:T(8,128)(2,1)S(1)} %get-tuple-element.19), channel_id=1, source_target_pairs={{0,12},{4,0},{8,4},{12,8},{1,13},{5,1},{9,5},{13,9},{2,14},{6,2},{... | collective-permute-start | bytes 294920 | tf_op jit(solution)/shard_map/ppermute | solution.py:17
  139.7 26.2 %collective-permute-start.17 = (bf16[128,512]{1,0:T(8,128)(2,1)S(1)}, bf16[128,512]{1,0:T(8,128)(2,1)S(1)}, u32[]{:S(2)}, u32[]{:S(2)}) collective-permute-start(bf16[128,512]{1,0:T(8,128)(2,1)S(1)} %get-tuple-element.57), channel_id=1, source_target_pairs={{0,12},{4,0},{8,4},{12,8},{1,13},{5,1},{9,5},{13,9},{2,14},{6,2},{... | collective-permute-start | bytes 393224 | tf_op jit(solution)/shard_map/ppermute | solution.py:17
  140.6 25.4 %collective-permute-start.16 = (bf16[128,512]{1,0:T(8,128)(2,1)S(1)}, bf16[128,512]{1,0:T(8,128)(2,1)S(1)}, u32[]{:S(2)}, u32[]{:S(2)}) collective-permute-start(bf16[128,512]{1,0:T(8,128)(2,1)S(1)} %get-tuple-element.58), channel_id=1, source_target_pairs={{0,8},{4,12},{8,0},{12,4},{1,9},{5,13},{9,1},{13,5},{2,10},{6,14},... | collective-permute-start | bytes 393224 | tf_op jit(solution)/shard_map/ppermute | solution.py:17
  144.9 6.0 %collective-permute-start.22 = (bf16[128,512]{1,0:T(8,128)(2,1)S(1)}, bf16[128,512]{1,0:T(8,128)(2,1)S(1)}, u32[]{:S(2)}, u32[]{:S(2)}) collective-permute-start(bf16[128,512]{1,0:T(8,128)(2,1)S(1)} %get-tuple-element.54), channel_id=1, source_target_pairs={{0,12},{4,0},{8,4},{12,8},{1,13},{5,1},{9,5},{13,9},{2,14},{6,2},{... | collective-permute-start | bytes 393224 | tf_op jit(solution)/shard_map/ppermute | solution.py:17
  147.6 15.5 %collective-permute-start.21 = (bf16[128,512]{1,0:T(8,128)(2,1)S(1)}, bf16[128,512]{1,0:T(8,128)(2,1)S(1)}, u32[]{:S(2)}, u32[]{:S(2)}) collective-permute-start(bf16[128,512]{1,0:T(8,128)(2,1)S(1)} %get-tuple-element.55), channel_id=1, source_target_pairs={{0,8},{4,12},{8,0},{12,4},{1,9},{5,13},{9,1},{13,5},{2,10},{6,14},... | collective-permute-start | bytes 393224 | tf_op jit(solution)/shard_map/ppermute | solution.py:17
  149.2 14.7 %collective-permute-start.20 = (bf16[128,512]{1,0:T(8,128)(2,1)S(1)}, bf16[128,512]{1,0:T(8,128)(2,1)S(1)}, u32[]{:S(2)}, u32[]{:S(2)}) collective-permute-start(bf16[128,512]{1,0:T(8,128)(2,1)S(1)} %get-tuple-element.53), channel_id=1, source_target_pairs={{0,4},{4,8},{8,12},{12,0},{1,5},{5,9},{9,13},{13,1},{2,6},{6,10},{... | collective-permute-start | bytes 393224 | tf_op jit(solution)/shard_map/ppermute | solution.py:17
  150.9 20.4 %copy-start.15 = (bf16[768,512]{1,0:T(8,128)(2,1)}, bf16[768,512]{1,0:T(8,128)(2,1)S(1)}, u32[]{:S(2)}) copy-start(bf16[768,512]{1,0:T(8,128)(2,1)S(1)} %constant_dynamic-update-slice_fusion.7) | copy-start | bytes 2359300
  150.9 15.1 %collective-permute-start.15 = (bf16[128,512]{1,0:T(8,128)(2,1)S(1)}, bf16[128,512]{1,0:T(8,128)(2,1)S(1)}, u32[]{:S(2)}, u32[]{:S(2)}) collective-permute-start(bf16[128,512]{1,0:T(8,128)(2,1)S(1)} %get-tuple-element.56), channel_id=1, source_target_pairs={{0,4},{4,8},{8,12},{12,0},{1,5},{5,9},{9,13},{13,1},{2,6},{6,10},{... | collective-permute-start | bytes 393224 | tf_op jit(solution)/shard_map/ppermute | solution.py:17
  163.1 23.9 %collective-permute-start.40 = (bf16[384,512]{1,0:T(8,128)(2,1)}, bf16[384,512]{1,0:T(8,128)(2,1)}, u32[]{:S(2)}, u32[]{:S(2)}) collective-permute-start(bf16[384,512]{1,0:T(8,128)(2,1)} %constant_dynamic-update-slice_fusion.8), channel_id=1, source_target_pairs={{0,2},{1,3},{2,0},{3,1},{4,6},{5,7},{6,4},{7,5},{8,10},{9,11},{10,... | collective-permute-start | bytes 1179656 | tf_op jit(solution)/shard_map/ppermute | solution.py:17
  164.0 73.8 %collective-permute-start.30 = (bf16[384,512]{1,0:T(8,128)(2,1)S(1)}, bf16[384,512]{1,0:T(8,128)(2,1)}, u32[]{:S(2)}, u32[]{:S(2)}) collective-permute-start(bf16[384,512]{1,0:T(8,128)(2,1)S(1)} %constant_dynamic-update-slice_fusion.20), channel_id=1, source_target_pairs={{0,2},{1,3},{2,0},{3,1},{4,6},{5,7},{6,4},{7,5},{8,10},{9,11},{10,... | collective-permute-start | bytes 1179656 | tf_op jit(solution)/shard_map/ppermute | solution.py:17
  165.9 3.9 %copy-start.23 = (bf16[512,512]{1,0:T(8,128)(2,1)}, bf16[512,512]{1,0:T(8,128)(2,1)S(1)}, u32[]{:S(2)}) copy-start(bf16[512,512]{1,0:T(8,128)(2,1)S(1)} %get-tuple-element.16) | copy-start | bytes 1572868
  165.9 8.2 %collective-permute-start.42 = (bf16[128,512]{1,0:T(8,128)(2,1)}, bf16[128,512]{1,0:T(8,128)(2,1)}, u32[]{:S(2)}, u32[]{:S(2)}) collective-permute-start(bf16[128,512]{1,0:T(8,128)(2,1)} %get-tuple-element.17), channel_id=1, source_target_pairs={{0,4},{4,8},{8,12},{12,0},{1,5},{5,9},{9,13},{13,1},{2,6},{6,10},{... | collective-permute-start | bytes 393224 | tf_op jit(solution)/shard_map/ppermute | solution.py:17
  166.0 10.7 %collective-permute-start.43 = (bf16[128,512]{1,0:T(8,128)(2,1)}, bf16[128,512]{1,0:T(8,128)(2,1)}, u32[]{:S(2)}, u32[]{:S(2)}) collective-permute-start(bf16[128,512]{1,0:T(8,128)(2,1)} %get-tuple-element.17), channel_id=1, source_target_pairs={{0,8},{4,12},{8,0},{12,4},{1,9},{5,13},{9,1},{13,5},{2,10},{6,14},... | collective-permute-start | bytes 393224 | tf_op jit(solution)/shard_map/ppermute | solution.py:17
  166.0 14.2 %collective-permute-start.44 = (bf16[128,512]{1,0:T(8,128)(2,1)}, bf16[128,512]{1,0:T(8,128)(2,1)}, u32[]{:S(2)}, u32[]{:S(2)}) collective-permute-start(bf16[128,512]{1,0:T(8,128)(2,1)} %get-tuple-element.17), channel_id=1, source_target_pairs={{0,12},{4,0},{8,4},{12,8},{1,13},{5,1},{9,5},{13,9},{2,14},{6,2},{... | collective-permute-start | bytes 393224 | tf_op jit(solution)/shard_map/ppermute | solution.py:17
  174.2 10.6 %collective-permute-start.32 = (bf16[128,512]{1,0:T(8,128)(2,1)}, bf16[128,512]{1,0:T(8,128)(2,1)S(1)}, u32[]{:S(2)}, u32[]{:S(2)}) collective-permute-start(bf16[128,512]{1,0:T(8,128)(2,1)} %get-tuple-element.21), channel_id=1, source_target_pairs={{0,4},{4,8},{8,12},{12,0},{1,5},{5,9},{9,13},{13,1},{2,6},{6,10},{... | collective-permute-start | bytes 393224 | tf_op jit(solution)/shard_map/ppermute | solution.py:17
  176.6 9.7 %collective-permute-start.33 = (bf16[128,512]{1,0:T(8,128)(2,1)}, bf16[128,512]{1,0:T(8,128)(2,1)S(1)}, u32[]{:S(2)}, u32[]{:S(2)}) collective-permute-start(bf16[128,512]{1,0:T(8,128)(2,1)} %get-tuple-element.21), channel_id=1, source_target_pairs={{0,8},{4,12},{8,0},{12,4},{1,9},{5,13},{9,1},{13,5},{2,10},{6,14},... | collective-permute-start | bytes 393224 | tf_op jit(solution)/shard_map/ppermute | solution.py:17
  180.3 8.5 %collective-permute-start.34 = (bf16[128,512]{1,0:T(8,128)(2,1)}, bf16[128,512]{1,0:T(8,128)(2,1)S(1)}, u32[]{:S(2)}, u32[]{:S(2)}) collective-permute-start(bf16[128,512]{1,0:T(8,128)(2,1)} %get-tuple-element.21), channel_id=1, source_target_pairs={{0,12},{4,0},{8,4},{12,8},{1,13},{5,1},{9,5},{13,9},{2,14},{6,2},{... | collective-permute-start | bytes 393224 | tf_op jit(solution)/shard_map/ppermute | solution.py:17
  184.8 55.1 %collective-permute-start.45 = (bf16[512,512]{1,0:T(8,128)(2,1)}, bf16[512,512]{1,0:T(8,128)(2,1)}, u32[]{:S(2)}, u32[]{:S(2)}) collective-permute-start(bf16[512,512]{1,0:T(8,128)(2,1)} %constant_dynamic-update-slice_fusion.2), channel_id=1, source_target_pairs={{0,2},{1,3},{2,0},{3,1},{4,6},{5,7},{6,4},{7,5},{8,10},{9,11},{10,... | collective-permute-start | bytes 1572872 | tf_op jit(solution)/shard_map/ppermute | solution.py:17
  188.8 54.0 %collective-permute-start.41 = (bf16[768,512]{1,0:T(8,128)(2,1)}, bf16[768,512]{1,0:T(8,128)(2,1)}, u32[]{:S(2)}, u32[]{:S(2)}) collective-permute-start(bf16[768,512]{1,0:T(8,128)(2,1)} %constant_dynamic-update-slice_fusion.6), channel_id=1, source_target_pairs={{0,1},{1,0},{2,3},{3,2},{4,5},{5,4},{6,7},{7,6},{8,9},{9,8},{10,11... | collective-permute-start | bytes 2359304 | tf_op jit(solution)/shard_map/ppermute | solution.py:21
  189.4 52.2 %collective-permute-start.35 = (bf16[512,512]{1,0:T(8,128)(2,1)}, bf16[512,512]{1,0:T(8,128)(2,1)}, u32[]{:S(2)}, u32[]{:S(2)}) collective-permute-start(bf16[512,512]{1,0:T(8,128)(2,1)} %constant_dynamic-update-slice_fusion.14), channel_id=1, source_target_pairs={{0,2},{1,3},{2,0},{3,1},{4,6},{5,7},{6,4},{7,5},{8,10},{9,11},{10,... | collective-permute-start | bytes 1572872 | tf_op jit(solution)/shard_map/ppermute | solution.py:17
  239.6 4.5 %collective-permute-start.31 = (bf16[768,512]{1,0:T(8,128)(2,1)}, bf16[768,512]{1,0:T(8,128)(2,1)S(1)}, u32[]{:S(2)}, u32[]{:S(2)}) collective-permute-start(bf16[768,512]{1,0:T(8,128)(2,1)} %constant_dynamic-update-slice_fusion.18), channel_id=1, source_target_pairs={{0,1},{1,0},{2,3},{3,2},{4,5},{5,4},{6,7},{7,6},{8,9},{9,8},{10,11... | collective-permute-start | bytes 2359304 | tf_op jit(solution)/shard_map/ppermute | solution.py:21
  239.8 3.1 %copy-start.16 = (bf16[768,512]{1,0:T(8,128)(2,1)S(1)}, bf16[768,512]{1,0:T(8,128)(2,1)}, u32[]{:S(2)}) copy-start(bf16[768,512]{1,0:T(8,128)(2,1)} %constant_dynamic-update-slice_fusion.6) | copy-start | bytes 2359300
  241.1 6.2 %collective-permute-start.46 = (bf16[1024,512]{1,0:T(8,128)(2,1)S(1)}, bf16[1024,512]{1,0:T(8,128)(2,1)S(1)}, u32[]{:S(2)}, u32[]{:S(2)}) collective-permute-start(bf16[1024,512]{1,0:T(8,128)(2,1)S(1)} %constant_dynamic-update-slice_fusion), channel_id=1, source_target_pairs={{0,1},{1,0},{2,3},{3,2},{4,5},{5,4},{6,7},{7,6},{8,9},{9,8},{10,11... | collective-permute-start | bytes 3145736 | tf_op jit(solution)/shard_map/ppermute | solution.py:21
  242.7 7.5 %collective-permute-start.36 = (bf16[1024,512]{1,0:T(8,128)(2,1)S(1)}, bf16[1024,512]{1,0:T(8,128)(2,1)S(1)}, u32[]{:S(2)}, u32[]{:S(2)}) collective-permute-start(bf16[1024,512]{1,0:T(8,128)(2,1)S(1)} %constant_dynamic-update-slice_fusion.12), channel_id=1, source_target_pairs={{0,1},{1,0},{2,3},{3,2},{4,5},{5,4},{6,7},{7,6},{8,9},{9,8},{10,11... | collective-permute-start | bytes 3145736 | tf_op jit(solution)/shard_map/ppermute | solution.py:21
  (18 other events, 27.0 us)

commit v2 on v0

v2 whole, which is shorter than its diff:
```python
import functools

import jax
import jax.numpy as jnp
from jax import lax
from jax.experimental import pallas as pl
from jax.experimental.pallas import tpu as pltpu
from jax.sharding import PartitionSpec as P

inv_weight = 25.0
var_weight = 25.0
cov_weight = 1.0
eps_var = 0.0001

VMEM = pl.BlockSpec(memory_space=pltpu.VMEM)
SMEM = pl.BlockSpec(memory_space=pltpu.SMEM)
PARAMS = pltpu.CompilerParams(vmem_limit_bytes=16 * 1024 * 1024)


class Chain:
    def __init__(self):
        self.last = None

    def __call__(self, kernel, outs, ins, scratch=()):
        specs = [SMEM if x.ndim == 1 else VMEM for x in ins]
        body = kernel
        if self.last is not None:
            ins, specs = [self.last] + list(ins), [pl.BlockSpec(memory_space=pl.ANY)] + specs

            def body(_, *refs):
                kernel(*refs)

        outs = pl.pallas_call(
            body,
            out_shape=outs,
            in_specs=specs,
            out_specs=[SMEM if out.shape == (1,) else VMEM for out in outs],
            scratch_shapes=scratch,
            compiler_params=PARAMS,
            cost_estimate=pl.CostEstimate(flops=1, bytes_accessed=1, transcendentals=0),
        )(*ins)
        self.last = outs[0]
        return outs


def array(shape, dtype):
    return jax.ShapeDtypeStruct(shape, dtype)


def shift(value, axis, count, step, inner):
    pairs = [
        (index, (index // inner + step) % count * inner + index % inner)
        for index in range(count * inner)
    ]
    return lax.ppermute(value, axis, pairs)


def partner_of(value, axis, bit):
    return lax.ppermute(value, axis, [(index, index ^ bit) for index in range(lax.axis_size(axis))])


def core_swap(value):
    return partner_of(value, "col", 1)


def dot_t(left, right):
    return lax.dot_general(
        left, right, (((1,), (1,)), ((), ())), preferred_element_type=jnp.float32
    )


def dot(left, right):
    return lax.dot_general(
        left, right, (((1,), (0,)), ((), ())), preferred_element_type=jnp.float32
    )


def sums_kernel(first, second, out):
    out[0:1, :] = jnp.sum(first[...].astype(jnp.float32), axis=0, keepdims=True)
    out[1:2, :] = jnp.sum(second[...].astype(jnp.float32), axis=0, keepdims=True)


def split_rows(values, count, rows):
    width = values[0].shape[1]
    ids = lax.broadcasted_iota(jnp.int32, (rows, width), 0)
    block = jnp.zeros((rows, width), jnp.float32)
    for index, rest in enumerate(values):
        for term in range(count):
            head = rest.astype(jnp.bfloat16).astype(jnp.float32)
            block = jnp.where(ids == index * count + term, head, block)
            rest = rest - head
    return block.astype(jnp.bfloat16)


def write_extra(out, main, extra):
    if out.dtype == jnp.bfloat16:
        out[main : main + 16, :] = split_rows([extra], 2, 16)
    else:
        ids = lax.broadcasted_iota(jnp.int32, (16, extra.shape[1]), 0)
        out[main : main + 16, :] = jnp.where(ids == 0, extra, 0.0)


def read_extra(ref, main):
    block = ref[main : main + 16, :].astype(jnp.float32)
    return block[0:1, :] + block[1:2, :]


def centre_kernel(total, first, second, sums, rounded_out, stats, sent):
    rows, width = first.shape
    found = []
    squares = []
    for index, view in enumerate((first, second)):
        centred = view[...].astype(jnp.float32) - sums[index : index + 1, :] / total
        rounded = centred.astype(jnp.bfloat16)
        rounded_out[index] = rounded
        wide = rounded.astype(jnp.float32)
        found.append(jnp.sum(centred * centred, axis=0, keepdims=True))
        squares.append(jnp.sum(wide * wide, axis=0, keepdims=True))
    differ = first[...].astype(jnp.float32) - second[...].astype(jnp.float32)
    found += squares + [jnp.sum(differ * differ, axis=0, keepdims=True)]
    ids = lax.broadcasted_iota(jnp.int32, (8, width), 0)
    block = jnp.zeros((8, width), jnp.float32)
    for index, value in enumerate(found):
        block = jnp.where(ids == index, value, block)
    stats[...] = block
    sent[:rows, :] = second[...]
    sent[rows:, :] = split_rows(found, 3, 16)


def near_place(tile_index, core, rows, tile):
    half, quarter = rows // 2, rows // 4
    square = tile_index < half // tile
    row = jnp.where(square, half * core + tile * tile_index, quarter * core + tile * tile_index - half)
    column = jnp.where(square, half * core, half)
    return square, pl.multiple_of(row, tile), pl.multiple_of(column, half)


def near_kernel(x_count, view, place, own, *rest):
    (top, bottom), (partner, keep, *sends) = rest[:2], rest[2:]
    core, x_place = place[0], place[1]
    rows = own.shape[1]
    half = rows // 2
    tile = rows // 4 // x_count
    partner[:half, :] = top[...]
    partner[half:, :] = bottom[...]
    row_ids = lax.broadcasted_iota(jnp.int32, (tile, half), 0)
    column_ids = lax.broadcasted_iota(jnp.int32, (tile, half), 1)
    for step in range(x_count):
        out = keep if step == 0 else sends[step - 1]
        extra = jnp.zeros((1, half), jnp.float32)
        for piece in range(3):
            index = (x_place + step) % x_count * 3 + piece
            square, row, column = near_place(index, core, rows, tile)
            diagonal = jnp.logical_and(square, column_ids == row_ids + tile * index)
            value = dot_t(own[view, pl.ds(row, tile), :], own[view, pl.ds(column, half), :])
            value = value + dot_t(
                partner[pl.ds(row, tile), :], partner[pl.ds(column, half), :]
            )
            extra = extra + jnp.sum(jnp.where(diagonal, value, 0.0), axis=0, keepdims=True)
            value = jnp.where(diagonal, 0.0, value)
            out[pl.ds(piece * tile, tile), :] = value.astype(out.dtype)
        write_extra(out, 3 * tile, extra)


def centre_other_kernel(total, index, other, sums, *outs):
    mean = sums[index : index + 1, :] / total
    stats = None
    if index == 1:
        stats, outs = outs[0], outs[1:]
    size = outs[0].shape[0]
    for step in range(4):
        at = slice(step * size, (step + 1) * size)
        outs[step][...] = (other[at, :].astype(jnp.float32) - mean).astype(jnp.bfloat16)
    if stats is not None:
        block = other[4 * size :, :].astype(jnp.float32)
        ids = lax.broadcasted_iota(jnp.int32, stats.shape, 0)
        value = jnp.zeros(stats.shape, jnp.float32)
        for row in range(5):
            at = 3 * row
            got = block[at : at + 1, :] + block[at + 1 : at + 2, :] + block[at + 2 : at + 3, :]
            value = jnp.where(ids == row, got, value)
        outs[4][...] = stats[...] + value


def add_kernel(main, *refs):
    out = refs[-1]
    value = refs[0][:main, :].astype(jnp.float32)
    for ref in refs[1:-1]:
        value = value + ref[:main, :].astype(jnp.float32)
    out[:main, :] = value.astype(out.dtype)
    if main < out.shape[0]:
        extra = read_extra(refs[0], main)
        for ref in refs[1:-1]:
            extra = extra + read_extra(ref, main)
        write_extra(out, main, extra)


def pick_kernel(place, mine, got, out):
    @pl.when(place[2] == 1)
    def _():
        out[...] = mine[...]

    @pl.when(place[2] == 0)
    def _():
        out[...] = got[...]


def loss_terms(total, feat, stats):
    spread = jnp.sqrt(stats[0:2, :] / (total - 1) + eps_var)
    norms = stats[2:4, :] / (total - 1)
    return (
        inv_weight * stats[4:5, :] / (total * feat)
        + var_weight * jnp.sum(jnp.maximum(1.0 - spread, 0.0), axis=0, keepdims=True) / feat
        - cov_weight * jnp.sum(norms * norms, axis=0, keepdims=True) / feat
    )


def far_kernel(x_count, view, total, feat, place, own, partner, *rest):
    others, swapped, outs = rest[:4], rest[4:8], rest[8:]
    stats = None
    if view == 1:
        stats, outs = outs[0], outs[1:]
    core, x_place = place[0], place[1]
    half = own.shape[1] // 2
    quarter = half // 2
    tile = half // x_count
    for block in range(2):
        for step in range(x_count):
            out = outs[block * x_count + step]
            part = (x_place + step) % x_count
            row = pl.ds(pl.multiple_of(half * core + tile * part, tile), tile)
            left, left_partner = own[view, row, :], partner[row, :]
            for side in range(2):
                at = 2 * block + side
                value = dot_t(left, others[at][...]) + dot_t(left_partner, swapped[at][...])
                out[:tile, side * quarter : (side + 1) * quarter] = value.astype(out.dtype)
            if out.shape[0] > tile:
                terms = loss_terms(total, feat, stats)
                terms = jnp.where(part == 0, terms, 0.0)
                if terms.shape[1] < half:
                    terms = jnp.concatenate(
                        [terms, jnp.zeros((1, half - terms.shape[1]), jnp.float32)], axis=1
                    )
                write_extra(out, tile, terms)


def near_product_kernel(
    x_count, index, total, feat, place, rounded, first, second, sums, stats, *rest
):
    parts, (base, squares, grid, columns) = rest[:-4], rest[-4:]
    core, x_place = place[0], place[1]
    rows, width = rounded.shape[1:]
    half = rows // 2
    tile = rows // 4 // x_count
    square_sum = jnp.float32(0.0)
    for side in range(2):
        owner = core if side == 0 else 1 - core
        extra = jnp.zeros((1, half), jnp.float32)
        for step in range(x_count):
            extra = extra + read_extra(parts[side * x_count + step], 3 * tile)
            for piece in range(3):
                at = (x_place + x_count - step) % x_count * 3 + piece
                _, row, column = near_place(at, owner, rows, tile)
                grid[pl.ds(row, tile), pl.ds(column, half)] = parts[side * x_count + step][
                    pl.ds(piece * tile, tile), :
                ]
        square_sum = square_sum + jnp.sum(extra * extra)
        columns[pl.ds(pl.multiple_of(half * owner, half), half), :] = jnp.broadcast_to(
            extra, (8, half)
        ).T
    grid[half:, :half] = grid[:half, half:].T
    scale = total * feat / 64.0
    spread = jnp.sqrt(stats[index : index + 1, :] / (total - 1) + eps_var)
    active = jnp.where(spread < 1.0, 1.0, 0.0)
    var_scale = scale * -var_weight * active / (feat * spread * (total - 1))
    cov_scale = scale * 4.0 * cov_weight / (feat * (total - 1)) / (total - 1)
    inv_scale = (1.0 - 2.0 * index) * scale * 2.0 * inv_weight / (total * feat)
    mean = sums[index : index + 1, :] / total
    norms = stats[index + 2 : index + 3, :]
    chunk = rows // 4
    for step in range(4):
        at = slice(step * chunk, (step + 1) * chunk)
        wide = grid[at, :].astype(jnp.float32)
        square_sum = square_sum + jnp.sum(wide * wide)
        product = dot(grid[at, :], rounded[index])
        product = product + (columns[at, 0:1] - norms) * rounded[
            index, at, :
        ].astype(jnp.float32)
        one, two = first[at, :].astype(jnp.float32), second[at, :].astype(jnp.float32)
        centred = (one if index == 0 else two) - mean
        base[at, :] = inv_scale * (one - two) + var_scale * centred + cov_scale * product
    squares[0] = square_sum


def far_product_kernel(x_count, total, feat, place, base, *rest):
    others, parts, grad = rest[:4], rest[4:-1], rest[-1]
    core, x_place = place[0], place[1]
    quarter = others[0].shape[0]
    half = 2 * quarter
    tile = half // x_count
    cov_scale = total * feat / 64.0 * 4.0 * cov_weight / (feat * (total - 1)) / (total - 1)
    for side in range(2):
        owner = core if side == 0 else 1 - core
        for step in range(x_count):
            at = (x_place + x_count - step) % x_count
            row = pl.ds(pl.multiple_of(half * owner + tile * at, tile), tile)
            product = jnp.zeros((tile, grad.shape[1]), jnp.float32)
            for block in range(2):
                part = parts[(block * 2 + side) * x_count + step]
                for index in range(2):
                    product = product + dot(
                        part[:tile, index * quarter : (index + 1) * quarter],
                        others[2 * block + index][...],
                    )
            grad[row, :] = base[row, :] + cov_scale * product


def squares_kernel(main, count, *refs):
    total = jnp.float32(0.0)
    terms = jnp.zeros((1, refs[0].shape[1]), jnp.float32)
    for ref in refs[:-2]:
        wide = ref[:main, :].astype(jnp.float32)
        total = total + jnp.sum(wide * wide)
        if ref.shape[0] > main:
            terms = terms + read_extra(ref, main)
    refs[-2][0] = total
    refs[-1][0] = jnp.sum(terms)


def on_device(first_view, second_view):
    dp_count = lax.axis_size("dp")
    row_count = lax.axis_size("row")
    col_count = lax.axis_size("col")
    rows, width = first_view.shape
    total = rows * dp_count
    feat = width * row_count * col_count
    half = rows // 2
    x_count = col_count // 2
    core = lax.axis_index("col") % 2
    x_place = lax.axis_index("col") // 2
    z_place = lax.axis_index("row")
    inner = 4 if row_count % 4 == 0 else 1
    middle = jnp.logical_or(z_place % 4 == 1, z_place % 4 == 2)
    place = jnp.stack([core, x_place, middle.astype(core.dtype)]).astype(jnp.int32)
    f32, bf16 = jnp.float32, jnp.bfloat16
    run = Chain()

    (sums,) = run(sums_kernel, [array((2, width), f32)], [first_view, second_view])
    sums_other = partner_of(sums, "dp", 1)
    first_sent, sums_other = lax.optimization_barrier((first_view, sums_other))
    others = [partner_of(first_sent, "dp", 1)]
    sums = sums + sums_other

    rounded, stats, second_sent = run(
        functools.partial(centre_kernel, total),
        [
            array((2, rows, width), bf16),
            array((8, width), f32),
            array((rows + 16, width), bf16),
        ],
        [first_view, second_view, sums],
    )
    others.append(partner_of(second_sent, "dp", 1))
    swapped = [
        [core_swap(rounded[view, :half]), core_swap(rounded[view, half:])] for view in range(2)
    ]

    def send_row(value, pairs):
        groups = range(0, row_count, inner)
        return lax.ppermute(value, "row", [(g + a, g + b) for g in groups for a, b in pairs])

    class Piece:
        def __init__(self, main, keep, sends):
            self.main, self.keep = main, keep
            self.like = array(keep.shape, bf16)
            self.got = [shift(sent, "col", x_count, i + 1, 2) for i, sent in enumerate(sends)]

        def add(self, values):
            (value,) = run(functools.partial(add_kernel, self.main), [self.like], values)
            return value

        def over_x(self):
            if inner == 4:
                value = self.add([self.keep] + self.got)
                self.got.append(send_row(value, [(0, 1), (3, 2)]))

        def inward(self):
            self.value = self.add([self.keep] + self.got)
            if inner == 4:
                self.got = send_row(self.value, [(1, 2), (2, 1)])

        def across(self):
            if inner == 4:
                self.value = self.add([self.value, self.got])
            bit = inner
            while bit < row_count:
                self.value = self.add([self.value, partner_of(self.value, "row", bit)])
                bit *= 2
            if inner == 4:
                self.got = send_row(self.value, [(1, 0), (2, 3)])

        def outward(self):
            if inner == 4:
                (self.value,) = run(pick_kernel, [self.like], [place, self.value, self.got])
            parts = [self.value]
            for step in range(1, x_count):
                parts.append(shift(self.value, "col", x_count, step, 2))
            self.parts = parts + [core_swap(part) for part in parts]

    near, far, rnd_others = [], [], []
    main = 3 * (rows // 4) // x_count
    tile = half // x_count

    def piece_outs(size):
        return [array((size, half), f32)] + [array((size, half), bf16)] * (x_count - 1)

    def near_gram(index):
        whole, *outs = run(
            functools.partial(near_kernel, x_count, index),
            [array((rows, width), bf16)] + piece_outs(main + 16),
            [place, rounded] + swapped[index],
        )
        swapped[index] = whole
        near.append(Piece(main, outs[0], outs[1:]))

    def far_centre(index):
        outs = [array((rows // 4, width), bf16)] * 4
        ins = [others[index], sums]
        if index == 1:
            outs, ins = outs + [array((8, width), f32)], ins + [stats]
        return run(functools.partial(centre_other_kernel, total, index), outs, ins)

    def far_gram(index, extra_ins):
        sizes = [tile + 16 * len(extra_ins), tile]
        outs = run(
            functools.partial(far_kernel, x_count, index, total, feat),
            piece_outs(sizes[0]) + piece_outs(sizes[1]),
            [place, rounded, swapped[index]]
            + rnd_others[index]
            + [core_swap(other) for other in rnd_others[index]]
            + extra_ins,
        )
        for block in range(2):
            keep, *sends = outs[block * x_count : (block + 1) * x_count]
            far.append(Piece(tile, keep, sends))

    def near_product(index):
        return run(
            functools.partial(near_product_kernel, x_count, index, total, feat),
            [array((rows, width), f32), array((1,), f32)],
            [place, rounded, first_view, second_view, sums, stats] + near[index].parts,
            scratch=[pltpu.VMEM((rows, rows), bf16), pltpu.VMEM((rows, 8), f32)],
        )

    def far_product(index, base):
        (grad,) = run(
            functools.partial(far_product_kernel, x_count, total, feat),
            [array((rows, width), f32)],
            [place, base]
            + rnd_others[index]
            + far[2 * index].parts
            + far[2 * index + 1].parts,
        )
        return grad

    near_gram(0)
    near_gram(1)
    near[0].over_x()
    rnd_others.append(list(far_centre(0)))
    far_gram(0, [])
    near[1].over_x()
    near[0].inward()
    far[0].over_x()
    far[1].over_x()
    near[1].inward()
    *found, stats = far_centre(1)
    rnd_others.append(found)
    near[0].across()
    far[0].inward()
    far_gram(1, [stats])
    far[1].inward()
    near[1].across()
    near[0].outward()
    far[0].across()
    far[2].over_x()
    far[1].across()
    far[3].over_x()
    near[1].outward()
    far[2].inward()
    far[0].outward()
    far[3].inward()
    far[1].outward()
    far[2].across()
    base_first, squares_first = near_product(0)
    base_second, squares_second = near_product(1)
    far[3].across()
    far[2].outward()
    grad_first = far_product(0, base_first)
    far[3].outward()
    squares_far, terms = run(
        functools.partial(squares_kernel, tile, x_count),
        [array((1,), f32), array((1,), f32)],
        [part for piece in far for part in piece.parts],
    )
    squares = squares_first[0] + squares_second[0] + squares_far[0]
    plane = squares / (total - 1) / (total - 1)
    plane_other = partner_of(plane, "dp", 1)
    grad_second = far_product(1, base_second)
    loss = terms[0] + cov_weight * (plane + plane_other) / feat
    return loss, grad_first, grad_second


def solution(mesh):
    return jax.shard_map(
        on_device,
        mesh=mesh,
        in_specs=(P("dp", ("row", "col")), P("dp", ("row", "col"))),
        out_specs=(P(), P("dp", ("row", "col")), P("dp", ("row", "col"))),
        check_vma=False,
    )
```

time: 715 us -> 170 us (0.24)
  waiting for transfers between devices: 547 us -> 56.2 us
  matrix products: 86.6 us -> 0 us
  starting transfers between devices: 0.31 us -> 66.1 us
  blocking collectives: 49.1 us -> 0 us
  Pallas kernels: 0 us -> 35.9 us
  other arithmetic: 13.9 us -> 0.08 us
  between operations: 17.6 us -> 5.51 us
    all_gather x6 -> x0, waiting for transfers between devices: 464 us -> none  [the longest x1 151 us: on_device(): lax.all_gather(wide_first, 'row', axis=1, tiled=True)]
    dot_general x4 -> x0, matrix products: 86.6 us -> none  [the longest x2 55.6 us: gram(): lax.dot_general(left, right, (((0,), (0,)), ((), ())), preferred_element_...]
    reduce_scatter x2 -> x0, waiting for transfers between devices: 81.5 us -> none  [the longest x1 74.5 us: on_device(): lax.psum_scatter(part_first, 'col', scatter_dimension=1, tiled=True)]
    ppermute x0 -> x58, starting transfers between devices: none -> 66.1 us  [the longest x18 37.2 us: send_row(): lax.ppermute(value, 'row', [(g + a, g + b) for g in groups for a, b in pa...]
    ppermute x0 -> x58, waiting for transfers between devices: none -> 56.2 us  [the longest x12 29 us: shift(): return lax.ppermute(value, axis, pairs)]
    psum x3 -> x0, blocking collectives: 49.1 us -> none  [the longest x1 38.3 us: on_device(): loss = lax.psum(local_loss, ('dp', 'row', 'col'))]
    pallas_call x0 -> x37, Pallas kernels: none -> 35.9 us  [__call__(): pl.pallas_call(body, out_shape=outs, in_specs=specs, out_specs=[SMEM if o...]
  transfers between devices with their start and end apart: 8 -> 58, of which waited for: 8 -> 16; matrix products, arithmetic and copies ran while one was open for 6% -> 1% of each run, Pallas kernels for 0% -> 18%
where the time goes in v2:
time: 170 us; the launch traced here: 169 us
  starting transfers between devices  66.1 us (39%)
  waiting for transfers between devices  56.2 us (33%)
  Pallas kernels  35.9 us (21%)
  between operations  5.51 us (3%)
  local copies, waits for them, and re-layouts  5.15 us (3%)
    ppermute x18, starting transfers between devices, send_row(): lax.ppermute(value, 'row', [(g + a, g + b) for g in groups for a, b in pa...  37.2 us
    pallas_call x37, Pallas kernels, __call__(): pl.pallas_call(body, out_shape=outs, in_specs=specs, out_specs=[SMEM if o...  35.9 us
    ppermute x12, waiting for transfers between devices, shift(): return lax.ppermute(value, axis, pairs)  29 us
    ppermute x18, waiting for transfers between devices, send_row(): lax.ppermute(value, 'row', [(g + a, g + b) for g in groups for a, b in pa...  18.7 us
    ppermute x12, starting transfers between devices, shift(): return lax.ppermute(value, axis, pairs)  15.4 us
    ppermute x28, starting transfers between devices, partner_of(): lax.ppermute(value, axis, [(index, index ^ bit) for index in range(lax.ax...  13.5 us
    ppermute x28, waiting for transfers between devices, partner_of(): lax.ppermute(value, axis, [(index, index ^ bit) for index in range(lax.ax...  8.5 us
    unnamed x10, local copies, waits for them, and re-layouts  3.79 us
  transfers between devices with their start and end apart: 58, of which 16 were waited for; matrix products, arithmetic and copies ran while one was open for 1% of the time, Pallas kernels for 18%

profile of v2, /device:TPU:0, one launch (start us, length us, event | category | flops | bytes accessed | tf_op | source)
XLA Modules:
  0.0 169.0 jit_solution(15870475756985811848)
XLA Ops:
  0.6 1.2 copy-done
  1.9 1.5 shard_map.49._
  3.4 3.0 %collective-permute-start = (f32[2,512]{1,0:T(2,128)S(1)}, f32[2,512]{1,0:T(2,128)S(1)}, u32[]{:S(2)}, u32[]{:S(2)}) collective-permute-start(f32[2,512]{1,0:T(2,128)S(1)} %shard_map.49._), channel_id=1, source_target_pairs={{0,16},{16,0},{1,17},{17,1},{2,18},{18,2},{3,19},{19,3},{4,20},{20... | collective-permute-start | bytes 12296 | tf_op jit(solution)/shard_map/ppermute | solution.py:59
  6.4 1.6 collective-permute-done
  8.0 2.8 %shard_map.50 = (bf16[2,1024,512]{2,1,0:T(8,128)(2,1)S(1)}, f32[8,512]{1,0:T(8,128)S(1)}, bf16[1040,512]{1,0:T(8,128)(2,1)S(1)}) custom-call(f32[2,512]{1,0:T(2,128)S(1)} %shard_map.49._, bf16[1024,512]{1,0:T(8,128)(2,1)} %refs_2_.3, bf16[1024,512]{1,0:T(8,128)(2,1)S(1)} %copy-done, f32[2,512]{1,0:T(2,128)S(1)} %add.26.refs_2_.refs_1_.refs_4_), custom_call_target="tpu_custom_call" | custom-call | flops 1 | bytes 1 | tf_op jit(solution)/shard_map/pallas_call | solution.py:33
  10.8 1.0 copy-done.3
  11.8 2.0 %collective-permute-start.6 = (bf16[1024,512]{1,0:T(8,128)(2,1)}, bf16[1024,512]{1,0:T(8,128)(2,1)S(1)}, u32[]{:S(2)}, u32[]{:S(2)}) collective-permute-start(bf16[1024,512]{1,0:T(8,128)(2,1)} %refs_2_.3), channel_id=1, source_target_pairs={{0,16},{16,0},{1,17},{17,1},{2,18},{18,2},{3,19},{19,3},{4,20},{20... | collective-permute-start | bytes 3145736 | tf_op jit(solution)/shard_map/ppermute | solution.py:59
  13.8 1.4 slice_bitcast_fusion
  16.3 1.2 collective-permute-done.1.refs_2_
  17.4 0.7 collective-permute-done.2.refs_3_
  18.2 3.5 %shard_map.51 = (bf16[1024,512]{1,0:T(8,128)(2,1)S(1)}, f32[400,512]{1,0:T(8,128)S(1)}, bf16[400,512]{1,0:T(8,128)(2,1)S(1)}) custom-call(bf16[2,1024,512]{2,1,0:T(8,128)(2,1)S(1)} %get-tuple-element.38._.refs_1_, s32[3]{0:T(128)S(1)} %pad_add_fusion.refs_0_, bf16[2,1024,512]{2,1,0:T(8,128)(2,1)S(1)} %get-tuple-element.38._.refs_1_, ...), custom_call_target="tpu_custom_call" | custom-call | flops 1 | bytes 1 | tf_op jit(solution)/shard_map/pallas_call | solution.py:33
  21.7 1.6 collective-permute-start.5
  23.7 3.5 %shard_map.52 = (bf16[1024,512]{1,0:T(8,128)(2,1)S(1)}, f32[400,512]{1,0:T(8,128)S(1)}, bf16[400,512]{1,0:T(8,128)(2,1)S(1)}) custom-call(bf16[1024,512]{1,0:T(8,128)(2,1)S(1)} %get-tuple-element.39._.refs_2_, s32[3]{0:T(128)S(1)} %pad_add_fusion.refs_0_, bf16[2,1024,512]{2,1,0:T(8,128)(2,1)S(1)} %get-tuple-element.38._.refs_1_, ...), custom_call_target="tpu_custom_call" | custom-call | flops 1 | bytes 1 | tf_op jit(solution)/shard_map/pallas_call | solution.py:33
  27.2 6.0 %collective-permute-done.5.refs_1_ = bf16[400,512]{1,0:T(8,128)(2,1)S(1)} collective-permute-done((bf16[400,512]{1,0:T(8,128)(2,1)S(1)}, bf16[400,512]{1,0:T(8,128)(2,1)S(1)}, u32[]{:S(2)}, u32[]{:S(2)}) %collective-permute-start.5) | collective-permute-done | bytes 409632 | tf_op jit(solution)/shard_map/ppermute | solution.py:55
  33.3 4.8 %collective-permute-done.6.refs_0_ = bf16[1024,512]{1,0:T(8,128)(2,1)S(1)} collective-permute-done((bf16[1024,512]{1,0:T(8,128)(2,1)}, bf16[1024,512]{1,0:T(8,128)(2,1)S(1)}, u32[]{:S(2)}, u32[]{:S(2)}) %collective-permute-start.6) | collective-permute-done | bytes 1048608 | tf_op jit(solution)/shard_map/ppermute | solution.py:59
  38.8 2.0 %collective-permute-start.11 = (bf16[400,512]{1,0:T(8,128)(2,1)S(1)}, bf16[400,512]{1,0:T(8,128)(2,1)S(1)}, u32[]{:S(2)}, u32[]{:S(2)}) collective-permute-start(bf16[400,512]{1,0:T(8,128)(2,1)S(1)} %get-tuple-element.50), channel_id=1, source_target_pairs={{0,2},{1,3},{2,0},{3,1},{4,6},{5,7},{6,4},{7,5},{8,10},{9,11},{10,... | collective-permute-start | bytes 1228808 | tf_op jit(solution)/shard_map/ppermute | solution.py:55
  41.3 3.5 %collective-permute-start.12 = (bf16[400,512]{1,0:T(8,128)(2,1)S(1)}, bf16[400,512]{1,0:T(8,128)(2,1)S(1)}, u32[]{:S(2)}, u32[]{:S(2)}) collective-permute-start(bf16[400,512]{1,0:T(8,128)(2,1)S(1)} %shard_map.53._), channel_id=1, source_target_pairs={{0,4},{12,8},{1,5},{13,9},{2,6},{14,10},{3,7},{15,11},{16,20},{28,... | collective-permute-start | bytes 1228808 | tf_op jit(solution)/shard_map/ppermute | solution.py:370
  44.9 1.8 %shard_map.55 = (f32[256,512]{1,0:T(8,128)S(1)}, bf16[256,512]{1,0:T(8,128)(2,1)S(1)}, f32[256,512]{1,0:T(8,128)S(1)}, bf16[256,512]{1,0:T(8,128)(2,1)S(1)}) custom-call(bf16[256,512]{1,0:T(8,128)(2,1)S(1)} %get-tuple-element.44._.refs_3_.refs_2_, s32[3]{0:T(128)S(1)} %pad_add_fusion.refs_0_, bf16[2,1024,512]{2,1,0:T(8,128)(2,1)S(1)} %get-tuple-element.38._.refs_1_, ...), custom_call_target="tpu_custom_call" | custom-call | flops 1 | bytes 1 | tf_op jit(solution)/shard_map/pallas_call | solution.py:33
  46.7 3.8 %collective-permute-done.11.refs_1_ = bf16[400,512]{1,0:T(8,128)(2,1)S(1)} collective-permute-done((bf16[400,512]{1,0:T(8,128)(2,1)S(1)}, bf16[400,512]{1,0:T(8,128)(2,1)S(1)}, u32[]{:S(2)}, u32[]{:S(2)}) %collective-permute-start.11) | collective-permute-done | bytes 409632 | tf_op jit(solution)/shard_map/ppermute | solution.py:55
  50.6 3.8 %collective-permute-start.15 = (bf16[400,512]{1,0:T(8,128)(2,1)S(1)}, bf16[400,512]{1,0:T(8,128)(2,1)S(1)}, u32[]{:S(2)}, u32[]{:S(2)}) collective-permute-start(bf16[400,512]{1,0:T(8,128)(2,1)S(1)} %shard_map.56._), channel_id=1, source_target_pairs={{0,4},{12,8},{1,5},{13,9},{2,6},{14,10},{3,7},{15,11},{16,20},{28,... | collective-permute-start | bytes 1228808 | tf_op jit(solution)/shard_map/ppermute | solution.py:370
  54.4 1.6 collective-permute-start.13
  56.6 0.7 collective-permute-start.17
  57.3 6.4 %collective-permute-done.13.refs_1_ = bf16[256,512]{1,0:T(8,128)(2,1)S(1)} collective-permute-done((bf16[256,512]{1,0:T(8,128)(2,1)S(1)}, bf16[256,512]{1,0:T(8,128)(2,1)S(1)}, u32[]{:S(2)}, u32[]{:S(2)}) %collective-permute-start.13) | collective-permute-done | bytes 262176 | tf_op jit(solution)/shard_map/ppermute | solution.py:55
  63.8 1.3 collective-permute-start.18
  65.1 2.2 %collective-permute-done.14.refs_1_ = bf16[256,512]{1,0:T(8,128)(2,1)S(1)} collective-permute-done((bf16[256,512]{1,0:T(8,128)(2,1)S(1)}, bf16[256,512]{1,0:T(8,128)(2,1)S(1)}, u32[]{:S(2)}, u32[]{:S(2)}) %collective-permute-start.14) | collective-permute-done | bytes 262176 | tf_op jit(solution)/shard_map/ppermute | solution.py:55
  68.3 0.7 collective-permute-start.24
  69.7 1.3 collective-permute-start.25
  71.0 4.6 %collective-permute-start.23 = (bf16[256,512]{1,0:T(8,128)(2,1)S(1)}, bf16[256,512]{1,0:T(8,128)(2,1)S(1)}, u32[]{:S(2)}, u32[]{:S(2)}) collective-permute-start(bf16[256,512]{1,0:T(8,128)(2,1)S(1)} %shard_map.59._), channel_id=1, source_target_pairs={{0,4},{12,8},{1,5},{13,9},{2,6},{14,10},{3,7},{15,11},{16,20},{28,... | collective-permute-start | bytes 786440 | tf_op jit(solution)/shard_map/ppermute | solution.py:370
  75.7 1.8 %shard_map.64 = (f32[272,512]{1,0:T(8,128)S(1)}, bf16[272,512]{1,0:T(8,128)(2,1)S(1)}, f32[256,512]{1,0:T(8,128)S(1)}, bf16[256,512]{1,0:T(8,128)(2,1)S(1)}) custom-call(bf16[256,512]{1,0:T(8,128)(2,1)S(1)} %shard_map.63._.refs_0_, s32[3]{0:T(128)S(1)} %pad_add_fusion.refs_0_, bf16[2,1024,512]{2,1,0:T(8,128)(2,1)S(1)} %get-tuple-element.38._.refs_1_, ...), custom_call_target="tpu_custom_call" | custom-call | flops 1 | bytes 1 | tf_op jit(solution)/shard_map/pallas_call | solution.py:33
  77.5 1.6 collective-permute-start.27
  79.1 0.7 collective-permute-start.26
  79.7 1.4 collective-permute-done.23.refs_2_
  81.4 1.3 collective-permute-start.30
  82.7 0.7 collective-permute-start.28
  83.3 1.6 collective-permute-start.29
  84.9 0.6 shard_map.67._.refs_6_
  85.5 0.6 collective-permute-start.36
  86.4 1.3 collective-permute-start.32
  87.8 8.4 %collective-permute-start.31 = (bf16[272,512]{1,0:T(8,128)(2,1)S(1)}, bf16[272,512]{1,0:T(8,128)(2,1)S(1)}, u32[]{:S(2)}, u32[]{:S(2)}) collective-permute-start(bf16[272,512]{1,0:T(8,128)(2,1)S(1)} %shard_map.69._), channel_id=1, source_target_pairs={{0,4},{12,8},{1,5},{13,9},{2,6},{14,10},{3,7},{15,11},{16,20},{28,... | collective-permute-start | bytes 835592 | tf_op jit(solution)/shard_map/ppermute | solution.py:370
  96.3 3.7 %collective-permute-start.33 = (bf16[256,512]{1,0:T(8,128)(2,1)S(1)}, bf16[256,512]{1,0:T(8,128)(2,1)S(1)}, u32[]{:S(2)}, u32[]{:S(2)}) collective-permute-start(bf16[256,512]{1,0:T(8,128)(2,1)S(1)} %shard_map.71._), channel_id=1, source_target_pairs={{0,4},{12,8},{1,5},{13,9},{2,6},{14,10},{3,7},{15,11},{16,20},{28,... | collective-permute-start | bytes 786440 | tf_op jit(solution)/shard_map/ppermute | solution.py:370
  100.1 0.6 shard_map.72._.refs_6_
  100.6 1.5 collective-permute-start.39
  102.2 1.5 collective-permute-start.34
  103.7 2.1 %collective-permute-done.33.refs_2_ = bf16[256,512]{1,0:T(8,128)(2,1)S(1)} collective-permute-done((bf16[256,512]{1,0:T(8,128)(2,1)S(1)}, bf16[256,512]{1,0:T(8,128)(2,1)S(1)}, u32[]{:S(2)}, u32[]{:S(2)}) %collective-permute-start.33) | collective-permute-done | bytes 262176 | tf_op jit(solution)/shard_map/ppermute | solution.py:370
  106.5 4.0 %collective-permute-done.34.refs_2_ = bf16[256,512]{1,0:T(8,128)(2,1)S(1)} collective-permute-done((bf16[256,512]{1,0:T(8,128)(2,1)S(1)}, bf16[256,512]{1,0:T(8,128)(2,1)S(1)}, u32[]{:S(2)}, u32[]{:S(2)}) %collective-permute-start.34) | collective-permute-done | bytes 262176 | tf_op jit(solution)/shard_map/ppermute | solution.py:370
  110.4 0.7 collective-permute-start.35
  112.6 1.3 collective-permute-start.43
  113.9 0.7 collective-permute-start.42
  114.6 0.6 collective-permute-start.47
  115.2 1.5 collective-permute-start.44
  116.7 3.5 %shard_map.78 = (f32[1024,512]{1,0:T(8,128)S(1)}, f32[1]{0:T(128)}) custom-call(bf16[272,512]{1,0:T(8,128)(2,1)S(1)} %shard_map.77._.refs_1_, s32[3]{0:T(128)S(1)} %pad_add_fusion.refs_0_, bf16[2,1024,512]{2,1,0:T(8,128)(2,1)S(1)} %get-tuple-element.38._.refs_1_, bf16[1024,512]{1,0:T(8,128)(2,1)} %refs_2_.3, bf16[1024,512]{1,0:T(8,128)(2,1)S(1)} %copy-done.1, ...), custom_call_target="tpu_custom_call" | custom-call | flops 1 | bytes 1 | tf_op jit(solution)/shard_map/pallas_call | solution.py:33
  120.2 3.5 %shard_map.79 = (f32[1024,512]{1,0:T(8,128)S(1)}, f32[1]{0:T(128)}) custom-call(f32[1024,512]{1,0:T(8,128)S(1)} %get-tuple-element.65._.refs_1_, s32[3]{0:T(128)S(1)} %pad_add_fusion.refs_0_, bf16[2,1024,512]{2,1,0:T(8,128)(2,1)S(1)} %get-tuple-element.38._.refs_1_, bf16[1024,512]{1,0:T(8,128)(2,1)} %refs_2_.3, bf16[1024,512]{1,0:T(8,128)(2,1)S(1)} %copy-done.1, ...), custom_call_target="tpu_custom_call" | custom-call | flops 1 | bytes 1 | tf_op jit(solution)/shard_map/pallas_call | solution.py:33
  124.4 4.5 %collective-permute-done.44.refs_7_.refs_1_ = bf16[256,512]{1,0:T(8,128)(2,1)S(1)} collective-permute-done((bf16[256,512]{1,0:T(8,128)(2,1)S(1)}, bf16[256,512]{1,0:T(8,128)(2,1)S(1)}, u32[]{:S(2)}, u32[]{:S(2)}) %collective-permute-start.44) | collective-permute-done | bytes 262176 | tf_op jit(solution)/shard_map/ppermute | solution.py:55
  129.0 1.3 collective-permute-start.50
  130.3 0.6 shard_map.81._.refs_8_.refs_6_
  130.9 0.6 collective-permute-start.51
  131.6 3.1 %shard_map.82._ = f32[1024,512]{1,0:T(8,128)} custom-call(bf16[272,512]{1,0:T(8,128)(2,1)S(1)} %shard_map.81._.refs_8_.refs_6_, s32[3]{0:T(128)S(1)} %pad_add_fusion.refs_0_, f32[1024,512]{1,0:T(8,128)S(1)} %get-tuple-element.65._.refs_1_, bf16[256,512]{1,0:T(8,128)(2,1)S(1)} %get-tuple-element.44._.refs_3_.refs_2_, ...), custom_call_target="tpu_custom_call" | custom-call | flops 1 | bytes 1 | tf_op jit(solution)/shard_map/pallas_call | solution.py:33
  134.7 11.2 %collective-permute-done.50.refs_2_ = bf16[256,512]{1,0:T(8,128)(2,1)S(1)} collective-permute-done((bf16[256,512]{1,0:T(8,128)(2,1)S(1)}, bf16[256,512]{1,0:T(8,128)(2,1)S(1)}, u32[]{:S(2)}, u32[]{:S(2)}) %collective-permute-start.50) | collective-permute-done | bytes 262176 | tf_op jit(solution)/shard_map/ppermute | solution.py:370
  145.9 1.6 copy-done.2
  148.0 1.8 %collective-permute-start.54 = (bf16[256,512]{1,0:T(8,128)(2,1)S(1)}, bf16[256,512]{1,0:T(8,128)(2,1)S(1)}, u32[]{:S(2)}, u32[]{:S(2)}) collective-permute-start(bf16[256,512]{1,0:T(8,128)(2,1)S(1)} %shard_map.83._.refs_12_.refs_10_), channel_id=1, source_target_pairs={{0,2},{1,3},{2,0},{3,1},{4,6},{5,7},{6,4},{7,5},{8,10},{9,11},{10,... | collective-permute-start | bytes 786440 | tf_op jit(solution)/shard_map/ppermute | solution.py:55
  150.4 5.9 %collective-permute-done.54.refs_13_.refs_11_ = bf16[256,512]{1,0:T(8,128)(2,1)S(1)} collective-permute-done((bf16[256,512]{1,0:T(8,128)(2,1)S(1)}, bf16[256,512]{1,0:T(8,128)(2,1)S(1)}, u32[]{:S(2)}, u32[]{:S(2)}) %collective-permute-start.54) | collective-permute-done | bytes 262176 | tf_op jit(solution)/shard_map/ppermute | solution.py:55
  157.8 1.5 shard_map.84
  160.0 2.9 %collective-permute-start.57 = (f32[]{:T(128)}, f32[]{:T(128)}, u32[]{:S(2)}, u32[]{:S(2)}) collective-permute-start(f32[]{:T(128)} %bitcast.8), channel_id=1, source_target_pairs={{0,16},{16,0},{1,17},{17,1},{2,18},{18,2},{3,19},{19,3},{4,20},{20... | collective-permute-start | bytes 20 | tf_op jit(solution)/shard_map/ppermute | solution.py:59
  162.9 3.8 %shard_map.85 = f32[1024,512]{1,0:T(8,128)} custom-call(f32[1]{0:T(128)} %get-tuple-element.70._, s32[3]{0:T(128)S(1)} %pad_add_fusion.refs_0_, f32[1024,512]{1,0:T(8,128)S(1)} %get-tuple-element.66._.refs_1_, bf16[256,512]{1,0:T(8,128)(2,1)S(1)} %get-tuple-element.56._.refs_3_.refs_2_, bf16[256,512]{1,0:T(8,128)(2,1)S(1)} %get-tuple-element.57.refs_4_.refs_3_, ...), custom_call_target="tpu_custom_call" | custom-call | flops 1 | bytes 1 | tf_op jit(solution)/shard_map/pallas_call | solution.py:33
  (102 shorter events, 10.3 us)
Async XLA Ops:
  0.6 1.2 copy-start
  3.4 4.6 %collective-permute-start = (f32[2,512]{1,0:T(2,128)S(1)}, f32[2,512]{1,0:T(2,128)S(1)}, u32[]{:S(2)}, u32[]{:S(2)}) collective-permute-start(f32[2,512]{1,0:T(2,128)S(1)} %shard_map.49._), channel_id=1, source_target_pairs={{0,16},{16,0},{1,17},{17,1},{2,18},{18,2},{3,19},{19,3},{4,20},{20... | collective-permute-start | bytes 12296 | tf_op jit(solution)/shard_map/ppermute | solution.py:59
  10.8 1.0 copy-start.3
  11.8 26.3 %collective-permute-start.6 = (bf16[1024,512]{1,0:T(8,128)(2,1)}, bf16[1024,512]{1,0:T(8,128)(2,1)S(1)}, u32[]{:S(2)}, u32[]{:S(2)}) collective-permute-start(bf16[1024,512]{1,0:T(8,128)(2,1)} %refs_2_.3), channel_id=1, source_target_pairs={{0,16},{16,0},{1,17},{17,1},{2,18},{18,2},{3,19},{19,3},{4,20},{20... | collective-permute-start | bytes 3145736 | tf_op jit(solution)/shard_map/ppermute | solution.py:59
  15.2 2.3 %collective-permute-start.1 = (bf16[512,512]{1,0:T(8,128)(2,1)}, bf16[512,512]{1,0:T(8,128)(2,1)}, u32[]{:S(2)}, u32[]{:S(2)}) collective-permute-start(bf16[512,512]{1,0:T(8,128)(2,1)} %get-tuple-element.74), channel_id=1, source_target_pairs={{0,1},{1,0},{2,3},{3,2},{4,5},{5,4},{6,7},{7,6},{8,9},{9,8},{10,11... | collective-permute-start | bytes 1572872 | tf_op jit(solution)/shard_map/ppermute | solution.py:59
  15.2 3.0 %collective-permute-start.2 = (bf16[512,512]{1,0:T(8,128)(2,1)}, bf16[512,512]{1,0:T(8,128)(2,1)}, u32[]{:S(2)}, u32[]{:S(2)}) collective-permute-start(bf16[512,512]{1,0:T(8,128)(2,1)} %get-tuple-element.73), channel_id=1, source_target_pairs={{0,1},{1,0},{2,3},{3,2},{4,5},{5,4},{6,7},{7,6},{8,9},{9,8},{10,11... | collective-permute-start | bytes 1572872 | tf_op jit(solution)/shard_map/ppermute | solution.py:59
  15.7 8.1 %collective-permute-start.3 = (bf16[512,512]{1,0:T(8,128)(2,1)}, bf16[512,512]{1,0:T(8,128)(2,1)}, u32[]{:S(2)}, u32[]{:S(2)}) collective-permute-start(bf16[512,512]{1,0:T(8,128)(2,1)} %get-tuple-element.72), channel_id=1, source_target_pairs={{0,1},{1,0},{2,3},{3,2},{4,5},{5,4},{6,7},{7,6},{8,9},{9,8},{10,11... | collective-permute-start | bytes 1572872 | tf_op jit(solution)/shard_map/ppermute | solution.py:59
  15.7 8.1 %collective-permute-start.4 = (bf16[512,512]{1,0:T(8,128)(2,1)}, bf16[512,512]{1,0:T(8,128)(2,1)}, u32[]{:S(2)}, u32[]{:S(2)}) collective-permute-start(bf16[512,512]{1,0:T(8,128)(2,1)} %get-tuple-element.71), channel_id=1, source_target_pairs={{0,1},{1,0},{2,3},{3,2},{4,5},{5,4},{6,7},{7,6},{8,9},{9,8},{10,11... | collective-permute-start | bytes 1572872 | tf_op jit(solution)/shard_map/ppermute | solution.py:59
  16.2 7.0 %copy-start.4 = (bf16[1040,512]{1,0:T(8,128)(2,1)S(1)}, bf16[1040,512]{1,0:T(8,128)(2,1)}, u32[]{:S(2)}) copy-start(bf16[1040,512]{1,0:T(8,128)(2,1)} %copy-done.3) | copy-start | bytes 3194884
  21.7 11.6 %collective-permute-start.5 = (bf16[400,512]{1,0:T(8,128)(2,1)S(1)}, bf16[400,512]{1,0:T(8,128)(2,1)S(1)}, u32[]{:S(2)}, u32[]{:S(2)}) collective-permute-start(bf16[400,512]{1,0:T(8,128)(2,1)S(1)} %get-tuple-element.42), channel_id=1, source_target_pairs={{0,2},{1,3},{2,0},{3,1},{4,6},{5,7},{6,4},{7,5},{8,10},{9,11},{10,... | collective-permute-start | bytes 1228808 | tf_op jit(solution)/shard_map/ppermute | solution.py:55
  23.2 44.3 %collective-permute-start.16 = (bf16[1040,512]{1,0:T(8,128)(2,1)S(1)}, bf16[1040,512]{1,0:T(8,128)(2,1)S(1)}, u32[]{:S(2)}, u32[]{:S(2)}) collective-permute-start(bf16[1040,512]{1,0:T(8,128)(2,1)S(1)} %copy-done.4), channel_id=1, source_target_pairs={{0,16},{16,0},{1,17},{17,1},{2,18},{18,2},{3,19},{19,3},{4,20},{20... | collective-permute-start | bytes 3194888 | tf_op jit(solution)/shard_map/ppermute | solution.py:59
  38.3 2.6 %collective-permute-start.10 = (bf16[256,512]{1,0:T(8,128)(2,1)S(1)}, bf16[256,512]{1,0:T(8,128)(2,1)S(1)}, u32[]{:S(2)}, u32[]{:S(2)}) collective-permute-start(bf16[256,512]{1,0:T(8,128)(2,1)S(1)} %get-tuple-element.47.refs_6_.refs_5_), channel_id=1, source_target_pairs={{0,1},{1,0},{2,3},{3,2},{4,5},{5,4},{6,7},{7,6},{8,9},{9,8},{10,11... | collective-permute-start | bytes 786440 | tf_op jit(solution)/shard_map/ppermute | solution.py:59
  38.3 3.0 %collective-permute-start.7 = (bf16[256,512]{1,0:T(8,128)(2,1)S(1)}, bf16[256,512]{1,0:T(8,128)(2,1)S(1)}, u32[]{:S(2)}, u32[]{:S(2)}) collective-permute-start(bf16[256,512]{1,0:T(8,128)(2,1)S(1)} %get-tuple-element.44._.refs_3_.refs_2_), channel_id=1, source_target_pairs={{0,1},{1,0},{2,3},{3,2},{4,5},{5,4},{6,7},{7,6},{8,9},{9,8},{10,11... | collective-permute-start | bytes 786440 | tf_op jit(solution)/shard_map/ppermute | solution.py:59
  38.8 11.7 %collective-permute-start.11 = (bf16[400,512]{1,0:T(8,128)(2,1)S(1)}, bf16[400,512]{1,0:T(8,128)(2,1)S(1)}, u32[]{:S(2)}, u32[]{:S(2)}) collective-permute-start(bf16[400,512]{1,0:T(8,128)(2,1)S(1)} %get-tuple-element.50), channel_id=1, source_target_pairs={{0,2},{1,3},{2,0},{3,1},{4,6},{5,7},{6,4},{7,5},{8,10},{9,11},{10,... | collective-permute-start | bytes 1228808 | tf_op jit(solution)/shard_map/ppermute | solution.py:55
  40.8 4.0 %collective-permute-start.8 = (bf16[256,512]{1,0:T(8,128)(2,1)S(1)}, bf16[256,512]{1,0:T(8,128)(2,1)S(1)}, u32[]{:S(2)}, u32[]{:S(2)}) collective-permute-start(bf16[256,512]{1,0:T(8,128)(2,1)S(1)} %get-tuple-element.45.refs_4_.refs_3_), channel_id=1, source_target_pairs={{0,1},{1,0},{2,3},{3,2},{4,5},{5,4},{6,7},{7,6},{8,9},{9,8},{10,11... | collective-permute-start | bytes 786440 | tf_op jit(solution)/shard_map/ppermute | solution.py:59
  40.8 4.0 %collective-permute-start.9 = (bf16[256,512]{1,0:T(8,128)(2,1)S(1)}, bf16[256,512]{1,0:T(8,128)(2,1)S(1)}, u32[]{:S(2)}, u32[]{:S(2)}) collective-permute-start(bf16[256,512]{1,0:T(8,128)(2,1)S(1)} %get-tuple-element.46.refs_5_.refs_4_), channel_id=1, source_target_pairs={{0,1},{1,0},{2,3},{3,2},{4,5},{5,4},{6,7},{7,6},{8,9},{9,8},{10,11... | collective-permute-start | bytes 786440 | tf_op jit(solution)/shard_map/ppermute | solution.py:59
  41.3 15.1 %collective-permute-start.12 = (bf16[400,512]{1,0:T(8,128)(2,1)S(1)}, bf16[400,512]{1,0:T(8,128)(2,1)S(1)}, u32[]{:S(2)}, u32[]{:S(2)}) collective-permute-start(bf16[400,512]{1,0:T(8,128)(2,1)S(1)} %shard_map.53._), channel_id=1, source_target_pairs={{0,4},{12,8},{1,5},{13,9},{2,6},{14,10},{3,7},{15,11},{16,20},{28,... | collective-permute-start | bytes 1228808 | tf_op jit(solution)/shard_map/ppermute | solution.py:370
  50.6 16.7 %collective-permute-start.15 = (bf16[400,512]{1,0:T(8,128)(2,1)S(1)}, bf16[400,512]{1,0:T(8,128)(2,1)S(1)}, u32[]{:S(2)}, u32[]{:S(2)}) collective-permute-start(bf16[400,512]{1,0:T(8,128)(2,1)S(1)} %shard_map.56._), channel_id=1, source_target_pairs={{0,4},{12,8},{1,5},{13,9},{2,6},{14,10},{3,7},{15,11},{16,20},{28,... | collective-permute-start | bytes 1228808 | tf_op jit(solution)/shard_map/ppermute | solution.py:370
  54.4 9.3 %collective-permute-start.13 = (bf16[256,512]{1,0:T(8,128)(2,1)S(1)}, bf16[256,512]{1,0:T(8,128)(2,1)S(1)}, u32[]{:S(2)}, u32[]{:S(2)}) collective-permute-start(bf16[256,512]{1,0:T(8,128)(2,1)S(1)} %get-tuple-element.51), channel_id=1, source_target_pairs={{0,2},{1,3},{2,0},{3,1},{4,6},{5,7},{6,4},{7,5},{8,10},{9,11},{10,... | collective-permute-start | bytes 786440 | tf_op jit(solution)/shard_map/ppermute | solution.py:55
  56.0 11.3 %collective-permute-start.14 = (bf16[256,512]{1,0:T(8,128)(2,1)S(1)}, bf16[256,512]{1,0:T(8,128)(2,1)S(1)}, u32[]{:S(2)}, u32[]{:S(2)}) collective-permute-start(bf16[256,512]{1,0:T(8,128)(2,1)S(1)} %get-tuple-element.53), channel_id=1, source_target_pairs={{0,2},{1,3},{2,0},{3,1},{4,6},{5,7},{6,4},{7,5},{8,10},{9,11},{10,... | collective-permute-start | bytes 786440 | tf_op jit(solution)/shard_map/ppermute | solution.py:55
  56.6 12.3 %collective-permute-start.17 = (bf16[400,512]{1,0:T(8,128)(2,1)S(1)}, bf16[400,512]{1,0:T(8,128)(2,1)S(1)}, u32[]{:S(2)}, u32[]{:S(2)}) collective-permute-start(bf16[400,512]{1,0:T(8,128)(2,1)S(1)} %shard_map.57._.refs_0_), channel_id=1, source_target_pairs={{4,8},{8,4},{5,9},{9,5},{6,10},{10,6},{7,11},{11,7},{20,24},{24,20... | collective-permute-start | bytes 1228808 | tf_op jit(solution)/shard_map/ppermute | solution.py:370
  63.8 5.4 %collective-permute-start.18 = (bf16[256,512]{1,0:T(8,128)(2,1)S(1)}, bf16[256,512]{1,0:T(8,128)(2,1)S(1)}, u32[]{:S(2)}, u32[]{:S(2)}) collective-permute-start(bf16[256,512]{1,0:T(8,128)(2,1)S(1)} %shard_map.58._), channel_id=1, source_target_pairs={{0,4},{12,8},{1,5},{13,9},{2,6},{14,10},{3,7},{15,11},{16,20},{28,... | collective-permute-start | bytes 786440 | tf_op jit(solution)/shard_map/ppermute | solution.py:370
  67.7 2.0 %collective-permute-start.19 = (bf16[256,512]{1,0:T(8,128)(2,1)S(1)}, bf16[256,512]{1,0:T(8,128)(2,1)S(1)}, u32[]{:S(2)}, u32[]{:S(2)}) collective-permute-start(bf16[256,512]{1,0:T(8,128)(2,1)S(1)} %get-tuple-element.56._.refs_3_.refs_2_), channel_id=1, source_target_pairs={{0,1},{1,0},{2,3},{3,2},{4,5},{5,4},{6,7},{7,6},{8,9},{9,8},{10,11... | collective-permute-start | bytes 786440 | tf_op jit(solution)/shard_map/ppermute | solution.py:59
  67.8 3.2 %collective-permute-start.20 = (bf16[256,512]{1,0:T(8,128)(2,1)S(1)}, bf16[256,512]{1,0:T(8,128)(2,1)S(1)}, u32[]{:S(2)}, u32[]{:S(2)}) collective-permute-start(bf16[256,512]{1,0:T(8,128)(2,1)S(1)} %get-tuple-element.57.refs_4_.refs_3_), channel_id=1, source_target_pairs={{0,1},{1,0},{2,3},{3,2},{4,5},{5,4},{6,7},{7,6},{8,9},{9,8},{10,11... | collective-permute-start | bytes 786440 | tf_op jit(solution)/shard_map/ppermute | solution.py:59
  68.3 13.0 %collective-permute-start.24 = (bf16[400,512]{1,0:T(8,128)(2,1)S(1)}, bf16[400,512]{1,0:T(8,128)(2,1)S(1)}, u32[]{:S(2)}, u32[]{:S(2)}) collective-permute-start(bf16[400,512]{1,0:T(8,128)(2,1)S(1)} %shard_map.60._.refs_0_), channel_id=1, source_target_pairs={{4,8},{8,4},{5,9},{9,5},{6,10},{10,6},{7,11},{11,7},{20,24},{24,20... | collective-permute-start | bytes 1228808 | tf_op jit(solution)/shard_map/ppermute | solution.py:370
  69.0 6.7 %collective-permute-start.21 = (bf16[256,512]{1,0:T(8,128)(2,1)S(1)}, bf16[256,512]{1,0:T(8,128)(2,1)S(1)}, u32[]{:S(2)}, u32[]{:S(2)}) collective-permute-start(bf16[256,512]{1,0:T(8,128)(2,1)S(1)} %get-tuple-element.58.refs_5_.refs_4_), channel_id=1, source_target_pairs={{0,1},{1,0},{2,3},{3,2},{4,5},{5,4},{6,7},{7,6},{8,9},{9,8},{10,11... | collective-permute-start | bytes 786440 | tf_op jit(solution)/shard_map/ppermute | solution.py:59
  69.1 6.6 %collective-permute-start.22 = (bf16[256,512]{1,0:T(8,128)(2,1)S(1)}, bf16[256,512]{1,0:T(8,128)(2,1)S(1)}, u32[]{:S(2)}, u32[]{:S(2)}) collective-permute-start(bf16[256,512]{1,0:T(8,128)(2,1)S(1)} %get-tuple-element.59.refs_6_.refs_5_), channel_id=1, source_target_pairs={{0,1},{1,0},{2,3},{3,2},{4,5},{5,4},{6,7},{7,6},{8,9},{9,8},{10,11... | collective-permute-start | bytes 786440 | tf_op jit(solution)/shard_map/ppermute | solution.py:59
  69.7 13.7 %collective-permute-start.25 = (bf16[400,512]{1,0:T(8,128)(2,1)S(1)}, bf16[400,512]{1,0:T(8,128)(2,1)S(1)}, u32[]{:S(2)}, u32[]{:S(2)}) collective-permute-start(bf16[400,512]{1,0:T(8,128)(2,1)S(1)} %shard_map.62._.refs_1_), channel_id=1, source_target_pairs={{4,0},{8,12},{5,1},{9,13},{6,2},{10,14},{7,3},{11,15},{20,16},{24,... | collective-permute-start | bytes 1228808 | tf_op jit(solution)/shard_map/ppermute | solution.py:370
  71.0 10.2 %collective-permute-start.23 = (bf16[256,512]{1,0:T(8,128)(2,1)S(1)}, bf16[256,512]{1,0:T(8,128)(2,1)S(1)}, u32[]{:S(2)}, u32[]{:S(2)}) collective-permute-start(bf16[256,512]{1,0:T(8,128)(2,1)S(1)} %shard_map.59._), channel_id=1, source_target_pairs={{0,4},{12,8},{1,5},{13,9},{2,6},{14,10},{3,7},{15,11},{16,20},{28,... | collective-permute-start | bytes 786440 | tf_op jit(solution)/shard_map/ppermute | solution.py:370
  77.5 8.9 %collective-permute-start.27 = (bf16[272,512]{1,0:T(8,128)(2,1)S(1)}, bf16[272,512]{1,0:T(8,128)(2,1)S(1)}, u32[]{:S(2)}, u32[]{:S(2)}) collective-permute-start(bf16[272,512]{1,0:T(8,128)(2,1)S(1)} %get-tuple-element.62), channel_id=1, source_target_pairs={{0,2},{1,3},{2,0},{3,1},{4,6},{5,7},{6,4},{7,5},{8,10},{9,11},{10,... | collective-permute-start | bytes 835592 | tf_op jit(solution)/shard_map/ppermute | solution.py:55
  79.1 6.4 %collective-permute-start.26 = (bf16[256,512]{1,0:T(8,128)(2,1)S(1)}, bf16[256,512]{1,0:T(8,128)(2,1)S(1)}, u32[]{:S(2)}, u32[]{:S(2)}) collective-permute-start(bf16[256,512]{1,0:T(8,128)(2,1)S(1)} %shard_map.63._.refs_0_), channel_id=1, source_target_pairs={{4,8},{8,4},{5,9},{9,5},{6,10},{10,6},{7,11},{11,7},{20,24},{24,20... | collective-permute-start | bytes 786440 | tf_op jit(solution)/shard_map/ppermute | solution.py:370
  81.4 18.7 %collective-permute-start.30 = (bf16[400,512]{1,0:T(8,128)(2,1)S(1)}, bf16[400,512]{1,0:T(8,128)(2,1)S(1)}, u32[]{:S(2)}, u32[]{:S(2)}) collective-permute-start(bf16[400,512]{1,0:T(8,128)(2,1)S(1)} %shard_map.66._.refs_1_), channel_id=1, source_target_pairs={{4,0},{8,12},{5,1},{9,13},{6,2},{10,14},{7,3},{11,15},{20,16},{24,... | collective-permute-start | bytes 1228808 | tf_op jit(solution)/shard_map/ppermute | solution.py:370
  82.7 5.1 %collective-permute-start.28 = (bf16[256,512]{1,0:T(8,128)(2,1)S(1)}, bf16[256,512]{1,0:T(8,128)(2,1)S(1)}, u32[]{:S(2)}, u32[]{:S(2)}) collective-permute-start(bf16[256,512]{1,0:T(8,128)(2,1)S(1)} %shard_map.65._.refs_0_), channel_id=1, source_target_pairs={{4,8},{8,4},{5,9},{9,5},{6,10},{10,6},{7,11},{11,7},{20,24},{24,20... | collective-permute-start | bytes 786440 | tf_op jit(solution)/shard_map/ppermute | solution.py:370
  83.3 12.9 %collective-permute-start.29 = (bf16[256,512]{1,0:T(8,128)(2,1)S(1)}, bf16[256,512]{1,0:T(8,128)(2,1)S(1)}, u32[]{:S(2)}, u32[]{:S(2)}) collective-permute-start(bf16[256,512]{1,0:T(8,128)(2,1)S(1)} %get-tuple-element.64), channel_id=1, source_target_pairs={{0,2},{1,3},{2,0},{3,1},{4,6},{5,7},{6,4},{7,5},{8,10},{9,11},{10,... | collective-permute-start | bytes 786440 | tf_op jit(solution)/shard_map/ppermute | solution.py:55
  85.5 20.8 %collective-permute-start.36 = (bf16[400,512]{1,0:T(8,128)(2,1)S(1)}, bf16[400,512]{1,0:T(8,128)(2,1)S(1)}, u32[]{:S(2)}, u32[]{:S(2)}) collective-permute-start(bf16[400,512]{1,0:T(8,128)(2,1)S(1)} %shard_map.67._.refs_6_), channel_id=1, source_target_pairs={{0,2},{1,3},{2,0},{3,1},{4,6},{5,7},{6,4},{7,5},{8,10},{9,11},{10,... | collective-permute-start | bytes 1228808 | tf_op jit(solution)/shard_map/ppermute | solution.py:55
  86.4 15.8 %collective-permute-start.32 = (bf16[256,512]{1,0:T(8,128)(2,1)S(1)}, bf16[256,512]{1,0:T(8,128)(2,1)S(1)}, u32[]{:S(2)}, u32[]{:S(2)}) collective-permute-start(bf16[256,512]{1,0:T(8,128)(2,1)S(1)} %shard_map.68._.refs_1_), channel_id=1, source_target_pairs={{4,0},{8,12},{5,1},{9,13},{6,2},{10,14},{7,3},{11,15},{20,16},{24,... | collective-permute-start | bytes 786440 | tf_op jit(solution)/shard_map/ppermute | solution.py:370
  87.8 18.1 %collective-permute-start.31 = (bf16[272,512]{1,0:T(8,128)(2,1)S(1)}, bf16[272,512]{1,0:T(8,128)(2,1)S(1)}, u32[]{:S(2)}, u32[]{:S(2)}) collective-permute-start(bf16[272,512]{1,0:T(8,128)(2,1)S(1)} %shard_map.69._), channel_id=1, source_target_pairs={{0,4},{12,8},{1,5},{13,9},{2,6},{14,10},{3,7},{15,11},{16,20},{28,... | collective-permute-start | bytes 835592 | tf_op jit(solution)/shard_map/ppermute | solution.py:370
  96.3 9.5 %collective-permute-start.33 = (bf16[256,512]{1,0:T(8,128)(2,1)S(1)}, bf16[256,512]{1,0:T(8,128)(2,1)S(1)}, u32[]{:S(2)}, u32[]{:S(2)}) collective-permute-start(bf16[256,512]{1,0:T(8,128)(2,1)S(1)} %shard_map.71._), channel_id=1, source_target_pairs={{0,4},{12,8},{1,5},{13,9},{2,6},{14,10},{3,7},{15,11},{16,20},{28,... | collective-permute-start | bytes 786440 | tf_op jit(solution)/shard_map/ppermute | solution.py:370
  100.6 10.5 %collective-permute-start.39 = (bf16[400,512]{1,0:T(8,128)(2,1)S(1)}, bf16[400,512]{1,0:T(8,128)(2,1)S(1)}, u32[]{:S(2)}, u32[]{:S(2)}) collective-permute-start(bf16[400,512]{1,0:T(8,128)(2,1)S(1)} %shard_map.72._.refs_6_), channel_id=1, source_target_pairs={{0,2},{1,3},{2,0},{3,1},{4,6},{5,7},{6,4},{7,5},{8,10},{9,11},{10,... | collective-permute-start | bytes 1228808 | tf_op jit(solution)/shard_map/ppermute | solution.py:55
  102.2 8.3 %collective-permute-start.34 = (bf16[256,512]{1,0:T(8,128)(2,1)S(1)}, bf16[256,512]{1,0:T(8,128)(2,1)S(1)}, u32[]{:S(2)}, u32[]{:S(2)}) collective-permute-start(bf16[256,512]{1,0:T(8,128)(2,1)S(1)} %shard_map.70._.refs_1_), channel_id=1, source_target_pairs={{4,0},{8,12},{5,1},{9,13},{6,2},{10,14},{7,3},{11,15},{20,16},{24,... | collective-permute-start | bytes 786440 | tf_op jit(solution)/shard_map/ppermute | solution.py:370
  105.8 8.1 %collective-permute-start.37 = (bf16[400,512]{1,0:T(8,128)(2,1)S(1)}, bf16[400,512]{1,0:T(8,128)(2,1)S(1)}, u32[]{:S(2)}, u32[]{:S(2)}) collective-permute-start(bf16[400,512]{1,0:T(8,128)(2,1)S(1)} %shard_map.67._.refs_6_), channel_id=1, source_target_pairs={{0,1},{1,0},{2,3},{3,2},{4,5},{5,4},{6,7},{7,6},{8,9},{9,8},{10,11... | collective-permute-start | bytes 1228808 | tf_op jit(solution)/shard_map/ppermute | solution.py:59
  105.8 8.8 %collective-permute-start.40 = (bf16[400,512]{1,0:T(8,128)(2,1)S(1)}, bf16[400,512]{1,0:T(8,128)(2,1)S(1)}, u32[]{:S(2)}, u32[]{:S(2)}) collective-permute-start(bf16[400,512]{1,0:T(8,128)(2,1)S(1)} %shard_map.72._.refs_6_), channel_id=1, source_target_pairs={{0,1},{1,0},{2,3},{3,2},{4,5},{5,4},{6,7},{7,6},{8,9},{9,8},{10,11... | collective-permute-start | bytes 1228808 | tf_op jit(solution)/shard_map/ppermute | solution.py:59
  106.3 8.9 %collective-permute-start.38 = (bf16[400,512]{1,0:T(8,128)(2,1)S(1)}, bf16[400,512]{1,0:T(8,128)(2,1)S(1)}, u32[]{:S(2)}, u32[]{:S(2)}) collective-permute-start(bf16[400,512]{1,0:T(8,128)(2,1)S(1)} %collective-permute-done.36.refs_7_), channel_id=1, source_target_pairs={{0,1},{1,0},{2,3},{3,2},{4,5},{5,4},{6,7},{7,6},{8,9},{9,8},{10,11... | collective-permute-start | bytes 1228808 | tf_op jit(solution)/shard_map/ppermute | solution.py:59
  110.4 2.0 %collective-permute-start.35 = (bf16[272,512]{1,0:T(8,128)(2,1)S(1)}, bf16[272,512]{1,0:T(8,128)(2,1)S(1)}, u32[]{:S(2)}, u32[]{:S(2)}) collective-permute-start(bf16[272,512]{1,0:T(8,128)(2,1)S(1)} %shard_map.73._.refs_0_), channel_id=1, source_target_pairs={{4,8},{8,4},{5,9},{9,5},{6,10},{10,6},{7,11},{11,7},{20,24},{24,20... | collective-permute-start | bytes 835592 | tf_op jit(solution)/shard_map/ppermute | solution.py:370
  111.1 5.5 %collective-permute-start.41 = (bf16[400,512]{1,0:T(8,128)(2,1)S(1)}, bf16[400,512]{1,0:T(8,128)(2,1)S(1)}, u32[]{:S(2)}, u32[]{:S(2)}) collective-permute-start(bf16[400,512]{1,0:T(8,128)(2,1)S(1)} %collective-permute-done.39.refs_7_), channel_id=1, source_target_pairs={{0,1},{1,0},{2,3},{3,2},{4,5},{5,4},{6,7},{7,6},{8,9},{9,8},{10,11... | collective-permute-start | bytes 1228808 | tf_op jit(solution)/shard_map/ppermute | solution.py:59
  111.8 4.9 %copy-start.1 = (bf16[1024,512]{1,0:T(8,128)(2,1)S(1)}, bf16[1024,512]{1,0:T(8,128)(2,1)}, u32[]{:S(2)}) copy-start(bf16[1024,512]{1,0:T(8,128)(2,1)} %refs_3_.3) | copy-start | bytes 3145732
  112.6 16.5 %collective-permute-start.43 = (bf16[272,512]{1,0:T(8,128)(2,1)S(1)}, bf16[272,512]{1,0:T(8,128)(2,1)S(1)}, u32[]{:S(2)}, u32[]{:S(2)}) collective-permute-start(bf16[272,512]{1,0:T(8,128)(2,1)S(1)} %shard_map.77._.refs_1_), channel_id=1, source_target_pairs={{4,0},{8,12},{5,1},{9,13},{6,2},{10,14},{7,3},{11,15},{20,16},{24,... | collective-permute-start | bytes 835592 | tf_op jit(solution)/shard_map/ppermute | solution.py:370
  113.9 9.9 %collective-permute-start.42 = (bf16[256,512]{1,0:T(8,128)(2,1)S(1)}, bf16[256,512]{1,0:T(8,128)(2,1)S(1)}, u32[]{:S(2)}, u32[]{:S(2)}) collective-permute-start(bf16[256,512]{1,0:T(8,128)(2,1)S(1)} %shard_map.75._.refs_0_), channel_id=1, source_target_pairs={{4,8},{8,4},{5,9},{9,5},{6,10},{10,6},{7,11},{11,7},{20,24},{24,20... | collective-permute-start | bytes 786440 | tf_op jit(solution)/shard_map/ppermute | solution.py:370
  114.6 9.8 %collective-permute-start.47 = (bf16[256,512]{1,0:T(8,128)(2,1)S(1)}, bf16[256,512]{1,0:T(8,128)(2,1)S(1)}, u32[]{:S(2)}, u32[]{:S(2)}) collective-permute-start(bf16[256,512]{1,0:T(8,128)(2,1)S(1)} %shard_map.76._.refs_10_.refs_4_), channel_id=1, source_target_pairs={{0,2},{1,3},{2,0},{3,1},{4,6},{5,7},{6,4},{7,5},{8,10},{9,11},{10,... | collective-permute-start | bytes 786440 | tf_op jit(solution)/shard_map/ppermute | solution.py:55
  115.2 13.8 %collective-permute-start.44 = (bf16[256,512]{1,0:T(8,128)(2,1)S(1)}, bf16[256,512]{1,0:T(8,128)(2,1)S(1)}, u32[]{:S(2)}, u32[]{:S(2)}) collective-permute-start(bf16[256,512]{1,0:T(8,128)(2,1)S(1)} %shard_map.74._.refs_6_.refs_0_), channel_id=1, source_target_pairs={{0,2},{1,3},{2,0},{3,1},{4,6},{5,7},{6,4},{7,5},{8,10},{9,11},{10,... | collective-permute-start | bytes 786440 | tf_op jit(solution)/shard_map/ppermute | solution.py:55
  116.7 14.3 %collective-permute-start.48 = (bf16[256,512]{1,0:T(8,128)(2,1)S(1)}, bf16[256,512]{1,0:T(8,128)(2,1)S(1)}, u32[]{:S(2)}, u32[]{:S(2)}) collective-permute-start(bf16[256,512]{1,0:T(8,128)(2,1)S(1)} %shard_map.76._.refs_10_.refs_4_), channel_id=1, source_target_pairs={{0,1},{1,0},{2,3},{3,2},{4,5},{5,4},{6,7},{7,6},{8,9},{9,8},{10,11... | collective-permute-start | bytes 786440 | tf_op jit(solution)/shard_map/ppermute | solution.py:59
  123.8 7.8 %collective-permute-start.45 = (bf16[256,512]{1,0:T(8,128)(2,1)S(1)}, bf16[256,512]{1,0:T(8,128)(2,1)S(1)}, u32[]{:S(2)}, u32[]{:S(2)}) collective-permute-start(bf16[256,512]{1,0:T(8,128)(2,1)S(1)} %shard_map.74._.refs_6_.refs_0_), channel_id=1, source_target_pairs={{0,1},{1,0},{2,3},{3,2},{4,5},{5,4},{6,7},{7,6},{8,9},{9,8},{10,11... | collective-permute-start | bytes 786440 | tf_op jit(solution)/shard_map/ppermute | solution.py:59
  124.3 7.2 %collective-permute-start.49 = (bf16[256,512]{1,0:T(8,128)(2,1)S(1)}, bf16[256,512]{1,0:T(8,128)(2,1)S(1)}, u32[]{:S(2)}, u32[]{:S(2)}) collective-permute-start(bf16[256,512]{1,0:T(8,128)(2,1)S(1)} %collective-permute-done.47.refs_11_.refs_5_), channel_id=1, source_target_pairs={{0,1},{1,0},{2,3},{3,2},{4,5},{5,4},{6,7},{7,6},{8,9},{9,8},{10,11... | collective-permute-start | bytes 786440 | tf_op jit(solution)/shard_map/ppermute | solution.py:59
  129.0 2.6 %collective-permute-start.46 = (bf16[256,512]{1,0:T(8,128)(2,1)S(1)}, bf16[256,512]{1,0:T(8,128)(2,1)S(1)}, u32[]{:S(2)}, u32[]{:S(2)}) collective-permute-start(bf16[256,512]{1,0:T(8,128)(2,1)S(1)} %collective-permute-done.44.refs_7_.refs_1_), channel_id=1, source_target_pairs={{0,1},{1,0},{2,3},{3,2},{4,5},{5,4},{6,7},{7,6},{8,9},{9,8},{10,11... | collective-permute-start | bytes 786440 | tf_op jit(solution)/shard_map/ppermute | solution.py:59
  129.0 16.8 %collective-permute-start.50 = (bf16[256,512]{1,0:T(8,128)(2,1)S(1)}, bf16[256,512]{1,0:T(8,128)(2,1)S(1)}, u32[]{:S(2)}, u32[]{:S(2)}) collective-permute-start(bf16[256,512]{1,0:T(8,128)(2,1)S(1)} %shard_map.80._.refs_1_), channel_id=1, source_target_pairs={{4,0},{8,12},{5,1},{9,13},{6,2},{10,14},{7,3},{11,15},{20,16},{24,... | collective-permute-start | bytes 786440 | tf_op jit(solution)/shard_map/ppermute | solution.py:370
  130.9 18.9 %collective-permute-start.51 = (bf16[272,512]{1,0:T(8,128)(2,1)S(1)}, bf16[272,512]{1,0:T(8,128)(2,1)S(1)}, u32[]{:S(2)}, u32[]{:S(2)}) collective-permute-start(bf16[272,512]{1,0:T(8,128)(2,1)S(1)} %shard_map.81._.refs_8_.refs_6_), channel_id=1, source_target_pairs={{0,2},{1,3},{2,0},{3,1},{4,6},{5,7},{6,4},{7,5},{8,10},{9,11},{10,... | collective-permute-start | bytes 835592 | tf_op jit(solution)/shard_map/ppermute | solution.py:55
  145.9 1.6 copy-start.2
  148.0 8.2 %collective-permute-start.54 = (bf16[256,512]{1,0:T(8,128)(2,1)S(1)}, bf16[256,512]{1,0:T(8,128)(2,1)S(1)}, u32[]{:S(2)}, u32[]{:S(2)}) collective-permute-start(bf16[256,512]{1,0:T(8,128)(2,1)S(1)} %shard_map.83._.refs_12_.refs_10_), channel_id=1, source_target_pairs={{0,2},{1,3},{2,0},{3,1},{4,6},{5,7},{6,4},{7,5},{8,10},{9,11},{10,... | collective-permute-start | bytes 786440 | tf_op jit(solution)/shard_map/ppermute | solution.py:55
  149.8 7.7 %collective-permute-start.52 = (bf16[272,512]{1,0:T(8,128)(2,1)S(1)}, bf16[272,512]{1,0:T(8,128)(2,1)S(1)}, u32[]{:S(2)}, u32[]{:S(2)}) collective-permute-start(bf16[272,512]{1,0:T(8,128)(2,1)S(1)} %shard_map.81._.refs_8_.refs_6_), channel_id=1, source_target_pairs={{0,1},{1,0},{2,3},{3,2},{4,5},{5,4},{6,7},{7,6},{8,9},{9,8},{10,11... | collective-permute-start | bytes 835592 | tf_op jit(solution)/shard_map/ppermute | solution.py:59
  149.8 7.7 %collective-permute-start.53 = (bf16[272,512]{1,0:T(8,128)(2,1)S(1)}, bf16[272,512]{1,0:T(8,128)(2,1)S(1)}, u32[]{:S(2)}, u32[]{:S(2)}) collective-permute-start(bf16[272,512]{1,0:T(8,128)(2,1)S(1)} %collective-permute-done.51.refs_9_.refs_7_), channel_id=1, source_target_pairs={{0,1},{1,0},{2,3},{3,2},{4,5},{5,4},{6,7},{7,6},{8,9},{9,8},{10,11... | collective-permute-start | bytes 835592 | tf_op jit(solution)/shard_map/ppermute | solution.py:59
  150.4 7.2 %collective-permute-start.55 = (bf16[256,512]{1,0:T(8,128)(2,1)S(1)}, bf16[256,512]{1,0:T(8,128)(2,1)S(1)}, u32[]{:S(2)}, u32[]{:S(2)}) collective-permute-start(bf16[256,512]{1,0:T(8,128)(2,1)S(1)} %shard_map.83._.refs_12_.refs_10_), channel_id=1, source_target_pairs={{0,1},{1,0},{2,3},{3,2},{4,5},{5,4},{6,7},{7,6},{8,9},{9,8},{10,11... | collective-permute-start | bytes 786440 | tf_op jit(solution)/shard_map/ppermute | solution.py:59
  156.2 1.5 collective-permute-start.56
  160.0 6.7 %collective-permute-start.57 = (f32[]{:T(128)}, f32[]{:T(128)}, u32[]{:S(2)}, u32[]{:S(2)}) collective-permute-start(f32[]{:T(128)} %bitcast.8), channel_id=1, source_target_pairs={{0,16},{16,0},{1,17},{17,1},{2,18},{18,2},{3,19},{19,3},{4,20},{20... | collective-permute-start | bytes 20 | tf_op jit(solution)/shard_map/ppermute | solution.py:59

commit v3 on v2

v3 whole, which is shorter than its diff:
```python
import functools

import jax
import jax.numpy as jnp
from jax import lax
from jax.experimental import pallas as pl
from jax.experimental.pallas import tpu as pltpu
from jax.sharding import PartitionSpec as P

inv_weight = 25.0
var_weight = 25.0
cov_weight = 1.0
eps_var = 0.0001

ORDER = (
    "g0", "g1", "x0", "c0", "x1", "f0", "i0", "x2", "i1", "c1", "m0", "i2", "x3", "f1", "i3",
    "m1", "o0", "m2", "x4", "m3", "x5", "o1", "i4", "o2", "i5", "m4", "o3", "p0", "p1", "m5",
    "o4", "q2", "q3", "o5", "q4", "s5", "q5",
)

VMEM = pl.BlockSpec(memory_space=pltpu.VMEM)
SMEM = pl.BlockSpec(memory_space=pltpu.SMEM)
MIB = 1024 * 1024


class Chain:
    def __init__(self):
        self.last = None

    def __call__(self, kernel, outs, ins, scratch=(), extra=0):
        specs = [SMEM if x.ndim == 1 else VMEM for x in ins]
        body = kernel
        if self.last is not None:
            ins, specs = [self.last] + list(ins), [pl.BlockSpec(memory_space=pl.ANY)] + specs

            def body(_, *refs):
                kernel(*refs)

        size = sum(x.size * x.dtype.itemsize for x in list(ins) + list(outs)) + extra
        outs = pl.pallas_call(
            body,
            out_shape=outs,
            in_specs=specs,
            out_specs=[VMEM] * len(outs),
            scratch_shapes=scratch,
            compiler_params=pltpu.CompilerParams(vmem_limit_bytes=(size // MIB + 4) * MIB),
            cost_estimate=pl.CostEstimate(flops=1, bytes_accessed=1, transcendentals=0),
        )(*ins)
        self.last = outs[0]
        return outs


def array(shape, dtype):
    return jax.ShapeDtypeStruct(shape, dtype)


def shift(value, axis, count, step, inner):
    pairs = [
        (index, (index // inner + step) % count * inner + index % inner)
        for index in range(count * inner)
    ]
    return lax.ppermute(value, axis, pairs)


def partner_of(value, axis, bit):
    return lax.ppermute(value, axis, [(index, index ^ bit) for index in range(lax.axis_size(axis))])


def core_swap(value):
    return partner_of(value, "col", 1)


def dot_t(left, right):
    return lax.dot_general(
        left, right, (((1,), (1,)), ((), ())), preferred_element_type=jnp.float32
    )


def dot(left, right):
    return lax.dot_general(
        left, right, (((1,), (0,)), ((), ())), preferred_element_type=jnp.float32
    )


def sums_kernel(first, second, out):
    out[0:1, :] = jnp.sum(first[...].astype(jnp.float32), axis=0, keepdims=True)
    out[1:2, :] = jnp.sum(second[...].astype(jnp.float32), axis=0, keepdims=True)


def write_extra(out, main, extra):
    ids = lax.broadcasted_iota(jnp.int32, (16, extra.shape[1]), 0)
    if out.dtype == jnp.bfloat16:
        high = extra.astype(jnp.bfloat16).astype(jnp.float32)
        block = jnp.where(ids == 0, high, jnp.where(ids == 1, extra - high, 0.0))
    else:
        block = jnp.where(ids == 0, extra, 0.0)
    out[main : main + 16, :] = block.astype(out.dtype)


def read_extra(ref, main):
    block = ref[main : main + 16, :].astype(jnp.float32)
    return block[0:1, :] + block[1:2, :]


def centre_kernel(total, first, second, sums, stats, *pieces):
    width = first.shape[1]
    size = pieces[0].shape[0]
    found = []
    squares = []
    for index, view in enumerate((first, second)):
        mean = sums[index : index + 1, :] / total
        variance = jnp.zeros((1, width), jnp.float32)
        square = jnp.zeros((1, width), jnp.float32)
        for step in range(4):
            at = slice(step * size, (step + 1) * size)
            centred = view[at, :].astype(jnp.float32) - mean
            rounded = centred.astype(jnp.bfloat16)
            pieces[4 * index + step][...] = rounded
            wide = rounded.astype(jnp.float32)
            variance = variance + jnp.sum(centred * centred, axis=0, keepdims=True)
            square = square + jnp.sum(wide * wide, axis=0, keepdims=True)
        found.append(variance)
        squares.append(square)
    differ = first[...].astype(jnp.float32) - second[...].astype(jnp.float32)
    found += squares + [jnp.sum(differ * differ, axis=0, keepdims=True)]
    ids = lax.broadcasted_iota(jnp.int32, (8, width), 0)
    block = jnp.zeros((8, width), jnp.float32)
    for index, value in enumerate(found):
        block = jnp.where(ids == index, value, block)
    stats[...] = block


def near_place(tile_index, core, rows, tile):
    half, quarter = rows // 2, rows // 4
    square = tile_index < half // tile
    row = jnp.where(square, half * core + tile * tile_index, quarter * core + tile * tile_index - half)
    column = jnp.where(square, half * core, half)
    return square, pl.multiple_of(row, tile), pl.multiple_of(column, half)


def near_kernel(x_count, place, *rest):
    pieces, swapped, (own, partner, keep, *sends) = rest[:4], rest[4:8], rest[8:]
    core, x_place = place[0], place[1]
    rows = own.shape[0]
    half = rows // 2
    tile = rows // 4 // x_count
    for whole, parts in ((own, pieces), (partner, swapped)):
        for step, part in enumerate(parts):
            whole[step * (half // 2) : (step + 1) * (half // 2), :] = part[...]
    row_ids = lax.broadcasted_iota(jnp.int32, (tile, half), 0)
    column_ids = lax.broadcasted_iota(jnp.int32, (tile, half), 1)
    for step in range(x_count):
        out = keep if step == 0 else sends[step - 1]
        extra = jnp.zeros((1, half), jnp.float32)
        for piece in range(3):
            index = (x_place + step) % x_count * 3 + piece
            square, row, column = near_place(index, core, rows, tile)
            diagonal = jnp.logical_and(square, column_ids == row_ids + tile * index)
            value = dot_t(own[pl.ds(row, tile), :], own[pl.ds(column, half), :])
            value = value + dot_t(
                partner[pl.ds(row, tile), :], partner[pl.ds(column, half), :]
            )
            extra = extra + jnp.sum(jnp.where(diagonal, value, 0.0), axis=0, keepdims=True)
            value = jnp.where(diagonal, 0.0, value)
            out[pl.ds(piece * tile, tile), :] = value.astype(out.dtype)
        write_extra(out, 3 * tile, extra)


def centre_other_kernel(total, index, other, sums, *outs):
    mean = sums[index : index + 1, :] / total
    size = outs[0].shape[0]
    for step, out in enumerate(outs):
        at = slice(step * size, (step + 1) * size)
        out[...] = (other[at, :].astype(jnp.float32) - mean).astype(jnp.bfloat16)


def add_kernel(main, *refs):
    out = refs[-1]
    value = refs[0][:main, :].astype(jnp.float32)
    for ref in refs[1:-1]:
        value = value + ref[:main, :].astype(jnp.float32)
    out[:main, :] = value.astype(out.dtype)
    if main < out.shape[0]:
        extra = read_extra(refs[0], main)
        for ref in refs[1:-1]:
            extra = extra + read_extra(ref, main)
        write_extra(out, main, extra)


def pick_kernel(place, mine, got, out):
    @pl.when(place[2] == 1)
    def _():
        out[...] = mine[...]

    @pl.when(place[2] == 0)
    def _():
        out[...] = got[...]


def loss_terms(total, feat, stats):
    spread = jnp.sqrt(stats[0:2, :] / (total - 1) + eps_var)
    norms = stats[2:4, :] / (total - 1)
    return (
        inv_weight * stats[4:5, :] / (total * feat)
        + var_weight * jnp.sum(jnp.maximum(1.0 - spread, 0.0), axis=0, keepdims=True) / feat
        - cov_weight * jnp.sum(norms * norms, axis=0, keepdims=True) / feat
    )


def far_kernel(x_count, total, feat, place, own, partner, *rest):
    others, swapped, outs = rest[:4], rest[4:8], rest[8:]
    stats = None
    if len(outs) > 2 * x_count:
        stats, outs = outs[0], outs[1:]
    core, x_place = place[0], place[1]
    half = own.shape[0] // 2
    size = half // 2
    tile = half // x_count
    for block in range(2):
        for step in range(x_count):
            out = outs[block * x_count + step]
            part = (x_place + step) % x_count
            row = pl.ds(pl.multiple_of(half * core + tile * part, tile), tile)
            left, left_partner = own[row, :], partner[row, :]
            for side in range(2):
                at = 2 * block + side
                value = dot_t(left, others[at][...]) + dot_t(left_partner, swapped[at][...])
                out[:tile, side * size : (side + 1) * size] = value.astype(out.dtype)
            if out.shape[0] > tile:
                terms = loss_terms(total, feat, stats)
                terms = jnp.where(part == 0, terms, 0.0)
                if terms.shape[1] < half:
                    terms = jnp.concatenate(
                        [terms, jnp.zeros((1, half - terms.shape[1]), jnp.float32)], axis=1
                    )
                write_extra(out, tile, terms)


def near_product_kernel(
    x_count, index, total, feat, place, rounded, first, second, sums, stats, *rest
):
    parts, (base, squares, grid, columns) = rest[:-4], rest[-4:]
    core, x_place = place[0], place[1]
    rows, width = rounded.shape
    half = rows // 2
    tile = rows // 4 // x_count
    square_sum = jnp.zeros((1, half), jnp.float32)
    for side in range(2):
        owner = core if side == 0 else 1 - core
        extra = jnp.zeros((1, half), jnp.float32)
        for step in range(x_count):
            extra = extra + read_extra(parts[side * x_count + step], 3 * tile)
            for piece in range(3):
                at = (x_place + x_count - step) % x_count * 3 + piece
                _, row, column = near_place(at, owner, rows, tile)
                grid[pl.ds(row, tile), pl.ds(column, half)] = parts[side * x_count + step][
                    pl.ds(piece * tile, tile), :
                ]
        square_sum = square_sum + extra * extra
        columns[pl.ds(pl.multiple_of(half * owner, half), half), :] = jnp.broadcast_to(
            extra, (8, half)
        ).T
    grid[half:, :half] = grid[:half, half:].T
    scale = total * feat / 64.0
    spread = jnp.sqrt(stats[index : index + 1, :] / (total - 1) + eps_var)
    active = jnp.where(spread < 1.0, 1.0, 0.0)
    var_scale = scale * -var_weight * active / (feat * spread * (total - 1))
    cov_scale = scale * 4.0 * cov_weight / (feat * (total - 1)) / (total - 1)
    inv_scale = (1.0 - 2.0 * index) * scale * 2.0 * inv_weight / (total * feat)
    mean = sums[index : index + 1, :] / total
    norms = stats[index + 2 : index + 3, :]
    chunk = rows // 4
    for step in range(4):
        at = slice(step * chunk, (step + 1) * chunk)
        wide = grid[at, :].astype(jnp.float32)
        row = jnp.sum(wide * wide, axis=0, keepdims=True)
        square_sum = square_sum + row[:, :half] + row[:, half:]
        product = dot(grid[at, :], rounded[...])
        product = product + (columns[at, 0:1] - norms) * rounded[at, :].astype(
            jnp.float32
        )
        one, two = first[at, :].astype(jnp.float32), second[at, :].astype(jnp.float32)
        centred = (one if index == 0 else two) - mean
        base[at, :] = inv_scale * (one - two) + var_scale * centred + cov_scale * product
    squares[...] = square_sum


def far_product_kernel(x_count, total, feat, place, base, *rest):
    others, parts = rest[:2], rest[2 : 2 + 2 * x_count]
    grad, *sums = rest[2 + 2 * x_count :]
    core, x_place = place[0], place[1]
    size = others[0].shape[0]
    half = 2 * size
    tile = half // x_count
    cov_scale = total * feat / 64.0 * 4.0 * cov_weight / (feat * (total - 1)) / (total - 1)
    for side in range(2):
        owner = core if side == 0 else 1 - core
        for step in range(x_count):
            at = (x_place + x_count - step) % x_count
            row = pl.ds(pl.multiple_of(half * owner + tile * at, tile), tile)
            part = parts[side * x_count + step]
            product = jnp.zeros((tile, grad.shape[1]), jnp.float32)
            for index in range(2):
                product = product + dot(
                    part[:tile, index * size : (index + 1) * size], others[index][...]
                )
            grad[row, :] = base[row, :] + cov_scale * product
    if sums:
        add_squares(tile, parts, *sums)


def add_squares(main, parts, squares, terms):
    total = jnp.zeros((1, parts[0].shape[1]), jnp.float32)
    extra = jnp.zeros((1, parts[0].shape[1]), jnp.float32)
    for part in parts:
        wide = part[:main, :].astype(jnp.float32)
        total = total + jnp.sum(wide * wide, axis=0, keepdims=True)
        if part.shape[0] > main:
            extra = extra + read_extra(part, main)
    squares[...] = total
    terms[...] = extra


def squares_kernel(main, total, count, *refs):
    parts, (plane, terms) = refs[count:-2], refs[-2:]
    add_squares(main, parts, plane, terms)
    value = plane[...]
    for ref in refs[:count]:
        value = value + ref[...]
    plane[...] = value / (total - 1) / (total - 1)


def on_device(first_view, second_view):
    dp_count = lax.axis_size("dp")
    row_count = lax.axis_size("row")
    col_count = lax.axis_size("col")
    rows, width = first_view.shape
    total = rows * dp_count
    feat = width * row_count * col_count
    half = rows // 2
    x_count = col_count // 2
    core = lax.axis_index("col") % 2
    x_place = lax.axis_index("col") // 2
    z_place = lax.axis_index("row")
    inner = 4 if row_count % 4 == 0 else 1
    middle = jnp.logical_or(z_place % 4 == 1, z_place % 4 == 2)
    place = jnp.stack([core, x_place, middle.astype(core.dtype)]).astype(jnp.int32)
    f32, bf16 = jnp.float32, jnp.bfloat16
    run = Chain()

    (sums,) = run(sums_kernel, [array((2, width), f32)], [first_view, second_view])
    sums_other = partner_of(sums, "dp", 1)
    first_sent, second_sent, sums_other = lax.optimization_barrier(
        (first_view, second_view, sums_other)
    )
    others = [partner_of(first_sent, "dp", 1), partner_of(second_sent, "dp", 1)]
    sums = sums + sums_other

    stats, *rounded = run(
        functools.partial(centre_kernel, total),
        [array((8, width), f32)] + [array((rows // 4, width), bf16)] * 8,
        [first_view, second_view, sums],
    )
    swapped = [core_swap(piece) for piece in rounded]
    stats = stats + partner_of(stats, "dp", 1)

    def send_row(value, pairs):
        groups = range(0, row_count, inner)
        return lax.ppermute(value, "row", [(g + a, g + b) for g in groups for a, b in pairs])

    class Piece:
        def __init__(self, main, keep, sends):
            self.main, self.keep = main, keep
            self.like = array(keep.shape, bf16)
            self.got = [shift(sent, "col", x_count, i + 1, 2) for i, sent in enumerate(sends)]

        def add(self, values):
            (value,) = run(functools.partial(add_kernel, self.main), [self.like], values)
            return value

        def over_x(self):
            if inner == 4:
                value = self.add([self.keep] + self.got)
                self.got.append(send_row(value, [(0, 1), (3, 2)]))

        def inward(self):
            self.value = self.add([self.keep] + self.got)
            if inner == 4:
                self.got = send_row(self.value, [(1, 2), (2, 1)])

        def across(self):
            if inner == 4:
                self.value = self.add([self.value, self.got])
            bit = inner
            while bit < row_count:
                self.value = self.add([self.value, partner_of(self.value, "row", bit)])
                bit *= 2
            if inner == 4:
                self.got = send_row(self.value, [(1, 0), (2, 3)])

        def outward(self):
            if inner == 4:
                (self.value,) = run(pick_kernel, [self.like], [place, self.value, self.got])
            parts = [self.value]
            for step in range(1, x_count):
                parts.append(shift(self.value, "col", x_count, step, 2))
            self.parts = parts + [core_swap(part) for part in parts]

    main = 3 * (rows // 4) // x_count
    tile = half // x_count
    pieces, wholes, found, base, squares = {}, {}, {}, {}, []

    def piece_outs(size):
        return [array((size, half), f32)] + [array((size, half), bf16)] * (x_count - 1)

    def near_gram(index):
        at = slice(4 * index, 4 * index + 4)
        own, partner, *outs = run(
            functools.partial(near_kernel, x_count),
            [array((rows, width), bf16)] * 2 + piece_outs(main + 16),
            [place] + rounded[at] + swapped[at],
        )
        wholes[index] = [own, partner]
        pieces[index] = Piece(main, outs[0], outs[1:])

    def far_centre(index):
        outs = [array((rows // 4, width), bf16)] * 4
        ins = [others[index], sums]
        found[index] = list(run(functools.partial(centre_other_kernel, total, index), outs, ins))

    def far_gram(index):
        outs = run(
            functools.partial(far_kernel, x_count, total, feat),
            piece_outs(tile + 16 * index) + piece_outs(tile),
            [place]
            + wholes[index]
            + found[index]
            + [core_swap(other) for other in found[index]]
            + [stats] * index,
        )
        for block in range(2):
            keep, *sends = outs[block * x_count : (block + 1) * x_count]
            pieces[2 + 2 * index + block] = Piece(tile, keep, sends)

    def near_product(index):
        base[index], value = run(
            functools.partial(near_product_kernel, x_count, index, total, feat),
            [array((rows, width), f32), array((1, half), f32)],
            [place, wholes[index][0], first_view, second_view, sums, stats]
            + pieces[index].parts,
            scratch=[pltpu.VMEM((rows, rows), bf16), pltpu.VMEM((rows, 8), f32)],
            extra=2 * rows * rows + 512 * rows,
        )
        squares.append(value)

    def far_product(index):
        view, block = index // 2 - 1, index % 2
        outs = [array((rows, width), f32)]
        if index < 5:
            outs += [array((1, half), f32)] * 2
        base[view], *value = run(
            functools.partial(far_product_kernel, x_count, total, feat),
            outs,
            [place, base[view]] + found[view][2 * block : 2 * block + 2] + pieces[index].parts,
        )
        squares.extend(value[:1])
        if index == 4:
            found["terms"] = value[1]

    def last_squares(index):
        plane, _ = run(
            functools.partial(squares_kernel, tile, total, len(squares)),
            [array((1, half), f32)] * 2,
            squares + pieces[index].parts,
        )
        found["plane"] = plane + partner_of(plane, "dp", 1)

    steps = {
        "g": near_gram,
        "c": far_centre,
        "f": far_gram,
        "x": lambda index: pieces[index].over_x(),
        "i": lambda index: pieces[index].inward(),
        "m": lambda index: pieces[index].across(),
        "o": lambda index: pieces[index].outward(),
        "p": near_product,
        "q": far_product,
        "s": last_squares,
    }
    for step in ORDER:
        steps[step[0]](int(step[1]))
    loss = jnp.sum(found["terms"] + cov_weight * found["plane"] / feat)
    return loss, base[0], base[1]


def solution(mesh):
    return jax.shard_map(
        on_device,
        mesh=mesh,
        in_specs=(P("dp", ("row", "col")), P("dp", ("row", "col"))),
        out_specs=(P(), P("dp", ("row", "col")), P("dp", ("row", "col"))),
        check_vma=False,
    )
```

time: 170 us -> 152 us (0.89)
  waiting for transfers between devices: 56.2 us -> 46 us
  between operations: 5.51 us -> 1.31 us
  local copies, waits for them, and re-layouts: 5.15 us -> 2.84 us
    ppermute x12, waiting for transfers between devices: 29 us -> 20.9 us  [shift(): return lax.ppermute(value, axis, pairs)]
    ppermute x12, starting transfers between devices: 15.4 us -> 12.1 us  [shift(): return lax.ppermute(value, axis, pairs)]
    unnamed x10 -> x18, local copies, waits for them, and re-layouts: 3.79 us -> 2.84 us
    ppermute x28 -> x33, waiting for transfers between devices: 8.5 us -> 7.81 us  [partner_of(): lax.ppermute(value, axis, [(index, index ^ bit) for index in range(lax.ax...]
    ppermute x28 -> x33, starting transfers between devices: 13.5 us -> 14 us  [partner_of(): lax.ppermute(value, axis, [(index, index ^ bit) for index in range(lax.ax...]
    pallas_call x37 -> x39, Pallas kernels: 35.9 us -> 35.7 us  [__call__(): pl.pallas_call(body, out_shape=outs, in_specs=specs, out_specs=[VMEM] * l...]
  transfers between devices with their start and end apart: 58 -> 63, of which waited for: 16 -> 21; matrix products, arithmetic and copies ran while one was open for 1% -> 0% of each run, Pallas kernels for 18% -> 22%
where the time goes in v3:
time: 152 us
  starting transfers between devices  64.9 us (43%)
  waiting for transfers between devices  46 us (30%)
  Pallas kernels  35.7 us (23%)
  local copies, waits for them, and re-layouts  2.84 us (2%)
    ppermute x18, starting transfers between devices, send_row(): lax.ppermute(value, 'row', [(g + a, g + b) for g in groups for a, b in pa...  38.8 us
    pallas_call x39, Pallas kernels, __call__(): pl.pallas_call(body, out_shape=outs, in_specs=specs, out_specs=[VMEM] * l...  35.7 us
    ppermute x12, waiting for transfers between devices, shift(): return lax.ppermute(value, axis, pairs)  20.9 us
    ppermute x18, waiting for transfers between devices, send_row(): lax.ppermute(value, 'row', [(g + a, g + b) for g in groups for a, b in pa...  17.4 us
    ppermute x33, starting transfers between devices, partner_of(): lax.ppermute(value, axis, [(index, index ^ bit) for index in range(lax.ax...  14 us
    ppermute x12, starting transfers between devices, shift(): return lax.ppermute(value, axis, pairs)  12.1 us
    ppermute x33, waiting for transfers between devices, partner_of(): lax.ppermute(value, axis, [(index, index ^ bit) for index in range(lax.ax...  7.81 us
  transfers between devices with their start and end apart: 63, of which 21 were waited for; matrix products, arithmetic and copies ran while one was open for 0% of the time, Pallas kernels for 22%

profile of v3, /device:TPU:0, one launch (start us, length us, event | category | flops | bytes accessed | tf_op | source)
XLA Modules:
  0.0 151.6 jit_solution(13855722703837924890)
XLA Ops:
  0.6 1.2 copy-done
  1.9 1.6 %shard_map.49._ = f32[2,512]{1,0:T(2,128)S(1)} custom-call(bf16[1024,512]{1,0:T(8,128)(2,1)} %refs_2_.3, bf16[1024,512]{1,0:T(8,128)(2,1)S(1)} %copy-done), custom_call_target="tpu_custom_call" | custom-call | flops 1 | bytes 1 | tf_op jit(solution)/shard_map/pallas_call | solution.py:40
  3.5 3.0 %collective-permute-start = (f32[2,512]{1,0:T(2,128)S(1)}, f32[2,512]{1,0:T(2,128)S(1)}, u32[]{:S(2)}, u32[]{:S(2)}) collective-permute-start(f32[2,512]{1,0:T(2,128)S(1)} %shard_map.49._), channel_id=1, source_target_pairs={{0,16},{16,0},{1,17},{17,1},{2,18},{18,2},{3,19},{19,3},{4,20},{20... | collective-permute-start | bytes 12296 | tf_op jit(solution)/shard_map/ppermute | solution.py:66
  6.5 1.6 %collective-permute-done = f32[2,512]{1,0:T(2,128)S(1)} collective-permute-done((f32[2,512]{1,0:T(2,128)S(1)}, f32[2,512]{1,0:T(2,128)S(1)}, u32[]{:S(2)}, u32[]{:S(2)}) %collective-permute-start) | collective-permute-done | bytes 4128 | tf_op jit(solution)/shard_map/ppermute | solution.py:66
  8.1 2.0 %collective-permute-start.10 = (bf16[1024,512]{1,0:T(8,128)(2,1)}, bf16[1024,512]{1,0:T(8,128)(2,1)S(1)}, u32[]{:S(2)}, u32[]{:S(2)}) collective-permute-start(bf16[1024,512]{1,0:T(8,128)(2,1)} %refs_2_.3), channel_id=1, source_target_pairs={{0,16},{16,0},{1,17},{17,1},{2,18},{18,2},{3,19},{19,3},{4,20},{20... | collective-permute-start | bytes 3145736 | tf_op jit(solution)/shard_map/ppermute | solution.py:66
  10.1 2.8 %shard_map.50 = (f32[8,512]{1,0:T(8,128)S(1)}, bf16[256,512]{1,0:T(8,128)(2,1)S(1)}, bf16[256,512]{1,0:T(8,128)(2,1)S(1)}, bf16[256,512]{1,0:T(8,128)(2,1)S(1)},...) custom-call(f32[2,512]{1,0:T(2,128)S(1)} %shard_map.49._, ...), custom_call_target="tpu_custom_call" | custom-call | flops 1 | bytes 1 | tf_op jit(solution)/shard_map/pallas_call | solution.py:40
  15.9 3.4 %shard_map.51 = (bf16[1024,512]{1,0:T(8,128)(2,1)S(1)}, bf16[1024,512]{1,0:T(8,128)(2,1)S(1)}, f32[400,512]{1,0:T(8,128)S(1)}, bf16[400,512]{1,0:T(8,128)(2,1)S(1)}) custom-call(f32[8,512]{1,0:T(8,128)S(1)} %get-tuple-element.52._, s32[3]{0:T(128)S(1)} %pad_add_fusion.refs_0_, bf16[256,512]{1,0:T(8,128)(2,1)S(1)} %get-tuple-element.53.refs_1_, ...), custom_call_target="tpu_custom_call" | custom-call | flops 1 | bytes 1 | tf_op jit(solution)/shard_map/pallas_call | solution.py:40
  19.4 1.6 %collective-permute-start.9 = (bf16[400,512]{1,0:T(8,128)(2,1)S(1)}, bf16[400,512]{1,0:T(8,128)(2,1)S(1)}, u32[]{:S(2)}, u32[]{:S(2)}) collective-permute-start(bf16[400,512]{1,0:T(8,128)(2,1)S(1)} %get-tuple-element.64), channel_id=1, source_target_pairs={{0,2},{1,3},{2,0},{3,1},{4,6},{5,7},{6,4},{7,5},{8,10},{9,11},{10,... | collective-permute-start | bytes 1228808 | tf_op jit(solution)/shard_map/ppermute | solution.py:62
  21.5 3.4 %shard_map.52 = (bf16[1024,512]{1,0:T(8,128)(2,1)S(1)}, bf16[1024,512]{1,0:T(8,128)(2,1)S(1)}, f32[400,512]{1,0:T(8,128)S(1)}, bf16[400,512]{1,0:T(8,128)(2,1)S(1)}) custom-call(bf16[1024,512]{1,0:T(8,128)(2,1)S(1)} %get-tuple-element.57._.refs_1_, s32[3]{0:T(128)S(1)} %pad_add_fusion.refs_0_, bf16[256,512]{1,0:T(8,128)(2,1)} %get-tuple-element.58.refs_1_, ...), custom_call_target="tpu_custom_call" | custom-call | flops 1 | bytes 1 | tf_op jit(solution)/shard_map/pallas_call | solution.py:40
  25.1 6.6 %collective-permute-done.9.refs_1_ = bf16[400,512]{1,0:T(8,128)(2,1)S(1)} collective-permute-done((bf16[400,512]{1,0:T(8,128)(2,1)S(1)}, bf16[400,512]{1,0:T(8,128)(2,1)S(1)}, u32[]{:S(2)}, u32[]{:S(2)}) %collective-permute-start.9) | collective-permute-done | bytes 409632 | tf_op jit(solution)/shard_map/ppermute | solution.py:62
  31.8 2.6 %collective-permute-done.10.refs_0_ = bf16[1024,512]{1,0:T(8,128)(2,1)S(1)} collective-permute-done((bf16[1024,512]{1,0:T(8,128)(2,1)}, bf16[1024,512]{1,0:T(8,128)(2,1)S(1)}, u32[]{:S(2)}, u32[]{:S(2)}) %collective-permute-start.10) | collective-permute-done | bytes 1048608 | tf_op jit(solution)/shard_map/ppermute | solution.py:66
  35.1 4.0 %collective-permute-start.16 = (bf16[400,512]{1,0:T(8,128)(2,1)S(1)}, bf16[400,512]{1,0:T(8,128)(2,1)S(1)}, u32[]{:S(2)}, u32[]{:S(2)}) collective-permute-start(bf16[400,512]{1,0:T(8,128)(2,1)S(1)} %shard_map.53._), channel_id=1, source_target_pairs={{0,4},{12,8},{1,5},{13,9},{2,6},{14,10},{3,7},{15,11},{16,20},{28,... | collective-permute-start | bytes 1228808 | tf_op jit(solution)/shard_map/ppermute | solution.py:369
  39.1 0.8 collective-permute-done.11.refs_1_
  40.6 3.5 %collective-permute-start.18 = (bf16[400,512]{1,0:T(8,128)(2,1)S(1)}, bf16[400,512]{1,0:T(8,128)(2,1)S(1)}, u32[]{:S(2)}, u32[]{:S(2)}) collective-permute-start(bf16[400,512]{1,0:T(8,128)(2,1)S(1)} %shard_map.55._), channel_id=1, source_target_pairs={{0,4},{12,8},{1,5},{13,9},{2,6},{14,10},{3,7},{15,11},{16,20},{28,... | collective-permute-start | bytes 1228808 | tf_op jit(solution)/shard_map/ppermute | solution.py:369
  44.1 1.8 %shard_map.56 = (f32[256,512]{1,0:T(8,128)S(1)}, bf16[256,512]{1,0:T(8,128)(2,1)S(1)}, f32[256,512]{1,0:T(8,128)S(1)}, bf16[256,512]{1,0:T(8,128)(2,1)S(1)}) custom-call(bf16[400,512]{1,0:T(8,128)(2,1)S(1)} %shard_map.55._, s32[3]{0:T(128)S(1)} %pad_add_fusion.refs_0_, bf16[1024,512]{1,0:T(8,128)(2,1)S(1)} %get-tuple-element.57._.refs_1_, ...), custom_call_target="tpu_custom_call" | custom-call | flops 1 | bytes 1 | tf_op jit(solution)/shard_map/pallas_call | solution.py:40
  45.9 1.6 %collective-permute-start.17 = (bf16[256,512]{1,0:T(8,128)(2,1)S(1)}, bf16[256,512]{1,0:T(8,128)(2,1)S(1)}, u32[]{:S(2)}, u32[]{:S(2)}) collective-permute-start(bf16[256,512]{1,0:T(8,128)(2,1)S(1)} %get-tuple-element.74), channel_id=1, source_target_pairs={{0,2},{1,3},{2,0},{3,1},{4,6},{5,7},{6,4},{7,5},{8,10},{9,11},{10,... | collective-permute-start | bytes 786440 | tf_op jit(solution)/shard_map/ppermute | solution.py:62
  47.5 1.4 collective-permute-done.16.refs_2_
  49.1 0.7 collective-permute-start.20
  49.8 1.6 %collective-permute-start.22 = (bf16[256,512]{1,0:T(8,128)(2,1)S(1)}, bf16[256,512]{1,0:T(8,128)(2,1)S(1)}, u32[]{:S(2)}, u32[]{:S(2)}) collective-permute-start(bf16[256,512]{1,0:T(8,128)(2,1)S(1)} %get-tuple-element.78), channel_id=1, source_target_pairs={{0,2},{1,3},{2,0},{3,1},{4,6},{5,7},{6,4},{7,5},{8,10},{9,11},{10,... | collective-permute-start | bytes 786440 | tf_op jit(solution)/shard_map/ppermute | solution.py:62
  51.3 3.9 %collective-permute-done.17.refs_1_ = bf16[256,512]{1,0:T(8,128)(2,1)S(1)} collective-permute-done((bf16[256,512]{1,0:T(8,128)(2,1)S(1)}, bf16[256,512]{1,0:T(8,128)(2,1)S(1)}, u32[]{:S(2)}, u32[]{:S(2)}) %collective-permute-start.17) | collective-permute-done | bytes 262176 | tf_op jit(solution)/shard_map/ppermute | solution.py:62
  55.3 3.3 %collective-permute-start.21 = (bf16[256,512]{1,0:T(8,128)(2,1)S(1)}, bf16[256,512]{1,0:T(8,128)(2,1)S(1)}, u32[]{:S(2)}, u32[]{:S(2)}) collective-permute-start(bf16[256,512]{1,0:T(8,128)(2,1)S(1)} %shard_map.58._), channel_id=1, source_target_pairs={{0,4},{12,8},{1,5},{13,9},{2,6},{14,10},{3,7},{15,11},{16,20},{28,... | collective-permute-start | bytes 786440 | tf_op jit(solution)/shard_map/ppermute | solution.py:369
  59.0 1.6 %collective-permute-start.27 = (f32[8,512]{1,0:T(8,128)S(1)}, f32[8,512]{1,0:T(8,128)S(1)}, u32[]{:S(2)}, u32[]{:S(2)}) collective-permute-start(f32[8,512]{1,0:T(8,128)S(1)} %get-tuple-element.52._), channel_id=1, source_target_pairs={{0,16},{16,0},{1,17},{17,1},{2,18},{18,2},{3,19},{19,3},{4,20},{20... | collective-permute-start | bytes 49160 | tf_op jit(solution)/shard_map/ppermute | solution.py:66
  60.6 2.2 %collective-permute-done.27 = f32[8,512]{1,0:T(8,128)S(1)} collective-permute-done((f32[8,512]{1,0:T(8,128)S(1)}, f32[8,512]{1,0:T(8,128)S(1)}, u32[]{:S(2)}, u32[]{:S(2)}) %collective-permute-start.27) | collective-permute-done | bytes 16416 | tf_op jit(solution)/shard_map/ppermute | solution.py:66
  62.8 0.7 collective-permute-start.29
  63.6 1.3 collective-permute-start.30
  65.8 6.2 %collective-permute-start.28 = (bf16[256,512]{1,0:T(8,128)(2,1)S(1)}, bf16[256,512]{1,0:T(8,128)(2,1)S(1)}, u32[]{:S(2)}, u32[]{:S(2)}) collective-permute-start(bf16[256,512]{1,0:T(8,128)(2,1)S(1)} %shard_map.63._), channel_id=1, source_target_pairs={{0,4},{12,8},{1,5},{13,9},{2,6},{14,10},{3,7},{15,11},{16,20},{28,... | collective-permute-start | bytes 786440 | tf_op jit(solution)/shard_map/ppermute | solution.py:369
  72.1 1.8 %shard_map.64 = (f32[272,512]{1,0:T(8,128)S(1)}, bf16[272,512]{1,0:T(8,128)(2,1)S(1)}, f32[256,512]{1,0:T(8,128)S(1)}, bf16[256,512]{1,0:T(8,128)(2,1)S(1)}) custom-call(bf16[256,512]{1,0:T(8,128)(2,1)S(1)} %shard_map.63._, s32[3]{0:T(128)S(1)} %pad_add_fusion.refs_0_, bf16[1024,512]{1,0:T(8,128)(2,1)S(1)} %get-tuple-element.62._.refs_1_, ...), custom_call_target="tpu_custom_call" | custom-call | flops 1 | bytes 1 | tf_op jit(solution)/shard_map/pallas_call | solution.py:40
  73.9 1.6 %collective-permute-start.32 = (bf16[272,512]{1,0:T(8,128)(2,1)S(1)}, bf16[272,512]{1,0:T(8,128)(2,1)S(1)}, u32[]{:S(2)}, u32[]{:S(2)}) collective-permute-start(bf16[272,512]{1,0:T(8,128)(2,1)S(1)} %get-tuple-element.84), channel_id=1, source_target_pairs={{0,2},{1,3},{2,0},{3,1},{4,6},{5,7},{6,4},{7,5},{8,10},{9,11},{10,... | collective-permute-start | bytes 835592 | tf_op jit(solution)/shard_map/ppermute | solution.py:62
  75.5 0.7 collective-permute-start.31
  76.1 1.8 %collective-permute-done.28.refs_2_ = bf16[256,512]{1,0:T(8,128)(2,1)S(1)} collective-permute-done((bf16[256,512]{1,0:T(8,128)(2,1)S(1)}, bf16[256,512]{1,0:T(8,128)(2,1)S(1)}, u32[]{:S(2)}, u32[]{:S(2)}) %collective-permute-start.28) | collective-permute-done | bytes 262176 | tf_op jit(solution)/shard_map/ppermute | solution.py:369
  78.0 1.5 collective-permute-start.34
  79.7 1.3 collective-permute-start.35
  81.0 0.7 collective-permute-start.33
  81.7 0.6 shard_map.67._.refs_6_
  82.3 0.6 collective-permute-start.41
  83.6 5.6 %collective-permute-start.36 = (bf16[272,512]{1,0:T(8,128)(2,1)S(1)}, bf16[272,512]{1,0:T(8,128)(2,1)S(1)}, u32[]{:S(2)}, u32[]{:S(2)}) collective-permute-start(bf16[272,512]{1,0:T(8,128)(2,1)S(1)} %shard_map.69._), channel_id=1, source_target_pairs={{0,4},{12,8},{1,5},{13,9},{2,6},{14,10},{3,7},{15,11},{16,20},{28,... | collective-permute-start | bytes 835592 | tf_op jit(solution)/shard_map/ppermute | solution.py:369
  89.2 1.3 collective-permute-start.37
  90.7 1.6 %collective-permute-done.35.refs_2_ = bf16[400,512]{1,0:T(8,128)(2,1)S(1)} collective-permute-done((bf16[400,512]{1,0:T(8,128)(2,1)S(1)}, bf16[400,512]{1,0:T(8,128)(2,1)S(1)}, u32[]{:S(2)}, u32[]{:S(2)}) %collective-permute-start.35) | collective-permute-done | bytes 409632 | tf_op jit(solution)/shard_map/ppermute | solution.py:369
  92.3 0.8 shard_map.72._.refs_6_
  93.8 4.4 %collective-permute-start.38 = (bf16[256,512]{1,0:T(8,128)(2,1)S(1)}, bf16[256,512]{1,0:T(8,128)(2,1)S(1)}, u32[]{:S(2)}, u32[]{:S(2)}) collective-permute-start(bf16[256,512]{1,0:T(8,128)(2,1)S(1)} %shard_map.71._), channel_id=1, source_target_pairs={{0,4},{12,8},{1,5},{13,9},{2,6},{14,10},{3,7},{15,11},{16,20},{28,... | collective-permute-start | bytes 786440 | tf_op jit(solution)/shard_map/ppermute | solution.py:369
  98.4 0.7 collective-permute-start.39
  99.1 1.3 collective-permute-start.40
  101.0 2.6 %collective-permute-done.38.refs_2_ = bf16[256,512]{1,0:T(8,128)(2,1)S(1)} collective-permute-done((bf16[256,512]{1,0:T(8,128)(2,1)S(1)}, bf16[256,512]{1,0:T(8,128)(2,1)S(1)}, u32[]{:S(2)}, u32[]{:S(2)}) %collective-permute-start.38) | collective-permute-done | bytes 262176 | tf_op jit(solution)/shard_map/ppermute | solution.py:369
  104.0 2.2 %collective-permute-done.44.refs_7_ = bf16[400,512]{1,0:T(8,128)(2,1)S(1)} collective-permute-done((bf16[400,512]{1,0:T(8,128)(2,1)S(1)}, bf16[400,512]{1,0:T(8,128)(2,1)S(1)}, u32[]{:S(2)}, u32[]{:S(2)}) %collective-permute-start.44) | collective-permute-done | bytes 409632 | tf_op jit(solution)/shard_map/ppermute | solution.py:62
  106.4 3.3 %collective-permute-done.40.refs_2_ = bf16[256,512]{1,0:T(8,128)(2,1)S(1)} collective-permute-done((bf16[256,512]{1,0:T(8,128)(2,1)S(1)}, bf16[256,512]{1,0:T(8,128)(2,1)S(1)}, u32[]{:S(2)}, u32[]{:S(2)}) %collective-permute-start.40) | collective-permute-done | bytes 262176 | tf_op jit(solution)/shard_map/ppermute | solution.py:369
  109.7 1.3 collective-permute-start.48
  111.6 0.7 collective-permute-start.47
  112.3 1.5 collective-permute-start.52
  113.8 3.2 %shard_map.78 = (f32[1024,512]{1,0:T(8,128)S(1)}, f32[1,512]{1,0:T(1,128)S(1)}) custom-call(bf16[256,512]{1,0:T(8,128)(2,1)S(1)} %shard_map.77._.refs_4_, s32[3]{0:T(128)S(1)} %pad_add_fusion.refs_0_, bf16[1024,512]{1,0:T(8,128)(2,1)S(1)} %get-tuple-element.57._.refs_1_, bf16[1024,512]{1,0:T(8,128)(2,1)} %refs_2_.3, bf16[1024,512]{1,0:T(8,128)(2,1)S(1)} %copy-done.1, ...), custom_call_target="tpu_custom_call" | custom-call | flops 1 | bytes 1 | tf_op jit(solution)/shard_map/pallas_call | solution.py:40
  117.5 3.2 %shard_map.79 = (f32[1024,512]{1,0:T(8,128)S(1)}, f32[1,512]{1,0:T(1,128)S(1)}) custom-call(f32[1024,512]{1,0:T(8,128)S(1)} %get-tuple-element.87._.refs_1_, s32[3]{0:T(128)S(1)} %pad_add_fusion.refs_0_, bf16[1024,512]{1,0:T(8,128)(2,1)S(1)} %get-tuple-element.62._.refs_1_, bf16[1024,512]{1,0:T(8,128)(2,1)} %refs_2_.3, bf16[1024,512]{1,0:T(8,128)(2,1)S(1)} %copy-done.1, ...), custom_call_target="tpu_custom_call" | custom-call | flops 1 | bytes 1 | tf_op jit(solution)/shard_map/pallas_call | solution.py:40
  121.4 1.3 collective-permute-start.55
  122.7 0.6 shard_map.81._.refs_4_
  123.3 0.7 collective-permute-start.56
  124.0 1.8 %shard_map.82 = (f32[1024,512]{1,0:T(8,128)S(1)}, f32[1,512]{1,0:T(1,128)S(1)}, f32[1,512]{1,0:T(1,128)}) custom-call(bf16[272,512]{1,0:T(8,128)(2,1)S(1)} %shard_map.81._.refs_4_, s32[3]{0:T(128)S(1)} %pad_add_fusion.refs_0_, f32[1024,512]{1,0:T(8,128)S(1)} %get-tuple-element.87._.refs_1_, bf16[256,512]{1,0:T(8,128)(2,1)S(1)} %get-tuple-element.66._.refs_3_.refs_2_, ...), custom_call_target="tpu_custom_call" | custom-call | flops 1 | bytes 1 | tf_op jit(solution)/shard_map/pallas_call | solution.py:40
  125.8 2.6 %shard_map.83 = (f32[1024,512]{1,0:T(8,128)}, f32[1,512]{1,0:T(1,128)S(1)}, f32[1,512]{1,0:T(1,128)}) custom-call(f32[1024,512]{1,0:T(8,128)S(1)} %get-tuple-element.89._.refs_1_, s32[3]{0:T(128)S(1)} %pad_add_fusion.refs_0_, f32[1024,512]{1,0:T(8,128)S(1)} %get-tuple-element.89._.refs_1_, bf16[256,512]{1,0:T(8,128)(2,1)S(1)} %get-tuple-element.71.refs_5_.refs_2_, ...), custom_call_target="tpu_custom_call" | custom-call | flops 1 | bytes 1 | tf_op jit(solution)/shard_map/pallas_call | solution.py:40
  128.4 6.3 %collective-permute-done.55.refs_2_ = bf16[256,512]{1,0:T(8,128)(2,1)S(1)} collective-permute-done((bf16[256,512]{1,0:T(8,128)(2,1)S(1)}, bf16[256,512]{1,0:T(8,128)(2,1)S(1)}, u32[]{:S(2)}, u32[]{:S(2)}) %collective-permute-start.55) | collective-permute-done | bytes 262176 | tf_op jit(solution)/shard_map/ppermute | solution.py:369
  134.7 1.6 %copy-done.2 = f32[1024,512]{1,0:T(8,128)S(1)} copy-done((f32[1024,512]{1,0:T(8,128)S(1)}, f32[1024,512]{1,0:T(8,128)}, u32[]{:S(2)}) %copy-start.2) | copy-done | bytes 2097176
  136.8 0.6 collective-permute-start.59
  137.9 6.7 %collective-permute-done.59.refs_6_.refs_5_ = bf16[256,512]{1,0:T(8,128)(2,1)S(1)} collective-permute-done((bf16[256,512]{1,0:T(8,128)(2,1)S(1)}, bf16[256,512]{1,0:T(8,128)(2,1)S(1)}, u32[]{:S(2)}, u32[]{:S(2)}) %collective-permute-start.59) | collective-permute-done | bytes 262176 | tf_op jit(solution)/shard_map/ppermute | solution.py:62
  144.7 1.3 shard_map.85
  146.2 0.6 shard_map.86
  146.8 1.5 %collective-permute-start.62 = (f32[1,512]{1,0:T(1,128)S(1)}, f32[1,512]{1,0:T(1,128)S(1)}, u32[]{:S(2)}, u32[]{:S(2)}) collective-permute-start(f32[1,512]{1,0:T(1,128)S(1)} %get-tuple-element.98._), channel_id=1, source_target_pairs={{0,16},{16,0},{1,17},{17,1},{2,18},{18,2},{3,19},{19,3},{4,20},{20... | collective-permute-start | bytes 6152 | tf_op jit(solution)/shard_map/ppermute | solution.py:66
  148.4 2.6 %shard_map.87 = f32[1024,512]{1,0:T(8,128)} custom-call(f32[1,512]{1,0:T(1,128)S(1)} %get-tuple-element.98._, s32[3]{0:T(128)S(1)} %pad_add_fusion.refs_0_, f32[1024,512]{1,0:T(8,128)S(1)} %get-tuple-element.92._.refs_1_, bf16[256,512]{1,0:T(8,128)(2,1)S(1)} %get-tuple-element.81.refs_5_.refs_2_, bf16[256,512]{1,0:T(8,128)(2,1)S(1)} %get-tuple-element.82.refs_6_.refs_3_, ...), custom_call_target="tpu_custom_call" | custom-call | flops 1 | bytes 1 | tf_op jit(solution)/shard_map/pallas_call | solution.py:40
  151.0 0.6 add_reduce_fusion
  (123 shorter events, 12.9 us)
Async XLA Ops:
  1.9 8.2 %copy-start.1 = (bf16[1024,512]{1,0:T(8,128)(2,1)S(1)}, bf16[1024,512]{1,0:T(8,128)(2,1)}, u32[]{:S(2)}) copy-start(bf16[1024,512]{1,0:T(8,128)(2,1)} %refs_3_.3) | copy-start | bytes 3145732
  3.5 4.6 %collective-permute-start = (f32[2,512]{1,0:T(2,128)S(1)}, f32[2,512]{1,0:T(2,128)S(1)}, u32[]{:S(2)}, u32[]{:S(2)}) collective-permute-start(f32[2,512]{1,0:T(2,128)S(1)} %shard_map.49._), channel_id=1, source_target_pairs={{0,16},{16,0},{1,17},{17,1},{2,18},{18,2},{3,19},{19,3},{4,20},{20... | collective-permute-start | bytes 12296 | tf_op jit(solution)/shard_map/ppermute | solution.py:66
  8.1 26.3 %collective-permute-start.10 = (bf16[1024,512]{1,0:T(8,128)(2,1)}, bf16[1024,512]{1,0:T(8,128)(2,1)S(1)}, u32[]{:S(2)}, u32[]{:S(2)}) collective-permute-start(bf16[1024,512]{1,0:T(8,128)(2,1)} %refs_2_.3), channel_id=1, source_target_pairs={{0,16},{16,0},{1,17},{17,1},{2,18},{18,2},{3,19},{19,3},{4,20},{20... | collective-permute-start | bytes 3145736 | tf_op jit(solution)/shard_map/ppermute | solution.py:66
  12.9 1.6 %collective-permute-start.1 = (bf16[256,512]{1,0:T(8,128)(2,1)S(1)}, bf16[256,512]{1,0:T(8,128)(2,1)S(1)}, u32[]{:S(2)}, u32[]{:S(2)}) collective-permute-start(bf16[256,512]{1,0:T(8,128)(2,1)S(1)} %get-tuple-element.53.refs_1_), channel_id=1, source_target_pairs={{0,1},{1,0},{2,3},{3,2},{4,5},{5,4},{6,7},{7,6},{8,9},{9,8},{10,11... | collective-permute-start | bytes 786440 | tf_op jit(solution)/shard_map/ppermute | solution.py:66
  13.0 2.0 %collective-permute-start.2 = (bf16[256,512]{1,0:T(8,128)(2,1)S(1)}, bf16[256,512]{1,0:T(8,128)(2,1)}, u32[]{:S(2)}, u32[]{:S(2)}) collective-permute-start(bf16[256,512]{1,0:T(8,128)(2,1)S(1)} %get-tuple-element.54.refs_2_), channel_id=1, source_target_pairs={{0,1},{1,0},{2,3},{3,2},{4,5},{5,4},{6,7},{7,6},{8,9},{9,8},{10,11... | collective-permute-start | bytes 786440 | tf_op jit(solution)/shard_map/ppermute | solution.py:66
  13.5 1.9 %collective-permute-start.3 = (bf16[256,512]{1,0:T(8,128)(2,1)S(1)}, bf16[256,512]{1,0:T(8,128)(2,1)}, u32[]{:S(2)}, u32[]{:S(2)}) collective-permute-start(bf16[256,512]{1,0:T(8,128)(2,1)S(1)} %get-tuple-element.55.refs_3_), channel_id=1, source_target_pairs={{0,1},{1,0},{2,3},{3,2},{4,5},{5,4},{6,7},{7,6},{8,9},{9,8},{10,11... | collective-permute-start | bytes 786440 | tf_op jit(solution)/shard_map/ppermute | solution.py:66
  13.6 2.2 %collective-permute-start.4 = (bf16[256,512]{1,0:T(8,128)(2,1)S(1)}, bf16[256,512]{1,0:T(8,128)(2,1)}, u32[]{:S(2)}, u32[]{:S(2)}) collective-permute-start(bf16[256,512]{1,0:T(8,128)(2,1)S(1)} %get-tuple-element.56.refs_4_), channel_id=1, source_target_pairs={{0,1},{1,0},{2,3},{3,2},{4,5},{5,4},{6,7},{7,6},{8,9},{9,8},{10,11... | collective-permute-start | bytes 786440 | tf_op jit(solution)/shard_map/ppermute | solution.py:66
  14.5 4.8 %collective-permute-start.5 = (bf16[256,512]{1,0:T(8,128)(2,1)}, bf16[256,512]{1,0:T(8,128)(2,1)}, u32[]{:S(2)}, u32[]{:S(2)}) collective-permute-start(bf16[256,512]{1,0:T(8,128)(2,1)} %get-tuple-element.58.refs_1_), channel_id=1, source_target_pairs={{0,1},{1,0},{2,3},{3,2},{4,5},{5,4},{6,7},{7,6},{8,9},{9,8},{10,11... | collective-permute-start | bytes 786440 | tf_op jit(solution)/shard_map/ppermute | solution.py:66
  15.0 5.9 %collective-permute-start.6 = (bf16[256,512]{1,0:T(8,128)(2,1)}, bf16[256,512]{1,0:T(8,128)(2,1)}, u32[]{:S(2)}, u32[]{:S(2)}) collective-permute-start(bf16[256,512]{1,0:T(8,128)(2,1)} %copy-done.3), channel_id=1, source_target_pairs={{0,1},{1,0},{2,3},{3,2},{4,5},{5,4},{6,7},{7,6},{8,9},{9,8},{10,11... | collective-permute-start | bytes 786440 | tf_op jit(solution)/shard_map/ppermute | solution.py:66
  15.4 6.0 %collective-permute-start.7 = (bf16[256,512]{1,0:T(8,128)(2,1)}, bf16[256,512]{1,0:T(8,128)(2,1)S(1)}, u32[]{:S(2)}, u32[]{:S(2)}) collective-permute-start(bf16[256,512]{1,0:T(8,128)(2,1)} %copy-done.5), channel_id=1, source_target_pairs={{0,1},{1,0},{2,3},{3,2},{4,5},{5,4},{6,7},{7,6},{8,9},{9,8},{10,11... | collective-permute-start | bytes 786440 | tf_op jit(solution)/shard_map/ppermute | solution.py:66
  15.8 5.7 %collective-permute-start.8 = (bf16[256,512]{1,0:T(8,128)(2,1)}, bf16[256,512]{1,0:T(8,128)(2,1)S(1)}, u32[]{:S(2)}, u32[]{:S(2)}) collective-permute-start(bf16[256,512]{1,0:T(8,128)(2,1)} %copy-done.7), channel_id=1, source_target_pairs={{0,1},{1,0},{2,3},{3,2},{4,5},{5,4},{6,7},{7,6},{8,9},{9,8},{10,11... | collective-permute-start | bytes 786440 | tf_op jit(solution)/shard_map/ppermute | solution.py:66
  19.4 12.4 %collective-permute-start.9 = (bf16[400,512]{1,0:T(8,128)(2,1)S(1)}, bf16[400,512]{1,0:T(8,128)(2,1)S(1)}, u32[]{:S(2)}, u32[]{:S(2)}) collective-permute-start(bf16[400,512]{1,0:T(8,128)(2,1)S(1)} %get-tuple-element.64), channel_id=1, source_target_pairs={{0,2},{1,3},{2,0},{3,1},{4,6},{5,7},{6,4},{7,5},{8,10},{9,11},{10,... | collective-permute-start | bytes 1228808 | tf_op jit(solution)/shard_map/ppermute | solution.py:62
  21.0 37.8 %collective-permute-start.19 = (bf16[1024,512]{1,0:T(8,128)(2,1)S(1)}, bf16[1024,512]{1,0:T(8,128)(2,1)S(1)}, u32[]{:S(2)}, u32[]{:S(2)}) collective-permute-start(bf16[1024,512]{1,0:T(8,128)(2,1)S(1)} %copy-done.1), channel_id=1, source_target_pairs={{0,16},{16,0},{1,17},{17,1},{2,18},{18,2},{3,19},{19,3},{4,20},{20... | collective-permute-start | bytes 3145736 | tf_op jit(solution)/shard_map/ppermute | solution.py:66
  24.9 15.0 %collective-permute-start.11 = (bf16[400,512]{1,0:T(8,128)(2,1)S(1)}, bf16[400,512]{1,0:T(8,128)(2,1)S(1)}, u32[]{:S(2)}, u32[]{:S(2)}) collective-permute-start(bf16[400,512]{1,0:T(8,128)(2,1)S(1)} %get-tuple-element.68), channel_id=1, source_target_pairs={{0,2},{1,3},{2,0},{3,1},{4,6},{5,7},{6,4},{7,5},{8,10},{9,11},{10,... | collective-permute-start | bytes 1228808 | tf_op jit(solution)/shard_map/ppermute | solution.py:62
  34.6 5.4 %collective-permute-start.12 = (bf16[256,512]{1,0:T(8,128)(2,1)S(1)}, bf16[256,512]{1,0:T(8,128)(2,1)S(1)}, u32[]{:S(2)}, u32[]{:S(2)}) collective-permute-start(bf16[256,512]{1,0:T(8,128)(2,1)S(1)} %get-tuple-element.66._.refs_3_.refs_2_), channel_id=1, source_target_pairs={{0,1},{1,0},{2,3},{3,2},{4,5},{5,4},{6,7},{7,6},{8,9},{9,8},{10,11... | collective-permute-start | bytes 786440 | tf_op jit(solution)/shard_map/ppermute | solution.py:66
  34.6 5.9 %collective-permute-start.13 = (bf16[256,512]{1,0:T(8,128)(2,1)S(1)}, bf16[256,512]{1,0:T(8,128)(2,1)S(1)}, u32[]{:S(2)}, u32[]{:S(2)}) collective-permute-start(bf16[256,512]{1,0:T(8,128)(2,1)S(1)} %get-tuple-element.70.refs_4_.refs_3_), channel_id=1, source_target_pairs={{0,1},{1,0},{2,3},{3,2},{4,5},{5,4},{6,7},{7,6},{8,9},{9,8},{10,11... | collective-permute-start | bytes 786440 | tf_op jit(solution)/shard_map/ppermute | solution.py:66
  35.1 13.8 %collective-permute-start.16 = (bf16[400,512]{1,0:T(8,128)(2,1)S(1)}, bf16[400,512]{1,0:T(8,128)(2,1)S(1)}, u32[]{:S(2)}, u32[]{:S(2)}) collective-permute-start(bf16[400,512]{1,0:T(8,128)(2,1)S(1)} %shard_map.53._), channel_id=1, source_target_pairs={{0,4},{12,8},{1,5},{13,9},{2,6},{14,10},{3,7},{15,11},{16,20},{28,... | collective-permute-start | bytes 1228808 | tf_op jit(solution)/shard_map/ppermute | solution.py:369
  40.0 4.1 %collective-permute-start.14 = (bf16[256,512]{1,0:T(8,128)(2,1)S(1)}, bf16[256,512]{1,0:T(8,128)(2,1)S(1)}, u32[]{:S(2)}, u32[]{:S(2)}) collective-permute-start(bf16[256,512]{1,0:T(8,128)(2,1)S(1)} %get-tuple-element.71.refs_5_.refs_2_), channel_id=1, source_target_pairs={{0,1},{1,0},{2,3},{3,2},{4,5},{5,4},{6,7},{7,6},{8,9},{9,8},{10,11... | collective-permute-start | bytes 786440 | tf_op jit(solution)/shard_map/ppermute | solution.py:66
  40.0 4.1 %collective-permute-start.15 = (bf16[256,512]{1,0:T(8,128)(2,1)S(1)}, bf16[256,512]{1,0:T(8,128)(2,1)S(1)}, u32[]{:S(2)}, u32[]{:S(2)}) collective-permute-start(bf16[256,512]{1,0:T(8,128)(2,1)S(1)} %get-tuple-element.72.refs_6_.refs_3_), channel_id=1, source_target_pairs={{0,1},{1,0},{2,3},{3,2},{4,5},{5,4},{6,7},{7,6},{8,9},{9,8},{10,11... | collective-permute-start | bytes 786440 | tf_op jit(solution)/shard_map/ppermute | solution.py:66
  40.6 18.0 %collective-permute-start.18 = (bf16[400,512]{1,0:T(8,128)(2,1)S(1)}, bf16[400,512]{1,0:T(8,128)(2,1)S(1)}, u32[]{:S(2)}, u32[]{:S(2)}) collective-permute-start(bf16[400,512]{1,0:T(8,128)(2,1)S(1)} %shard_map.55._), channel_id=1, source_target_pairs={{0,4},{12,8},{1,5},{13,9},{2,6},{14,10},{3,7},{15,11},{16,20},{28,... | collective-permute-start | bytes 1228808 | tf_op jit(solution)/shard_map/ppermute | solution.py:369
  45.9 9.3 %collective-permute-start.17 = (bf16[256,512]{1,0:T(8,128)(2,1)S(1)}, bf16[256,512]{1,0:T(8,128)(2,1)S(1)}, u32[]{:S(2)}, u32[]{:S(2)}) collective-permute-start(bf16[256,512]{1,0:T(8,128)(2,1)S(1)} %get-tuple-element.74), channel_id=1, source_target_pairs={{0,2},{1,3},{2,0},{3,1},{4,6},{5,7},{6,4},{7,5},{8,10},{9,11},{10,... | collective-permute-start | bytes 786440 | tf_op jit(solution)/shard_map/ppermute | solution.py:62
  49.1 13.7 %collective-permute-start.20 = (bf16[400,512]{1,0:T(8,128)(2,1)S(1)}, bf16[400,512]{1,0:T(8,128)(2,1)S(1)}, u32[]{:S(2)}, u32[]{:S(2)}) collective-permute-start(bf16[400,512]{1,0:T(8,128)(2,1)S(1)} %shard_map.57._.refs_0_), channel_id=1, source_target_pairs={{4,8},{8,4},{5,9},{9,5},{6,10},{10,6},{7,11},{11,7},{20,24},{24,20... | collective-permute-start | bytes 1228808 | tf_op jit(solution)/shard_map/ppermute | solution.py:369
  49.8 13.8 %collective-permute-start.22 = (bf16[256,512]{1,0:T(8,128)(2,1)S(1)}, bf16[256,512]{1,0:T(8,128)(2,1)S(1)}, u32[]{:S(2)}, u32[]{:S(2)}) collective-permute-start(bf16[256,512]{1,0:T(8,128)(2,1)S(1)} %get-tuple-element.78), channel_id=1, source_target_pairs={{0,2},{1,3},{2,0},{3,1},{4,6},{5,7},{6,4},{7,5},{8,10},{9,11},{10,... | collective-permute-start | bytes 786440 | tf_op jit(solution)/shard_map/ppermute | solution.py:62
  55.3 9.7 %collective-permute-start.21 = (bf16[256,512]{1,0:T(8,128)(2,1)S(1)}, bf16[256,512]{1,0:T(8,128)(2,1)S(1)}, u32[]{:S(2)}, u32[]{:S(2)}) collective-permute-start(bf16[256,512]{1,0:T(8,128)(2,1)S(1)} %shard_map.58._), channel_id=1, source_target_pairs={{0,4},{12,8},{1,5},{13,9},{2,6},{14,10},{3,7},{15,11},{16,20},{28,... | collective-permute-start | bytes 786440 | tf_op jit(solution)/shard_map/ppermute | solution.py:369
  58.9 6.6 %collective-permute-start.23 = (bf16[256,512]{1,0:T(8,128)(2,1)S(1)}, bf16[256,512]{1,0:T(8,128)(2,1)S(1)}, u32[]{:S(2)}, u32[]{:S(2)}) collective-permute-start(bf16[256,512]{1,0:T(8,128)(2,1)S(1)} %get-tuple-element.76._.refs_3_.refs_2_), channel_id=1, source_target_pairs={{0,1},{1,0},{2,3},{3,2},{4,5},{5,4},{6,7},{7,6},{8,9},{9,8},{10,11... | collective-permute-start | bytes 786440 | tf_op jit(solution)/shard_map/ppermute | solution.py:66
  59.0 3.8 %collective-permute-start.27 = (f32[8,512]{1,0:T(8,128)S(1)}, f32[8,512]{1,0:T(8,128)S(1)}, u32[]{:S(2)}, u32[]{:S(2)}) collective-permute-start(f32[8,512]{1,0:T(8,128)S(1)} %get-tuple-element.52._), channel_id=1, source_target_pairs={{0,16},{16,0},{1,17},{17,1},{2,18},{18,2},{3,19},{19,3},{4,20},{20... | collective-permute-start | bytes 49160 | tf_op jit(solution)/shard_map/ppermute | solution.py:66
  62.8 3.0 %collective-permute-start.24 = (bf16[256,512]{1,0:T(8,128)(2,1)S(1)}, bf16[256,512]{1,0:T(8,128)(2,1)S(1)}, u32[]{:S(2)}, u32[]{:S(2)}) collective-permute-start(bf16[256,512]{1,0:T(8,128)(2,1)S(1)} %get-tuple-element.80.refs_4_.refs_3_), channel_id=1, source_target_pairs={{0,1},{1,0},{2,3},{3,2},{4,5},{5,4},{6,7},{7,6},{8,9},{9,8},{10,11... | collective-permute-start | bytes 786440 | tf_op jit(solution)/shard_map/ppermute | solution.py:66
  62.8 16.7 %collective-permute-start.29 = (bf16[400,512]{1,0:T(8,128)(2,1)S(1)}, bf16[400,512]{1,0:T(8,128)(2,1)S(1)}, u32[]{:S(2)}, u32[]{:S(2)}) collective-permute-start(bf16[400,512]{1,0:T(8,128)(2,1)S(1)} %shard_map.59._.refs_0_), channel_id=1, source_target_pairs={{4,8},{8,4},{5,9},{9,5},{6,10},{10,6},{7,11},{11,7},{20,24},{24,20... | collective-permute-start | bytes 1228808 | tf_op jit(solution)/shard_map/ppermute | solution.py:369
  63.6 17.3 %collective-permute-start.30 = (bf16[400,512]{1,0:T(8,128)(2,1)S(1)}, bf16[400,512]{1,0:T(8,128)(2,1)S(1)}, u32[]{:S(2)}, u32[]{:S(2)}) collective-permute-start(bf16[400,512]{1,0:T(8,128)(2,1)S(1)} %shard_map.61._.refs_1_), channel_id=1, source_target_pairs={{4,0},{8,12},{5,1},{9,13},{6,2},{10,14},{7,3},{11,15},{20,16},{24,... | collective-permute-start | bytes 1228808 | tf_op jit(solution)/shard_map/ppermute | solution.py:369
  64.9 7.1 %collective-permute-start.25 = (bf16[256,512]{1,0:T(8,128)(2,1)S(1)}, bf16[256,512]{1,0:T(8,128)(2,1)S(1)}, u32[]{:S(2)}, u32[]{:S(2)}) collective-permute-start(bf16[256,512]{1,0:T(8,128)(2,1)S(1)} %get-tuple-element.81.refs_5_.refs_2_), channel_id=1, source_target_pairs={{0,1},{1,0},{2,3},{3,2},{4,5},{5,4},{6,7},{7,6},{8,9},{9,8},{10,11... | collective-permute-start | bytes 786440 | tf_op jit(solution)/shard_map/ppermute | solution.py:66
  65.5 6.5 %collective-permute-start.26 = (bf16[256,512]{1,0:T(8,128)(2,1)S(1)}, bf16[256,512]{1,0:T(8,128)(2,1)S(1)}, u32[]{:S(2)}, u32[]{:S(2)}) collective-permute-start(bf16[256,512]{1,0:T(8,128)(2,1)S(1)} %get-tuple-element.82.refs_6_.refs_3_), channel_id=1, source_target_pairs={{0,1},{1,0},{2,3},{3,2},{4,5},{5,4},{6,7},{7,6},{8,9},{9,8},{10,11... | collective-permute-start | bytes 786440 | tf_op jit(solution)/shard_map/ppermute | solution.py:66
  65.8 12.2 %collective-permute-start.28 = (bf16[256,512]{1,0:T(8,128)(2,1)S(1)}, bf16[256,512]{1,0:T(8,128)(2,1)S(1)}, u32[]{:S(2)}, u32[]{:S(2)}) collective-permute-start(bf16[256,512]{1,0:T(8,128)(2,1)S(1)} %shard_map.63._), channel_id=1, source_target_pairs={{0,4},{12,8},{1,5},{13,9},{2,6},{14,10},{3,7},{15,11},{16,20},{28,... | collective-permute-start | bytes 786440 | tf_op jit(solution)/shard_map/ppermute | solution.py:369
  73.9 9.6 %collective-permute-start.32 = (bf16[272,512]{1,0:T(8,128)(2,1)S(1)}, bf16[272,512]{1,0:T(8,128)(2,1)S(1)}, u32[]{:S(2)}, u32[]{:S(2)}) collective-permute-start(bf16[272,512]{1,0:T(8,128)(2,1)S(1)} %get-tuple-element.84), channel_id=1, source_target_pairs={{0,2},{1,3},{2,0},{3,1},{4,6},{5,7},{6,4},{7,5},{8,10},{9,11},{10,... | collective-permute-start | bytes 835592 | tf_op jit(solution)/shard_map/ppermute | solution.py:62
  75.5 6.8 %collective-permute-start.31 = (bf16[256,512]{1,0:T(8,128)(2,1)S(1)}, bf16[256,512]{1,0:T(8,128)(2,1)S(1)}, u32[]{:S(2)}, u32[]{:S(2)}) collective-permute-start(bf16[256,512]{1,0:T(8,128)(2,1)S(1)} %shard_map.62._.refs_0_), channel_id=1, source_target_pairs={{4,8},{8,4},{5,9},{9,5},{6,10},{10,6},{7,11},{11,7},{20,24},{24,20... | collective-permute-start | bytes 786440 | tf_op jit(solution)/shard_map/ppermute | solution.py:369
  78.0 11.2 %collective-permute-start.34 = (bf16[256,512]{1,0:T(8,128)(2,1)S(1)}, bf16[256,512]{1,0:T(8,128)(2,1)S(1)}, u32[]{:S(2)}, u32[]{:S(2)}) collective-permute-start(bf16[256,512]{1,0:T(8,128)(2,1)S(1)} %get-tuple-element.86), channel_id=1, source_target_pairs={{0,2},{1,3},{2,0},{3,1},{4,6},{5,7},{6,4},{7,5},{8,10},{9,11},{10,... | collective-permute-start | bytes 786440 | tf_op jit(solution)/shard_map/ppermute | solution.py:62
  79.7 12.6 %collective-permute-start.35 = (bf16[400,512]{1,0:T(8,128)(2,1)S(1)}, bf16[400,512]{1,0:T(8,128)(2,1)S(1)}, u32[]{:S(2)}, u32[]{:S(2)}) collective-permute-start(bf16[400,512]{1,0:T(8,128)(2,1)S(1)} %shard_map.66._.refs_1_), channel_id=1, source_target_pairs={{4,0},{8,12},{5,1},{9,13},{6,2},{10,14},{7,3},{11,15},{20,16},{24,... | collective-permute-start | bytes 1228808 | tf_op jit(solution)/shard_map/ppermute | solution.py:369
  81.0 9.5 %collective-permute-start.33 = (bf16[256,512]{1,0:T(8,128)(2,1)S(1)}, bf16[256,512]{1,0:T(8,128)(2,1)S(1)}, u32[]{:S(2)}, u32[]{:S(2)}) collective-permute-start(bf16[256,512]{1,0:T(8,128)(2,1)S(1)} %shard_map.65._.refs_0_), channel_id=1, source_target_pairs={{4,8},{8,4},{5,9},{9,5},{6,10},{10,6},{7,11},{11,7},{20,24},{24,20... | collective-permute-start | bytes 786440 | tf_op jit(solution)/shard_map/ppermute | solution.py:369
  82.3 16.8 %collective-permute-start.41 = (bf16[400,512]{1,0:T(8,128)(2,1)S(1)}, bf16[400,512]{1,0:T(8,128)(2,1)S(1)}, u32[]{:S(2)}, u32[]{:S(2)}) collective-permute-start(bf16[400,512]{1,0:T(8,128)(2,1)S(1)} %shard_map.67._.refs_6_), channel_id=1, source_target_pairs={{0,2},{1,3},{2,0},{3,1},{4,6},{5,7},{6,4},{7,5},{8,10},{9,11},{10,... | collective-permute-start | bytes 1228808 | tf_op jit(solution)/shard_map/ppermute | solution.py:62
  83.6 10.3 %collective-permute-start.36 = (bf16[272,512]{1,0:T(8,128)(2,1)S(1)}, bf16[272,512]{1,0:T(8,128)(2,1)S(1)}, u32[]{:S(2)}, u32[]{:S(2)}) collective-permute-start(bf16[272,512]{1,0:T(8,128)(2,1)S(1)} %shard_map.69._), channel_id=1, source_target_pairs={{0,4},{12,8},{1,5},{13,9},{2,6},{14,10},{3,7},{15,11},{16,20},{28,... | collective-permute-start | bytes 835592 | tf_op jit(solution)/shard_map/ppermute | solution.py:369
  89.2 9.2 %collective-permute-start.37 = (bf16[256,512]{1,0:T(8,128)(2,1)S(1)}, bf16[256,512]{1,0:T(8,128)(2,1)S(1)}, u32[]{:S(2)}, u32[]{:S(2)}) collective-permute-start(bf16[256,512]{1,0:T(8,128)(2,1)S(1)} %shard_map.68._.refs_1_), channel_id=1, source_target_pairs={{4,0},{8,12},{5,1},{9,13},{6,2},{10,14},{7,3},{11,15},{20,16},{24,... | collective-permute-start | bytes 786440 | tf_op jit(solution)/shard_map/ppermute | solution.py:369
  90.5 8.7 %collective-permute-start.42 = (bf16[400,512]{1,0:T(8,128)(2,1)S(1)}, bf16[400,512]{1,0:T(8,128)(2,1)S(1)}, u32[]{:S(2)}, u32[]{:S(2)}) collective-permute-start(bf16[400,512]{1,0:T(8,128)(2,1)S(1)} %shard_map.67._.refs_6_), channel_id=1, source_target_pairs={{0,1},{1,0},{2,3},{3,2},{4,5},{5,4},{6,7},{7,6},{8,9},{9,8},{10,11... | collective-permute-start | bytes 1228808 | tf_op jit(solution)/shard_map/ppermute | solution.py:66
  93.1 13.2 %collective-permute-start.44 = (bf16[400,512]{1,0:T(8,128)(2,1)S(1)}, bf16[400,512]{1,0:T(8,128)(2,1)S(1)}, u32[]{:S(2)}, u32[]{:S(2)}) collective-permute-start(bf16[400,512]{1,0:T(8,128)(2,1)S(1)} %shard_map.72._.refs_6_), channel_id=1, source_target_pairs={{0,2},{1,3},{2,0},{3,1},{4,6},{5,7},{6,4},{7,5},{8,10},{9,11},{10,... | collective-permute-start | bytes 1228808 | tf_op jit(solution)/shard_map/ppermute | solution.py:62
  93.8 9.8 %collective-permute-start.38 = (bf16[256,512]{1,0:T(8,128)(2,1)S(1)}, bf16[256,512]{1,0:T(8,128)(2,1)S(1)}, u32[]{:S(2)}, u32[]{:S(2)}) collective-permute-start(bf16[256,512]{1,0:T(8,128)(2,1)S(1)} %shard_map.71._), channel_id=1, source_target_pairs={{0,4},{12,8},{1,5},{13,9},{2,6},{14,10},{3,7},{15,11},{16,20},{28,... | collective-permute-start | bytes 786440 | tf_op jit(solution)/shard_map/ppermute | solution.py:369
  98.4 5.7 %collective-permute-start.39 = (bf16[272,512]{1,0:T(8,128)(2,1)S(1)}, bf16[272,512]{1,0:T(8,128)(2,1)S(1)}, u32[]{:S(2)}, u32[]{:S(2)}) collective-permute-start(bf16[272,512]{1,0:T(8,128)(2,1)S(1)} %shard_map.73._.refs_0_), channel_id=1, source_target_pairs={{4,8},{8,4},{5,9},{9,5},{6,10},{10,6},{7,11},{11,7},{20,24},{24,20... | collective-permute-start | bytes 835592 | tf_op jit(solution)/shard_map/ppermute | solution.py:369
  99.1 13.2 %collective-permute-start.45 = (bf16[400,512]{1,0:T(8,128)(2,1)S(1)}, bf16[400,512]{1,0:T(8,128)(2,1)S(1)}, u32[]{:S(2)}, u32[]{:S(2)}) collective-permute-start(bf16[400,512]{1,0:T(8,128)(2,1)S(1)} %shard_map.72._.refs_6_), channel_id=1, source_target_pairs={{0,1},{1,0},{2,3},{3,2},{4,5},{5,4},{6,7},{7,6},{8,9},{9,8},{10,11... | collective-permute-start | bytes 1228808 | tf_op jit(solution)/shard_map/ppermute | solution.py:66
  99.1 10.6 %collective-permute-start.40 = (bf16[256,512]{1,0:T(8,128)(2,1)S(1)}, bf16[256,512]{1,0:T(8,128)(2,1)S(1)}, u32[]{:S(2)}, u32[]{:S(2)}) collective-permute-start(bf16[256,512]{1,0:T(8,128)(2,1)S(1)} %shard_map.70._.refs_1_), channel_id=1, source_target_pairs={{4,0},{8,12},{5,1},{9,13},{6,2},{10,14},{7,3},{11,15},{20,16},{24,... | collective-permute-start | bytes 786440 | tf_op jit(solution)/shard_map/ppermute | solution.py:369
  103.6 8.0 %collective-permute-start.49 = (bf16[256,512]{1,0:T(8,128)(2,1)S(1)}, bf16[256,512]{1,0:T(8,128)(2,1)S(1)}, u32[]{:S(2)}, u32[]{:S(2)}) collective-permute-start(bf16[256,512]{1,0:T(8,128)(2,1)S(1)} %shard_map.74._.refs_4_), channel_id=1, source_target_pairs={{0,2},{1,3},{2,0},{3,1},{4,6},{5,7},{6,4},{7,5},{8,10},{9,11},{10,... | collective-permute-start | bytes 786440 | tf_op jit(solution)/shard_map/ppermute | solution.py:62
  104.0 9.7 %collective-permute-start.43 = (bf16[400,512]{1,0:T(8,128)(2,1)S(1)}, bf16[400,512]{1,0:T(8,128)(2,1)S(1)}, u32[]{:S(2)}, u32[]{:S(2)}) collective-permute-start(bf16[400,512]{1,0:T(8,128)(2,1)S(1)} %collective-permute-done.41.refs_7_), channel_id=1, source_target_pairs={{0,1},{1,0},{2,3},{3,2},{4,5},{5,4},{6,7},{7,6},{8,9},{9,8},{10,11... | collective-permute-start | bytes 1228808 | tf_op jit(solution)/shard_map/ppermute | solution.py:66
  106.2 10.7 %collective-permute-start.46 = (bf16[400,512]{1,0:T(8,128)(2,1)S(1)}, bf16[400,512]{1,0:T(8,128)(2,1)S(1)}, u32[]{:S(2)}, u32[]{:S(2)}) collective-permute-start(bf16[400,512]{1,0:T(8,128)(2,1)S(1)} %collective-permute-done.44.refs_7_), channel_id=1, source_target_pairs={{0,1},{1,0},{2,3},{3,2},{4,5},{5,4},{6,7},{7,6},{8,9},{9,8},{10,11... | collective-permute-start | bytes 1228808 | tf_op jit(solution)/shard_map/ppermute | solution.py:66
  109.7 11.7 %collective-permute-start.48 = (bf16[272,512]{1,0:T(8,128)(2,1)S(1)}, bf16[272,512]{1,0:T(8,128)(2,1)S(1)}, u32[]{:S(2)}, u32[]{:S(2)}) collective-permute-start(bf16[272,512]{1,0:T(8,128)(2,1)S(1)} %shard_map.76._.refs_1_), channel_id=1, source_target_pairs={{4,0},{8,12},{5,1},{9,13},{6,2},{10,14},{7,3},{11,15},{20,16},{24,... | collective-permute-start | bytes 835592 | tf_op jit(solution)/shard_map/ppermute | solution.py:369
  111.6 9.1 %collective-permute-start.47 = (bf16[256,512]{1,0:T(8,128)(2,1)S(1)}, bf16[256,512]{1,0:T(8,128)(2,1)S(1)}, u32[]{:S(2)}, u32[]{:S(2)}) collective-permute-start(bf16[256,512]{1,0:T(8,128)(2,1)S(1)} %shard_map.75._.refs_0_), channel_id=1, source_target_pairs={{4,8},{8,4},{5,9},{9,5},{6,10},{10,6},{7,11},{11,7},{20,24},{24,20... | collective-permute-start | bytes 786440 | tf_op jit(solution)/shard_map/ppermute | solution.py:369
  112.3 8.5 %collective-permute-start.52 = (bf16[256,512]{1,0:T(8,128)(2,1)S(1)}, bf16[256,512]{1,0:T(8,128)(2,1)S(1)}, u32[]{:S(2)}, u32[]{:S(2)}) collective-permute-start(bf16[256,512]{1,0:T(8,128)(2,1)S(1)} %shard_map.77._.refs_4_), channel_id=1, source_target_pairs={{0,2},{1,3},{2,0},{3,1},{4,6},{5,7},{6,4},{7,5},{8,10},{9,11},{10,... | collective-permute-start | bytes 786440 | tf_op jit(solution)/shard_map/ppermute | solution.py:62
  113.8 9.5 %collective-permute-start.50 = (bf16[256,512]{1,0:T(8,128)(2,1)S(1)}, bf16[256,512]{1,0:T(8,128)(2,1)S(1)}, u32[]{:S(2)}, u32[]{:S(2)}) collective-permute-start(bf16[256,512]{1,0:T(8,128)(2,1)S(1)} %shard_map.74._.refs_4_), channel_id=1, source_target_pairs={{0,1},{1,0},{2,3},{3,2},{4,5},{5,4},{6,7},{7,6},{8,9},{9,8},{10,11... | collective-permute-start | bytes 786440 | tf_op jit(solution)/shard_map/ppermute | solution.py:66
  117.0 7.0 %collective-permute-start.51 = (bf16[256,512]{1,0:T(8,128)(2,1)S(1)}, bf16[256,512]{1,0:T(8,128)(2,1)S(1)}, u32[]{:S(2)}, u32[]{:S(2)}) collective-permute-start(bf16[256,512]{1,0:T(8,128)(2,1)S(1)} %collective-permute-done.49.refs_5_), channel_id=1, source_target_pairs={{0,1},{1,0},{2,3},{3,2},{4,5},{5,4},{6,7},{7,6},{8,9},{9,8},{10,11... | collective-permute-start | bytes 786440 | tf_op jit(solution)/shard_map/ppermute | solution.py:66
  120.7 5.0 %collective-permute-start.53 = (bf16[256,512]{1,0:T(8,128)(2,1)S(1)}, bf16[256,512]{1,0:T(8,128)(2,1)S(1)}, u32[]{:S(2)}, u32[]{:S(2)}) collective-permute-start(bf16[256,512]{1,0:T(8,128)(2,1)S(1)} %shard_map.77._.refs_4_), channel_id=1, source_target_pairs={{0,1},{1,0},{2,3},{3,2},{4,5},{5,4},{6,7},{7,6},{8,9},{9,8},{10,11... | collective-permute-start | bytes 786440 | tf_op jit(solution)/shard_map/ppermute | solution.py:66
  120.8 4.9 %collective-permute-start.54 = (bf16[256,512]{1,0:T(8,128)(2,1)S(1)}, bf16[256,512]{1,0:T(8,128)(2,1)S(1)}, u32[]{:S(2)}, u32[]{:S(2)}) collective-permute-start(bf16[256,512]{1,0:T(8,128)(2,1)S(1)} %collective-permute-done.52.refs_5_), channel_id=1, source_target_pairs={{0,1},{1,0},{2,3},{3,2},{4,5},{5,4},{6,7},{7,6},{8,9},{9,8},{10,11... | collective-permute-start | bytes 786440 | tf_op jit(solution)/shard_map/ppermute | solution.py:66
  121.4 13.2 %collective-permute-start.55 = (bf16[256,512]{1,0:T(8,128)(2,1)S(1)}, bf16[256,512]{1,0:T(8,128)(2,1)S(1)}, u32[]{:S(2)}, u32[]{:S(2)}) collective-permute-start(bf16[256,512]{1,0:T(8,128)(2,1)S(1)} %shard_map.80._.refs_1_), channel_id=1, source_target_pairs={{4,0},{8,12},{5,1},{9,13},{6,2},{10,14},{7,3},{11,15},{20,16},{24,... | collective-permute-start | bytes 786440 | tf_op jit(solution)/shard_map/ppermute | solution.py:369
  123.3 14.1 %collective-permute-start.56 = (bf16[272,512]{1,0:T(8,128)(2,1)S(1)}, bf16[272,512]{1,0:T(8,128)(2,1)S(1)}, u32[]{:S(2)}, u32[]{:S(2)}) collective-permute-start(bf16[272,512]{1,0:T(8,128)(2,1)S(1)} %shard_map.81._.refs_4_), channel_id=1, source_target_pairs={{0,2},{1,3},{2,0},{3,1},{4,6},{5,7},{6,4},{7,5},{8,10},{9,11},{10,... | collective-permute-start | bytes 835592 | tf_op jit(solution)/shard_map/ppermute | solution.py:62
  136.8 7.8 %collective-permute-start.59 = (bf16[256,512]{1,0:T(8,128)(2,1)S(1)}, bf16[256,512]{1,0:T(8,128)(2,1)S(1)}, u32[]{:S(2)}, u32[]{:S(2)}) collective-permute-start(bf16[256,512]{1,0:T(8,128)(2,1)S(1)} %shard_map.84._.refs_5_.refs_4_), channel_id=1, source_target_pairs={{0,2},{1,3},{2,0},{3,1},{4,6},{5,7},{6,4},{7,5},{8,10},{9,11},{10,... | collective-permute-start | bytes 786440 | tf_op jit(solution)/shard_map/ppermute | solution.py:62
  137.4 7.2 %collective-permute-start.57 = (bf16[272,512]{1,0:T(8,128)(2,1)S(1)}, bf16[272,512]{1,0:T(8,128)(2,1)S(1)}, u32[]{:S(2)}, u32[]{:S(2)}) collective-permute-start(bf16[272,512]{1,0:T(8,128)(2,1)S(1)} %shard_map.81._.refs_4_), channel_id=1, source_target_pairs={{0,1},{1,0},{2,3},{3,2},{4,5},{5,4},{6,7},{7,6},{8,9},{9,8},{10,11... | collective-permute-start | bytes 835592 | tf_op jit(solution)/shard_map/ppermute | solution.py:66
  137.4 7.2 %collective-permute-start.58 = (bf16[272,512]{1,0:T(8,128)(2,1)S(1)}, bf16[272,512]{1,0:T(8,128)(2,1)S(1)}, u32[]{:S(2)}, u32[]{:S(2)}) collective-permute-start(bf16[272,512]{1,0:T(8,128)(2,1)S(1)} %collective-permute-done.56.refs_5_), channel_id=1, source_target_pairs={{0,1},{1,0},{2,3},{3,2},{4,5},{5,4},{6,7},{7,6},{8,9},{9,8},{10,11... | collective-permute-start | bytes 835592 | tf_op jit(solution)/shard_map/ppermute | solution.py:66
  137.9 8.0 %collective-permute-start.60 = (bf16[256,512]{1,0:T(8,128)(2,1)S(1)}, bf16[256,512]{1,0:T(8,128)(2,1)S(1)}, u32[]{:S(2)}, u32[]{:S(2)}) collective-permute-start(bf16[256,512]{1,0:T(8,128)(2,1)S(1)} %shard_map.84._.refs_5_.refs_4_), channel_id=1, source_target_pairs={{0,1},{1,0},{2,3},{3,2},{4,5},{5,4},{6,7},{7,6},{8,9},{9,8},{10,11... | collective-permute-start | bytes 786440 | tf_op jit(solution)/shard_map/ppermute | solution.py:66
  144.7 1.5 %collective-permute-start.61 = (bf16[256,512]{1,0:T(8,128)(2,1)S(1)}, bf16[256,512]{1,0:T(8,128)(2,1)S(1)}, u32[]{:S(2)}, u32[]{:S(2)}) collective-permute-start(bf16[256,512]{1,0:T(8,128)(2,1)S(1)} %collective-permute-done.59.refs_6_.refs_5_), channel_id=1, source_target_pairs={{0,1},{1,0},{2,3},{3,2},{4,5},{5,4},{6,7},{7,6},{8,9},{9,8},{10,11... | collective-permute-start | bytes 786440 | tf_op jit(solution)/shard_map/ppermute | solution.py:66
  146.8 4.1 %collective-permute-start.62 = (f32[1,512]{1,0:T(1,128)S(1)}, f32[1,512]{1,0:T(1,128)S(1)}, u32[]{:S(2)}, u32[]{:S(2)}) collective-permute-start(f32[1,512]{1,0:T(1,128)S(1)} %get-tuple-element.98._), channel_id=1, source_target_pairs={{0,16},{16,0},{1,17},{17,1},{2,18},{18,2},{3,19},{19,3},{4,20},{20... | collective-permute-start | bytes 6152 | tf_op jit(solution)/shard_map/ppermute | solution.py:66
  (8 other events, 26.7 us)

commit v4 on v3

--- a/solution.py
+++ b/solution.py
@@ -13,13 +13,12 @@
 eps_var = 0.0001
 
 ORDER = (
-    "g0", "g1", "x0", "c0", "x1", "f0", "i0", "x2", "i1", "c1", "m0", "i2", "x3", "f1", "i3",
-    "m1", "o0", "m2", "x4", "m3", "x5", "o1", "i4", "o2", "i5", "m4", "o3", "p0", "p1", "m5",
-    "o4", "q2", "q3", "o5", "q4", "s5", "q5",
+    "g0", "g1", "x0", "c0", "x1", "f0", "i0", "x2", "x3", "i1", "c1", "m0", "i2", "f1", "t5",
+    "i3", "m1", "o0", "m2", "x4", "m3", "x5", "o1", "i4", "o2", "i5", "m4", "o3", "m5", "o4",
+    "p0", "p1", "o5", "q2", "q3", "q4", "e5", "s5", "q5",
 )
 
 VMEM = pl.BlockSpec(memory_space=pltpu.VMEM)
-SMEM = pl.BlockSpec(memory_space=pltpu.SMEM)
 MIB = 1024 * 1024
 
 
@@ -28,7 +27,7 @@
         self.last = None
 
     def __call__(self, kernel, outs, ins, scratch=(), extra=0):
-        specs = [SMEM if x.ndim == 1 else VMEM for x in ins]
+        specs = [VMEM] * len(ins)
         body = kernel
         if self.last is not None:
             ins, specs = [self.last] + list(ins), [pl.BlockSpec(memory_space=pl.ANY)] + specs
@@ -82,9 +81,38 @@
     )
 
 
-def sums_kernel(first, second, out):
-    out[0:1, :] = jnp.sum(first[...].astype(jnp.float32), axis=0, keepdims=True)
-    out[1:2, :] = jnp.sum(second[...].astype(jnp.float32), axis=0, keepdims=True)
+def sums_kernel(first, second, out, held, sems):
+    count = held.shape[0]
+    size = held.shape[1]
+    copies = []
+    for at in range(count):
+        view = (first, second)[at % 2]
+        rows = view.at[pl.ds(at // 2 * size, size), :]
+        copies.append(pltpu.make_async_copy(rows, held.at[at], sems.at[at]))
+        copies[-1].start()
+    totals = [jnp.zeros((1, held.shape[2]), jnp.float32)] * 2
+    for at, copy in enumerate(copies):
+        copy.wait()
+        part = jnp.sum(held[at].astype(jnp.float32), axis=0, keepdims=True)
+        totals[at % 2] = totals[at % 2] + part
+    out[0:1, :] = totals[0]
+    out[1:2, :] = totals[1]
+
+
+def column_sums(first, second):
+    rows, width = first.shape
+    return pl.pallas_call(
+        sums_kernel,
+        out_shape=array((2, width), jnp.float32),
+        in_specs=[pl.BlockSpec(memory_space=pl.ANY)] * 2,
+        out_specs=VMEM,
+        scratch_shapes=[
+            pltpu.VMEM((8, rows // 4, width), jnp.bfloat16),
+            pltpu.SemaphoreType.DMA((8,)),
+        ],
+        compiler_params=pltpu.CompilerParams(vmem_limit_bytes=8 * MIB),
+        cost_estimate=pl.CostEstimate(flops=1, bytes_accessed=1, transcendentals=0),
+    )(first, second)
 
 
 def write_extra(out, main, extra):
@@ -130,6 +158,11 @@
     stats[...] = block
 
 
+def whereabouts():
+    core = lax.axis_index("col") % 2
+    return core, lax.axis_index("col") // 2
+
+
 def near_place(tile_index, core, rows, tile):
     half, quarter = rows // 2, rows // 4
     square = tile_index < half // tile
@@ -138,9 +171,9 @@
     return square, pl.multiple_of(row, tile), pl.multiple_of(column, half)
 
 
-def near_kernel(x_count, place, *rest):
+def near_kernel(x_count, *rest):
     pieces, swapped, (own, partner, keep, *sends) = rest[:4], rest[4:8], rest[8:]
-    core, x_place = place[0], place[1]
+    core, x_place = whereabouts()
     rows = own.shape[0]
     half = rows // 2
     tile = rows // 4 // x_count
@@ -175,44 +208,61 @@
 
 
 def add_kernel(main, *refs):
-    out = refs[-1]
-    value = refs[0][:main, :].astype(jnp.float32)
-    for ref in refs[1:-1]:
-        value = value + ref[:main, :].astype(jnp.float32)
-    out[:main, :] = value.astype(out.dtype)
+    ins, out = refs[:-1], refs[-1]
+    values = [ref[:main, :].astype(jnp.float32) for ref in ins if ref.shape[0] > 1]
+    out[:main, :] = sum(values[1:], values[0]).astype(out.dtype)
     if main < out.shape[0]:
-        extra = read_extra(refs[0], main)
-        for ref in refs[1:-1]:
-            extra = extra + read_extra(ref, main)
-        write_extra(out, main, extra)
-
-
-def pick_kernel(place, mine, got, out):
-    @pl.when(place[2] == 1)
+        extras = [ref[...] for ref in ins if ref.shape[0] == 1]
+        extras += [read_extra(ref, main) for ref in ins if ref.shape[0] > main]
+        write_extra(out, main, sum(extras[1:], extras[0]))
+
+
+def pick_kernel(mine, got, out):
+    z_place = lax.axis_index("row") % 4
+    middle = jnp.logical_or(z_place == 1, z_place == 2)
+
+    @pl.when(middle)
     def _():
         out[...] = mine[...]
 
-    @pl.when(place[2] == 0)
+    @pl.when(jnp.logical_not(middle))
     def _():
         out[...] = got[...]
 
 
-def loss_terms(total, feat, stats):
-    spread = jnp.sqrt(stats[0:2, :] / (total - 1) + eps_var)
-    norms = stats[2:4, :] / (total - 1)
-    return (
-        inv_weight * stats[4:5, :] / (total * feat)
-        + var_weight * jnp.sum(jnp.maximum(1.0 - spread, 0.0), axis=0, keepdims=True) / feat
-        - cov_weight * jnp.sum(norms * norms, axis=0, keepdims=True) / feat
-    )
-
-
-def far_kernel(x_count, total, feat, place, own, partner, *rest):
+def stats_kernel(total, feat, stats, sums, first, second, stats_out, terms):
+    width = first.shape[1]
+    found = []
+    squares = []
+    for index, view in enumerate((first, second)):
+        centred = view[...].astype(jnp.float32) - sums[index : index + 1, :] / total
+        wide = centred.astype(jnp.bfloat16).astype(jnp.float32)
+        found.append(jnp.sum(centred * centred, axis=0, keepdims=True))
+        squares.append(jnp.sum(wide * wide, axis=0, keepdims=True))
+    differ = first[...].astype(jnp.float32) - second[...].astype(jnp.float32)
+    found += squares + [jnp.sum(differ * differ, axis=0, keepdims=True)]
+    found = [value + stats[at : at + 1, :] for at, value in enumerate(found)]
+    ids = lax.broadcasted_iota(jnp.int32, stats.shape, 0)
+    block = jnp.zeros(stats.shape, jnp.float32)
+    for index, value in enumerate(found):
+        block = jnp.where(ids == index, value, block)
+    stats_out[...] = block
+    value = inv_weight * found[4] / (total * feat)
+    for index in range(2):
+        spread = jnp.sqrt(found[index] / (total - 1) + eps_var)
+        norms = found[index + 2] / (total - 1)
+        value = value + var_weight * jnp.maximum(1.0 - spread, 0.0) / feat
+        value = value - cov_weight * norms * norms / feat
+    if terms.shape[1] > width:
+        value = jnp.concatenate(
+            [value, jnp.zeros((1, terms.shape[1] - width), jnp.float32)], axis=1
+        )
+    terms[...] = value
+
+
+def far_kernel(x_count, own, partner, *rest):
     others, swapped, outs = rest[:4], rest[4:8], rest[8:]
-    stats = None
-    if len(outs) > 2 * x_count:
-        stats, outs = outs[0], outs[1:]
-    core, x_place = place[0], place[1]
+    core, x_place = whereabouts()
     half = own.shape[0] // 2
     size = half // 2
     tile = half // x_count
@@ -226,21 +276,13 @@
                 at = 2 * block + side
                 value = dot_t(left, others[at][...]) + dot_t(left_partner, swapped[at][...])
                 out[:tile, side * size : (side + 1) * size] = value.astype(out.dtype)
-            if out.shape[0] > tile:
-                terms = loss_terms(total, feat, stats)
-                terms = jnp.where(part == 0, terms, 0.0)
-                if terms.shape[1] < half:
-                    terms = jnp.concatenate(
-                        [terms, jnp.zeros((1, half - terms.shape[1]), jnp.float32)], axis=1
-                    )
-                write_extra(out, tile, terms)
 
 
 def near_product_kernel(
-    x_count, index, total, feat, place, rounded, first, second, sums, stats, *rest
+    x_count, index, total, feat, rounded, first, second, sums, stats, *rest
 ):
     parts, (base, squares, grid, columns) = rest[:-4], rest[-4:]
-    core, x_place = place[0], place[1]
+    core, x_place = whereabouts()
     rows, width = rounded.shape
     half = rows // 2
     tile = rows // 4 // x_count
@@ -285,10 +327,10 @@
     squares[...] = square_sum
 
 
-def far_product_kernel(x_count, total, feat, place, base, *rest):
+def far_product_kernel(x_count, total, feat, base, *rest):
     others, parts = rest[:2], rest[2 : 2 + 2 * x_count]
     grad, *sums = rest[2 + 2 * x_count :]
-    core, x_place = place[0], place[1]
+    core, x_place = whereabouts()
     size = others[0].shape[0]
     half = 2 * size
     tile = half // x_count
@@ -339,16 +381,11 @@
     feat = width * row_count * col_count
     half = rows // 2
     x_count = col_count // 2
-    core = lax.axis_index("col") % 2
-    x_place = lax.axis_index("col") // 2
-    z_place = lax.axis_index("row")
     inner = 4 if row_count % 4 == 0 else 1
-    middle = jnp.logical_or(z_place % 4 == 1, z_place % 4 == 2)
-    place = jnp.stack([core, x_place, middle.astype(core.dtype)]).astype(jnp.int32)
     f32, bf16 = jnp.float32, jnp.bfloat16
     run = Chain()
 
-    (sums,) = run(sums_kernel, [array((2, width), f32)], [first_view, second_view])
+    sums = column_sums(first_view, second_view)
     sums_other = partner_of(sums, "dp", 1)
     first_sent, second_sent, sums_other = lax.optimization_barrier(
         (first_view, second_view, sums_other)
@@ -362,7 +399,7 @@
         [first_view, second_view, sums],
     )
     swapped = [core_swap(piece) for piece in rounded]
-    stats = stats + partner_of(stats, "dp", 1)
+    stats_all = []
 
     def send_row(value, pairs):
         groups = range(0, row_count, inner)
@@ -370,9 +407,13 @@
 
     class Piece:
         def __init__(self, main, keep, sends):
-            self.main, self.keep = main, keep
+            self.main, self.keep, self.row = main, keep, []
             self.like = array(keep.shape, bf16)
             self.got = [shift(sent, "col", x_count, i + 1, 2) for i, sent in enumerate(sends)]
+
+        def extra(self, row):
+            self.row = row
+            self.like = array((self.main + 16, half), bf16)
 
         def add(self, values):
             (value,) = run(functools.partial(add_kernel, self.main), [self.like], values)
@@ -380,11 +421,11 @@
 
         def over_x(self):
             if inner == 4:
-                value = self.add([self.keep] + self.got)
+                value = self.add([self.keep] + self.got + self.row)
                 self.got.append(send_row(value, [(0, 1), (3, 2)]))
 
         def inward(self):
-            self.value = self.add([self.keep] + self.got)
+            self.value = self.add([self.keep] + self.got + self.row)
             if inner == 4:
                 self.got = send_row(self.value, [(1, 2), (2, 1)])
 
@@ -400,11 +441,17 @@
 
         def outward(self):
             if inner == 4:
-                (self.value,) = run(pick_kernel, [self.like], [place, self.value, self.got])
+                (self.value,) = run(pick_kernel, [self.like], [self.value, self.got])
             parts = [self.value]
             for step in range(1, x_count):
                 parts.append(shift(self.value, "col", x_count, step, 2))
             self.parts = parts + [core_swap(part) for part in parts]
+
+        def swap_after(self, value):
+            parts = self.parts[:x_count]
+            *late, value = lax.optimization_barrier((*parts[1:], value))
+            self.parts = self.parts[: x_count + 1] + [core_swap(part) for part in late]
+            return value
 
     main = 3 * (rows // 4) // x_count
     tile = half // x_count
@@ -418,7 +465,7 @@
         own, partner, *outs = run(
             functools.partial(near_kernel, x_count),
             [array((rows, width), bf16)] * 2 + piece_outs(main + 16),
-            [place] + rounded[at] + swapped[at],
+            rounded[at] + swapped[at],
         )
         wholes[index] = [own, partner]
         pieces[index] = Piece(main, outs[0], outs[1:])
@@ -430,23 +477,28 @@
 
     def far_gram(index):
         outs = run(
-            functools.partial(far_kernel, x_count, total, feat),
-            piece_outs(tile + 16 * index) + piece_outs(tile),
-            [place]
-            + wholes[index]
-            + found[index]
-            + [core_swap(other) for other in found[index]]
-            + [stats] * index,
+            functools.partial(far_kernel, x_count),
+            piece_outs(tile) * 2,
+            wholes[index] + found[index] + [core_swap(other) for other in found[index]],
         )
         for block in range(2):
             keep, *sends = outs[block * x_count : (block + 1) * x_count]
             pieces[2 + 2 * index + block] = Piece(tile, keep, sends)
+
+    def other_stats(index):
+        outs = run(
+            functools.partial(stats_kernel, total, feat),
+            [array((8, width), f32), array((1, half), f32)],
+            [stats, sums] + others,
+        )
+        stats_all.append(outs[0])
+        pieces[index].extra([outs[1]])
 
     def near_product(index):
         base[index], value = run(
             functools.partial(near_product_kernel, x_count, index, total, feat),
             [array((rows, width), f32), array((1, half), f32)],
-            [place, wholes[index][0], first_view, second_view, sums, stats]
+            [wholes[index][0], first_view, second_view, sums, stats_all[0]]
             + pieces[index].parts,
             scratch=[pltpu.VMEM((rows, rows), bf16), pltpu.VMEM((rows, 8), f32)],
             extra=2 * rows * rows + 512 * rows,
@@ -461,14 +513,15 @@
         base[view], *value = run(
             functools.partial(far_product_kernel, x_count, total, feat),
             outs,
-            [place, base[view]] + found[view][2 * block : 2 * block + 2] + pieces[index].parts,
+            [base[view]] + found[view][2 * block : 2 * block + 2] + pieces[index].parts,
         )
         squares.extend(value[:1])
-        if index == 4:
-            found["terms"] = value[1]
+
+    def last_swap(index):
+        base[1] = pieces[index].swap_after(base[1])
 
     def last_squares(index):
-        plane, _ = run(
+        plane, found["terms"] = run(
             functools.partial(squares_kernel, tile, total, len(squares)),
             [array((1, half), f32)] * 2,
             squares + pieces[index].parts,
@@ -486,6 +539,8 @@
         "p": near_product,
         "q": far_product,
         "s": last_squares,
+        "t": other_stats,
+        "e": last_swap,
     }
     for step in ORDER:
         steps[step[0]](int(step[1]))

time: 152 us -> 149 us (0.980)
  Pallas kernels: 35.7 us -> 28.5 us
  waiting for transfers between devices: 46 us -> 51 us
    pallas_call x39, Pallas kernels: 35.7 us -> 27.1 us  [__call__(): pl.pallas_call(body, out_shape=outs, in_specs=specs, out_specs=[VMEM] * l...]
    ppermute x12, waiting for transfers between devices: 20.9 us -> 23.8 us  [shift(): return lax.ppermute(value, axis, pairs)]
    ppermute x18, waiting for transfers between devices: 17.4 us -> 19 us  [send_row(): lax.ppermute(value, 'row', [(g + a, g + b) for g in groups for a, b in pa...]
    ppermute x33 -> x32, starting transfers between devices: 14 us -> 12.9 us  [partner_of(): lax.ppermute(value, axis, [(index, index ^ bit) for index in range(lax.ax...]
    ppermute x33 -> x32, waiting for transfers between devices: 7.81 us -> 8.19 us  [partner_of(): lax.ppermute(value, axis, [(index, index ^ bit) for index in range(lax.ax...]
  transfers between devices with their start and end apart: 63 -> 62, of which waited for: 21 -> 21; matrix products, arithmetic and copies ran while one was open for 0% -> 0% of each run, Pallas kernels for 22% -> 18%
where the time goes in v4:
time: 149 us; the launch traced here: 148 us
  starting transfers between devices  63.8 us (43%)
  waiting for transfers between devices  51 us (34%)
  Pallas kernels  28.5 us (19%)
  local copies, waits for them, and re-layouts  2.81 us (2%)
    ppermute x18, starting transfers between devices, send_row(): lax.ppermute(value, 'row', [(g + a, g + b) for g in groups for a, b in pa...  37.9 us
    pallas_call x39, Pallas kernels, __call__(): pl.pallas_call(body, out_shape=outs, in_specs=specs, out_specs=[VMEM] * l...  27.1 us
    ppermute x12, waiting for transfers between devices, shift(): return lax.ppermute(value, axis, pairs)  23.8 us
    ppermute x18, waiting for transfers between devices, send_row(): lax.ppermute(value, 'row', [(g + a, g + b) for g in groups for a, b in pa...  19 us
    ppermute x12, starting transfers between devices, shift(): return lax.ppermute(value, axis, pairs)  13 us
    ppermute x32, starting transfers between devices, partner_of(): lax.ppermute(value, axis, [(index, index ^ bit) for index in range(lax.ax...  12.9 us
    ppermute x32, waiting for transfers between devices, partner_of(): lax.ppermute(value, axis, [(index, index ^ bit) for index in range(lax.ax...  8.19 us
  transfers between devices with their start and end apart: 62, of which 21 were waited for; matrix products, arithmetic and copies ran while one was open for 0% of the time, Pallas kernels for 18%

profile of v4, /device:TPU:0, one launch (start us, length us, event | category | flops | bytes accessed | tf_op | source)
XLA Modules:
  0.0 147.9 jit_solution(2147347359889977410)
XLA Ops:
  0.6 1.2 copy-done
  1.9 1.5 shard_map.49
  3.3 3.0 %collective-permute-start = (f32[2,512]{1,0:T(2,128)S(1)}, f32[2,512]{1,0:T(2,128)S(1)}, u32[]{:S(2)}, u32[]{:S(2)}) collective-permute-start(f32[2,512]{1,0:T(2,128)S(1)} %shard_map.49), channel_id=1, source_target_pairs={{0,16},{16,0},{1,17},{17,1},{2,18},{18,2},{3,19},{19,3},{4,20},{20... | collective-permute-start | bytes 12296 | tf_op jit(solution)/shard_map/ppermute | solution.py:65
  6.4 1.6 %collective-permute-done = f32[2,512]{1,0:T(2,128)S(1)} collective-permute-done((f32[2,512]{1,0:T(2,128)S(1)}, f32[2,512]{1,0:T(2,128)S(1)}, u32[]{:S(2)}, u32[]{:S(2)}) %collective-permute-start) | collective-permute-done | bytes 4128 | tf_op jit(solution)/shard_map/ppermute | solution.py:65
  7.9 2.0 %collective-permute-start.10 = (bf16[1024,512]{1,0:T(8,128)(2,1)}, bf16[1024,512]{1,0:T(8,128)(2,1)S(1)}, u32[]{:S(2)}, u32[]{:S(2)}) collective-permute-start(bf16[1024,512]{1,0:T(8,128)(2,1)} %refs_1_.3), channel_id=1, source_target_pairs={{0,16},{16,0},{1,17},{17,1},{2,18},{18,2},{3,19},{19,3},{4,20},{20... | collective-permute-start | bytes 3145736 | tf_op jit(solution)/shard_map/ppermute | solution.py:65
  10.0 2.9 %shard_map.50 = (f32[8,512]{1,0:T(8,128)S(1)}, bf16[256,512]{1,0:T(8,128)(2,1)S(1)}, bf16[256,512]{1,0:T(8,128)(2,1)S(1)}, bf16[256,512]{1,0:T(8,128)(2,1)S(1)},...) custom-call(bf16[1024,512]{1,0:T(8,128)(2,1)} %refs_1_.3, ...), custom_call_target="tpu_custom_call" | custom-call | flops 1 | bytes 1 | tf_op jit(solution)/shard_map/pallas_call | solution.py:39
  13.9 0.5 collective-permute-done.1.refs_4_
  15.7 2.3 %shard_map.51 = (bf16[1024,512]{1,0:T(8,128)(2,1)S(1)}, bf16[1024,512]{1,0:T(8,128)(2,1)S(1)}, f32[400,512]{1,0:T(8,128)S(1)}, bf16[400,512]{1,0:T(8,128)(2,1)S(1)}) custom-call(f32[8,512]{1,0:T(8,128)S(1)} %get-tuple-element.56._.refs_0_, bf16[256,512]{1,0:T(8,128)(2,1)S(1)} %get-tuple-element.57.refs_0_, bf16[256,512]{1,0:T(8,128)(2,1)S(1)} %get-tuple-element.58.refs_1_, ...), custom_call_target="tpu_custom_call" | custom-call | flops 1 | bytes 1 | tf_op jit(solution)/shard_map/pallas_call | solution.py:39
  18.0 1.6 %collective-permute-start.9 = (bf16[400,512]{1,0:T(8,128)(2,1)S(1)}, bf16[400,512]{1,0:T(8,128)(2,1)S(1)}, u32[]{:S(2)}, u32[]{:S(2)}) collective-permute-start(bf16[400,512]{1,0:T(8,128)(2,1)S(1)} %get-tuple-element.68), channel_id=1, source_target_pairs={{0,2},{1,3},{2,0},{3,1},{4,6},{5,7},{6,4},{7,5},{8,10},{9,11},{10,... | collective-permute-start | bytes 1228808 | tf_op jit(solution)/shard_map/ppermute | solution.py:61
  19.6 0.5 collective-permute-start.20
  20.1 2.3 %shard_map.52 = (bf16[1024,512]{1,0:T(8,128)(2,1)S(1)}, bf16[1024,512]{1,0:T(8,128)(2,1)S(1)}, f32[400,512]{1,0:T(8,128)S(1)}, bf16[400,512]{1,0:T(8,128)(2,1)S(1)}) custom-call(bf16[1024,512]{1,0:T(8,128)(2,1)S(1)} %get-tuple-element.61._.refs_0_, bf16[256,512]{1,0:T(8,128)(2,1)S(1)} %get-tuple-element.62.refs_0_, ...), custom_call_target="tpu_custom_call" | custom-call | flops 1 | bytes 1 | tf_op jit(solution)/shard_map/pallas_call | solution.py:39
  22.6 7.8 %collective-permute-done.9.refs_1_ = bf16[400,512]{1,0:T(8,128)(2,1)S(1)} collective-permute-done((bf16[400,512]{1,0:T(8,128)(2,1)S(1)}, bf16[400,512]{1,0:T(8,128)(2,1)S(1)}, u32[]{:S(2)}, u32[]{:S(2)}) %collective-permute-start.9) | collective-permute-done | bytes 409632 | tf_op jit(solution)/shard_map/ppermute | solution.py:61
  30.5 3.7 %collective-permute-done.10.refs_0_.refs_2_ = bf16[1024,512]{1,0:T(8,128)(2,1)S(1)} collective-permute-done((bf16[1024,512]{1,0:T(8,128)(2,1)}, bf16[1024,512]{1,0:T(8,128)(2,1)S(1)}, u32[]{:S(2)}, u32[]{:S(2)}) %collective-permute-start.10) | collective-permute-done | bytes 1048608 | tf_op jit(solution)/shard_map/ppermute | solution.py:65
  35.0 4.0 %collective-permute-start.16 = (bf16[400,512]{1,0:T(8,128)(2,1)S(1)}, bf16[400,512]{1,0:T(8,128)(2,1)S(1)}, u32[]{:S(2)}, u32[]{:S(2)}) collective-permute-start(bf16[400,512]{1,0:T(8,128)(2,1)S(1)} %shard_map.53._), channel_id=1, source_target_pairs={{0,4},{12,8},{1,5},{13,9},{2,6},{14,10},{3,7},{15,11},{16,20},{28,... | collective-permute-start | bytes 1228808 | tf_op jit(solution)/shard_map/ppermute | solution.py:406
  39.7 3.0 %collective-permute-start.19 = (bf16[400,512]{1,0:T(8,128)(2,1)S(1)}, bf16[400,512]{1,0:T(8,128)(2,1)S(1)}, u32[]{:S(2)}, u32[]{:S(2)}) collective-permute-start(bf16[400,512]{1,0:T(8,128)(2,1)S(1)} %shard_map.55._), channel_id=1, source_target_pairs={{0,4},{12,8},{1,5},{13,9},{2,6},{14,10},{3,7},{15,11},{16,20},{28,... | collective-permute-start | bytes 1228808 | tf_op jit(solution)/shard_map/ppermute | solution.py:406
  42.8 1.3 shard_map.56
  44.0 1.6 %collective-permute-start.17 = (bf16[256,512]{1,0:T(8,128)(2,1)S(1)}, bf16[256,512]{1,0:T(8,128)(2,1)S(1)}, u32[]{:S(2)}, u32[]{:S(2)}) collective-permute-start(bf16[256,512]{1,0:T(8,128)(2,1)S(1)} %get-tuple-element.78), channel_id=1, source_target_pairs={{0,2},{1,3},{2,0},{3,1},{4,6},{5,7},{6,4},{7,5},{8,10},{9,11},{10,... | collective-permute-start | bytes 786440 | tf_op jit(solution)/shard_map/ppermute | solution.py:61
  45.6 0.5 collective-permute-start.18
  46.1 2.7 %collective-permute-done.16.refs_2_ = bf16[400,512]{1,0:T(8,128)(2,1)S(1)} collective-permute-done((bf16[400,512]{1,0:T(8,128)(2,1)S(1)}, bf16[400,512]{1,0:T(8,128)(2,1)S(1)}, u32[]{:S(2)}, u32[]{:S(2)}) %collective-permute-start.16) | collective-permute-done | bytes 409632 | tf_op jit(solution)/shard_map/ppermute | solution.py:406
  49.0 0.7 collective-permute-start.21
  49.7 3.6 %collective-permute-done.17.refs_1_ = bf16[256,512]{1,0:T(8,128)(2,1)S(1)} collective-permute-done((bf16[256,512]{1,0:T(8,128)(2,1)S(1)}, bf16[256,512]{1,0:T(8,128)(2,1)S(1)}, u32[]{:S(2)}, u32[]{:S(2)}) %collective-permute-start.17) | collective-permute-done | bytes 262176 | tf_op jit(solution)/shard_map/ppermute | solution.py:61
  53.4 3.6 %collective-permute-start.22 = (bf16[256,512]{1,0:T(8,128)(2,1)S(1)}, bf16[256,512]{1,0:T(8,128)(2,1)S(1)}, u32[]{:S(2)}, u32[]{:S(2)}) collective-permute-start(bf16[256,512]{1,0:T(8,128)(2,1)S(1)} %shard_map.58._), channel_id=1, source_target_pairs={{0,4},{12,8},{1,5},{13,9},{2,6},{14,10},{3,7},{15,11},{16,20},{28,... | collective-permute-start | bytes 786440 | tf_op jit(solution)/shard_map/ppermute | solution.py:406
  57.0 0.7 collective-permute-done.18.refs_1_
  58.6 0.7 collective-permute-start.28
  59.4 1.3 collective-permute-start.29
  60.7 1.6 %collective-permute-done.22.refs_2_ = bf16[256,512]{1,0:T(8,128)(2,1)S(1)} collective-permute-done((bf16[256,512]{1,0:T(8,128)(2,1)S(1)}, bf16[256,512]{1,0:T(8,128)(2,1)S(1)}, u32[]{:S(2)}, u32[]{:S(2)}) %collective-permute-start.22) | collective-permute-done | bytes 262176 | tf_op jit(solution)/shard_map/ppermute | solution.py:406
  62.8 5.5 %collective-permute-start.27 = (bf16[256,512]{1,0:T(8,128)(2,1)S(1)}, bf16[256,512]{1,0:T(8,128)(2,1)S(1)}, u32[]{:S(2)}, u32[]{:S(2)}) collective-permute-start(bf16[256,512]{1,0:T(8,128)(2,1)S(1)} %shard_map.59._), channel_id=1, source_target_pairs={{0,4},{12,8},{1,5},{13,9},{2,6},{14,10},{3,7},{15,11},{16,20},{28,... | collective-permute-start | bytes 786440 | tf_op jit(solution)/shard_map/ppermute | solution.py:406
  68.5 0.9 collective-permute-start.30
  69.4 1.3 shard_map.64
  70.7 1.6 %collective-permute-start.31 = (bf16[256,512]{1,0:T(8,128)(2,1)S(1)}, bf16[256,512]{1,0:T(8,128)(2,1)S(1)}, u32[]{:S(2)}, u32[]{:S(2)}) collective-permute-start(bf16[256,512]{1,0:T(8,128)(2,1)S(1)} %get-tuple-element.89), channel_id=1, source_target_pairs={{0,2},{1,3},{2,0},{3,1},{4,6},{5,7},{6,4},{7,5},{8,10},{9,11},{10,... | collective-permute-start | bytes 786440 | tf_op jit(solution)/shard_map/ppermute | solution.py:61
  72.2 1.7 %shard_map.65 = (f32[8,512]{1,0:T(8,128)S(1)}, f32[1,512]{1,0:T(1,128)S(1)}) custom-call(f32[256,512]{1,0:T(8,128)S(1)} %get-tuple-element.87._.refs_0_, f32[8,512]{1,0:T(8,128)S(1)} %get-tuple-element.56._.refs_0_, f32[2,512]{1,0:T(2,128)S(1)} %add.9.sums.refs_1_.refs_3_, bf16[1024,512]{1,0:T(8,128)(2,1)S(1)} %collective-permute-done.10.refs_0_.refs_2_, ...), custom_call_target="tpu_custom_call" | custom-call | flops 1 | bytes 1 | tf_op jit(solution)/shard_map/pallas_call | solution.py:39
  74.4 1.3 collective-permute-start.34
  75.7 0.7 collective-permute-start.32
  76.4 1.6 %collective-permute-start.33 = (bf16[256,512]{1,0:T(8,128)(2,1)S(1)}, bf16[256,512]{1,0:T(8,128)(2,1)S(1)}, u32[]{:S(2)}, u32[]{:S(2)}) collective-permute-start(bf16[256,512]{1,0:T(8,128)(2,1)S(1)} %get-tuple-element.91), channel_id=1, source_target_pairs={{0,2},{1,3},{2,0},{3,1},{4,6},{5,7},{6,4},{7,5},{8,10},{9,11},{10,... | collective-permute-start | bytes 786440 | tf_op jit(solution)/shard_map/ppermute | solution.py:61
  78.1 1.1 collective-permute-done.31.refs_1_
  79.2 5.2 %collective-permute-start.35 = (bf16[256,512]{1,0:T(8,128)(2,1)S(1)}, bf16[256,512]{1,0:T(8,128)(2,1)S(1)}, u32[]{:S(2)}, u32[]{:S(2)}) collective-permute-start(bf16[256,512]{1,0:T(8,128)(2,1)S(1)} %shard_map.70._), channel_id=1, source_target_pairs={{0,4},{12,8},{1,5},{13,9},{2,6},{14,10},{3,7},{15,11},{16,20},{28,... | collective-permute-start | bytes 786440 | tf_op jit(solution)/shard_map/ppermute | solution.py:406
  84.4 1.3 collective-permute-start.36
  85.9 4.6 %collective-permute-start.37 = (bf16[272,512]{1,0:T(8,128)(2,1)S(1)}, bf16[272,512]{1,0:T(8,128)(2,1)S(1)}, u32[]{:S(2)}, u32[]{:S(2)}) collective-permute-start(bf16[272,512]{1,0:T(8,128)(2,1)S(1)} %shard_map.72._), channel_id=1, source_target_pairs={{0,4},{12,8},{1,5},{13,9},{2,6},{14,10},{3,7},{15,11},{16,20},{28,... | collective-permute-start | bytes 835592 | tf_op jit(solution)/shard_map/ppermute | solution.py:406
  90.5 0.9 collective-permute-start.42
  91.4 1.2 collective-permute-start.45
  92.7 1.3 collective-permute-start.39
  94.6 0.7 collective-permute-start.38
  95.5 5.4 %collective-permute-done.39.refs_1_ = bf16[256,512]{1,0:T(8,128)(2,1)S(1)} collective-permute-done((bf16[256,512]{1,0:T(8,128)(2,1)S(1)}, bf16[256,512]{1,0:T(8,128)(2,1)S(1)}, u32[]{:S(2)}, u32[]{:S(2)}) %collective-permute-start.39) | collective-permute-done | bytes 262176 | tf_op jit(solution)/shard_map/ppermute | solution.py:406
  100.9 0.7 collective-permute-start.40
  101.6 1.3 collective-permute-done.42.refs_6_
  103.4 4.9 %collective-permute-done.45.refs_6_ = bf16[400,512]{1,0:T(8,128)(2,1)S(1)} collective-permute-done((bf16[400,512]{1,0:T(8,128)(2,1)S(1)}, bf16[400,512]{1,0:T(8,128)(2,1)S(1)}, u32[]{:S(2)}, u32[]{:S(2)}) %collective-permute-start.45) | collective-permute-done | bytes 409632 | tf_op jit(solution)/shard_map/ppermute | solution.py:61
  108.4 1.3 collective-permute-start.41
  109.7 0.9 collective-permute-start.49
  110.8 8.3 %collective-permute-done.41.refs_1_ = bf16[256,512]{1,0:T(8,128)(2,1)S(1)} collective-permute-done((bf16[256,512]{1,0:T(8,128)(2,1)S(1)}, bf16[256,512]{1,0:T(8,128)(2,1)S(1)}, u32[]{:S(2)}, u32[]{:S(2)}) %collective-permute-start.41) | collective-permute-done | bytes 262176 | tf_op jit(solution)/shard_map/ppermute | solution.py:406
  119.0 1.3 collective-permute-start.48
  120.5 0.9 collective-permute-start.52
  121.6 1.2 collective-permute-start.55
  122.7 3.1 %shard_map.81 = (f32[1024,512]{1,0:T(8,128)S(1)}, f32[1,512]{1,0:T(1,128)S(1)}) custom-call(bf16[256,512]{1,0:T(8,128)(2,1)S(1)} %shard_map.80._.refs_3_, bf16[1024,512]{1,0:T(8,128)(2,1)S(1)} %get-tuple-element.61._.refs_0_, bf16[1024,512]{1,0:T(8,128)(2,1)} %refs_1_.3, bf16[1024,512]{1,0:T(8,128)(2,1)S(1)} %copy-done.1, ...), custom_call_target="tpu_custom_call" | custom-call | flops 1 | bytes 1 | tf_op jit(solution)/shard_map/pallas_call | solution.py:39
  125.9 3.1 %shard_map.82 = (f32[1024,512]{1,0:T(8,128)S(1)}, f32[1,512]{1,0:T(1,128)S(1)}) custom-call(f32[1024,512]{1,0:T(8,128)S(1)} %get-tuple-element.93._.refs_0_, bf16[1024,512]{1,0:T(8,128)(2,1)S(1)} %get-tuple-element.66._.refs_0_, bf16[1024,512]{1,0:T(8,128)(2,1)} %refs_1_.3, bf16[1024,512]{1,0:T(8,128)(2,1)S(1)} %copy-done.1, ...), custom_call_target="tpu_custom_call" | custom-call | flops 1 | bytes 1 | tf_op jit(solution)/shard_map/pallas_call | solution.py:39
  129.5 0.9 collective-permute-start.58
  131.0 4.3 %collective-permute-done.55.refs_4_ = bf16[256,512]{1,0:T(8,128)(2,1)S(1)} collective-permute-done((bf16[256,512]{1,0:T(8,128)(2,1)S(1)}, bf16[256,512]{1,0:T(8,128)(2,1)S(1)}, u32[]{:S(2)}, u32[]{:S(2)}) %collective-permute-start.55) | collective-permute-done | bytes 262176 | tf_op jit(solution)/shard_map/ppermute | solution.py:61
  135.3 1.3 shard_map.84
  137.1 2.1 %shard_map.85 = (f32[1024,512]{1,0:T(8,128)}, f32[1,512]{1,0:T(1,128)S(1)}, f32[1,512]{1,0:T(1,128)}) custom-call(f32[1024,512]{1,0:T(8,128)S(1)} %get-tuple-element.95._.refs_0_, f32[1024,512]{1,0:T(8,128)S(1)} %get-tuple-element.95._.refs_0_, bf16[256,512]{1,0:T(8,128)(2,1)S(1)} %get-tuple-element.75.refs_4_.refs_1_, ...), custom_call_target="tpu_custom_call" | custom-call | flops 1 | bytes 1 | tf_op jit(solution)/shard_map/pallas_call | solution.py:39
  139.2 1.6 %copy-done.2 = f32[1024,512]{1,0:T(8,128)S(1)} copy-done((f32[1024,512]{1,0:T(8,128)S(1)}, f32[1024,512]{1,0:T(8,128)}, u32[]{:S(2)}) %copy-start.2) | copy-done | bytes 2097176
  140.7 1.3 shard_map.86
  142.0 1.5 %collective-permute-done.60.refs_8_.refs_6_ = bf16[272,512]{1,0:T(8,128)(2,1)S(1)} collective-permute-done((bf16[272,512]{1,0:T(8,128)(2,1)S(1)}, bf16[272,512]{1,0:T(8,128)(2,1)S(1)}, u32[]{:S(2)}, u32[]{:S(2)}) %collective-permute-start.60) | collective-permute-done | bytes 278560 | tf_op jit(solution)/shard_map/ppermute | solution.py:65
  143.7 1.6 %collective-permute-start.61 = (f32[1,512]{1,0:T(1,128)S(1)}, f32[1,512]{1,0:T(1,128)S(1)}, u32[]{:S(2)}, u32[]{:S(2)}) collective-permute-start(f32[1,512]{1,0:T(1,128)S(1)} %get-tuple-element.105._), channel_id=1, source_target_pairs={{0,16},{16,0},{1,17},{17,1},{2,18},{18,2},{3,19},{19,3},{4,20},{20... | collective-permute-start | bytes 6152 | tf_op jit(solution)/shard_map/ppermute | solution.py:65
  145.3 2.0 %shard_map.88 = f32[1024,512]{1,0:T(8,128)} custom-call(f32[1,512]{1,0:T(1,128)S(1)} %get-tuple-element.105._, f32[1024,512]{1,0:T(8,128)S(1)} %get-tuple-element.106._.refs_0_, bf16[256,512]{1,0:T(8,128)(2,1)S(1)} %get-tuple-element.85.refs_4_.refs_1_, bf16[256,512]{1,0:T(8,128)(2,1)S(1)} %get-tuple-element.86.refs_5_.refs_2_, ...), custom_call_target="tpu_custom_call" | custom-call | flops 1 | bytes 1 | tf_op jit(solution)/shard_map/pallas_call | solution.py:39
  147.3 0.6 add_reduce_fusion
  (108 shorter events, 10.2 us)
Async XLA Ops:
  1.9 8.1 %copy-start.1 = (bf16[1024,512]{1,0:T(8,128)(2,1)S(1)}, bf16[1024,512]{1,0:T(8,128)(2,1)}, u32[]{:S(2)}) copy-start(bf16[1024,512]{1,0:T(8,128)(2,1)} %refs_2_.3) | copy-start | bytes 3145732
  3.3 4.6 %collective-permute-start = (f32[2,512]{1,0:T(2,128)S(1)}, f32[2,512]{1,0:T(2,128)S(1)}, u32[]{:S(2)}, u32[]{:S(2)}) collective-permute-start(f32[2,512]{1,0:T(2,128)S(1)} %shard_map.49), channel_id=1, source_target_pairs={{0,16},{16,0},{1,17},{17,1},{2,18},{18,2},{3,19},{19,3},{4,20},{20... | collective-permute-start | bytes 12296 | tf_op jit(solution)/shard_map/ppermute | solution.py:65
  7.9 26.3 %collective-permute-start.10 = (bf16[1024,512]{1,0:T(8,128)(2,1)}, bf16[1024,512]{1,0:T(8,128)(2,1)S(1)}, u32[]{:S(2)}, u32[]{:S(2)}) collective-permute-start(bf16[1024,512]{1,0:T(8,128)(2,1)} %refs_1_.3), channel_id=1, source_target_pairs={{0,16},{16,0},{1,17},{17,1},{2,18},{18,2},{3,19},{19,3},{4,20},{20... | collective-permute-start | bytes 3145736 | tf_op jit(solution)/shard_map/ppermute | solution.py:65
  12.9 1.6 %collective-permute-start.1 = (bf16[256,512]{1,0:T(8,128)(2,1)S(1)}, bf16[256,512]{1,0:T(8,128)(2,1)S(1)}, u32[]{:S(2)}, u32[]{:S(2)}) collective-permute-start(bf16[256,512]{1,0:T(8,128)(2,1)S(1)} %get-tuple-element.57.refs_0_), channel_id=1, source_target_pairs={{0,1},{1,0},{2,3},{3,2},{4,5},{5,4},{6,7},{7,6},{8,9},{9,8},{10,11... | collective-permute-start | bytes 786440 | tf_op jit(solution)/shard_map/ppermute | solution.py:65
  12.9 1.9 %collective-permute-start.2 = (bf16[256,512]{1,0:T(8,128)(2,1)S(1)}, bf16[256,512]{1,0:T(8,128)(2,1)S(1)}, u32[]{:S(2)}, u32[]{:S(2)}) collective-permute-start(bf16[256,512]{1,0:T(8,128)(2,1)S(1)} %get-tuple-element.58.refs_1_), channel_id=1, source_target_pairs={{0,1},{1,0},{2,3},{3,2},{4,5},{5,4},{6,7},{7,6},{8,9},{9,8},{10,11... | collective-permute-start | bytes 786440 | tf_op jit(solution)/shard_map/ppermute | solution.py:65
  13.4 1.8 %collective-permute-start.3 = (bf16[256,512]{1,0:T(8,128)(2,1)S(1)}, bf16[256,512]{1,0:T(8,128)(2,1)S(1)}, u32[]{:S(2)}, u32[]{:S(2)}) collective-permute-start(bf16[256,512]{1,0:T(8,128)(2,1)S(1)} %get-tuple-element.59.refs_2_), channel_id=1, source_target_pairs={{0,1},{1,0},{2,3},{3,2},{4,5},{5,4},{6,7},{7,6},{8,9},{9,8},{10,11... | collective-permute-start | bytes 786440 | tf_op jit(solution)/shard_map/ppermute | solution.py:65
  13.5 2.1 %collective-permute-start.4 = (bf16[256,512]{1,0:T(8,128)(2,1)S(1)}, bf16[256,512]{1,0:T(8,128)(2,1)S(1)}, u32[]{:S(2)}, u32[]{:S(2)}) collective-permute-start(bf16[256,512]{1,0:T(8,128)(2,1)S(1)} %get-tuple-element.60.refs_3_), channel_id=1, source_target_pairs={{0,1},{1,0},{2,3},{3,2},{4,5},{5,4},{6,7},{7,6},{8,9},{9,8},{10,11... | collective-permute-start | bytes 786440 | tf_op jit(solution)/shard_map/ppermute | solution.py:65
  14.5 3.6 %collective-permute-start.5 = (bf16[256,512]{1,0:T(8,128)(2,1)S(1)}, bf16[256,512]{1,0:T(8,128)(2,1)S(1)}, u32[]{:S(2)}, u32[]{:S(2)}) collective-permute-start(bf16[256,512]{1,0:T(8,128)(2,1)S(1)} %get-tuple-element.62.refs_0_), channel_id=1, source_target_pairs={{0,1},{1,0},{2,3},{3,2},{4,5},{5,4},{6,7},{7,6},{8,9},{9,8},{10,11... | collective-permute-start | bytes 786440 | tf_op jit(solution)/shard_map/ppermute | solution.py:65
  14.8 4.8 %collective-permute-start.6 = (bf16[256,512]{1,0:T(8,128)(2,1)S(1)}, bf16[256,512]{1,0:T(8,128)(2,1)S(1)}, u32[]{:S(2)}, u32[]{:S(2)}) collective-permute-start(bf16[256,512]{1,0:T(8,128)(2,1)S(1)} %get-tuple-element.63.refs_1_), channel_id=1, source_target_pairs={{0,1},{1,0},{2,3},{3,2},{4,5},{5,4},{6,7},{7,6},{8,9},{9,8},{10,11... | collective-permute-start | bytes 786440 | tf_op jit(solution)/shard_map/ppermute | solution.py:65
  15.2 4.9 %collective-permute-start.7 = (bf16[256,512]{1,0:T(8,128)(2,1)S(1)}, bf16[256,512]{1,0:T(8,128)(2,1)S(1)}, u32[]{:S(2)}, u32[]{:S(2)}) collective-permute-start(bf16[256,512]{1,0:T(8,128)(2,1)S(1)} %get-tuple-element.64.refs_2_), channel_id=1, source_target_pairs={{0,1},{1,0},{2,3},{3,2},{4,5},{5,4},{6,7},{7,6},{8,9},{9,8},{10,11... | collective-permute-start | bytes 786440 | tf_op jit(solution)/shard_map/ppermute | solution.py:65
  15.6 4.5 %collective-permute-start.8 = (bf16[256,512]{1,0:T(8,128)(2,1)S(1)}, bf16[256,512]{1,0:T(8,128)(2,1)S(1)}, u32[]{:S(2)}, u32[]{:S(2)}) collective-permute-start(bf16[256,512]{1,0:T(8,128)(2,1)S(1)} %get-tuple-element.65.refs_3_), channel_id=1, source_target_pairs={{0,1},{1,0},{2,3},{3,2},{4,5},{5,4},{6,7},{7,6},{8,9},{9,8},{10,11... | collective-permute-start | bytes 786440 | tf_op jit(solution)/shard_map/ppermute | solution.py:65
  18.0 12.4 %collective-permute-start.9 = (bf16[400,512]{1,0:T(8,128)(2,1)S(1)}, bf16[400,512]{1,0:T(8,128)(2,1)S(1)}, u32[]{:S(2)}, u32[]{:S(2)}) collective-permute-start(bf16[400,512]{1,0:T(8,128)(2,1)S(1)} %get-tuple-element.68), channel_id=1, source_target_pairs={{0,2},{1,3},{2,0},{3,1},{4,6},{5,7},{6,4},{7,5},{8,10},{9,11},{10,... | collective-permute-start | bytes 1228808 | tf_op jit(solution)/shard_map/ppermute | solution.py:61
  19.6 38.3 %collective-permute-start.20 = (bf16[1024,512]{1,0:T(8,128)(2,1)S(1)}, bf16[1024,512]{1,0:T(8,128)(2,1)S(1)}, u32[]{:S(2)}, u32[]{:S(2)}) collective-permute-start(bf16[1024,512]{1,0:T(8,128)(2,1)S(1)} %copy-done.1), channel_id=1, source_target_pairs={{0,16},{16,0},{1,17},{17,1},{2,18},{18,2},{3,19},{19,3},{4,20},{20... | collective-permute-start | bytes 3145736 | tf_op jit(solution)/shard_map/ppermute | solution.py:65
  22.4 16.6 %collective-permute-start.11 = (bf16[400,512]{1,0:T(8,128)(2,1)S(1)}, bf16[400,512]{1,0:T(8,128)(2,1)S(1)}, u32[]{:S(2)}, u32[]{:S(2)}) collective-permute-start(bf16[400,512]{1,0:T(8,128)(2,1)S(1)} %get-tuple-element.72), channel_id=1, source_target_pairs={{0,2},{1,3},{2,0},{3,1},{4,6},{5,7},{6,4},{7,5},{8,10},{9,11},{10,... | collective-permute-start | bytes 1228808 | tf_op jit(solution)/shard_map/ppermute | solution.py:61
  34.4 4.7 %collective-permute-start.12 = (bf16[256,512]{1,0:T(8,128)(2,1)S(1)}, bf16[256,512]{1,0:T(8,128)(2,1)S(1)}, u32[]{:S(2)}, u32[]{:S(2)}) collective-permute-start(bf16[256,512]{1,0:T(8,128)(2,1)S(1)} %get-tuple-element.70._.refs_2_.refs_1_), channel_id=1, source_target_pairs={{0,1},{1,0},{2,3},{3,2},{4,5},{5,4},{6,7},{7,6},{8,9},{9,8},{10,11... | collective-permute-start | bytes 786440 | tf_op jit(solution)/shard_map/ppermute | solution.py:65
  34.5 5.2 %collective-permute-start.13 = (bf16[256,512]{1,0:T(8,128)(2,1)S(1)}, bf16[256,512]{1,0:T(8,128)(2,1)S(1)}, u32[]{:S(2)}, u32[]{:S(2)}) collective-permute-start(bf16[256,512]{1,0:T(8,128)(2,1)S(1)} %get-tuple-element.74.refs_3_.refs_2_), channel_id=1, source_target_pairs={{0,1},{1,0},{2,3},{3,2},{4,5},{5,4},{6,7},{7,6},{8,9},{9,8},{10,11... | collective-permute-start | bytes 786440 | tf_op jit(solution)/shard_map/ppermute | solution.py:65
  35.0 13.8 %collective-permute-start.16 = (bf16[400,512]{1,0:T(8,128)(2,1)S(1)}, bf16[400,512]{1,0:T(8,128)(2,1)S(1)}, u32[]{:S(2)}, u32[]{:S(2)}) collective-permute-start(bf16[400,512]{1,0:T(8,128)(2,1)S(1)} %shard_map.53._), channel_id=1, source_target_pairs={{0,4},{12,8},{1,5},{13,9},{2,6},{14,10},{3,7},{15,11},{16,20},{28,... | collective-permute-start | bytes 1228808 | tf_op jit(solution)/shard_map/ppermute | solution.py:406
  39.0 3.7 %collective-permute-start.14 = (bf16[256,512]{1,0:T(8,128)(2,1)S(1)}, bf16[256,512]{1,0:T(8,128)(2,1)S(1)}, u32[]{:S(2)}, u32[]{:S(2)}) collective-permute-start(bf16[256,512]{1,0:T(8,128)(2,1)S(1)} %get-tuple-element.75.refs_4_.refs_1_), channel_id=1, source_target_pairs={{0,1},{1,0},{2,3},{3,2},{4,5},{5,4},{6,7},{7,6},{8,9},{9,8},{10,11... | collective-permute-start | bytes 786440 | tf_op jit(solution)/shard_map/ppermute | solution.py:65
  39.1 3.6 %collective-permute-start.15 = (bf16[256,512]{1,0:T(8,128)(2,1)S(1)}, bf16[256,512]{1,0:T(8,128)(2,1)S(1)}, u32[]{:S(2)}, u32[]{:S(2)}) collective-permute-start(bf16[256,512]{1,0:T(8,128)(2,1)S(1)} %get-tuple-element.76.refs_5_.refs_2_), channel_id=1, source_target_pairs={{0,1},{1,0},{2,3},{3,2},{4,5},{5,4},{6,7},{7,6},{8,9},{9,8},{10,11... | collective-permute-start | bytes 786440 | tf_op jit(solution)/shard_map/ppermute | solution.py:65
  39.7 18.0 %collective-permute-start.19 = (bf16[400,512]{1,0:T(8,128)(2,1)S(1)}, bf16[400,512]{1,0:T(8,128)(2,1)S(1)}, u32[]{:S(2)}, u32[]{:S(2)}) collective-permute-start(bf16[400,512]{1,0:T(8,128)(2,1)S(1)} %shard_map.55._), channel_id=1, source_target_pairs={{0,4},{12,8},{1,5},{13,9},{2,6},{14,10},{3,7},{15,11},{16,20},{28,... | collective-permute-start | bytes 1228808 | tf_op jit(solution)/shard_map/ppermute | solution.py:406
  44.0 9.3 %collective-permute-start.17 = (bf16[256,512]{1,0:T(8,128)(2,1)S(1)}, bf16[256,512]{1,0:T(8,128)(2,1)S(1)}, u32[]{:S(2)}, u32[]{:S(2)}) collective-permute-start(bf16[256,512]{1,0:T(8,128)(2,1)S(1)} %get-tuple-element.78), channel_id=1, source_target_pairs={{0,2},{1,3},{2,0},{3,1},{4,6},{5,7},{6,4},{7,5},{8,10},{9,11},{10,... | collective-permute-start | bytes 786440 | tf_op jit(solution)/shard_map/ppermute | solution.py:61
  45.6 12.1 %collective-permute-start.18 = (bf16[256,512]{1,0:T(8,128)(2,1)S(1)}, bf16[256,512]{1,0:T(8,128)(2,1)S(1)}, u32[]{:S(2)}, u32[]{:S(2)}) collective-permute-start(bf16[256,512]{1,0:T(8,128)(2,1)S(1)} %get-tuple-element.80), channel_id=1, source_target_pairs={{0,2},{1,3},{2,0},{3,1},{4,6},{5,7},{6,4},{7,5},{8,10},{9,11},{10,... | collective-permute-start | bytes 786440 | tf_op jit(solution)/shard_map/ppermute | solution.py:61
  49.0 10.3 %collective-permute-start.21 = (bf16[400,512]{1,0:T(8,128)(2,1)S(1)}, bf16[400,512]{1,0:T(8,128)(2,1)S(1)}, u32[]{:S(2)}, u32[]{:S(2)}) collective-permute-start(bf16[400,512]{1,0:T(8,128)(2,1)S(1)} %shard_map.57._.refs_0_), channel_id=1, source_target_pairs={{4,8},{8,4},{5,9},{9,5},{6,10},{10,6},{7,11},{11,7},{20,24},{24,20... | collective-permute-start | bytes 1228808 | tf_op jit(solution)/shard_map/ppermute | solution.py:406
  53.4 8.9 %collective-permute-start.22 = (bf16[256,512]{1,0:T(8,128)(2,1)S(1)}, bf16[256,512]{1,0:T(8,128)(2,1)S(1)}, u32[]{:S(2)}, u32[]{:S(2)}) collective-permute-start(bf16[256,512]{1,0:T(8,128)(2,1)S(1)} %shard_map.58._), channel_id=1, source_target_pairs={{0,4},{12,8},{1,5},{13,9},{2,6},{14,10},{3,7},{15,11},{16,20},{28,... | collective-permute-start | bytes 786440 | tf_op jit(solution)/shard_map/ppermute | solution.py:406
  58.1 4.3 %collective-permute-start.23 = (bf16[256,512]{1,0:T(8,128)(2,1)S(1)}, bf16[256,512]{1,0:T(8,128)(2,1)S(1)}, u32[]{:S(2)}, u32[]{:S(2)}) collective-permute-start(bf16[256,512]{1,0:T(8,128)(2,1)S(1)} %get-tuple-element.82._.refs_2_.refs_1_), channel_id=1, source_target_pairs={{0,1},{1,0},{2,3},{3,2},{4,5},{5,4},{6,7},{7,6},{8,9},{9,8},{10,11... | collective-permute-start | bytes 786440 | tf_op jit(solution)/shard_map/ppermute | solution.py:65
  58.1 4.7 %collective-permute-start.24 = (bf16[256,512]{1,0:T(8,128)(2,1)S(1)}, bf16[256,512]{1,0:T(8,128)(2,1)S(1)}, u32[]{:S(2)}, u32[]{:S(2)}) collective-permute-start(bf16[256,512]{1,0:T(8,128)(2,1)S(1)} %get-tuple-element.84.refs_3_.refs_2_), channel_id=1, source_target_pairs={{0,1},{1,0},{2,3},{3,2},{4,5},{5,4},{6,7},{7,6},{8,9},{9,8},{10,11... | collective-permute-start | bytes 786440 | tf_op jit(solution)/shard_map/ppermute | solution.py:65
  58.6 15.6 %collective-permute-start.28 = (bf16[400,512]{1,0:T(8,128)(2,1)S(1)}, bf16[400,512]{1,0:T(8,128)(2,1)S(1)}, u32[]{:S(2)}, u32[]{:S(2)}) collective-permute-start(bf16[400,512]{1,0:T(8,128)(2,1)S(1)} %shard_map.60._.refs_0_), channel_id=1, source_target_pairs={{4,8},{8,4},{5,9},{9,5},{6,10},{10,6},{7,11},{11,7},{20,24},{24,20... | collective-permute-start | bytes 1228808 | tf_op jit(solution)/shard_map/ppermute | solution.py:406
  59.4 16.9 %collective-permute-start.29 = (bf16[400,512]{1,0:T(8,128)(2,1)S(1)}, bf16[400,512]{1,0:T(8,128)(2,1)S(1)}, u32[]{:S(2)}, u32[]{:S(2)}) collective-permute-start(bf16[400,512]{1,0:T(8,128)(2,1)S(1)} %shard_map.62._.refs_0_), channel_id=1, source_target_pairs={{4,0},{8,12},{5,1},{9,13},{6,2},{10,14},{7,3},{11,15},{20,16},{24,... | collective-permute-start | bytes 1228808 | tf_op jit(solution)/shard_map/ppermute | solution.py:406
  62.3 6.2 %collective-permute-start.25 = (bf16[256,512]{1,0:T(8,128)(2,1)S(1)}, bf16[256,512]{1,0:T(8,128)(2,1)S(1)}, u32[]{:S(2)}, u32[]{:S(2)}) collective-permute-start(bf16[256,512]{1,0:T(8,128)(2,1)S(1)} %get-tuple-element.85.refs_4_.refs_1_), channel_id=1, source_target_pairs={{0,1},{1,0},{2,3},{3,2},{4,5},{5,4},{6,7},{7,6},{8,9},{9,8},{10,11... | collective-permute-start | bytes 786440 | tf_op jit(solution)/shard_map/ppermute | solution.py:65
  62.3 7.0 %collective-permute-start.26 = (bf16[256,512]{1,0:T(8,128)(2,1)S(1)}, bf16[256,512]{1,0:T(8,128)(2,1)S(1)}, u32[]{:S(2)}, u32[]{:S(2)}) collective-permute-start(bf16[256,512]{1,0:T(8,128)(2,1)S(1)} %get-tuple-element.86.refs_5_.refs_2_), channel_id=1, source_target_pairs={{0,1},{1,0},{2,3},{3,2},{4,5},{5,4},{6,7},{7,6},{8,9},{9,8},{10,11... | collective-permute-start | bytes 786440 | tf_op jit(solution)/shard_map/ppermute | solution.py:65
  62.8 11.3 %collective-permute-start.27 = (bf16[256,512]{1,0:T(8,128)(2,1)S(1)}, bf16[256,512]{1,0:T(8,128)(2,1)S(1)}, u32[]{:S(2)}, u32[]{:S(2)}) collective-permute-start(bf16[256,512]{1,0:T(8,128)(2,1)S(1)} %shard_map.59._), channel_id=1, source_target_pairs={{0,4},{12,8},{1,5},{13,9},{2,6},{14,10},{3,7},{15,11},{16,20},{28,... | collective-permute-start | bytes 786440 | tf_op jit(solution)/shard_map/ppermute | solution.py:406
  68.5 9.5 %collective-permute-start.30 = (bf16[256,512]{1,0:T(8,128)(2,1)S(1)}, bf16[256,512]{1,0:T(8,128)(2,1)S(1)}, u32[]{:S(2)}, u32[]{:S(2)}) collective-permute-start(bf16[256,512]{1,0:T(8,128)(2,1)S(1)} %shard_map.63._.refs_0_), channel_id=1, source_target_pairs={{4,8},{8,4},{5,9},{9,5},{6,10},{10,6},{7,11},{11,7},{20,24},{24,20... | collective-permute-start | bytes 786440 | tf_op jit(solution)/shard_map/ppermute | solution.py:406
  70.7 8.5 %collective-permute-start.31 = (bf16[256,512]{1,0:T(8,128)(2,1)S(1)}, bf16[256,512]{1,0:T(8,128)(2,1)S(1)}, u32[]{:S(2)}, u32[]{:S(2)}) collective-permute-start(bf16[256,512]{1,0:T(8,128)(2,1)S(1)} %get-tuple-element.89), channel_id=1, source_target_pairs={{0,2},{1,3},{2,0},{3,1},{4,6},{5,7},{6,4},{7,5},{8,10},{9,11},{10,... | collective-permute-start | bytes 786440 | tf_op jit(solution)/shard_map/ppermute | solution.py:61
  74.4 17.0 %collective-permute-start.34 = (bf16[400,512]{1,0:T(8,128)(2,1)S(1)}, bf16[400,512]{1,0:T(8,128)(2,1)S(1)}, u32[]{:S(2)}, u32[]{:S(2)}) collective-permute-start(bf16[400,512]{1,0:T(8,128)(2,1)S(1)} %shard_map.67._.refs_0_), channel_id=1, source_target_pairs={{4,0},{8,12},{5,1},{9,13},{6,2},{10,14},{7,3},{11,15},{20,16},{24,... | collective-permute-start | bytes 1228808 | tf_op jit(solution)/shard_map/ppermute | solution.py:406
  75.7 10.0 %collective-permute-start.32 = (bf16[256,512]{1,0:T(8,128)(2,1)S(1)}, bf16[256,512]{1,0:T(8,128)(2,1)S(1)}, u32[]{:S(2)}, u32[]{:S(2)}) collective-permute-start(bf16[256,512]{1,0:T(8,128)(2,1)S(1)} %shard_map.66._.refs_0_), channel_id=1, source_target_pairs={{4,8},{8,4},{5,9},{9,5},{6,10},{10,6},{7,11},{11,7},{20,24},{24,20... | collective-permute-start | bytes 786440 | tf_op jit(solution)/shard_map/ppermute | solution.py:406
  76.4 9.4 %collective-permute-start.33 = (bf16[256,512]{1,0:T(8,128)(2,1)S(1)}, bf16[256,512]{1,0:T(8,128)(2,1)S(1)}, u32[]{:S(2)}, u32[]{:S(2)}) collective-permute-start(bf16[256,512]{1,0:T(8,128)(2,1)S(1)} %get-tuple-element.91), channel_id=1, source_target_pairs={{0,2},{1,3},{2,0},{3,1},{4,6},{5,7},{6,4},{7,5},{8,10},{9,11},{10,... | collective-permute-start | bytes 786440 | tf_op jit(solution)/shard_map/ppermute | solution.py:61
  79.2 13.4 %collective-permute-start.35 = (bf16[256,512]{1,0:T(8,128)(2,1)S(1)}, bf16[256,512]{1,0:T(8,128)(2,1)S(1)}, u32[]{:S(2)}, u32[]{:S(2)}) collective-permute-start(bf16[256,512]{1,0:T(8,128)(2,1)S(1)} %shard_map.70._), channel_id=1, source_target_pairs={{0,4},{12,8},{1,5},{13,9},{2,6},{14,10},{3,7},{15,11},{16,20},{28,... | collective-permute-start | bytes 786440 | tf_op jit(solution)/shard_map/ppermute | solution.py:406
  84.4 9.5 %collective-permute-start.36 = (bf16[256,512]{1,0:T(8,128)(2,1)S(1)}, bf16[256,512]{1,0:T(8,128)(2,1)S(1)}, u32[]{:S(2)}, u32[]{:S(2)}) collective-permute-start(bf16[256,512]{1,0:T(8,128)(2,1)S(1)} %shard_map.69._.refs_0_), channel_id=1, source_target_pairs={{4,0},{8,12},{5,1},{9,13},{6,2},{10,14},{7,3},{11,15},{20,16},{24,... | collective-permute-start | bytes 786440 | tf_op jit(solution)/shard_map/ppermute | solution.py:406
  85.9 8.7 %collective-permute-start.37 = (bf16[272,512]{1,0:T(8,128)(2,1)S(1)}, bf16[272,512]{1,0:T(8,128)(2,1)S(1)}, u32[]{:S(2)}, u32[]{:S(2)}) collective-permute-start(bf16[272,512]{1,0:T(8,128)(2,1)S(1)} %shard_map.72._), channel_id=1, source_target_pairs={{0,4},{12,8},{1,5},{13,9},{2,6},{14,10},{3,7},{15,11},{16,20},{28,... | collective-permute-start | bytes 835592 | tf_op jit(solution)/shard_map/ppermute | solution.py:406
  90.5 12.5 %collective-permute-start.42 = (bf16[400,512]{1,0:T(8,128)(2,1)S(1)}, bf16[400,512]{1,0:T(8,128)(2,1)S(1)}, u32[]{:S(2)}, u32[]{:S(2)}) collective-permute-start(bf16[400,512]{1,0:T(8,128)(2,1)S(1)} %shard_map.68._.refs_5_), channel_id=1, source_target_pairs={{0,2},{1,3},{2,0},{3,1},{4,6},{5,7},{6,4},{7,5},{8,10},{9,11},{10,... | collective-permute-start | bytes 1228808 | tf_op jit(solution)/shard_map/ppermute | solution.py:61
  91.4 17.0 %collective-permute-start.45 = (bf16[400,512]{1,0:T(8,128)(2,1)S(1)}, bf16[400,512]{1,0:T(8,128)(2,1)S(1)}, u32[]{:S(2)}, u32[]{:S(2)}) collective-permute-start(bf16[400,512]{1,0:T(8,128)(2,1)S(1)} %shard_map.73._.refs_5_), channel_id=1, source_target_pairs={{0,2},{1,3},{2,0},{3,1},{4,6},{5,7},{6,4},{7,5},{8,10},{9,11},{10,... | collective-permute-start | bytes 1228808 | tf_op jit(solution)/shard_map/ppermute | solution.py:61
  92.7 8.3 %collective-permute-start.39 = (bf16[256,512]{1,0:T(8,128)(2,1)S(1)}, bf16[256,512]{1,0:T(8,128)(2,1)S(1)}, u32[]{:S(2)}, u32[]{:S(2)}) collective-permute-start(bf16[256,512]{1,0:T(8,128)(2,1)S(1)} %shard_map.71._.refs_0_), channel_id=1, source_target_pairs={{4,0},{8,12},{5,1},{9,13},{6,2},{10,14},{7,3},{11,15},{20,16},{24,... | collective-permute-start | bytes 786440 | tf_op jit(solution)/shard_map/ppermute | solution.py:406
  94.0 14.5 %collective-permute-start.43 = (bf16[400,512]{1,0:T(8,128)(2,1)S(1)}, bf16[400,512]{1,0:T(8,128)(2,1)S(1)}, u32[]{:S(2)}, u32[]{:S(2)}) collective-permute-start(bf16[400,512]{1,0:T(8,128)(2,1)S(1)} %shard_map.68._.refs_5_), channel_id=1, source_target_pairs={{0,1},{1,0},{2,3},{3,2},{4,5},{5,4},{6,7},{7,6},{8,9},{9,8},{10,11... | collective-permute-start | bytes 1228808 | tf_op jit(solution)/shard_map/ppermute | solution.py:65
  94.6 8.3 %collective-permute-start.38 = (bf16[256,512]{1,0:T(8,128)(2,1)S(1)}, bf16[256,512]{1,0:T(8,128)(2,1)S(1)}, u32[]{:S(2)}, u32[]{:S(2)}) collective-permute-start(bf16[256,512]{1,0:T(8,128)(2,1)S(1)} %shard_map.74._.refs_0_), channel_id=1, source_target_pairs={{4,8},{8,4},{5,9},{9,5},{6,10},{10,6},{7,11},{11,7},{20,24},{24,20... | collective-permute-start | bytes 786440 | tf_op jit(solution)/shard_map/ppermute | solution.py:406
  100.9 8.8 %collective-permute-start.40 = (bf16[272,512]{1,0:T(8,128)(2,1)S(1)}, bf16[272,512]{1,0:T(8,128)(2,1)S(1)}, u32[]{:S(2)}, u32[]{:S(2)}) collective-permute-start(bf16[272,512]{1,0:T(8,128)(2,1)S(1)} %shard_map.76._.refs_0_), channel_id=1, source_target_pairs={{4,8},{8,4},{5,9},{9,5},{6,10},{10,6},{7,11},{11,7},{20,24},{24,20... | collective-permute-start | bytes 835592 | tf_op jit(solution)/shard_map/ppermute | solution.py:406
  102.9 17.5 %collective-permute-start.46 = (bf16[400,512]{1,0:T(8,128)(2,1)S(1)}, bf16[400,512]{1,0:T(8,128)(2,1)S(1)}, u32[]{:S(2)}, u32[]{:S(2)}) collective-permute-start(bf16[400,512]{1,0:T(8,128)(2,1)S(1)} %shard_map.73._.refs_5_), channel_id=1, source_target_pairs={{0,1},{1,0},{2,3},{3,2},{4,5},{5,4},{6,7},{7,6},{8,9},{9,8},{10,11... | collective-permute-start | bytes 1228808 | tf_op jit(solution)/shard_map/ppermute | solution.py:65
  102.9 18.5 %collective-permute-start.44 = (bf16[400,512]{1,0:T(8,128)(2,1)S(1)}, bf16[400,512]{1,0:T(8,128)(2,1)S(1)}, u32[]{:S(2)}, u32[]{:S(2)}) collective-permute-start(bf16[400,512]{1,0:T(8,128)(2,1)S(1)} %collective-permute-done.42.refs_6_), channel_id=1, source_target_pairs={{0,1},{1,0},{2,3},{3,2},{4,5},{5,4},{6,7},{7,6},{8,9},{9,8},{10,11... | collective-permute-start | bytes 1228808 | tf_op jit(solution)/shard_map/ppermute | solution.py:65
  108.4 13.2 %collective-permute-start.47 = (bf16[400,512]{1,0:T(8,128)(2,1)S(1)}, bf16[400,512]{1,0:T(8,128)(2,1)S(1)}, u32[]{:S(2)}, u32[]{:S(2)}) collective-permute-start(bf16[400,512]{1,0:T(8,128)(2,1)S(1)} %collective-permute-done.45.refs_6_), channel_id=1, source_target_pairs={{0,1},{1,0},{2,3},{3,2},{4,5},{5,4},{6,7},{7,6},{8,9},{9,8},{10,11... | collective-permute-start | bytes 1228808 | tf_op jit(solution)/shard_map/ppermute | solution.py:65
  108.4 10.6 %collective-permute-start.41 = (bf16[256,512]{1,0:T(8,128)(2,1)S(1)}, bf16[256,512]{1,0:T(8,128)(2,1)S(1)}, u32[]{:S(2)}, u32[]{:S(2)}) collective-permute-start(bf16[256,512]{1,0:T(8,128)(2,1)S(1)} %shard_map.77._.refs_0_), channel_id=1, source_target_pairs={{4,0},{8,12},{5,1},{9,13},{6,2},{10,14},{7,3},{11,15},{20,16},{24,... | collective-permute-start | bytes 786440 | tf_op jit(solution)/shard_map/ppermute | solution.py:406
  109.7 10.6 %collective-permute-start.49 = (bf16[256,512]{1,0:T(8,128)(2,1)S(1)}, bf16[256,512]{1,0:T(8,128)(2,1)S(1)}, u32[]{:S(2)}, u32[]{:S(2)}) collective-permute-start(bf16[256,512]{1,0:T(8,128)(2,1)S(1)} %shard_map.75._.refs_3_), channel_id=1, source_target_pairs={{0,2},{1,3},{2,0},{3,1},{4,6},{5,7},{6,4},{7,5},{8,10},{9,11},{10,... | collective-permute-start | bytes 786440 | tf_op jit(solution)/shard_map/ppermute | solution.py:61
  119.0 10.2 %collective-permute-start.48 = (bf16[272,512]{1,0:T(8,128)(2,1)S(1)}, bf16[272,512]{1,0:T(8,128)(2,1)S(1)}, u32[]{:S(2)}, u32[]{:S(2)}) collective-permute-start(bf16[272,512]{1,0:T(8,128)(2,1)S(1)} %shard_map.79._.refs_0_), channel_id=1, source_target_pairs={{4,0},{8,12},{5,1},{9,13},{6,2},{10,14},{7,3},{11,15},{20,16},{24,... | collective-permute-start | bytes 835592 | tf_op jit(solution)/shard_map/ppermute | solution.py:406
  120.4 10.0 %collective-permute-start.50 = (bf16[256,512]{1,0:T(8,128)(2,1)S(1)}, bf16[256,512]{1,0:T(8,128)(2,1)S(1)}, u32[]{:S(2)}, u32[]{:S(2)}) collective-permute-start(bf16[256,512]{1,0:T(8,128)(2,1)S(1)} %shard_map.75._.refs_3_), channel_id=1, source_target_pairs={{0,1},{1,0},{2,3},{3,2},{4,5},{5,4},{6,7},{7,6},{8,9},{9,8},{10,11... | collective-permute-start | bytes 786440 | tf_op jit(solution)/shard_map/ppermute | solution.py:65
  120.5 9.9 %collective-permute-start.52 = (bf16[256,512]{1,0:T(8,128)(2,1)S(1)}, bf16[256,512]{1,0:T(8,128)(2,1)S(1)}, u32[]{:S(2)}, u32[]{:S(2)}) collective-permute-start(bf16[256,512]{1,0:T(8,128)(2,1)S(1)} %shard_map.78._.refs_3_), channel_id=1, source_target_pairs={{0,2},{1,3},{2,0},{3,1},{4,6},{5,7},{6,4},{7,5},{8,10},{9,11},{10,... | collective-permute-start | bytes 786440 | tf_op jit(solution)/shard_map/ppermute | solution.py:61
  121.4 9.5 %collective-permute-start.51 = (bf16[256,512]{1,0:T(8,128)(2,1)S(1)}, bf16[256,512]{1,0:T(8,128)(2,1)S(1)}, u32[]{:S(2)}, u32[]{:S(2)}) collective-permute-start(bf16[256,512]{1,0:T(8,128)(2,1)S(1)} %collective-permute-done.49.refs_4_), channel_id=1, source_target_pairs={{0,1},{1,0},{2,3},{3,2},{4,5},{5,4},{6,7},{7,6},{8,9},{9,8},{10,11... | collective-permute-start | bytes 786440 | tf_op jit(solution)/shard_map/ppermute | solution.py:65
  121.6 13.7 %collective-permute-start.55 = (bf16[256,512]{1,0:T(8,128)(2,1)S(1)}, bf16[256,512]{1,0:T(8,128)(2,1)S(1)}, u32[]{:S(2)}, u32[]{:S(2)}) collective-permute-start(bf16[256,512]{1,0:T(8,128)(2,1)S(1)} %shard_map.80._.refs_3_), channel_id=1, source_target_pairs={{0,2},{1,3},{2,0},{3,1},{4,6},{5,7},{6,4},{7,5},{8,10},{9,11},{10,... | collective-permute-start | bytes 786440 | tf_op jit(solution)/shard_map/ppermute | solution.py:61
  129.5 12.6 %collective-permute-start.58 = (bf16[272,512]{1,0:T(8,128)(2,1)S(1)}, bf16[272,512]{1,0:T(8,128)(2,1)S(1)}, u32[]{:S(2)}, u32[]{:S(2)}) collective-permute-start(bf16[272,512]{1,0:T(8,128)(2,1)S(1)} %shard_map.83._.refs_5_.refs_3_), channel_id=1, source_target_pairs={{0,2},{1,3},{2,0},{3,1},{4,6},{5,7},{6,4},{7,5},{8,10},{9,11},{10,... | collective-permute-start | bytes 835592 | tf_op jit(solution)/shard_map/ppermute | solution.py:61
  130.4 6.2 %collective-permute-start.53 = (bf16[256,512]{1,0:T(8,128)(2,1)S(1)}, bf16[256,512]{1,0:T(8,128)(2,1)S(1)}, u32[]{:S(2)}, u32[]{:S(2)}) collective-permute-start(bf16[256,512]{1,0:T(8,128)(2,1)S(1)} %shard_map.78._.refs_3_), channel_id=1, source_target_pairs={{0,1},{1,0},{2,3},{3,2},{4,5},{5,4},{6,7},{7,6},{8,9},{9,8},{10,11... | collective-permute-start | bytes 786440 | tf_op jit(solution)/shard_map/ppermute | solution.py:65
  130.4 6.7 %collective-permute-start.54 = (bf16[256,512]{1,0:T(8,128)(2,1)S(1)}, bf16[256,512]{1,0:T(8,128)(2,1)S(1)}, u32[]{:S(2)}, u32[]{:S(2)}) collective-permute-start(bf16[256,512]{1,0:T(8,128)(2,1)S(1)} %collective-permute-done.52.refs_4_), channel_id=1, source_target_pairs={{0,1},{1,0},{2,3},{3,2},{4,5},{5,4},{6,7},{7,6},{8,9},{9,8},{10,11... | collective-permute-start | bytes 786440 | tf_op jit(solution)/shard_map/ppermute | solution.py:65
  130.9 8.2 %collective-permute-start.56 = (bf16[256,512]{1,0:T(8,128)(2,1)S(1)}, bf16[256,512]{1,0:T(8,128)(2,1)S(1)}, u32[]{:S(2)}, u32[]{:S(2)}) collective-permute-start(bf16[256,512]{1,0:T(8,128)(2,1)S(1)} %shard_map.80._.refs_3_), channel_id=1, source_target_pairs={{0,1},{1,0},{2,3},{3,2},{4,5},{5,4},{6,7},{7,6},{8,9},{9,8},{10,11... | collective-permute-start | bytes 786440 | tf_op jit(solution)/shard_map/ppermute | solution.py:65
  135.3 3.9 %collective-permute-start.57 = (bf16[256,512]{1,0:T(8,128)(2,1)S(1)}, bf16[256,512]{1,0:T(8,128)(2,1)S(1)}, u32[]{:S(2)}, u32[]{:S(2)}) collective-permute-start(bf16[256,512]{1,0:T(8,128)(2,1)S(1)} %collective-permute-done.55.refs_4_), channel_id=1, source_target_pairs={{0,1},{1,0},{2,3},{3,2},{4,5},{5,4},{6,7},{7,6},{8,9},{9,8},{10,11... | collective-permute-start | bytes 786440 | tf_op jit(solution)/shard_map/ppermute | solution.py:65
  136.6 5.5 %collective-permute-start.59 = (bf16[272,512]{1,0:T(8,128)(2,1)S(1)}, bf16[272,512]{1,0:T(8,128)(2,1)S(1)}, u32[]{:S(2)}, u32[]{:S(2)}) collective-permute-start(bf16[272,512]{1,0:T(8,128)(2,1)S(1)} %shard_map.83._.refs_5_.refs_3_), channel_id=1, source_target_pairs={{0,1},{1,0},{2,3},{3,2},{4,5},{5,4},{6,7},{7,6},{8,9},{9,8},{10,11... | collective-permute-start | bytes 835592 | tf_op jit(solution)/shard_map/ppermute | solution.py:65
  139.1 1.6 %copy-start.2 = (f32[1024,512]{1,0:T(8,128)S(1)}, f32[1024,512]{1,0:T(8,128)}, u32[]{:S(2)}) copy-start(f32[1024,512]{1,0:T(8,128)} %get-tuple-element.53._) | copy-start | bytes 6291460
  142.0 1.6 %collective-permute-start.60 = (bf16[272,512]{1,0:T(8,128)(2,1)S(1)}, bf16[272,512]{1,0:T(8,128)(2,1)S(1)}, u32[]{:S(2)}, u32[]{:S(2)}) collective-permute-start(bf16[272,512]{1,0:T(8,128)(2,1)S(1)} %collective-permute-done.58.refs_6_.refs_4_), channel_id=1, source_target_pairs={{0,1},{1,0},{2,3},{3,2},{4,5},{5,4},{6,7},{7,6},{8,9},{9,8},{10,11... | collective-permute-start | bytes 835592 | tf_op jit(solution)/shard_map/ppermute | solution.py:65
  143.7 3.6 %collective-permute-start.61 = (f32[1,512]{1,0:T(1,128)S(1)}, f32[1,512]{1,0:T(1,128)S(1)}, u32[]{:S(2)}, u32[]{:S(2)}) collective-permute-start(f32[1,512]{1,0:T(1,128)S(1)} %get-tuple-element.105._), channel_id=1, source_target_pairs={{0,16},{16,0},{1,17},{17,1},{2,18},{18,2},{3,19},{19,3},{4,20},{20... | collective-permute-start | bytes 6152 | tf_op jit(solution)/shard_map/ppermute | solution.py:65
  (1 other events, 1.2 us)

commit v5 on v4

--- a/solution.py
+++ b/solution.py
@@ -13,8 +13,8 @@
 eps_var = 0.0001
 
 ORDER = (
-    "g0", "g1", "x0", "c0", "x1", "f0", "i0", "x2", "x3", "i1", "c1", "m0", "i2", "f1", "t5",
-    "i3", "m1", "o0", "m2", "x4", "m3", "x5", "o1", "i4", "o2", "i5", "m4", "o3", "m5", "o4",
+    "g0", "g1", "x0", "c0", "x1", "i0", "f0", "x2", "x3", "i1", "c1", "m0", "i2", "f1", "t5",
+    "m1", "i3", "o0", "m2", "x4", "m3", "x5", "o1", "i4", "i5", "m4", "o3", "o2", "o4", "m5",
     "p0", "p1", "o5", "q2", "q3", "q4", "e5", "s5", "q5",
 )
 

time: 149 us -> 144 us (0.966)
  Pallas kernels: 28.5 us -> 23.9 us
    pallas_call x39, Pallas kernels: 27.1 us -> 23.4 us  [__call__(): pl.pallas_call(body, out_shape=outs, in_specs=specs, out_specs=[VMEM] * l...]
    ppermute x18, waiting for transfers between devices: 19 us -> 16.9 us  [send_row(): lax.ppermute(value, 'row', [(g + a, g + b) for g in groups for a, b in pa...]
    unnamed x6 -> x10, local copies, waits for them, and re-layouts: 2.81 us -> 4.04 us
  transfers between devices with their start and end apart: 62 -> 62, of which waited for: 21 -> 20; matrix products, arithmetic and copies ran while one was open for 0% -> 0% of each run, Pallas kernels for 18% -> 15%
where the time goes in v5:
time: 144 us
  starting transfers between devices  63.4 us (44%)
  waiting for transfers between devices  50.6 us (35%)
  Pallas kernels  23.9 us (17%)
  local copies, waits for them, and re-layouts  4.04 us (3%)
    ppermute x18, starting transfers between devices, send_row(): lax.ppermute(value, 'row', [(g + a, g + b) for g in groups for a, b in pa...  37.1 us
    ppermute x12, waiting for transfers between devices, shift(): return lax.ppermute(value, axis, pairs)  24.2 us
    pallas_call x39, Pallas kernels, __call__(): pl.pallas_call(body, out_shape=outs, in_specs=specs, out_specs=[VMEM] * l...  23.4 us
    ppermute x18, waiting for transfers between devices, send_row(): lax.ppermute(value, 'row', [(g + a, g + b) for g in groups for a, b in pa...  16.9 us
    ppermute x12, starting transfers between devices, shift(): return lax.ppermute(value, axis, pairs)  13.9 us
    ppermute x32, starting transfers between devices, partner_of(): lax.ppermute(value, axis, [(index, index ^ bit) for index in range(lax.ax...  12.4 us
    ppermute x32, waiting for transfers between devices, partner_of(): lax.ppermute(value, axis, [(index, index ^ bit) for index in range(lax.ax...  9.38 us
    unnamed x10, local copies, waits for them, and re-layouts  4.04 us
  transfers between devices with their start and end apart: 62, of which 20 were waited for; matrix products, arithmetic and copies ran while one was open for 0% of the time, Pallas kernels for 15%

profile of v5, /device:TPU:0, one launch (start us, length us, event | category | flops | bytes accessed | tf_op | source)
XLA Modules:
  0.0 143.8 jit_solution(9857073251738193034)
XLA Ops:
  0.6 1.2 copy-done
  1.9 1.2 copy-done.2
  3.1 0.6 shard_map.49
  3.7 3.0 %collective-permute-start = (f32[2,512]{1,0:T(2,128)S(1)}, f32[2,512]{1,0:T(2,128)S(1)}, u32[]{:S(2)}, u32[]{:S(2)}) collective-permute-start(f32[2,512]{1,0:T(2,128)S(1)} %shard_map.49), channel_id=1, source_target_pairs={{0,16},{16,0},{1,17},{17,1},{2,18},{18,2},{3,19},{19,3},{4,20},{20... | collective-permute-start | bytes 12296 | tf_op jit(solution)/shard_map/ppermute | solution.py:65
  6.7 1.6 %collective-permute-done = f32[2,512]{1,0:T(2,128)S(1)} collective-permute-done((f32[2,512]{1,0:T(2,128)S(1)}, f32[2,512]{1,0:T(2,128)S(1)}, u32[]{:S(2)}, u32[]{:S(2)}) %collective-permute-start) | collective-permute-done | bytes 4128 | tf_op jit(solution)/shard_map/ppermute | solution.py:65
  8.3 1.6 %shard_map.50 = (f32[8,512]{1,0:T(8,128)S(1)}, bf16[256,512]{1,0:T(8,128)(2,1)S(1)}, bf16[256,512]{1,0:T(8,128)(2,1)S(1)}, bf16[256,512]{1,0:T(8,128)(2,1)S(1)},...) custom-call(bf16[1024,512]{1,0:T(8,128)(2,1)S(1)} %copy-done.1, ...), custom_call_target="tpu_custom_call" | custom-call | flops 1 | bytes 1 | tf_op jit(solution)/shard_map/pallas_call | solution.py:39
  9.9 2.1 %collective-permute-start.10 = (bf16[1024,512]{1,0:T(8,128)(2,1)S(1)}, bf16[1024,512]{1,0:T(8,128)(2,1)S(1)}, u32[]{:S(2)}, u32[]{:S(2)}) collective-permute-start(bf16[1024,512]{1,0:T(8,128)(2,1)S(1)} %copy-done.1), channel_id=1, source_target_pairs={{0,16},{16,0},{1,17},{17,1},{2,18},{18,2},{3,19},{19,3},{4,20},{20... | collective-permute-start | bytes 3145736 | tf_op jit(solution)/shard_map/ppermute | solution.py:65
  13.1 0.5 collective-permute-done.2.refs_5_
  14.3 2.3 %shard_map.51 = (bf16[1024,512]{1,0:T(8,128)(2,1)S(1)}, bf16[1024,512]{1,0:T(8,128)(2,1)S(1)}, f32[400,512]{1,0:T(8,128)S(1)}, bf16[400,512]{1,0:T(8,128)(2,1)S(1)}) custom-call(f32[8,512]{1,0:T(8,128)S(1)} %get-tuple-element.56._.refs_0_, bf16[256,512]{1,0:T(8,128)(2,1)S(1)} %get-tuple-element.57.refs_0_, bf16[256,512]{1,0:T(8,128)(2,1)S(1)} %get-tuple-element.58.refs_1_, ...), custom_call_target="tpu_custom_call" | custom-call | flops 1 | bytes 1 | tf_op jit(solution)/shard_map/pallas_call | solution.py:39
  16.6 1.6 %collective-permute-start.9 = (bf16[400,512]{1,0:T(8,128)(2,1)S(1)}, bf16[400,512]{1,0:T(8,128)(2,1)S(1)}, u32[]{:S(2)}, u32[]{:S(2)}) collective-permute-start(bf16[400,512]{1,0:T(8,128)(2,1)S(1)} %get-tuple-element.68), channel_id=1, source_target_pairs={{0,2},{1,3},{2,0},{3,1},{4,6},{5,7},{6,4},{7,5},{8,10},{9,11},{10,... | collective-permute-start | bytes 1228808 | tf_op jit(solution)/shard_map/ppermute | solution.py:61
  18.2 0.5 collective-permute-start.7
  18.7 1.0 collective-permute-done.6.refs_5_
  20.5 2.3 %shard_map.52 = (bf16[1024,512]{1,0:T(8,128)(2,1)S(1)}, bf16[1024,512]{1,0:T(8,128)(2,1)S(1)}, f32[400,512]{1,0:T(8,128)S(1)}, bf16[400,512]{1,0:T(8,128)(2,1)S(1)}) custom-call(bf16[1024,512]{1,0:T(8,128)(2,1)S(1)} %get-tuple-element.61._.refs_0_, bf16[256,512]{1,0:T(8,128)(2,1)S(1)} %get-tuple-element.62.refs_0_, ...), custom_call_target="tpu_custom_call" | custom-call | flops 1 | bytes 1 | tf_op jit(solution)/shard_map/pallas_call | solution.py:39
  22.8 0.6 collective-permute-start.11
  23.3 5.6 %collective-permute-done.9.refs_1_ = bf16[400,512]{1,0:T(8,128)(2,1)S(1)} collective-permute-done((bf16[400,512]{1,0:T(8,128)(2,1)S(1)}, bf16[400,512]{1,0:T(8,128)(2,1)S(1)}, u32[]{:S(2)}, u32[]{:S(2)}) %collective-permute-start.9) | collective-permute-done | bytes 409632 | tf_op jit(solution)/shard_map/ppermute | solution.py:61
  29.1 3.5 %collective-permute-start.12 = (bf16[400,512]{1,0:T(8,128)(2,1)S(1)}, bf16[400,512]{1,0:T(8,128)(2,1)S(1)}, u32[]{:S(2)}, u32[]{:S(2)}) collective-permute-start(bf16[400,512]{1,0:T(8,128)(2,1)S(1)} %shard_map.53._), channel_id=1, source_target_pairs={{0,4},{12,8},{1,5},{13,9},{2,6},{14,10},{3,7},{15,11},{16,20},{28,... | collective-permute-start | bytes 1228808 | tf_op jit(solution)/shard_map/ppermute | solution.py:406
  32.6 3.4 %collective-permute-done.10.refs_0_.refs_2_ = bf16[1024,512]{1,0:T(8,128)(2,1)S(1)} collective-permute-done((bf16[1024,512]{1,0:T(8,128)(2,1)S(1)}, bf16[1024,512]{1,0:T(8,128)(2,1)S(1)}, u32[]{:S(2)}, u32[]{:S(2)}) %collective-permute-start.10) | collective-permute-done | bytes 1048608 | tf_op jit(solution)/shard_map/ppermute | solution.py:65
  37.0 3.0 %collective-permute-done.12.refs_2_ = bf16[400,512]{1,0:T(8,128)(2,1)S(1)} collective-permute-done((bf16[400,512]{1,0:T(8,128)(2,1)S(1)}, bf16[400,512]{1,0:T(8,128)(2,1)S(1)}, u32[]{:S(2)}, u32[]{:S(2)}) %collective-permute-start.12) | collective-permute-done | bytes 409632 | tf_op jit(solution)/shard_map/ppermute | solution.py:406
  40.1 4.4 %collective-permute-start.19 = (bf16[400,512]{1,0:T(8,128)(2,1)S(1)}, bf16[400,512]{1,0:T(8,128)(2,1)S(1)}, u32[]{:S(2)}, u32[]{:S(2)}) collective-permute-start(bf16[400,512]{1,0:T(8,128)(2,1)S(1)} %shard_map.55._), channel_id=1, source_target_pairs={{0,4},{12,8},{1,5},{13,9},{2,6},{14,10},{3,7},{15,11},{16,20},{28,... | collective-permute-start | bytes 1228808 | tf_op jit(solution)/shard_map/ppermute | solution.py:406
  44.7 1.3 shard_map.57
  46.0 1.6 %collective-permute-start.17 = (bf16[256,512]{1,0:T(8,128)(2,1)S(1)}, bf16[256,512]{1,0:T(8,128)(2,1)S(1)}, u32[]{:S(2)}, u32[]{:S(2)}) collective-permute-start(bf16[256,512]{1,0:T(8,128)(2,1)S(1)} %get-tuple-element.78), channel_id=1, source_target_pairs={{0,2},{1,3},{2,0},{3,1},{4,6},{5,7},{6,4},{7,5},{8,10},{9,11},{10,... | collective-permute-start | bytes 786440 | tf_op jit(solution)/shard_map/ppermute | solution.py:61
  48.1 0.7 collective-permute-start.21
  48.8 6.4 %collective-permute-done.17.refs_1_ = bf16[256,512]{1,0:T(8,128)(2,1)S(1)} collective-permute-done((bf16[256,512]{1,0:T(8,128)(2,1)S(1)}, bf16[256,512]{1,0:T(8,128)(2,1)S(1)}, u32[]{:S(2)}, u32[]{:S(2)}) %collective-permute-start.17) | collective-permute-done | bytes 262176 | tf_op jit(solution)/shard_map/ppermute | solution.py:61
  55.3 1.3 collective-permute-start.22
  56.6 3.5 %collective-permute-done.18.refs_1_ = bf16[256,512]{1,0:T(8,128)(2,1)S(1)} collective-permute-done((bf16[256,512]{1,0:T(8,128)(2,1)S(1)}, bf16[256,512]{1,0:T(8,128)(2,1)S(1)}, u32[]{:S(2)}, u32[]{:S(2)}) %collective-permute-start.18) | collective-permute-done | bytes 262176 | tf_op jit(solution)/shard_map/ppermute | solution.py:61
  61.1 0.7 collective-permute-start.27
  62.5 1.3 collective-permute-start.29
  63.8 4.6 %collective-permute-start.28 = (bf16[256,512]{1,0:T(8,128)(2,1)S(1)}, bf16[256,512]{1,0:T(8,128)(2,1)S(1)}, u32[]{:S(2)}, u32[]{:S(2)}) collective-permute-start(bf16[256,512]{1,0:T(8,128)(2,1)S(1)} %shard_map.59._), channel_id=1, source_target_pairs={{0,4},{12,8},{1,5},{13,9},{2,6},{14,10},{3,7},{15,11},{16,20},{28,... | collective-permute-start | bytes 786440 | tf_op jit(solution)/shard_map/ppermute | solution.py:406
  68.5 0.9 collective-permute-start.30
  69.4 1.3 shard_map.64
  70.7 1.6 %collective-permute-start.31 = (bf16[256,512]{1,0:T(8,128)(2,1)S(1)}, bf16[256,512]{1,0:T(8,128)(2,1)S(1)}, u32[]{:S(2)}, u32[]{:S(2)}) collective-permute-start(bf16[256,512]{1,0:T(8,128)(2,1)S(1)} %get-tuple-element.89), channel_id=1, source_target_pairs={{0,2},{1,3},{2,0},{3,1},{4,6},{5,7},{6,4},{7,5},{8,10},{9,11},{10,... | collective-permute-start | bytes 786440 | tf_op jit(solution)/shard_map/ppermute | solution.py:61
  72.3 1.7 %shard_map.65 = (f32[8,512]{1,0:T(8,128)S(1)}, f32[1,512]{1,0:T(1,128)S(1)}) custom-call(f32[256,512]{1,0:T(8,128)S(1)} %get-tuple-element.87._.refs_0_, f32[8,512]{1,0:T(8,128)S(1)} %get-tuple-element.56._.refs_0_, f32[2,512]{1,0:T(2,128)S(1)} %add.9.sums.refs_1_.refs_3_, bf16[1024,512]{1,0:T(8,128)(2,1)S(1)} %collective-permute-done.10.refs_0_.refs_2_, ...), custom_call_target="tpu_custom_call" | custom-call | flops 1 | bytes 1 | tf_op jit(solution)/shard_map/pallas_call | solution.py:39
  74.0 1.3 collective-permute-start.34
  75.5 0.7 collective-permute-start.32
  76.2 1.3 collective-permute-start.33
  77.6 1.4 collective-permute-done.31.refs_1_
  79.0 5.3 %collective-permute-start.35 = (bf16[256,512]{1,0:T(8,128)(2,1)S(1)}, bf16[256,512]{1,0:T(8,128)(2,1)S(1)}, u32[]{:S(2)}, u32[]{:S(2)}) collective-permute-start(bf16[256,512]{1,0:T(8,128)(2,1)S(1)} %shard_map.70._), channel_id=1, source_target_pairs={{0,4},{12,8},{1,5},{13,9},{2,6},{14,10},{3,7},{15,11},{16,20},{28,... | collective-permute-start | bytes 786440 | tf_op jit(solution)/shard_map/ppermute | solution.py:406
  84.5 6.1 %collective-permute-start.36 = (bf16[272,512]{1,0:T(8,128)(2,1)S(1)}, bf16[272,512]{1,0:T(8,128)(2,1)S(1)}, u32[]{:S(2)}, u32[]{:S(2)}) collective-permute-start(bf16[272,512]{1,0:T(8,128)(2,1)S(1)} %shard_map.72._), channel_id=1, source_target_pairs={{0,4},{12,8},{1,5},{13,9},{2,6},{14,10},{3,7},{15,11},{16,20},{28,... | collective-permute-start | bytes 835592 | tf_op jit(solution)/shard_map/ppermute | solution.py:406
  90.7 0.7 collective-permute-start.37
  91.4 0.6 collective-permute-start.42
  92.0 1.5 %collective-permute-start.45 = (bf16[400,512]{1,0:T(8,128)(2,1)S(1)}, bf16[400,512]{1,0:T(8,128)(2,1)S(1)}, u32[]{:S(2)}, u32[]{:S(2)}) collective-permute-start(bf16[400,512]{1,0:T(8,128)(2,1)S(1)} %shard_map.73._.refs_5_), channel_id=1, source_target_pairs={{0,2},{1,3},{2,0},{3,1},{4,6},{5,7},{6,4},{7,5},{8,10},{9,11},{10,... | collective-permute-start | bytes 1228808 | tf_op jit(solution)/shard_map/ppermute | solution.py:61
  93.5 1.3 collective-permute-start.39
  94.9 0.7 collective-permute-start.41
  95.6 1.3 collective-permute-start.38
  97.0 7.6 %collective-permute-done.39.refs_1_ = bf16[256,512]{1,0:T(8,128)(2,1)S(1)} collective-permute-done((bf16[256,512]{1,0:T(8,128)(2,1)S(1)}, bf16[256,512]{1,0:T(8,128)(2,1)S(1)}, u32[]{:S(2)}, u32[]{:S(2)}) %collective-permute-start.39) | collective-permute-done | bytes 262176 | tf_op jit(solution)/shard_map/ppermute | solution.py:406
  104.6 1.3 collective-permute-start.40
  105.9 4.2 %collective-permute-done.38.refs_1_ = bf16[256,512]{1,0:T(8,128)(2,1)S(1)} collective-permute-done((bf16[256,512]{1,0:T(8,128)(2,1)S(1)}, bf16[256,512]{1,0:T(8,128)(2,1)S(1)}, u32[]{:S(2)}, u32[]{:S(2)}) %collective-permute-start.38) | collective-permute-done | bytes 262176 | tf_op jit(solution)/shard_map/ppermute | solution.py:406
  110.1 0.5 collective-permute-start.46
  110.8 2.2 %collective-permute-done.40.refs_1_ = bf16[256,512]{1,0:T(8,128)(2,1)S(1)} collective-permute-done((bf16[256,512]{1,0:T(8,128)(2,1)S(1)}, bf16[256,512]{1,0:T(8,128)(2,1)S(1)}, u32[]{:S(2)}, u32[]{:S(2)}) %collective-permute-start.40) | collective-permute-done | bytes 262176 | tf_op jit(solution)/shard_map/ppermute | solution.py:406
  112.9 1.8 %collective-permute-start.49 = (bf16[256,512]{1,0:T(8,128)(2,1)S(1)}, bf16[256,512]{1,0:T(8,128)(2,1)S(1)}, u32[]{:S(2)}, u32[]{:S(2)}) collective-permute-start(bf16[256,512]{1,0:T(8,128)(2,1)S(1)} %shard_map.78._.refs_3_), channel_id=1, source_target_pairs={{0,2},{1,3},{2,0},{3,1},{4,6},{5,7},{6,4},{7,5},{8,10},{9,11},{10,... | collective-permute-start | bytes 786440 | tf_op jit(solution)/shard_map/ppermute | solution.py:61
  114.8 1.3 collective-permute-start.48
  116.5 3.9 %collective-permute-done.49.refs_4_ = bf16[256,512]{1,0:T(8,128)(2,1)S(1)} collective-permute-done((bf16[256,512]{1,0:T(8,128)(2,1)S(1)}, bf16[256,512]{1,0:T(8,128)(2,1)S(1)}, u32[]{:S(2)}, u32[]{:S(2)}) %collective-permute-start.49) | collective-permute-done | bytes 262176 | tf_op jit(solution)/shard_map/ppermute | solution.py:61
  120.4 2.5 %collective-permute-start.55 = (bf16[256,512]{1,0:T(8,128)(2,1)S(1)}, bf16[256,512]{1,0:T(8,128)(2,1)S(1)}, u32[]{:S(2)}, u32[]{:S(2)}) collective-permute-start(bf16[256,512]{1,0:T(8,128)(2,1)S(1)} %shard_map.79._.refs_3_), channel_id=1, source_target_pairs={{0,2},{1,3},{2,0},{3,1},{4,6},{5,7},{6,4},{7,5},{8,10},{9,11},{10,... | collective-permute-start | bytes 786440 | tf_op jit(solution)/shard_map/ppermute | solution.py:61
  122.9 1.9 %shard_map.81 = (f32[1024,512]{1,0:T(8,128)S(1)}, f32[1,512]{1,0:T(1,128)S(1)}) custom-call(bf16[272,512]{1,0:T(8,128)(2,1)S(1)} %shard_map.80._.refs_0_, bf16[1024,512]{1,0:T(8,128)(2,1)S(1)} %get-tuple-element.61._.refs_0_, bf16[1024,512]{1,0:T(8,128)(2,1)S(1)} %copy-done.1, bf16[1024,512]{1,0:T(8,128)(2,1)S(1)} %copy-done.3, ...), custom_call_target="tpu_custom_call" | custom-call | flops 1 | bytes 1 | tf_op jit(solution)/shard_map/pallas_call | solution.py:39
  124.8 1.9 %shard_map.82 = (f32[1024,512]{1,0:T(8,128)S(1)}, f32[1,512]{1,0:T(1,128)S(1)}) custom-call(f32[1024,512]{1,0:T(8,128)S(1)} %get-tuple-element.93._.refs_0_, bf16[1024,512]{1,0:T(8,128)(2,1)S(1)} %get-tuple-element.66._.refs_0_, bf16[1024,512]{1,0:T(8,128)(2,1)S(1)} %copy-done.1, bf16[1024,512]{1,0:T(8,128)(2,1)S(1)} %copy-done.3, ...), custom_call_target="tpu_custom_call" | custom-call | flops 1 | bytes 1 | tf_op jit(solution)/shard_map/pallas_call | solution.py:39
  127.9 3.2 %collective-permute-done.55.refs_4_ = bf16[256,512]{1,0:T(8,128)(2,1)S(1)} collective-permute-done((bf16[256,512]{1,0:T(8,128)(2,1)S(1)}, bf16[256,512]{1,0:T(8,128)(2,1)S(1)}, u32[]{:S(2)}, u32[]{:S(2)}) %collective-permute-start.55) | collective-permute-done | bytes 262176 | tf_op jit(solution)/shard_map/ppermute | solution.py:61
  131.1 1.3 shard_map.84
  132.9 2.1 %shard_map.85 = (f32[1024,512]{1,0:T(8,128)}, f32[1,512]{1,0:T(1,128)S(1)}, f32[1,512]{1,0:T(1,128)}) custom-call(f32[1024,512]{1,0:T(8,128)S(1)} %get-tuple-element.95._.refs_0_, f32[1024,512]{1,0:T(8,128)S(1)} %get-tuple-element.95._.refs_0_, bf16[256,512]{1,0:T(8,128)(2,1)S(1)} %get-tuple-element.75.refs_4_.refs_1_, ...), custom_call_target="tpu_custom_call" | custom-call | flops 1 | bytes 1 | tf_op jit(solution)/shard_map/pallas_call | solution.py:39
  135.0 1.6 %copy-done.4 = f32[1024,512]{1,0:T(8,128)S(1)} copy-done((f32[1024,512]{1,0:T(8,128)S(1)}, f32[1024,512]{1,0:T(8,128)}, u32[]{:S(2)}) %copy-start.4) | copy-done | bytes 2097176
  136.6 1.3 shard_map.86
  137.9 1.5 %collective-permute-done.60.refs_8_.refs_6_ = bf16[272,512]{1,0:T(8,128)(2,1)S(1)} collective-permute-done((bf16[272,512]{1,0:T(8,128)(2,1)S(1)}, bf16[272,512]{1,0:T(8,128)(2,1)S(1)}, u32[]{:S(2)}, u32[]{:S(2)}) %collective-permute-start.60) | collective-permute-done | bytes 278560 | tf_op jit(solution)/shard_map/ppermute | solution.py:65
  139.5 1.4 collective-permute-start.61
  140.9 2.0 %shard_map.88 = f32[1024,512]{1,0:T(8,128)} custom-call(f32[1,512]{1,0:T(1,128)S(1)} %get-tuple-element.105._, f32[1024,512]{1,0:T(8,128)S(1)} %get-tuple-element.106._.refs_0_, bf16[256,512]{1,0:T(8,128)(2,1)S(1)} %get-tuple-element.85.refs_4_.refs_1_, bf16[256,512]{1,0:T(8,128)(2,1)S(1)} %get-tuple-element.86.refs_5_.refs_2_, ...), custom_call_target="tpu_custom_call" | custom-call | flops 1 | bytes 1 | tf_op jit(solution)/shard_map/pallas_call | solution.py:39
  143.2 0.6 add_reduce_fusion
  (112 shorter events, 9.7 us)
Async XLA Ops:
  3.1 5.2 %copy-start.1 = (bf16[1024,512]{1,0:T(8,128)(2,1)S(1)}, bf16[1024,512]{1,0:T(8,128)(2,1)}, u32[]{:S(2)}) copy-start(bf16[1024,512]{1,0:T(8,128)(2,1)} %refs_1_.3) | copy-start | bytes 3145732
  3.1 5.2 %copy-start.3 = (bf16[1024,512]{1,0:T(8,128)(2,1)S(1)}, bf16[1024,512]{1,0:T(8,128)(2,1)}, u32[]{:S(2)}) copy-start(bf16[1024,512]{1,0:T(8,128)(2,1)} %refs_2_.3) | copy-start | bytes 3145732
  3.7 4.6 %collective-permute-start = (f32[2,512]{1,0:T(2,128)S(1)}, f32[2,512]{1,0:T(2,128)S(1)}, u32[]{:S(2)}, u32[]{:S(2)}) collective-permute-start(f32[2,512]{1,0:T(2,128)S(1)} %shard_map.49), channel_id=1, source_target_pairs={{0,16},{16,0},{1,17},{17,1},{2,18},{18,2},{3,19},{19,3},{4,20},{20... | collective-permute-start | bytes 12296 | tf_op jit(solution)/shard_map/ppermute | solution.py:65
  9.9 2.8 %collective-permute-start.1 = (bf16[256,512]{1,0:T(8,128)(2,1)S(1)}, bf16[256,512]{1,0:T(8,128)(2,1)S(1)}, u32[]{:S(2)}, u32[]{:S(2)}) collective-permute-start(bf16[256,512]{1,0:T(8,128)(2,1)S(1)} %get-tuple-element.57.refs_0_), channel_id=1, source_target_pairs={{0,1},{1,0},{2,3},{3,2},{4,5},{5,4},{6,7},{7,6},{8,9},{9,8},{10,11... | collective-permute-start | bytes 786440 | tf_op jit(solution)/shard_map/ppermute | solution.py:65
  9.9 26.1 %collective-permute-start.10 = (bf16[1024,512]{1,0:T(8,128)(2,1)S(1)}, bf16[1024,512]{1,0:T(8,128)(2,1)S(1)}, u32[]{:S(2)}, u32[]{:S(2)}) collective-permute-start(bf16[1024,512]{1,0:T(8,128)(2,1)S(1)} %copy-done.1), channel_id=1, source_target_pairs={{0,16},{16,0},{1,17},{17,1},{2,18},{18,2},{3,19},{19,3},{4,20},{20... | collective-permute-start | bytes 3145736 | tf_op jit(solution)/shard_map/ppermute | solution.py:65
  12.0 1.5 %collective-permute-start.2 = (bf16[256,512]{1,0:T(8,128)(2,1)S(1)}, bf16[256,512]{1,0:T(8,128)(2,1)S(1)}, u32[]{:S(2)}, u32[]{:S(2)}) collective-permute-start(bf16[256,512]{1,0:T(8,128)(2,1)S(1)} %get-tuple-element.58.refs_1_), channel_id=1, source_target_pairs={{0,1},{1,0},{2,3},{3,2},{4,5},{5,4},{6,7},{7,6},{8,9},{9,8},{10,11... | collective-permute-start | bytes 786440 | tf_op jit(solution)/shard_map/ppermute | solution.py:65
  12.2 1.7 %collective-permute-start.3 = (bf16[256,512]{1,0:T(8,128)(2,1)S(1)}, bf16[256,512]{1,0:T(8,128)(2,1)S(1)}, u32[]{:S(2)}, u32[]{:S(2)}) collective-permute-start(bf16[256,512]{1,0:T(8,128)(2,1)S(1)} %get-tuple-element.59.refs_2_), channel_id=1, source_target_pairs={{0,1},{1,0},{2,3},{3,2},{4,5},{5,4},{6,7},{7,6},{8,9},{9,8},{10,11... | collective-permute-start | bytes 786440 | tf_op jit(solution)/shard_map/ppermute | solution.py:65
  12.5 1.8 %collective-permute-start.4 = (bf16[256,512]{1,0:T(8,128)(2,1)S(1)}, bf16[256,512]{1,0:T(8,128)(2,1)S(1)}, u32[]{:S(2)}, u32[]{:S(2)}) collective-permute-start(bf16[256,512]{1,0:T(8,128)(2,1)S(1)} %get-tuple-element.60.refs_3_), channel_id=1, source_target_pairs={{0,1},{1,0},{2,3},{3,2},{4,5},{5,4},{6,7},{7,6},{8,9},{9,8},{10,11... | collective-permute-start | bytes 786440 | tf_op jit(solution)/shard_map/ppermute | solution.py:65
  12.7 6.0 %collective-permute-start.5 = (bf16[256,512]{1,0:T(8,128)(2,1)S(1)}, bf16[256,512]{1,0:T(8,128)(2,1)S(1)}, u32[]{:S(2)}, u32[]{:S(2)}) collective-permute-start(bf16[256,512]{1,0:T(8,128)(2,1)S(1)} %get-tuple-element.62.refs_0_), channel_id=1, source_target_pairs={{0,1},{1,0},{2,3},{3,2},{4,5},{5,4},{6,7},{7,6},{8,9},{9,8},{10,11... | collective-permute-start | bytes 786440 | tf_op jit(solution)/shard_map/ppermute | solution.py:65
  16.6 12.4 %collective-permute-start.9 = (bf16[400,512]{1,0:T(8,128)(2,1)S(1)}, bf16[400,512]{1,0:T(8,128)(2,1)S(1)}, u32[]{:S(2)}, u32[]{:S(2)}) collective-permute-start(bf16[400,512]{1,0:T(8,128)(2,1)S(1)} %get-tuple-element.68), channel_id=1, source_target_pairs={{0,2},{1,3},{2,0},{3,1},{4,6},{5,7},{6,4},{7,5},{8,10},{9,11},{10,... | collective-permute-start | bytes 1228808 | tf_op jit(solution)/shard_map/ppermute | solution.py:61
  18.2 1.5 %collective-permute-start.6 = (bf16[256,512]{1,0:T(8,128)(2,1)S(1)}, bf16[256,512]{1,0:T(8,128)(2,1)S(1)}, u32[]{:S(2)}, u32[]{:S(2)}) collective-permute-start(bf16[256,512]{1,0:T(8,128)(2,1)S(1)} %get-tuple-element.63.refs_1_), channel_id=1, source_target_pairs={{0,1},{1,0},{2,3},{3,2},{4,5},{5,4},{6,7},{7,6},{8,9},{9,8},{10,11... | collective-permute-start | bytes 786440 | tf_op jit(solution)/shard_map/ppermute | solution.py:65
  18.2 2.0 %collective-permute-start.7 = (bf16[256,512]{1,0:T(8,128)(2,1)S(1)}, bf16[256,512]{1,0:T(8,128)(2,1)S(1)}, u32[]{:S(2)}, u32[]{:S(2)}) collective-permute-start(bf16[256,512]{1,0:T(8,128)(2,1)S(1)} %get-tuple-element.64.refs_2_), channel_id=1, source_target_pairs={{0,1},{1,0},{2,3},{3,2},{4,5},{5,4},{6,7},{7,6},{8,9},{9,8},{10,11... | collective-permute-start | bytes 786440 | tf_op jit(solution)/shard_map/ppermute | solution.py:65
  18.7 1.8 %collective-permute-start.8 = (bf16[256,512]{1,0:T(8,128)(2,1)S(1)}, bf16[256,512]{1,0:T(8,128)(2,1)S(1)}, u32[]{:S(2)}, u32[]{:S(2)}) collective-permute-start(bf16[256,512]{1,0:T(8,128)(2,1)S(1)} %get-tuple-element.65.refs_3_), channel_id=1, source_target_pairs={{0,1},{1,0},{2,3},{3,2},{4,5},{5,4},{6,7},{7,6},{8,9},{9,8},{10,11... | collective-permute-start | bytes 786440 | tf_op jit(solution)/shard_map/ppermute | solution.py:65
  19.7 40.6 %collective-permute-start.20 = (bf16[1024,512]{1,0:T(8,128)(2,1)S(1)}, bf16[1024,512]{1,0:T(8,128)(2,1)S(1)}, u32[]{:S(2)}, u32[]{:S(2)}) collective-permute-start(bf16[1024,512]{1,0:T(8,128)(2,1)S(1)} %copy-done.3), channel_id=1, source_target_pairs={{0,16},{16,0},{1,17},{17,1},{2,18},{18,2},{3,19},{19,3},{4,20},{20... | collective-permute-start | bytes 3145736 | tf_op jit(solution)/shard_map/ppermute | solution.py:65
  22.8 14.2 %collective-permute-start.11 = (bf16[400,512]{1,0:T(8,128)(2,1)S(1)}, bf16[400,512]{1,0:T(8,128)(2,1)S(1)}, u32[]{:S(2)}, u32[]{:S(2)}) collective-permute-start(bf16[400,512]{1,0:T(8,128)(2,1)S(1)} %get-tuple-element.72), channel_id=1, source_target_pairs={{0,2},{1,3},{2,0},{3,1},{4,6},{5,7},{6,4},{7,5},{8,10},{9,11},{10,... | collective-permute-start | bytes 1228808 | tf_op jit(solution)/shard_map/ppermute | solution.py:61
  29.1 10.9 %collective-permute-start.12 = (bf16[400,512]{1,0:T(8,128)(2,1)S(1)}, bf16[400,512]{1,0:T(8,128)(2,1)S(1)}, u32[]{:S(2)}, u32[]{:S(2)}) collective-permute-start(bf16[400,512]{1,0:T(8,128)(2,1)S(1)} %shard_map.53._), channel_id=1, source_target_pairs={{0,4},{12,8},{1,5},{13,9},{2,6},{14,10},{3,7},{15,11},{16,20},{28,... | collective-permute-start | bytes 1228808 | tf_op jit(solution)/shard_map/ppermute | solution.py:406
  36.2 3.9 %collective-permute-start.13 = (bf16[256,512]{1,0:T(8,128)(2,1)S(1)}, bf16[256,512]{1,0:T(8,128)(2,1)S(1)}, u32[]{:S(2)}, u32[]{:S(2)}) collective-permute-start(bf16[256,512]{1,0:T(8,128)(2,1)S(1)} %get-tuple-element.70._.refs_2_.refs_1_), channel_id=1, source_target_pairs={{0,1},{1,0},{2,3},{3,2},{4,5},{5,4},{6,7},{7,6},{8,9},{9,8},{10,11... | collective-permute-start | bytes 786440 | tf_op jit(solution)/shard_map/ppermute | solution.py:65
  36.3 8.4 %collective-permute-start.14 = (bf16[256,512]{1,0:T(8,128)(2,1)S(1)}, bf16[256,512]{1,0:T(8,128)(2,1)S(1)}, u32[]{:S(2)}, u32[]{:S(2)}) collective-permute-start(bf16[256,512]{1,0:T(8,128)(2,1)S(1)} %get-tuple-element.74.refs_3_.refs_2_), channel_id=1, source_target_pairs={{0,1},{1,0},{2,3},{3,2},{4,5},{5,4},{6,7},{7,6},{8,9},{9,8},{10,11... | collective-permute-start | bytes 786440 | tf_op jit(solution)/shard_map/ppermute | solution.py:65
  37.0 7.7 %collective-permute-start.15 = (bf16[256,512]{1,0:T(8,128)(2,1)S(1)}, bf16[256,512]{1,0:T(8,128)(2,1)S(1)}, u32[]{:S(2)}, u32[]{:S(2)}) collective-permute-start(bf16[256,512]{1,0:T(8,128)(2,1)S(1)} %get-tuple-element.75.refs_4_.refs_1_), channel_id=1, source_target_pairs={{0,1},{1,0},{2,3},{3,2},{4,5},{5,4},{6,7},{7,6},{8,9},{9,8},{10,11... | collective-permute-start | bytes 786440 | tf_op jit(solution)/shard_map/ppermute | solution.py:65
  40.0 4.7 %collective-permute-start.16 = (bf16[256,512]{1,0:T(8,128)(2,1)S(1)}, bf16[256,512]{1,0:T(8,128)(2,1)S(1)}, u32[]{:S(2)}, u32[]{:S(2)}) collective-permute-start(bf16[256,512]{1,0:T(8,128)(2,1)S(1)} %get-tuple-element.76.refs_5_.refs_2_), channel_id=1, source_target_pairs={{0,1},{1,0},{2,3},{3,2},{4,5},{5,4},{6,7},{7,6},{8,9},{9,8},{10,11... | collective-permute-start | bytes 786440 | tf_op jit(solution)/shard_map/ppermute | solution.py:65
  40.1 20.1 %collective-permute-start.19 = (bf16[400,512]{1,0:T(8,128)(2,1)S(1)}, bf16[400,512]{1,0:T(8,128)(2,1)S(1)}, u32[]{:S(2)}, u32[]{:S(2)}) collective-permute-start(bf16[400,512]{1,0:T(8,128)(2,1)S(1)} %shard_map.55._), channel_id=1, source_target_pairs={{0,4},{12,8},{1,5},{13,9},{2,6},{14,10},{3,7},{15,11},{16,20},{28,... | collective-permute-start | bytes 1228808 | tf_op jit(solution)/shard_map/ppermute | solution.py:406
  46.0 9.2 %collective-permute-start.17 = (bf16[256,512]{1,0:T(8,128)(2,1)S(1)}, bf16[256,512]{1,0:T(8,128)(2,1)S(1)}, u32[]{:S(2)}, u32[]{:S(2)}) collective-permute-start(bf16[256,512]{1,0:T(8,128)(2,1)S(1)} %get-tuple-element.78), channel_id=1, source_target_pairs={{0,2},{1,3},{2,0},{3,1},{4,6},{5,7},{6,4},{7,5},{8,10},{9,11},{10,... | collective-permute-start | bytes 786440 | tf_op jit(solution)/shard_map/ppermute | solution.py:61
  47.6 12.5 %collective-permute-start.18 = (bf16[256,512]{1,0:T(8,128)(2,1)S(1)}, bf16[256,512]{1,0:T(8,128)(2,1)S(1)}, u32[]{:S(2)}, u32[]{:S(2)}) collective-permute-start(bf16[256,512]{1,0:T(8,128)(2,1)S(1)} %get-tuple-element.80), channel_id=1, source_target_pairs={{0,2},{1,3},{2,0},{3,1},{4,6},{5,7},{6,4},{7,5},{8,10},{9,11},{10,... | collective-permute-start | bytes 786440 | tf_op jit(solution)/shard_map/ppermute | solution.py:61
  48.1 13.7 %collective-permute-start.21 = (bf16[400,512]{1,0:T(8,128)(2,1)S(1)}, bf16[400,512]{1,0:T(8,128)(2,1)S(1)}, u32[]{:S(2)}, u32[]{:S(2)}) collective-permute-start(bf16[400,512]{1,0:T(8,128)(2,1)S(1)} %shard_map.56._.refs_0_), channel_id=1, source_target_pairs={{4,8},{8,4},{5,9},{9,5},{6,10},{10,6},{7,11},{11,7},{20,24},{24,20... | collective-permute-start | bytes 1228808 | tf_op jit(solution)/shard_map/ppermute | solution.py:406
  55.3 6.7 %collective-permute-start.22 = (bf16[256,512]{1,0:T(8,128)(2,1)S(1)}, bf16[256,512]{1,0:T(8,128)(2,1)S(1)}, u32[]{:S(2)}, u32[]{:S(2)}) collective-permute-start(bf16[256,512]{1,0:T(8,128)(2,1)S(1)} %shard_map.58._), channel_id=1, source_target_pairs={{0,4},{12,8},{1,5},{13,9},{2,6},{14,10},{3,7},{15,11},{16,20},{28,... | collective-permute-start | bytes 786440 | tf_op jit(solution)/shard_map/ppermute | solution.py:406
  60.5 2.0 %collective-permute-start.23 = (bf16[256,512]{1,0:T(8,128)(2,1)S(1)}, bf16[256,512]{1,0:T(8,128)(2,1)S(1)}, u32[]{:S(2)}, u32[]{:S(2)}) collective-permute-start(bf16[256,512]{1,0:T(8,128)(2,1)S(1)} %get-tuple-element.82._.refs_2_.refs_1_), channel_id=1, source_target_pairs={{0,1},{1,0},{2,3},{3,2},{4,5},{5,4},{6,7},{7,6},{8,9},{9,8},{10,11... | collective-permute-start | bytes 786440 | tf_op jit(solution)/shard_map/ppermute | solution.py:65
  60.6 3.2 %collective-permute-start.24 = (bf16[256,512]{1,0:T(8,128)(2,1)S(1)}, bf16[256,512]{1,0:T(8,128)(2,1)S(1)}, u32[]{:S(2)}, u32[]{:S(2)}) collective-permute-start(bf16[256,512]{1,0:T(8,128)(2,1)S(1)} %get-tuple-element.84.refs_3_.refs_2_), channel_id=1, source_target_pairs={{0,1},{1,0},{2,3},{3,2},{4,5},{5,4},{6,7},{7,6},{8,9},{9,8},{10,11... | collective-permute-start | bytes 786440 | tf_op jit(solution)/shard_map/ppermute | solution.py:65
  61.1 12.8 %collective-permute-start.27 = (bf16[400,512]{1,0:T(8,128)(2,1)S(1)}, bf16[400,512]{1,0:T(8,128)(2,1)S(1)}, u32[]{:S(2)}, u32[]{:S(2)}) collective-permute-start(bf16[400,512]{1,0:T(8,128)(2,1)S(1)} %shard_map.60._.refs_0_), channel_id=1, source_target_pairs={{4,8},{8,4},{5,9},{9,5},{6,10},{10,6},{7,11},{11,7},{20,24},{24,20... | collective-permute-start | bytes 1228808 | tf_op jit(solution)/shard_map/ppermute | solution.py:406
  61.8 6.7 %collective-permute-start.25 = (bf16[256,512]{1,0:T(8,128)(2,1)S(1)}, bf16[256,512]{1,0:T(8,128)(2,1)S(1)}, u32[]{:S(2)}, u32[]{:S(2)}) collective-permute-start(bf16[256,512]{1,0:T(8,128)(2,1)S(1)} %get-tuple-element.85.refs_4_.refs_1_), channel_id=1, source_target_pairs={{0,1},{1,0},{2,3},{3,2},{4,5},{5,4},{6,7},{7,6},{8,9},{9,8},{10,11... | collective-permute-start | bytes 786440 | tf_op jit(solution)/shard_map/ppermute | solution.py:65
  61.9 7.4 %collective-permute-start.26 = (bf16[256,512]{1,0:T(8,128)(2,1)S(1)}, bf16[256,512]{1,0:T(8,128)(2,1)S(1)}, u32[]{:S(2)}, u32[]{:S(2)}) collective-permute-start(bf16[256,512]{1,0:T(8,128)(2,1)S(1)} %get-tuple-element.86.refs_5_.refs_2_), channel_id=1, source_target_pairs={{0,1},{1,0},{2,3},{3,2},{4,5},{5,4},{6,7},{7,6},{8,9},{9,8},{10,11... | collective-permute-start | bytes 786440 | tf_op jit(solution)/shard_map/ppermute | solution.py:65
  62.5 13.7 %collective-permute-start.29 = (bf16[400,512]{1,0:T(8,128)(2,1)S(1)}, bf16[400,512]{1,0:T(8,128)(2,1)S(1)}, u32[]{:S(2)}, u32[]{:S(2)}) collective-permute-start(bf16[400,512]{1,0:T(8,128)(2,1)S(1)} %shard_map.62._.refs_0_), channel_id=1, source_target_pairs={{4,0},{8,12},{5,1},{9,13},{6,2},{10,14},{7,3},{11,15},{20,16},{24,... | collective-permute-start | bytes 1228808 | tf_op jit(solution)/shard_map/ppermute | solution.py:406
  63.8 11.5 %collective-permute-start.28 = (bf16[256,512]{1,0:T(8,128)(2,1)S(1)}, bf16[256,512]{1,0:T(8,128)(2,1)S(1)}, u32[]{:S(2)}, u32[]{:S(2)}) collective-permute-start(bf16[256,512]{1,0:T(8,128)(2,1)S(1)} %shard_map.59._), channel_id=1, source_target_pairs={{0,4},{12,8},{1,5},{13,9},{2,6},{14,10},{3,7},{15,11},{16,20},{28,... | collective-permute-start | bytes 786440 | tf_op jit(solution)/shard_map/ppermute | solution.py:406
  68.5 9.0 %collective-permute-start.30 = (bf16[256,512]{1,0:T(8,128)(2,1)S(1)}, bf16[256,512]{1,0:T(8,128)(2,1)S(1)}, u32[]{:S(2)}, u32[]{:S(2)}) collective-permute-start(bf16[256,512]{1,0:T(8,128)(2,1)S(1)} %shard_map.63._.refs_0_), channel_id=1, source_target_pairs={{4,8},{8,4},{5,9},{9,5},{6,10},{10,6},{7,11},{11,7},{20,24},{24,20... | collective-permute-start | bytes 786440 | tf_op jit(solution)/shard_map/ppermute | solution.py:406
  70.7 8.3 %collective-permute-start.31 = (bf16[256,512]{1,0:T(8,128)(2,1)S(1)}, bf16[256,512]{1,0:T(8,128)(2,1)S(1)}, u32[]{:S(2)}, u32[]{:S(2)}) collective-permute-start(bf16[256,512]{1,0:T(8,128)(2,1)S(1)} %get-tuple-element.89), channel_id=1, source_target_pairs={{0,2},{1,3},{2,0},{3,1},{4,6},{5,7},{6,4},{7,5},{8,10},{9,11},{10,... | collective-permute-start | bytes 786440 | tf_op jit(solution)/shard_map/ppermute | solution.py:61
  74.0 16.5 %collective-permute-start.34 = (bf16[400,512]{1,0:T(8,128)(2,1)S(1)}, bf16[400,512]{1,0:T(8,128)(2,1)S(1)}, u32[]{:S(2)}, u32[]{:S(2)}) collective-permute-start(bf16[400,512]{1,0:T(8,128)(2,1)S(1)} %shard_map.66._.refs_0_), channel_id=1, source_target_pairs={{4,0},{8,12},{5,1},{9,13},{6,2},{10,14},{7,3},{11,15},{20,16},{24,... | collective-permute-start | bytes 1228808 | tf_op jit(solution)/shard_map/ppermute | solution.py:406
  75.5 8.9 %collective-permute-start.32 = (bf16[256,512]{1,0:T(8,128)(2,1)S(1)}, bf16[256,512]{1,0:T(8,128)(2,1)S(1)}, u32[]{:S(2)}, u32[]{:S(2)}) collective-permute-start(bf16[256,512]{1,0:T(8,128)(2,1)S(1)} %shard_map.67._.refs_0_), channel_id=1, source_target_pairs={{4,8},{8,4},{5,9},{9,5},{6,10},{10,6},{7,11},{11,7},{20,24},{24,20... | collective-permute-start | bytes 786440 | tf_op jit(solution)/shard_map/ppermute | solution.py:406
  76.2 8.2 %collective-permute-start.33 = (bf16[256,512]{1,0:T(8,128)(2,1)S(1)}, bf16[256,512]{1,0:T(8,128)(2,1)S(1)}, u32[]{:S(2)}, u32[]{:S(2)}) collective-permute-start(bf16[256,512]{1,0:T(8,128)(2,1)S(1)} %get-tuple-element.91), channel_id=1, source_target_pairs={{0,2},{1,3},{2,0},{3,1},{4,6},{5,7},{6,4},{7,5},{8,10},{9,11},{10,... | collective-permute-start | bytes 786440 | tf_op jit(solution)/shard_map/ppermute | solution.py:61
  79.0 11.6 %collective-permute-start.35 = (bf16[256,512]{1,0:T(8,128)(2,1)S(1)}, bf16[256,512]{1,0:T(8,128)(2,1)S(1)}, u32[]{:S(2)}, u32[]{:S(2)}) collective-permute-start(bf16[256,512]{1,0:T(8,128)(2,1)S(1)} %shard_map.70._), channel_id=1, source_target_pairs={{0,4},{12,8},{1,5},{13,9},{2,6},{14,10},{3,7},{15,11},{16,20},{28,... | collective-permute-start | bytes 786440 | tf_op jit(solution)/shard_map/ppermute | solution.py:406
  84.5 10.3 %collective-permute-start.36 = (bf16[272,512]{1,0:T(8,128)(2,1)S(1)}, bf16[272,512]{1,0:T(8,128)(2,1)S(1)}, u32[]{:S(2)}, u32[]{:S(2)}) collective-permute-start(bf16[272,512]{1,0:T(8,128)(2,1)S(1)} %shard_map.72._), channel_id=1, source_target_pairs={{0,4},{12,8},{1,5},{13,9},{2,6},{14,10},{3,7},{15,11},{16,20},{28,... | collective-permute-start | bytes 835592 | tf_op jit(solution)/shard_map/ppermute | solution.py:406
  90.7 4.9 %collective-permute-start.37 = (bf16[256,512]{1,0:T(8,128)(2,1)S(1)}, bf16[256,512]{1,0:T(8,128)(2,1)S(1)}, u32[]{:S(2)}, u32[]{:S(2)}) collective-permute-start(bf16[256,512]{1,0:T(8,128)(2,1)S(1)} %shard_map.74._.refs_0_), channel_id=1, source_target_pairs={{4,8},{8,4},{5,9},{9,5},{6,10},{10,6},{7,11},{11,7},{20,24},{24,20... | collective-permute-start | bytes 786440 | tf_op jit(solution)/shard_map/ppermute | solution.py:406
  91.4 14.4 %collective-permute-start.42 = (bf16[400,512]{1,0:T(8,128)(2,1)S(1)}, bf16[400,512]{1,0:T(8,128)(2,1)S(1)}, u32[]{:S(2)}, u32[]{:S(2)}) collective-permute-start(bf16[400,512]{1,0:T(8,128)(2,1)S(1)} %shard_map.68._.refs_5_), channel_id=1, source_target_pairs={{0,2},{1,3},{2,0},{3,1},{4,6},{5,7},{6,4},{7,5},{8,10},{9,11},{10,... | collective-permute-start | bytes 1228808 | tf_op jit(solution)/shard_map/ppermute | solution.py:61
  92.0 18.6 %collective-permute-start.45 = (bf16[400,512]{1,0:T(8,128)(2,1)S(1)}, bf16[400,512]{1,0:T(8,128)(2,1)S(1)}, u32[]{:S(2)}, u32[]{:S(2)}) collective-permute-start(bf16[400,512]{1,0:T(8,128)(2,1)S(1)} %shard_map.73._.refs_5_), channel_id=1, source_target_pairs={{0,2},{1,3},{2,0},{3,1},{4,6},{5,7},{6,4},{7,5},{8,10},{9,11},{10,... | collective-permute-start | bytes 1228808 | tf_op jit(solution)/shard_map/ppermute | solution.py:61
  93.5 11.1 %collective-permute-start.39 = (bf16[256,512]{1,0:T(8,128)(2,1)S(1)}, bf16[256,512]{1,0:T(8,128)(2,1)S(1)}, u32[]{:S(2)}, u32[]{:S(2)}) collective-permute-start(bf16[256,512]{1,0:T(8,128)(2,1)S(1)} %shard_map.69._.refs_0_), channel_id=1, source_target_pairs={{4,0},{8,12},{5,1},{9,13},{6,2},{10,14},{7,3},{11,15},{20,16},{24,... | collective-permute-start | bytes 786440 | tf_op jit(solution)/shard_map/ppermute | solution.py:406
  94.9 15.2 %collective-permute-start.41 = (bf16[272,512]{1,0:T(8,128)(2,1)S(1)}, bf16[272,512]{1,0:T(8,128)(2,1)S(1)}, u32[]{:S(2)}, u32[]{:S(2)}) collective-permute-start(bf16[272,512]{1,0:T(8,128)(2,1)S(1)} %shard_map.75._.refs_0_), channel_id=1, source_target_pairs={{4,8},{8,4},{5,9},{9,5},{6,10},{10,6},{7,11},{11,7},{20,24},{24,20... | collective-permute-start | bytes 835592 | tf_op jit(solution)/shard_map/ppermute | solution.py:406
  95.6 14.5 %collective-permute-start.38 = (bf16[256,512]{1,0:T(8,128)(2,1)S(1)}, bf16[256,512]{1,0:T(8,128)(2,1)S(1)}, u32[]{:S(2)}, u32[]{:S(2)}) collective-permute-start(bf16[256,512]{1,0:T(8,128)(2,1)S(1)} %shard_map.71._.refs_0_), channel_id=1, source_target_pairs={{4,0},{8,12},{5,1},{9,13},{6,2},{10,14},{7,3},{11,15},{20,16},{24,... | collective-permute-start | bytes 786440 | tf_op jit(solution)/shard_map/ppermute | solution.py:406
  104.6 8.4 %collective-permute-start.40 = (bf16[256,512]{1,0:T(8,128)(2,1)S(1)}, bf16[256,512]{1,0:T(8,128)(2,1)S(1)}, u32[]{:S(2)}, u32[]{:S(2)}) collective-permute-start(bf16[256,512]{1,0:T(8,128)(2,1)S(1)} %shard_map.76._.refs_0_), channel_id=1, source_target_pairs={{4,0},{8,12},{5,1},{9,13},{6,2},{10,14},{7,3},{11,15},{20,16},{24,... | collective-permute-start | bytes 786440 | tf_op jit(solution)/shard_map/ppermute | solution.py:406
  105.9 9.0 %collective-permute-start.43 = (bf16[400,512]{1,0:T(8,128)(2,1)S(1)}, bf16[400,512]{1,0:T(8,128)(2,1)S(1)}, u32[]{:S(2)}, u32[]{:S(2)}) collective-permute-start(bf16[400,512]{1,0:T(8,128)(2,1)S(1)} %shard_map.68._.refs_5_), channel_id=1, source_target_pairs={{0,1},{1,0},{2,3},{3,2},{4,5},{5,4},{6,7},{7,6},{8,9},{9,8},{10,11... | collective-permute-start | bytes 1228808 | tf_op jit(solution)/shard_map/ppermute | solution.py:65
  110.1 6.0 %collective-permute-start.44 = (bf16[400,512]{1,0:T(8,128)(2,1)S(1)}, bf16[400,512]{1,0:T(8,128)(2,1)S(1)}, u32[]{:S(2)}, u32[]{:S(2)}) collective-permute-start(bf16[400,512]{1,0:T(8,128)(2,1)S(1)} %collective-permute-done.42.refs_6_), channel_id=1, source_target_pairs={{0,1},{1,0},{2,3},{3,2},{4,5},{5,4},{6,7},{7,6},{8,9},{9,8},{10,11... | collective-permute-start | bytes 1228808 | tf_op jit(solution)/shard_map/ppermute | solution.py:65
  110.1 6.1 %collective-permute-start.46 = (bf16[400,512]{1,0:T(8,128)(2,1)S(1)}, bf16[400,512]{1,0:T(8,128)(2,1)S(1)}, u32[]{:S(2)}, u32[]{:S(2)}) collective-permute-start(bf16[400,512]{1,0:T(8,128)(2,1)S(1)} %shard_map.73._.refs_5_), channel_id=1, source_target_pairs={{0,1},{1,0},{2,3},{3,2},{4,5},{5,4},{6,7},{7,6},{8,9},{9,8},{10,11... | collective-permute-start | bytes 1228808 | tf_op jit(solution)/shard_map/ppermute | solution.py:65
  110.6 9.8 %collective-permute-start.47 = (bf16[400,512]{1,0:T(8,128)(2,1)S(1)}, bf16[400,512]{1,0:T(8,128)(2,1)S(1)}, u32[]{:S(2)}, u32[]{:S(2)}) collective-permute-start(bf16[400,512]{1,0:T(8,128)(2,1)S(1)} %collective-permute-done.45.refs_6_), channel_id=1, source_target_pairs={{0,1},{1,0},{2,3},{3,2},{4,5},{5,4},{6,7},{7,6},{8,9},{9,8},{10,11... | collective-permute-start | bytes 1228808 | tf_op jit(solution)/shard_map/ppermute | solution.py:65
  112.9 7.5 %collective-permute-start.49 = (bf16[256,512]{1,0:T(8,128)(2,1)S(1)}, bf16[256,512]{1,0:T(8,128)(2,1)S(1)}, u32[]{:S(2)}, u32[]{:S(2)}) collective-permute-start(bf16[256,512]{1,0:T(8,128)(2,1)S(1)} %shard_map.78._.refs_3_), channel_id=1, source_target_pairs={{0,2},{1,3},{2,0},{3,1},{4,6},{5,7},{6,4},{7,5},{8,10},{9,11},{10,... | collective-permute-start | bytes 786440 | tf_op jit(solution)/shard_map/ppermute | solution.py:61
  114.8 11.9 %collective-permute-start.48 = (bf16[272,512]{1,0:T(8,128)(2,1)S(1)}, bf16[272,512]{1,0:T(8,128)(2,1)S(1)}, u32[]{:S(2)}, u32[]{:S(2)}) collective-permute-start(bf16[272,512]{1,0:T(8,128)(2,1)S(1)} %shard_map.80._.refs_0_), channel_id=1, source_target_pairs={{4,0},{8,12},{5,1},{9,13},{6,2},{10,14},{7,3},{11,15},{20,16},{24,... | collective-permute-start | bytes 835592 | tf_op jit(solution)/shard_map/ppermute | solution.py:406
  116.1 11.0 %collective-permute-start.50 = (bf16[256,512]{1,0:T(8,128)(2,1)S(1)}, bf16[256,512]{1,0:T(8,128)(2,1)S(1)}, u32[]{:S(2)}, u32[]{:S(2)}) collective-permute-start(bf16[256,512]{1,0:T(8,128)(2,1)S(1)} %shard_map.78._.refs_3_), channel_id=1, source_target_pairs={{0,1},{1,0},{2,3},{3,2},{4,5},{5,4},{6,7},{7,6},{8,9},{9,8},{10,11... | collective-permute-start | bytes 786440 | tf_op jit(solution)/shard_map/ppermute | solution.py:65
  116.2 11.2 %collective-permute-start.52 = (bf16[256,512]{1,0:T(8,128)(2,1)S(1)}, bf16[256,512]{1,0:T(8,128)(2,1)S(1)}, u32[]{:S(2)}, u32[]{:S(2)}) collective-permute-start(bf16[256,512]{1,0:T(8,128)(2,1)S(1)} %shard_map.77._.refs_3_), channel_id=1, source_target_pairs={{0,2},{1,3},{2,0},{3,1},{4,6},{5,7},{6,4},{7,5},{8,10},{9,11},{10,... | collective-permute-start | bytes 786440 | tf_op jit(solution)/shard_map/ppermute | solution.py:61
  120.4 7.3 %collective-permute-start.51 = (bf16[256,512]{1,0:T(8,128)(2,1)S(1)}, bf16[256,512]{1,0:T(8,128)(2,1)S(1)}, u32[]{:S(2)}, u32[]{:S(2)}) collective-permute-start(bf16[256,512]{1,0:T(8,128)(2,1)S(1)} %collective-permute-done.49.refs_4_), channel_id=1, source_target_pairs={{0,1},{1,0},{2,3},{3,2},{4,5},{5,4},{6,7},{7,6},{8,9},{9,8},{10,11... | collective-permute-start | bytes 786440 | tf_op jit(solution)/shard_map/ppermute | solution.py:65
  120.4 10.7 %collective-permute-start.55 = (bf16[256,512]{1,0:T(8,128)(2,1)S(1)}, bf16[256,512]{1,0:T(8,128)(2,1)S(1)}, u32[]{:S(2)}, u32[]{:S(2)}) collective-permute-start(bf16[256,512]{1,0:T(8,128)(2,1)S(1)} %shard_map.79._.refs_3_), channel_id=1, source_target_pairs={{0,2},{1,3},{2,0},{3,1},{4,6},{5,7},{6,4},{7,5},{8,10},{9,11},{10,... | collective-permute-start | bytes 786440 | tf_op jit(solution)/shard_map/ppermute | solution.py:61
  127.0 10.8 %collective-permute-start.58 = (bf16[272,512]{1,0:T(8,128)(2,1)S(1)}, bf16[272,512]{1,0:T(8,128)(2,1)S(1)}, u32[]{:S(2)}, u32[]{:S(2)}) collective-permute-start(bf16[272,512]{1,0:T(8,128)(2,1)S(1)} %shard_map.83._.refs_5_.refs_3_), channel_id=1, source_target_pairs={{0,2},{1,3},{2,0},{3,1},{4,6},{5,7},{6,4},{7,5},{8,10},{9,11},{10,... | collective-permute-start | bytes 835592 | tf_op jit(solution)/shard_map/ppermute | solution.py:61
  127.1 5.2 %collective-permute-start.53 = (bf16[256,512]{1,0:T(8,128)(2,1)S(1)}, bf16[256,512]{1,0:T(8,128)(2,1)S(1)}, u32[]{:S(2)}, u32[]{:S(2)}) collective-permute-start(bf16[256,512]{1,0:T(8,128)(2,1)S(1)} %shard_map.77._.refs_3_), channel_id=1, source_target_pairs={{0,1},{1,0},{2,3},{3,2},{4,5},{5,4},{6,7},{7,6},{8,9},{9,8},{10,11... | collective-permute-start | bytes 786440 | tf_op jit(solution)/shard_map/ppermute | solution.py:65
  127.4 5.5 %collective-permute-start.54 = (bf16[256,512]{1,0:T(8,128)(2,1)S(1)}, bf16[256,512]{1,0:T(8,128)(2,1)S(1)}, u32[]{:S(2)}, u32[]{:S(2)}) collective-permute-start(bf16[256,512]{1,0:T(8,128)(2,1)S(1)} %collective-permute-done.52.refs_4_), channel_id=1, source_target_pairs={{0,1},{1,0},{2,3},{3,2},{4,5},{5,4},{6,7},{7,6},{8,9},{9,8},{10,11... | collective-permute-start | bytes 786440 | tf_op jit(solution)/shard_map/ppermute | solution.py:65
  127.7 7.3 %collective-permute-start.56 = (bf16[256,512]{1,0:T(8,128)(2,1)S(1)}, bf16[256,512]{1,0:T(8,128)(2,1)S(1)}, u32[]{:S(2)}, u32[]{:S(2)}) collective-permute-start(bf16[256,512]{1,0:T(8,128)(2,1)S(1)} %shard_map.79._.refs_3_), channel_id=1, source_target_pairs={{0,1},{1,0},{2,3},{3,2},{4,5},{5,4},{6,7},{7,6},{8,9},{9,8},{10,11... | collective-permute-start | bytes 786440 | tf_op jit(solution)/shard_map/ppermute | solution.py:65
  131.1 3.9 %collective-permute-start.57 = (bf16[256,512]{1,0:T(8,128)(2,1)S(1)}, bf16[256,512]{1,0:T(8,128)(2,1)S(1)}, u32[]{:S(2)}, u32[]{:S(2)}) collective-permute-start(bf16[256,512]{1,0:T(8,128)(2,1)S(1)} %collective-permute-done.55.refs_4_), channel_id=1, source_target_pairs={{0,1},{1,0},{2,3},{3,2},{4,5},{5,4},{6,7},{7,6},{8,9},{9,8},{10,11... | collective-permute-start | bytes 786440 | tf_op jit(solution)/shard_map/ppermute | solution.py:65
  132.4 5.5 %collective-permute-start.59 = (bf16[272,512]{1,0:T(8,128)(2,1)S(1)}, bf16[272,512]{1,0:T(8,128)(2,1)S(1)}, u32[]{:S(2)}, u32[]{:S(2)}) collective-permute-start(bf16[272,512]{1,0:T(8,128)(2,1)S(1)} %shard_map.83._.refs_5_.refs_3_), channel_id=1, source_target_pairs={{0,1},{1,0},{2,3},{3,2},{4,5},{5,4},{6,7},{7,6},{8,9},{9,8},{10,11... | collective-permute-start | bytes 835592 | tf_op jit(solution)/shard_map/ppermute | solution.py:65
  137.9 1.6 %collective-permute-start.60 = (bf16[272,512]{1,0:T(8,128)(2,1)S(1)}, bf16[272,512]{1,0:T(8,128)(2,1)S(1)}, u32[]{:S(2)}, u32[]{:S(2)}) collective-permute-start(bf16[272,512]{1,0:T(8,128)(2,1)S(1)} %collective-permute-done.58.refs_6_.refs_4_), channel_id=1, source_target_pairs={{0,1},{1,0},{2,3},{3,2},{4,5},{5,4},{6,7},{7,6},{8,9},{9,8},{10,11... | collective-permute-start | bytes 835592 | tf_op jit(solution)/shard_map/ppermute | solution.py:65
  139.5 3.6 %collective-permute-start.61 = (f32[1,512]{1,0:T(1,128)S(1)}, f32[1,512]{1,0:T(1,128)S(1)}, u32[]{:S(2)}, u32[]{:S(2)}) collective-permute-start(f32[1,512]{1,0:T(1,128)S(1)} %get-tuple-element.105._), channel_id=1, source_target_pairs={{0,16},{16,0},{1,17},{17,1},{2,18},{18,2},{3,19},{19,3},{4,20},{20... | collective-permute-start | bytes 6152 | tf_op jit(solution)/shard_map/ppermute | solution.py:65
  (3 other events, 4.0 us)

commit v6 on v5

--- a/solution.py
+++ b/solution.py
@@ -42,7 +42,7 @@
             in_specs=specs,
             out_specs=[VMEM] * len(outs),
             scratch_shapes=scratch,
-            compiler_params=pltpu.CompilerParams(vmem_limit_bytes=(size // MIB + 4) * MIB),
+            compiler_params=pltpu.CompilerParams(vmem_limit_bytes=(size // MIB + 2) * MIB),
             cost_estimate=pl.CostEstimate(flops=1, bytes_accessed=1, transcendentals=0),
         )(*ins)
         self.last = outs[0]

time: 144 us -> 144 us (level)
  no operation moved by 1% of the time
where the time goes in v6:
time: 144 us
  starting transfers between devices  63.4 us (44%)
  waiting for transfers between devices  50.6 us (35%)
  Pallas kernels  23.9 us (17%)
  local copies, waits for them, and re-layouts  4.04 us (3%)
    ppermute x18, starting transfers between devices, send_row(): lax.ppermute(value, 'row', [(g + a, g + b) for g in groups for a, b in pa...  37.1 us
    ppermute x12, waiting for transfers between devices, shift(): return lax.ppermute(value, axis, pairs)  24.2 us
    pallas_call x39, Pallas kernels, __call__(): pl.pallas_call(body, out_shape=outs, in_specs=specs, out_specs=[VMEM] * l...  23.4 us
    ppermute x18, waiting for transfers between devices, send_row(): lax.ppermute(value, 'row', [(g + a, g + b) for g in groups for a, b in pa...  16.9 us
    ppermute x12, starting transfers between devices, shift(): return lax.ppermute(value, axis, pairs)  13.9 us
    ppermute x32, starting transfers between devices, partner_of(): lax.ppermute(value, axis, [(index, index ^ bit) for index in range(lax.ax...  12.4 us
    ppermute x32, waiting for transfers between devices, partner_of(): lax.ppermute(value, axis, [(index, index ^ bit) for index in range(lax.ax...  9.38 us
    unnamed x10, local copies, waits for them, and re-layouts  4.04 us
  transfers between devices with their start and end apart: 62, of which 20 were waited for; matrix products, arithmetic and copies ran while one was open for 0% of the time, Pallas kernels for 15%

profile of v6, /device:TPU:0, one launch (start us, length us, event | category | flops | bytes accessed | tf_op | source)
XLA Modules:
  0.0 143.8 jit_solution(13558025602445792853)
XLA Ops:
  0.6 1.2 copy-done
  1.9 1.2 copy-done.2
  3.1 0.6 shard_map.49
  3.7 3.0 %collective-permute-start = (f32[2,512]{1,0:T(2,128)S(1)}, f32[2,512]{1,0:T(2,128)S(1)}, u32[]{:S(2)}, u32[]{:S(2)}) collective-permute-start(f32[2,512]{1,0:T(2,128)S(1)} %shard_map.49), channel_id=1, source_target_pairs={{0,16},{16,0},{1,17},{17,1},{2,18},{18,2},{3,19},{19,3},{4,20},{20... | collective-permute-start | bytes 12296 | tf_op jit(solution)/shard_map/ppermute | solution.py:65
  6.7 1.6 %collective-permute-done = f32[2,512]{1,0:T(2,128)S(1)} collective-permute-done((f32[2,512]{1,0:T(2,128)S(1)}, f32[2,512]{1,0:T(2,128)S(1)}, u32[]{:S(2)}, u32[]{:S(2)}) %collective-permute-start) | collective-permute-done | bytes 4128 | tf_op jit(solution)/shard_map/ppermute | solution.py:65
  8.3 1.6 %shard_map.50 = (f32[8,512]{1,0:T(8,128)S(1)}, bf16[256,512]{1,0:T(8,128)(2,1)S(1)}, bf16[256,512]{1,0:T(8,128)(2,1)S(1)}, bf16[256,512]{1,0:T(8,128)(2,1)S(1)},...) custom-call(bf16[1024,512]{1,0:T(8,128)(2,1)S(1)} %copy-done.1, ...), custom_call_target="tpu_custom_call" | custom-call | flops 1 | bytes 1 | tf_op jit(solution)/shard_map/pallas_call | solution.py:39
  9.9 2.1 %collective-permute-start.10 = (bf16[1024,512]{1,0:T(8,128)(2,1)S(1)}, bf16[1024,512]{1,0:T(8,128)(2,1)S(1)}, u32[]{:S(2)}, u32[]{:S(2)}) collective-permute-start(bf16[1024,512]{1,0:T(8,128)(2,1)S(1)} %copy-done.1), channel_id=1, source_target_pairs={{0,16},{16,0},{1,17},{17,1},{2,18},{18,2},{3,19},{19,3},{4,20},{20... | collective-permute-start | bytes 3145736 | tf_op jit(solution)/shard_map/ppermute | solution.py:65
  13.1 0.5 collective-permute-done.2.refs_5_
  14.3 2.3 %shard_map.51 = (bf16[1024,512]{1,0:T(8,128)(2,1)S(1)}, bf16[1024,512]{1,0:T(8,128)(2,1)S(1)}, f32[400,512]{1,0:T(8,128)S(1)}, bf16[400,512]{1,0:T(8,128)(2,1)S(1)}) custom-call(f32[8,512]{1,0:T(8,128)S(1)} %get-tuple-element.56._.refs_0_, bf16[256,512]{1,0:T(8,128)(2,1)S(1)} %get-tuple-element.57.refs_0_, bf16[256,512]{1,0:T(8,128)(2,1)S(1)} %get-tuple-element.58.refs_1_, ...), custom_call_target="tpu_custom_call" | custom-call | flops 1 | bytes 1 | tf_op jit(solution)/shard_map/pallas_call | solution.py:39
  16.6 1.6 %collective-permute-start.9 = (bf16[400,512]{1,0:T(8,128)(2,1)S(1)}, bf16[400,512]{1,0:T(8,128)(2,1)S(1)}, u32[]{:S(2)}, u32[]{:S(2)}) collective-permute-start(bf16[400,512]{1,0:T(8,128)(2,1)S(1)} %get-tuple-element.68), channel_id=1, source_target_pairs={{0,2},{1,3},{2,0},{3,1},{4,6},{5,7},{6,4},{7,5},{8,10},{9,11},{10,... | collective-permute-start | bytes 1228808 | tf_op jit(solution)/shard_map/ppermute | solution.py:61
  18.2 0.5 collective-permute-start.7
  18.7 1.0 collective-permute-done.6.refs_5_
  20.5 2.3 %shard_map.52 = (bf16[1024,512]{1,0:T(8,128)(2,1)S(1)}, bf16[1024,512]{1,0:T(8,128)(2,1)S(1)}, f32[400,512]{1,0:T(8,128)S(1)}, bf16[400,512]{1,0:T(8,128)(2,1)S(1)}) custom-call(bf16[1024,512]{1,0:T(8,128)(2,1)S(1)} %get-tuple-element.61._.refs_0_, bf16[256,512]{1,0:T(8,128)(2,1)S(1)} %get-tuple-element.62.refs_0_, ...), custom_call_target="tpu_custom_call" | custom-call | flops 1 | bytes 1 | tf_op jit(solution)/shard_map/pallas_call | solution.py:39
  22.8 0.6 collective-permute-start.11
  23.3 5.6 %collective-permute-done.9.refs_1_ = bf16[400,512]{1,0:T(8,128)(2,1)S(1)} collective-permute-done((bf16[400,512]{1,0:T(8,128)(2,1)S(1)}, bf16[400,512]{1,0:T(8,128)(2,1)S(1)}, u32[]{:S(2)}, u32[]{:S(2)}) %collective-permute-start.9) | collective-permute-done | bytes 409632 | tf_op jit(solution)/shard_map/ppermute | solution.py:61
  29.1 3.5 %collective-permute-start.12 = (bf16[400,512]{1,0:T(8,128)(2,1)S(1)}, bf16[400,512]{1,0:T(8,128)(2,1)S(1)}, u32[]{:S(2)}, u32[]{:S(2)}) collective-permute-start(bf16[400,512]{1,0:T(8,128)(2,1)S(1)} %shard_map.53._), channel_id=1, source_target_pairs={{0,4},{12,8},{1,5},{13,9},{2,6},{14,10},{3,7},{15,11},{16,20},{28,... | collective-permute-start | bytes 1228808 | tf_op jit(solution)/shard_map/ppermute | solution.py:406
  32.6 3.4 %collective-permute-done.10.refs_0_.refs_2_ = bf16[1024,512]{1,0:T(8,128)(2,1)S(1)} collective-permute-done((bf16[1024,512]{1,0:T(8,128)(2,1)S(1)}, bf16[1024,512]{1,0:T(8,128)(2,1)S(1)}, u32[]{:S(2)}, u32[]{:S(2)}) %collective-permute-start.10) | collective-permute-done | bytes 1048608 | tf_op jit(solution)/shard_map/ppermute | solution.py:65
  37.0 3.0 %collective-permute-done.12.refs_2_ = bf16[400,512]{1,0:T(8,128)(2,1)S(1)} collective-permute-done((bf16[400,512]{1,0:T(8,128)(2,1)S(1)}, bf16[400,512]{1,0:T(8,128)(2,1)S(1)}, u32[]{:S(2)}, u32[]{:S(2)}) %collective-permute-start.12) | collective-permute-done | bytes 409632 | tf_op jit(solution)/shard_map/ppermute | solution.py:406
  40.1 4.4 %collective-permute-start.19 = (bf16[400,512]{1,0:T(8,128)(2,1)S(1)}, bf16[400,512]{1,0:T(8,128)(2,1)S(1)}, u32[]{:S(2)}, u32[]{:S(2)}) collective-permute-start(bf16[400,512]{1,0:T(8,128)(2,1)S(1)} %shard_map.55._), channel_id=1, source_target_pairs={{0,4},{12,8},{1,5},{13,9},{2,6},{14,10},{3,7},{15,11},{16,20},{28,... | collective-permute-start | bytes 1228808 | tf_op jit(solution)/shard_map/ppermute | solution.py:406
  44.7 1.3 shard_map.57
  46.0 1.6 %collective-permute-start.17 = (bf16[256,512]{1,0:T(8,128)(2,1)S(1)}, bf16[256,512]{1,0:T(8,128)(2,1)S(1)}, u32[]{:S(2)}, u32[]{:S(2)}) collective-permute-start(bf16[256,512]{1,0:T(8,128)(2,1)S(1)} %get-tuple-element.78), channel_id=1, source_target_pairs={{0,2},{1,3},{2,0},{3,1},{4,6},{5,7},{6,4},{7,5},{8,10},{9,11},{10,... | collective-permute-start | bytes 786440 | tf_op jit(solution)/shard_map/ppermute | solution.py:61
  48.1 0.7 collective-permute-start.21
  48.8 6.4 %collective-permute-done.17.refs_1_ = bf16[256,512]{1,0:T(8,128)(2,1)S(1)} collective-permute-done((bf16[256,512]{1,0:T(8,128)(2,1)S(1)}, bf16[256,512]{1,0:T(8,128)(2,1)S(1)}, u32[]{:S(2)}, u32[]{:S(2)}) %collective-permute-start.17) | collective-permute-done | bytes 262176 | tf_op jit(solution)/shard_map/ppermute | solution.py:61
  55.3 1.3 collective-permute-start.22
  56.6 3.5 %collective-permute-done.18.refs_1_ = bf16[256,512]{1,0:T(8,128)(2,1)S(1)} collective-permute-done((bf16[256,512]{1,0:T(8,128)(2,1)S(1)}, bf16[256,512]{1,0:T(8,128)(2,1)S(1)}, u32[]{:S(2)}, u32[]{:S(2)}) %collective-permute-start.18) | collective-permute-done | bytes 262176 | tf_op jit(solution)/shard_map/ppermute | solution.py:61
  61.1 0.7 collective-permute-start.27
  62.5 1.3 collective-permute-start.29
  63.8 4.6 %collective-permute-start.28 = (bf16[256,512]{1,0:T(8,128)(2,1)S(1)}, bf16[256,512]{1,0:T(8,128)(2,1)S(1)}, u32[]{:S(2)}, u32[]{:S(2)}) collective-permute-start(bf16[256,512]{1,0:T(8,128)(2,1)S(1)} %shard_map.59._), channel_id=1, source_target_pairs={{0,4},{12,8},{1,5},{13,9},{2,6},{14,10},{3,7},{15,11},{16,20},{28,... | collective-permute-start | bytes 786440 | tf_op jit(solution)/shard_map/ppermute | solution.py:406
  68.5 0.9 collective-permute-start.30
  69.4 1.3 shard_map.64
  70.7 1.6 %collective-permute-start.31 = (bf16[256,512]{1,0:T(8,128)(2,1)S(1)}, bf16[256,512]{1,0:T(8,128)(2,1)S(1)}, u32[]{:S(2)}, u32[]{:S(2)}) collective-permute-start(bf16[256,512]{1,0:T(8,128)(2,1)S(1)} %get-tuple-element.89), channel_id=1, source_target_pairs={{0,2},{1,3},{2,0},{3,1},{4,6},{5,7},{6,4},{7,5},{8,10},{9,11},{10,... | collective-permute-start | bytes 786440 | tf_op jit(solution)/shard_map/ppermute | solution.py:61
  72.3 1.7 %shard_map.65 = (f32[8,512]{1,0:T(8,128)S(1)}, f32[1,512]{1,0:T(1,128)S(1)}) custom-call(f32[256,512]{1,0:T(8,128)S(1)} %get-tuple-element.87._.refs_0_, f32[8,512]{1,0:T(8,128)S(1)} %get-tuple-element.56._.refs_0_, f32[2,512]{1,0:T(2,128)S(1)} %add.9.sums.refs_1_.refs_3_, bf16[1024,512]{1,0:T(8,128)(2,1)S(1)} %collective-permute-done.10.refs_0_.refs_2_, ...), custom_call_target="tpu_custom_call" | custom-call | flops 1 | bytes 1 | tf_op jit(solution)/shard_map/pallas_call | solution.py:39
  74.0 1.3 collective-permute-start.34
  75.5 0.7 collective-permute-start.32
  76.2 1.3 collective-permute-start.33
  77.6 1.4 collective-permute-done.31.refs_1_
  79.0 5.3 %collective-permute-start.35 = (bf16[256,512]{1,0:T(8,128)(2,1)S(1)}, bf16[256,512]{1,0:T(8,128)(2,1)S(1)}, u32[]{:S(2)}, u32[]{:S(2)}) collective-permute-start(bf16[256,512]{1,0:T(8,128)(2,1)S(1)} %shard_map.70._), channel_id=1, source_target_pairs={{0,4},{12,8},{1,5},{13,9},{2,6},{14,10},{3,7},{15,11},{16,20},{28,... | collective-permute-start | bytes 786440 | tf_op jit(solution)/shard_map/ppermute | solution.py:406
  84.5 6.1 %collective-permute-start.36 = (bf16[272,512]{1,0:T(8,128)(2,1)S(1)}, bf16[272,512]{1,0:T(8,128)(2,1)S(1)}, u32[]{:S(2)}, u32[]{:S(2)}) collective-permute-start(bf16[272,512]{1,0:T(8,128)(2,1)S(1)} %shard_map.72._), channel_id=1, source_target_pairs={{0,4},{12,8},{1,5},{13,9},{2,6},{14,10},{3,7},{15,11},{16,20},{28,... | collective-permute-start | bytes 835592 | tf_op jit(solution)/shard_map/ppermute | solution.py:406
  90.7 0.7 collective-permute-start.37
  91.4 0.6 collective-permute-start.42
  92.0 1.5 %collective-permute-start.45 = (bf16[400,512]{1,0:T(8,128)(2,1)S(1)}, bf16[400,512]{1,0:T(8,128)(2,1)S(1)}, u32[]{:S(2)}, u32[]{:S(2)}) collective-permute-start(bf16[400,512]{1,0:T(8,128)(2,1)S(1)} %shard_map.73._.refs_5_), channel_id=1, source_target_pairs={{0,2},{1,3},{2,0},{3,1},{4,6},{5,7},{6,4},{7,5},{8,10},{9,11},{10,... | collective-permute-start | bytes 1228808 | tf_op jit(solution)/shard_map/ppermute | solution.py:61
  93.5 1.3 collective-permute-start.39
  94.9 0.7 collective-permute-start.41
  95.6 1.3 collective-permute-start.38
  97.0 7.6 %collective-permute-done.39.refs_1_ = bf16[256,512]{1,0:T(8,128)(2,1)S(1)} collective-permute-done((bf16[256,512]{1,0:T(8,128)(2,1)S(1)}, bf16[256,512]{1,0:T(8,128)(2,1)S(1)}, u32[]{:S(2)}, u32[]{:S(2)}) %collective-permute-start.39) | collective-permute-done | bytes 262176 | tf_op jit(solution)/shard_map/ppermute | solution.py:406
  104.6 1.3 collective-permute-start.40
  105.9 4.2 %collective-permute-done.38.refs_1_ = bf16[256,512]{1,0:T(8,128)(2,1)S(1)} collective-permute-done((bf16[256,512]{1,0:T(8,128)(2,1)S(1)}, bf16[256,512]{1,0:T(8,128)(2,1)S(1)}, u32[]{:S(2)}, u32[]{:S(2)}) %collective-permute-start.38) | collective-permute-done | bytes 262176 | tf_op jit(solution)/shard_map/ppermute | solution.py:406
  110.1 0.5 collective-permute-start.46
  110.8 2.2 %collective-permute-done.40.refs_1_ = bf16[256,512]{1,0:T(8,128)(2,1)S(1)} collective-permute-done((bf16[256,512]{1,0:T(8,128)(2,1)S(1)}, bf16[256,512]{1,0:T(8,128)(2,1)S(1)}, u32[]{:S(2)}, u32[]{:S(2)}) %collective-permute-start.40) | collective-permute-done | bytes 262176 | tf_op jit(solution)/shard_map/ppermute | solution.py:406
  112.9 1.8 %collective-permute-start.49 = (bf16[256,512]{1,0:T(8,128)(2,1)S(1)}, bf16[256,512]{1,0:T(8,128)(2,1)S(1)}, u32[]{:S(2)}, u32[]{:S(2)}) collective-permute-start(bf16[256,512]{1,0:T(8,128)(2,1)S(1)} %shard_map.78._.refs_3_), channel_id=1, source_target_pairs={{0,2},{1,3},{2,0},{3,1},{4,6},{5,7},{6,4},{7,5},{8,10},{9,11},{10,... | collective-permute-start | bytes 786440 | tf_op jit(solution)/shard_map/ppermute | solution.py:61
  114.8 1.3 collective-permute-start.48
  116.5 3.9 %collective-permute-done.49.refs_4_ = bf16[256,512]{1,0:T(8,128)(2,1)S(1)} collective-permute-done((bf16[256,512]{1,0:T(8,128)(2,1)S(1)}, bf16[256,512]{1,0:T(8,128)(2,1)S(1)}, u32[]{:S(2)}, u32[]{:S(2)}) %collective-permute-start.49) | collective-permute-done | bytes 262176 | tf_op jit(solution)/shard_map/ppermute | solution.py:61
  120.4 2.5 %collective-permute-start.55 = (bf16[256,512]{1,0:T(8,128)(2,1)S(1)}, bf16[256,512]{1,0:T(8,128)(2,1)S(1)}, u32[]{:S(2)}, u32[]{:S(2)}) collective-permute-start(bf16[256,512]{1,0:T(8,128)(2,1)S(1)} %shard_map.79._.refs_3_), channel_id=1, source_target_pairs={{0,2},{1,3},{2,0},{3,1},{4,6},{5,7},{6,4},{7,5},{8,10},{9,11},{10,... | collective-permute-start | bytes 786440 | tf_op jit(solution)/shard_map/ppermute | solution.py:61
  122.9 1.9 %shard_map.81 = (f32[1024,512]{1,0:T(8,128)S(1)}, f32[1,512]{1,0:T(1,128)S(1)}) custom-call(bf16[272,512]{1,0:T(8,128)(2,1)S(1)} %shard_map.80._.refs_0_, bf16[1024,512]{1,0:T(8,128)(2,1)S(1)} %get-tuple-element.61._.refs_0_, bf16[1024,512]{1,0:T(8,128)(2,1)S(1)} %copy-done.1, bf16[1024,512]{1,0:T(8,128)(2,1)S(1)} %copy-done.3, ...), custom_call_target="tpu_custom_call" | custom-call | flops 1 | bytes 1 | tf_op jit(solution)/shard_map/pallas_call | solution.py:39
  124.8 1.9 %shard_map.82 = (f32[1024,512]{1,0:T(8,128)S(1)}, f32[1,512]{1,0:T(1,128)S(1)}) custom-call(f32[1024,512]{1,0:T(8,128)S(1)} %get-tuple-element.93._.refs_0_, bf16[1024,512]{1,0:T(8,128)(2,1)S(1)} %get-tuple-element.66._.refs_0_, bf16[1024,512]{1,0:T(8,128)(2,1)S(1)} %copy-done.1, bf16[1024,512]{1,0:T(8,128)(2,1)S(1)} %copy-done.3, ...), custom_call_target="tpu_custom_call" | custom-call | flops 1 | bytes 1 | tf_op jit(solution)/shard_map/pallas_call | solution.py:39
  127.9 3.2 %collective-permute-done.55.refs_4_ = bf16[256,512]{1,0:T(8,128)(2,1)S(1)} collective-permute-done((bf16[256,512]{1,0:T(8,128)(2,1)S(1)}, bf16[256,512]{1,0:T(8,128)(2,1)S(1)}, u32[]{:S(2)}, u32[]{:S(2)}) %collective-permute-start.55) | collective-permute-done | bytes 262176 | tf_op jit(solution)/shard_map/ppermute | solution.py:61
  131.1 1.3 shard_map.84
  132.9 2.1 %shard_map.85 = (f32[1024,512]{1,0:T(8,128)}, f32[1,512]{1,0:T(1,128)S(1)}, f32[1,512]{1,0:T(1,128)}) custom-call(f32[1024,512]{1,0:T(8,128)S(1)} %get-tuple-element.95._.refs_0_, f32[1024,512]{1,0:T(8,128)S(1)} %get-tuple-element.95._.refs_0_, bf16[256,512]{1,0:T(8,128)(2,1)S(1)} %get-tuple-element.75.refs_4_.refs_1_, ...), custom_call_target="tpu_custom_call" | custom-call | flops 1 | bytes 1 | tf_op jit(solution)/shard_map/pallas_call | solution.py:39
  135.0 1.6 %copy-done.4 = f32[1024,512]{1,0:T(8,128)S(1)} copy-done((f32[1024,512]{1,0:T(8,128)S(1)}, f32[1024,512]{1,0:T(8,128)}, u32[]{:S(2)}) %copy-start.4) | copy-done | bytes 2097176
  136.6 1.3 shard_map.86
  137.9 1.5 %collective-permute-done.60.refs_8_.refs_6_ = bf16[272,512]{1,0:T(8,128)(2,1)S(1)} collective-permute-done((bf16[272,512]{1,0:T(8,128)(2,1)S(1)}, bf16[272,512]{1,0:T(8,128)(2,1)S(1)}, u32[]{:S(2)}, u32[]{:S(2)}) %collective-permute-start.60) | collective-permute-done | bytes 278560 | tf_op jit(solution)/shard_map/ppermute | solution.py:65
  139.5 1.4 collective-permute-start.61
  140.9 2.0 %shard_map.88 = f32[1024,512]{1,0:T(8,128)} custom-call(f32[1,512]{1,0:T(1,128)S(1)} %get-tuple-element.105._, f32[1024,512]{1,0:T(8,128)S(1)} %get-tuple-element.106._.refs_0_, bf16[256,512]{1,0:T(8,128)(2,1)S(1)} %get-tuple-element.85.refs_4_.refs_1_, bf16[256,512]{1,0:T(8,128)(2,1)S(1)} %get-tuple-element.86.refs_5_.refs_2_, ...), custom_call_target="tpu_custom_call" | custom-call | flops 1 | bytes 1 | tf_op jit(solution)/shard_map/pallas_call | solution.py:39
  143.2 0.6 add_reduce_fusion
  (112 shorter events, 9.7 us)
Async XLA Ops:
  3.1 5.2 %copy-start.1 = (bf16[1024,512]{1,0:T(8,128)(2,1)S(1)}, bf16[1024,512]{1,0:T(8,128)(2,1)}, u32[]{:S(2)}) copy-start(bf16[1024,512]{1,0:T(8,128)(2,1)} %refs_1_.3) | copy-start | bytes 3145732
  3.1 5.2 %copy-start.3 = (bf16[1024,512]{1,0:T(8,128)(2,1)S(1)}, bf16[1024,512]{1,0:T(8,128)(2,1)}, u32[]{:S(2)}) copy-start(bf16[1024,512]{1,0:T(8,128)(2,1)} %refs_2_.3) | copy-start | bytes 3145732
  3.7 4.6 %collective-permute-start = (f32[2,512]{1,0:T(2,128)S(1)}, f32[2,512]{1,0:T(2,128)S(1)}, u32[]{:S(2)}, u32[]{:S(2)}) collective-permute-start(f32[2,512]{1,0:T(2,128)S(1)} %shard_map.49), channel_id=1, source_target_pairs={{0,16},{16,0},{1,17},{17,1},{2,18},{18,2},{3,19},{19,3},{4,20},{20... | collective-permute-start | bytes 12296 | tf_op jit(solution)/shard_map/ppermute | solution.py:65
  9.9 2.8 %collective-permute-start.1 = (bf16[256,512]{1,0:T(8,128)(2,1)S(1)}, bf16[256,512]{1,0:T(8,128)(2,1)S(1)}, u32[]{:S(2)}, u32[]{:S(2)}) collective-permute-start(bf16[256,512]{1,0:T(8,128)(2,1)S(1)} %get-tuple-element.57.refs_0_), channel_id=1, source_target_pairs={{0,1},{1,0},{2,3},{3,2},{4,5},{5,4},{6,7},{7,6},{8,9},{9,8},{10,11... | collective-permute-start | bytes 786440 | tf_op jit(solution)/shard_map/ppermute | solution.py:65
  9.9 26.1 %collective-permute-start.10 = (bf16[1024,512]{1,0:T(8,128)(2,1)S(1)}, bf16[1024,512]{1,0:T(8,128)(2,1)S(1)}, u32[]{:S(2)}, u32[]{:S(2)}) collective-permute-start(bf16[1024,512]{1,0:T(8,128)(2,1)S(1)} %copy-done.1), channel_id=1, source_target_pairs={{0,16},{16,0},{1,17},{17,1},{2,18},{18,2},{3,19},{19,3},{4,20},{20... | collective-permute-start | bytes 3145736 | tf_op jit(solution)/shard_map/ppermute | solution.py:65
  12.0 1.5 %collective-permute-start.2 = (bf16[256,512]{1,0:T(8,128)(2,1)S(1)}, bf16[256,512]{1,0:T(8,128)(2,1)S(1)}, u32[]{:S(2)}, u32[]{:S(2)}) collective-permute-start(bf16[256,512]{1,0:T(8,128)(2,1)S(1)} %get-tuple-element.58.refs_1_), channel_id=1, source_target_pairs={{0,1},{1,0},{2,3},{3,2},{4,5},{5,4},{6,7},{7,6},{8,9},{9,8},{10,11... | collective-permute-start | bytes 786440 | tf_op jit(solution)/shard_map/ppermute | solution.py:65
  12.2 1.7 %collective-permute-start.3 = (bf16[256,512]{1,0:T(8,128)(2,1)S(1)}, bf16[256,512]{1,0:T(8,128)(2,1)S(1)}, u32[]{:S(2)}, u32[]{:S(2)}) collective-permute-start(bf16[256,512]{1,0:T(8,128)(2,1)S(1)} %get-tuple-element.59.refs_2_), channel_id=1, source_target_pairs={{0,1},{1,0},{2,3},{3,2},{4,5},{5,4},{6,7},{7,6},{8,9},{9,8},{10,11... | collective-permute-start | bytes 786440 | tf_op jit(solution)/shard_map/ppermute | solution.py:65
  12.5 1.8 %collective-permute-start.4 = (bf16[256,512]{1,0:T(8,128)(2,1)S(1)}, bf16[256,512]{1,0:T(8,128)(2,1)S(1)}, u32[]{:S(2)}, u32[]{:S(2)}) collective-permute-start(bf16[256,512]{1,0:T(8,128)(2,1)S(1)} %get-tuple-element.60.refs_3_), channel_id=1, source_target_pairs={{0,1},{1,0},{2,3},{3,2},{4,5},{5,4},{6,7},{7,6},{8,9},{9,8},{10,11... | collective-permute-start | bytes 786440 | tf_op jit(solution)/shard_map/ppermute | solution.py:65
  12.7 6.0 %collective-permute-start.5 = (bf16[256,512]{1,0:T(8,128)(2,1)S(1)}, bf16[256,512]{1,0:T(8,128)(2,1)S(1)}, u32[]{:S(2)}, u32[]{:S(2)}) collective-permute-start(bf16[256,512]{1,0:T(8,128)(2,1)S(1)} %get-tuple-element.62.refs_0_), channel_id=1, source_target_pairs={{0,1},{1,0},{2,3},{3,2},{4,5},{5,4},{6,7},{7,6},{8,9},{9,8},{10,11... | collective-permute-start | bytes 786440 | tf_op jit(solution)/shard_map/ppermute | solution.py:65
  16.6 12.4 %collective-permute-start.9 = (bf16[400,512]{1,0:T(8,128)(2,1)S(1)}, bf16[400,512]{1,0:T(8,128)(2,1)S(1)}, u32[]{:S(2)}, u32[]{:S(2)}) collective-permute-start(bf16[400,512]{1,0:T(8,128)(2,1)S(1)} %get-tuple-element.68), channel_id=1, source_target_pairs={{0,2},{1,3},{2,0},{3,1},{4,6},{5,7},{6,4},{7,5},{8,10},{9,11},{10,... | collective-permute-start | bytes 1228808 | tf_op jit(solution)/shard_map/ppermute | solution.py:61
  18.2 1.5 %collective-permute-start.6 = (bf16[256,512]{1,0:T(8,128)(2,1)S(1)}, bf16[256,512]{1,0:T(8,128)(2,1)S(1)}, u32[]{:S(2)}, u32[]{:S(2)}) collective-permute-start(bf16[256,512]{1,0:T(8,128)(2,1)S(1)} %get-tuple-element.63.refs_1_), channel_id=1, source_target_pairs={{0,1},{1,0},{2,3},{3,2},{4,5},{5,4},{6,7},{7,6},{8,9},{9,8},{10,11... | collective-permute-start | bytes 786440 | tf_op jit(solution)/shard_map/ppermute | solution.py:65
  18.2 2.0 %collective-permute-start.7 = (bf16[256,512]{1,0:T(8,128)(2,1)S(1)}, bf16[256,512]{1,0:T(8,128)(2,1)S(1)}, u32[]{:S(2)}, u32[]{:S(2)}) collective-permute-start(bf16[256,512]{1,0:T(8,128)(2,1)S(1)} %get-tuple-element.64.refs_2_), channel_id=1, source_target_pairs={{0,1},{1,0},{2,3},{3,2},{4,5},{5,4},{6,7},{7,6},{8,9},{9,8},{10,11... | collective-permute-start | bytes 786440 | tf_op jit(solution)/shard_map/ppermute | solution.py:65
  18.7 1.8 %collective-permute-start.8 = (bf16[256,512]{1,0:T(8,128)(2,1)S(1)}, bf16[256,512]{1,0:T(8,128)(2,1)S(1)}, u32[]{:S(2)}, u32[]{:S(2)}) collective-permute-start(bf16[256,512]{1,0:T(8,128)(2,1)S(1)} %get-tuple-element.65.refs_3_), channel_id=1, source_target_pairs={{0,1},{1,0},{2,3},{3,2},{4,5},{5,4},{6,7},{7,6},{8,9},{9,8},{10,11... | collective-permute-start | bytes 786440 | tf_op jit(solution)/shard_map/ppermute | solution.py:65
  19.7 40.6 %collective-permute-start.20 = (bf16[1024,512]{1,0:T(8,128)(2,1)S(1)}, bf16[1024,512]{1,0:T(8,128)(2,1)S(1)}, u32[]{:S(2)}, u32[]{:S(2)}) collective-permute-start(bf16[1024,512]{1,0:T(8,128)(2,1)S(1)} %copy-done.3), channel_id=1, source_target_pairs={{0,16},{16,0},{1,17},{17,1},{2,18},{18,2},{3,19},{19,3},{4,20},{20... | collective-permute-start | bytes 3145736 | tf_op jit(solution)/shard_map/ppermute | solution.py:65
  22.8 14.2 %collective-permute-start.11 = (bf16[400,512]{1,0:T(8,128)(2,1)S(1)}, bf16[400,512]{1,0:T(8,128)(2,1)S(1)}, u32[]{:S(2)}, u32[]{:S(2)}) collective-permute-start(bf16[400,512]{1,0:T(8,128)(2,1)S(1)} %get-tuple-element.72), channel_id=1, source_target_pairs={{0,2},{1,3},{2,0},{3,1},{4,6},{5,7},{6,4},{7,5},{8,10},{9,11},{10,... | collective-permute-start | bytes 1228808 | tf_op jit(solution)/shard_map/ppermute | solution.py:61
  29.1 10.9 %collective-permute-start.12 = (bf16[400,512]{1,0:T(8,128)(2,1)S(1)}, bf16[400,512]{1,0:T(8,128)(2,1)S(1)}, u32[]{:S(2)}, u32[]{:S(2)}) collective-permute-start(bf16[400,512]{1,0:T(8,128)(2,1)S(1)} %shard_map.53._), channel_id=1, source_target_pairs={{0,4},{12,8},{1,5},{13,9},{2,6},{14,10},{3,7},{15,11},{16,20},{28,... | collective-permute-start | bytes 1228808 | tf_op jit(solution)/shard_map/ppermute | solution.py:406
  36.2 3.9 %collective-permute-start.13 = (bf16[256,512]{1,0:T(8,128)(2,1)S(1)}, bf16[256,512]{1,0:T(8,128)(2,1)S(1)}, u32[]{:S(2)}, u32[]{:S(2)}) collective-permute-start(bf16[256,512]{1,0:T(8,128)(2,1)S(1)} %get-tuple-element.70._.refs_2_.refs_1_), channel_id=1, source_target_pairs={{0,1},{1,0},{2,3},{3,2},{4,5},{5,4},{6,7},{7,6},{8,9},{9,8},{10,11... | collective-permute-start | bytes 786440 | tf_op jit(solution)/shard_map/ppermute | solution.py:65
  36.3 8.4 %collective-permute-start.14 = (bf16[256,512]{1,0:T(8,128)(2,1)S(1)}, bf16[256,512]{1,0:T(8,128)(2,1)S(1)}, u32[]{:S(2)}, u32[]{:S(2)}) collective-permute-start(bf16[256,512]{1,0:T(8,128)(2,1)S(1)} %get-tuple-element.74.refs_3_.refs_2_), channel_id=1, source_target_pairs={{0,1},{1,0},{2,3},{3,2},{4,5},{5,4},{6,7},{7,6},{8,9},{9,8},{10,11... | collective-permute-start | bytes 786440 | tf_op jit(solution)/shard_map/ppermute | solution.py:65
  37.0 7.7 %collective-permute-start.15 = (bf16[256,512]{1,0:T(8,128)(2,1)S(1)}, bf16[256,512]{1,0:T(8,128)(2,1)S(1)}, u32[]{:S(2)}, u32[]{:S(2)}) collective-permute-start(bf16[256,512]{1,0:T(8,128)(2,1)S(1)} %get-tuple-element.75.refs_4_.refs_1_), channel_id=1, source_target_pairs={{0,1},{1,0},{2,3},{3,2},{4,5},{5,4},{6,7},{7,6},{8,9},{9,8},{10,11... | collective-permute-start | bytes 786440 | tf_op jit(solution)/shard_map/ppermute | solution.py:65
  40.0 4.7 %collective-permute-start.16 = (bf16[256,512]{1,0:T(8,128)(2,1)S(1)}, bf16[256,512]{1,0:T(8,128)(2,1)S(1)}, u32[]{:S(2)}, u32[]{:S(2)}) collective-permute-start(bf16[256,512]{1,0:T(8,128)(2,1)S(1)} %get-tuple-element.76.refs_5_.refs_2_), channel_id=1, source_target_pairs={{0,1},{1,0},{2,3},{3,2},{4,5},{5,4},{6,7},{7,6},{8,9},{9,8},{10,11... | collective-permute-start | bytes 786440 | tf_op jit(solution)/shard_map/ppermute | solution.py:65
  40.1 20.1 %collective-permute-start.19 = (bf16[400,512]{1,0:T(8,128)(2,1)S(1)}, bf16[400,512]{1,0:T(8,128)(2,1)S(1)}, u32[]{:S(2)}, u32[]{:S(2)}) collective-permute-start(bf16[400,512]{1,0:T(8,128)(2,1)S(1)} %shard_map.55._), channel_id=1, source_target_pairs={{0,4},{12,8},{1,5},{13,9},{2,6},{14,10},{3,7},{15,11},{16,20},{28,... | collective-permute-start | bytes 1228808 | tf_op jit(solution)/shard_map/ppermute | solution.py:406
  46.0 9.2 %collective-permute-start.17 = (bf16[256,512]{1,0:T(8,128)(2,1)S(1)}, bf16[256,512]{1,0:T(8,128)(2,1)S(1)}, u32[]{:S(2)}, u32[]{:S(2)}) collective-permute-start(bf16[256,512]{1,0:T(8,128)(2,1)S(1)} %get-tuple-element.78), channel_id=1, source_target_pairs={{0,2},{1,3},{2,0},{3,1},{4,6},{5,7},{6,4},{7,5},{8,10},{9,11},{10,... | collective-permute-start | bytes 786440 | tf_op jit(solution)/shard_map/ppermute | solution.py:61
  47.6 12.5 %collective-permute-start.18 = (bf16[256,512]{1,0:T(8,128)(2,1)S(1)}, bf16[256,512]{1,0:T(8,128)(2,1)S(1)}, u32[]{:S(2)}, u32[]{:S(2)}) collective-permute-start(bf16[256,512]{1,0:T(8,128)(2,1)S(1)} %get-tuple-element.80), channel_id=1, source_target_pairs={{0,2},{1,3},{2,0},{3,1},{4,6},{5,7},{6,4},{7,5},{8,10},{9,11},{10,... | collective-permute-start | bytes 786440 | tf_op jit(solution)/shard_map/ppermute | solution.py:61
  48.1 13.7 %collective-permute-start.21 = (bf16[400,512]{1,0:T(8,128)(2,1)S(1)}, bf16[400,512]{1,0:T(8,128)(2,1)S(1)}, u32[]{:S(2)}, u32[]{:S(2)}) collective-permute-start(bf16[400,512]{1,0:T(8,128)(2,1)S(1)} %shard_map.56._.refs_0_), channel_id=1, source_target_pairs={{4,8},{8,4},{5,9},{9,5},{6,10},{10,6},{7,11},{11,7},{20,24},{24,20... | collective-permute-start | bytes 1228808 | tf_op jit(solution)/shard_map/ppermute | solution.py:406
  55.3 6.7 %collective-permute-start.22 = (bf16[256,512]{1,0:T(8,128)(2,1)S(1)}, bf16[256,512]{1,0:T(8,128)(2,1)S(1)}, u32[]{:S(2)}, u32[]{:S(2)}) collective-permute-start(bf16[256,512]{1,0:T(8,128)(2,1)S(1)} %shard_map.58._), channel_id=1, source_target_pairs={{0,4},{12,8},{1,5},{13,9},{2,6},{14,10},{3,7},{15,11},{16,20},{28,... | collective-permute-start | bytes 786440 | tf_op jit(solution)/shard_map/ppermute | solution.py:406
  60.5 2.0 %collective-permute-start.23 = (bf16[256,512]{1,0:T(8,128)(2,1)S(1)}, bf16[256,512]{1,0:T(8,128)(2,1)S(1)}, u32[]{:S(2)}, u32[]{:S(2)}) collective-permute-start(bf16[256,512]{1,0:T(8,128)(2,1)S(1)} %get-tuple-element.82._.refs_2_.refs_1_), channel_id=1, source_target_pairs={{0,1},{1,0},{2,3},{3,2},{4,5},{5,4},{6,7},{7,6},{8,9},{9,8},{10,11... | collective-permute-start | bytes 786440 | tf_op jit(solution)/shard_map/ppermute | solution.py:65
  60.6 3.2 %collective-permute-start.24 = (bf16[256,512]{1,0:T(8,128)(2,1)S(1)}, bf16[256,512]{1,0:T(8,128)(2,1)S(1)}, u32[]{:S(2)}, u32[]{:S(2)}) collective-permute-start(bf16[256,512]{1,0:T(8,128)(2,1)S(1)} %get-tuple-element.84.refs_3_.refs_2_), channel_id=1, source_target_pairs={{0,1},{1,0},{2,3},{3,2},{4,5},{5,4},{6,7},{7,6},{8,9},{9,8},{10,11... | collective-permute-start | bytes 786440 | tf_op jit(solution)/shard_map/ppermute | solution.py:65
  61.1 12.8 %collective-permute-start.27 = (bf16[400,512]{1,0:T(8,128)(2,1)S(1)}, bf16[400,512]{1,0:T(8,128)(2,1)S(1)}, u32[]{:S(2)}, u32[]{:S(2)}) collective-permute-start(bf16[400,512]{1,0:T(8,128)(2,1)S(1)} %shard_map.60._.refs_0_), channel_id=1, source_target_pairs={{4,8},{8,4},{5,9},{9,5},{6,10},{10,6},{7,11},{11,7},{20,24},{24,20... | collective-permute-start | bytes 1228808 | tf_op jit(solution)/shard_map/ppermute | solution.py:406
  61.8 6.7 %collective-permute-start.25 = (bf16[256,512]{1,0:T(8,128)(2,1)S(1)}, bf16[256,512]{1,0:T(8,128)(2,1)S(1)}, u32[]{:S(2)}, u32[]{:S(2)}) collective-permute-start(bf16[256,512]{1,0:T(8,128)(2,1)S(1)} %get-tuple-element.85.refs_4_.refs_1_), channel_id=1, source_target_pairs={{0,1},{1,0},{2,3},{3,2},{4,5},{5,4},{6,7},{7,6},{8,9},{9,8},{10,11... | collective-permute-start | bytes 786440 | tf_op jit(solution)/shard_map/ppermute | solution.py:65
  61.9 7.4 %collective-permute-start.26 = (bf16[256,512]{1,0:T(8,128)(2,1)S(1)}, bf16[256,512]{1,0:T(8,128)(2,1)S(1)}, u32[]{:S(2)}, u32[]{:S(2)}) collective-permute-start(bf16[256,512]{1,0:T(8,128)(2,1)S(1)} %get-tuple-element.86.refs_5_.refs_2_), channel_id=1, source_target_pairs={{0,1},{1,0},{2,3},{3,2},{4,5},{5,4},{6,7},{7,6},{8,9},{9,8},{10,11... | collective-permute-start | bytes 786440 | tf_op jit(solution)/shard_map/ppermute | solution.py:65
  62.5 13.7 %collective-permute-start.29 = (bf16[400,512]{1,0:T(8,128)(2,1)S(1)}, bf16[400,512]{1,0:T(8,128)(2,1)S(1)}, u32[]{:S(2)}, u32[]{:S(2)}) collective-permute-start(bf16[400,512]{1,0:T(8,128)(2,1)S(1)} %shard_map.62._.refs_0_), channel_id=1, source_target_pairs={{4,0},{8,12},{5,1},{9,13},{6,2},{10,14},{7,3},{11,15},{20,16},{24,... | collective-permute-start | bytes 1228808 | tf_op jit(solution)/shard_map/ppermute | solution.py:406
  63.8 11.5 %collective-permute-start.28 = (bf16[256,512]{1,0:T(8,128)(2,1)S(1)}, bf16[256,512]{1,0:T(8,128)(2,1)S(1)}, u32[]{:S(2)}, u32[]{:S(2)}) collective-permute-start(bf16[256,512]{1,0:T(8,128)(2,1)S(1)} %shard_map.59._), channel_id=1, source_target_pairs={{0,4},{12,8},{1,5},{13,9},{2,6},{14,10},{3,7},{15,11},{16,20},{28,... | collective-permute-start | bytes 786440 | tf_op jit(solution)/shard_map/ppermute | solution.py:406
  68.5 9.0 %collective-permute-start.30 = (bf16[256,512]{1,0:T(8,128)(2,1)S(1)}, bf16[256,512]{1,0:T(8,128)(2,1)S(1)}, u32[]{:S(2)}, u32[]{:S(2)}) collective-permute-start(bf16[256,512]{1,0:T(8,128)(2,1)S(1)} %shard_map.63._.refs_0_), channel_id=1, source_target_pairs={{4,8},{8,4},{5,9},{9,5},{6,10},{10,6},{7,11},{11,7},{20,24},{24,20... | collective-permute-start | bytes 786440 | tf_op jit(solution)/shard_map/ppermute | solution.py:406
  70.7 8.3 %collective-permute-start.31 = (bf16[256,512]{1,0:T(8,128)(2,1)S(1)}, bf16[256,512]{1,0:T(8,128)(2,1)S(1)}, u32[]{:S(2)}, u32[]{:S(2)}) collective-permute-start(bf16[256,512]{1,0:T(8,128)(2,1)S(1)} %get-tuple-element.89), channel_id=1, source_target_pairs={{0,2},{1,3},{2,0},{3,1},{4,6},{5,7},{6,4},{7,5},{8,10},{9,11},{10,... | collective-permute-start | bytes 786440 | tf_op jit(solution)/shard_map/ppermute | solution.py:61
  74.0 16.5 %collective-permute-start.34 = (bf16[400,512]{1,0:T(8,128)(2,1)S(1)}, bf16[400,512]{1,0:T(8,128)(2,1)S(1)}, u32[]{:S(2)}, u32[]{:S(2)}) collective-permute-start(bf16[400,512]{1,0:T(8,128)(2,1)S(1)} %shard_map.66._.refs_0_), channel_id=1, source_target_pairs={{4,0},{8,12},{5,1},{9,13},{6,2},{10,14},{7,3},{11,15},{20,16},{24,... | collective-permute-start | bytes 1228808 | tf_op jit(solution)/shard_map/ppermute | solution.py:406
  75.5 8.9 %collective-permute-start.32 = (bf16[256,512]{1,0:T(8,128)(2,1)S(1)}, bf16[256,512]{1,0:T(8,128)(2,1)S(1)}, u32[]{:S(2)}, u32[]{:S(2)}) collective-permute-start(bf16[256,512]{1,0:T(8,128)(2,1)S(1)} %shard_map.67._.refs_0_), channel_id=1, source_target_pairs={{4,8},{8,4},{5,9},{9,5},{6,10},{10,6},{7,11},{11,7},{20,24},{24,20... | collective-permute-start | bytes 786440 | tf_op jit(solution)/shard_map/ppermute | solution.py:406
  76.2 8.2 %collective-permute-start.33 = (bf16[256,512]{1,0:T(8,128)(2,1)S(1)}, bf16[256,512]{1,0:T(8,128)(2,1)S(1)}, u32[]{:S(2)}, u32[]{:S(2)}) collective-permute-start(bf16[256,512]{1,0:T(8,128)(2,1)S(1)} %get-tuple-element.91), channel_id=1, source_target_pairs={{0,2},{1,3},{2,0},{3,1},{4,6},{5,7},{6,4},{7,5},{8,10},{9,11},{10,... | collective-permute-start | bytes 786440 | tf_op jit(solution)/shard_map/ppermute | solution.py:61
  79.0 11.6 %collective-permute-start.35 = (bf16[256,512]{1,0:T(8,128)(2,1)S(1)}, bf16[256,512]{1,0:T(8,128)(2,1)S(1)}, u32[]{:S(2)}, u32[]{:S(2)}) collective-permute-start(bf16[256,512]{1,0:T(8,128)(2,1)S(1)} %shard_map.70._), channel_id=1, source_target_pairs={{0,4},{12,8},{1,5},{13,9},{2,6},{14,10},{3,7},{15,11},{16,20},{28,... | collective-permute-start | bytes 786440 | tf_op jit(solution)/shard_map/ppermute | solution.py:406
  84.5 10.3 %collective-permute-start.36 = (bf16[272,512]{1,0:T(8,128)(2,1)S(1)}, bf16[272,512]{1,0:T(8,128)(2,1)S(1)}, u32[]{:S(2)}, u32[]{:S(2)}) collective-permute-start(bf16[272,512]{1,0:T(8,128)(2,1)S(1)} %shard_map.72._), channel_id=1, source_target_pairs={{0,4},{12,8},{1,5},{13,9},{2,6},{14,10},{3,7},{15,11},{16,20},{28,... | collective-permute-start | bytes 835592 | tf_op jit(solution)/shard_map/ppermute | solution.py:406
  90.7 4.9 %collective-permute-start.37 = (bf16[256,512]{1,0:T(8,128)(2,1)S(1)}, bf16[256,512]{1,0:T(8,128)(2,1)S(1)}, u32[]{:S(2)}, u32[]{:S(2)}) collective-permute-start(bf16[256,512]{1,0:T(8,128)(2,1)S(1)} %shard_map.74._.refs_0_), channel_id=1, source_target_pairs={{4,8},{8,4},{5,9},{9,5},{6,10},{10,6},{7,11},{11,7},{20,24},{24,20... | collective-permute-start | bytes 786440 | tf_op jit(solution)/shard_map/ppermute | solution.py:406
  91.4 14.4 %collective-permute-start.42 = (bf16[400,512]{1,0:T(8,128)(2,1)S(1)}, bf16[400,512]{1,0:T(8,128)(2,1)S(1)}, u32[]{:S(2)}, u32[]{:S(2)}) collective-permute-start(bf16[400,512]{1,0:T(8,128)(2,1)S(1)} %shard_map.68._.refs_5_), channel_id=1, source_target_pairs={{0,2},{1,3},{2,0},{3,1},{4,6},{5,7},{6,4},{7,5},{8,10},{9,11},{10,... | collective-permute-start | bytes 1228808 | tf_op jit(solution)/shard_map/ppermute | solution.py:61
  92.0 18.6 %collective-permute-start.45 = (bf16[400,512]{1,0:T(8,128)(2,1)S(1)}, bf16[400,512]{1,0:T(8,128)(2,1)S(1)}, u32[]{:S(2)}, u32[]{:S(2)}) collective-permute-start(bf16[400,512]{1,0:T(8,128)(2,1)S(1)} %shard_map.73._.refs_5_), channel_id=1, source_target_pairs={{0,2},{1,3},{2,0},{3,1},{4,6},{5,7},{6,4},{7,5},{8,10},{9,11},{10,... | collective-permute-start | bytes 1228808 | tf_op jit(solution)/shard_map/ppermute | solution.py:61
  93.5 11.1 %collective-permute-start.39 = (bf16[256,512]{1,0:T(8,128)(2,1)S(1)}, bf16[256,512]{1,0:T(8,128)(2,1)S(1)}, u32[]{:S(2)}, u32[]{:S(2)}) collective-permute-start(bf16[256,512]{1,0:T(8,128)(2,1)S(1)} %shard_map.69._.refs_0_), channel_id=1, source_target_pairs={{4,0},{8,12},{5,1},{9,13},{6,2},{10,14},{7,3},{11,15},{20,16},{24,... | collective-permute-start | bytes 786440 | tf_op jit(solution)/shard_map/ppermute | solution.py:406
  94.9 15.2 %collective-permute-start.41 = (bf16[272,512]{1,0:T(8,128)(2,1)S(1)}, bf16[272,512]{1,0:T(8,128)(2,1)S(1)}, u32[]{:S(2)}, u32[]{:S(2)}) collective-permute-start(bf16[272,512]{1,0:T(8,128)(2,1)S(1)} %shard_map.75._.refs_0_), channel_id=1, source_target_pairs={{4,8},{8,4},{5,9},{9,5},{6,10},{10,6},{7,11},{11,7},{20,24},{24,20... | collective-permute-start | bytes 835592 | tf_op jit(solution)/shard_map/ppermute | solution.py:406
  95.6 14.5 %collective-permute-start.38 = (bf16[256,512]{1,0:T(8,128)(2,1)S(1)}, bf16[256,512]{1,0:T(8,128)(2,1)S(1)}, u32[]{:S(2)}, u32[]{:S(2)}) collective-permute-start(bf16[256,512]{1,0:T(8,128)(2,1)S(1)} %shard_map.71._.refs_0_), channel_id=1, source_target_pairs={{4,0},{8,12},{5,1},{9,13},{6,2},{10,14},{7,3},{11,15},{20,16},{24,... | collective-permute-start | bytes 786440 | tf_op jit(solution)/shard_map/ppermute | solution.py:406
  104.6 8.4 %collective-permute-start.40 = (bf16[256,512]{1,0:T(8,128)(2,1)S(1)}, bf16[256,512]{1,0:T(8,128)(2,1)S(1)}, u32[]{:S(2)}, u32[]{:S(2)}) collective-permute-start(bf16[256,512]{1,0:T(8,128)(2,1)S(1)} %shard_map.76._.refs_0_), channel_id=1, source_target_pairs={{4,0},{8,12},{5,1},{9,13},{6,2},{10,14},{7,3},{11,15},{20,16},{24,... | collective-permute-start | bytes 786440 | tf_op jit(solution)/shard_map/ppermute | solution.py:406
  105.9 9.0 %collective-permute-start.43 = (bf16[400,512]{1,0:T(8,128)(2,1)S(1)}, bf16[400,512]{1,0:T(8,128)(2,1)S(1)}, u32[]{:S(2)}, u32[]{:S(2)}) collective-permute-start(bf16[400,512]{1,0:T(8,128)(2,1)S(1)} %shard_map.68._.refs_5_), channel_id=1, source_target_pairs={{0,1},{1,0},{2,3},{3,2},{4,5},{5,4},{6,7},{7,6},{8,9},{9,8},{10,11... | collective-permute-start | bytes 1228808 | tf_op jit(solution)/shard_map/ppermute | solution.py:65
  110.1 6.0 %collective-permute-start.44 = (bf16[400,512]{1,0:T(8,128)(2,1)S(1)}, bf16[400,512]{1,0:T(8,128)(2,1)S(1)}, u32[]{:S(2)}, u32[]{:S(2)}) collective-permute-start(bf16[400,512]{1,0:T(8,128)(2,1)S(1)} %collective-permute-done.42.refs_6_), channel_id=1, source_target_pairs={{0,1},{1,0},{2,3},{3,2},{4,5},{5,4},{6,7},{7,6},{8,9},{9,8},{10,11... | collective-permute-start | bytes 1228808 | tf_op jit(solution)/shard_map/ppermute | solution.py:65
  110.1 6.1 %collective-permute-start.46 = (bf16[400,512]{1,0:T(8,128)(2,1)S(1)}, bf16[400,512]{1,0:T(8,128)(2,1)S(1)}, u32[]{:S(2)}, u32[]{:S(2)}) collective-permute-start(bf16[400,512]{1,0:T(8,128)(2,1)S(1)} %shard_map.73._.refs_5_), channel_id=1, source_target_pairs={{0,1},{1,0},{2,3},{3,2},{4,5},{5,4},{6,7},{7,6},{8,9},{9,8},{10,11... | collective-permute-start | bytes 1228808 | tf_op jit(solution)/shard_map/ppermute | solution.py:65
  110.6 9.8 %collective-permute-start.47 = (bf16[400,512]{1,0:T(8,128)(2,1)S(1)}, bf16[400,512]{1,0:T(8,128)(2,1)S(1)}, u32[]{:S(2)}, u32[]{:S(2)}) collective-permute-start(bf16[400,512]{1,0:T(8,128)(2,1)S(1)} %collective-permute-done.45.refs_6_), channel_id=1, source_target_pairs={{0,1},{1,0},{2,3},{3,2},{4,5},{5,4},{6,7},{7,6},{8,9},{9,8},{10,11... | collective-permute-start | bytes 1228808 | tf_op jit(solution)/shard_map/ppermute | solution.py:65
  112.9 7.5 %collective-permute-start.49 = (bf16[256,512]{1,0:T(8,128)(2,1)S(1)}, bf16[256,512]{1,0:T(8,128)(2,1)S(1)}, u32[]{:S(2)}, u32[]{:S(2)}) collective-permute-start(bf16[256,512]{1,0:T(8,128)(2,1)S(1)} %shard_map.78._.refs_3_), channel_id=1, source_target_pairs={{0,2},{1,3},{2,0},{3,1},{4,6},{5,7},{6,4},{7,5},{8,10},{9,11},{10,... | collective-permute-start | bytes 786440 | tf_op jit(solution)/shard_map/ppermute | solution.py:61
  114.8 11.9 %collective-permute-start.48 = (bf16[272,512]{1,0:T(8,128)(2,1)S(1)}, bf16[272,512]{1,0:T(8,128)(2,1)S(1)}, u32[]{:S(2)}, u32[]{:S(2)}) collective-permute-start(bf16[272,512]{1,0:T(8,128)(2,1)S(1)} %shard_map.80._.refs_0_), channel_id=1, source_target_pairs={{4,0},{8,12},{5,1},{9,13},{6,2},{10,14},{7,3},{11,15},{20,16},{24,... | collective-permute-start | bytes 835592 | tf_op jit(solution)/shard_map/ppermute | solution.py:406
  116.1 11.0 %collective-permute-start.50 = (bf16[256,512]{1,0:T(8,128)(2,1)S(1)}, bf16[256,512]{1,0:T(8,128)(2,1)S(1)}, u32[]{:S(2)}, u32[]{:S(2)}) collective-permute-start(bf16[256,512]{1,0:T(8,128)(2,1)S(1)} %shard_map.78._.refs_3_), channel_id=1, source_target_pairs={{0,1},{1,0},{2,3},{3,2},{4,5},{5,4},{6,7},{7,6},{8,9},{9,8},{10,11... | collective-permute-start | bytes 786440 | tf_op jit(solution)/shard_map/ppermute | solution.py:65
  116.2 11.2 %collective-permute-start.52 = (bf16[256,512]{1,0:T(8,128)(2,1)S(1)}, bf16[256,512]{1,0:T(8,128)(2,1)S(1)}, u32[]{:S(2)}, u32[]{:S(2)}) collective-permute-start(bf16[256,512]{1,0:T(8,128)(2,1)S(1)} %shard_map.77._.refs_3_), channel_id=1, source_target_pairs={{0,2},{1,3},{2,0},{3,1},{4,6},{5,7},{6,4},{7,5},{8,10},{9,11},{10,... | collective-permute-start | bytes 786440 | tf_op jit(solution)/shard_map/ppermute | solution.py:61
  120.4 7.3 %collective-permute-start.51 = (bf16[256,512]{1,0:T(8,128)(2,1)S(1)}, bf16[256,512]{1,0:T(8,128)(2,1)S(1)}, u32[]{:S(2)}, u32[]{:S(2)}) collective-permute-start(bf16[256,512]{1,0:T(8,128)(2,1)S(1)} %collective-permute-done.49.refs_4_), channel_id=1, source_target_pairs={{0,1},{1,0},{2,3},{3,2},{4,5},{5,4},{6,7},{7,6},{8,9},{9,8},{10,11... | collective-permute-start | bytes 786440 | tf_op jit(solution)/shard_map/ppermute | solution.py:65
  120.4 10.7 %collective-permute-start.55 = (bf16[256,512]{1,0:T(8,128)(2,1)S(1)}, bf16[256,512]{1,0:T(8,128)(2,1)S(1)}, u32[]{:S(2)}, u32[]{:S(2)}) collective-permute-start(bf16[256,512]{1,0:T(8,128)(2,1)S(1)} %shard_map.79._.refs_3_), channel_id=1, source_target_pairs={{0,2},{1,3},{2,0},{3,1},{4,6},{5,7},{6,4},{7,5},{8,10},{9,11},{10,... | collective-permute-start | bytes 786440 | tf_op jit(solution)/shard_map/ppermute | solution.py:61
  127.0 10.8 %collective-permute-start.58 = (bf16[272,512]{1,0:T(8,128)(2,1)S(1)}, bf16[272,512]{1,0:T(8,128)(2,1)S(1)}, u32[]{:S(2)}, u32[]{:S(2)}) collective-permute-start(bf16[272,512]{1,0:T(8,128)(2,1)S(1)} %shard_map.83._.refs_5_.refs_3_), channel_id=1, source_target_pairs={{0,2},{1,3},{2,0},{3,1},{4,6},{5,7},{6,4},{7,5},{8,10},{9,11},{10,... | collective-permute-start | bytes 835592 | tf_op jit(solution)/shard_map/ppermute | solution.py:61
  127.1 5.2 %collective-permute-start.53 = (bf16[256,512]{1,0:T(8,128)(2,1)S(1)}, bf16[256,512]{1,0:T(8,128)(2,1)S(1)}, u32[]{:S(2)}, u32[]{:S(2)}) collective-permute-start(bf16[256,512]{1,0:T(8,128)(2,1)S(1)} %shard_map.77._.refs_3_), channel_id=1, source_target_pairs={{0,1},{1,0},{2,3},{3,2},{4,5},{5,4},{6,7},{7,6},{8,9},{9,8},{10,11... | collective-permute-start | bytes 786440 | tf_op jit(solution)/shard_map/ppermute | solution.py:65
  127.4 5.5 %collective-permute-start.54 = (bf16[256,512]{1,0:T(8,128)(2,1)S(1)}, bf16[256,512]{1,0:T(8,128)(2,1)S(1)}, u32[]{:S(2)}, u32[]{:S(2)}) collective-permute-start(bf16[256,512]{1,0:T(8,128)(2,1)S(1)} %collective-permute-done.52.refs_4_), channel_id=1, source_target_pairs={{0,1},{1,0},{2,3},{3,2},{4,5},{5,4},{6,7},{7,6},{8,9},{9,8},{10,11... | collective-permute-start | bytes 786440 | tf_op jit(solution)/shard_map/ppermute | solution.py:65
  127.7 7.3 %collective-permute-start.56 = (bf16[256,512]{1,0:T(8,128)(2,1)S(1)}, bf16[256,512]{1,0:T(8,128)(2,1)S(1)}, u32[]{:S(2)}, u32[]{:S(2)}) collective-permute-start(bf16[256,512]{1,0:T(8,128)(2,1)S(1)} %shard_map.79._.refs_3_), channel_id=1, source_target_pairs={{0,1},{1,0},{2,3},{3,2},{4,5},{5,4},{6,7},{7,6},{8,9},{9,8},{10,11... | collective-permute-start | bytes 786440 | tf_op jit(solution)/shard_map/ppermute | solution.py:65
  131.1 3.9 %collective-permute-start.57 = (bf16[256,512]{1,0:T(8,128)(2,1)S(1)}, bf16[256,512]{1,0:T(8,128)(2,1)S(1)}, u32[]{:S(2)}, u32[]{:S(2)}) collective-permute-start(bf16[256,512]{1,0:T(8,128)(2,1)S(1)} %collective-permute-done.55.refs_4_), channel_id=1, source_target_pairs={{0,1},{1,0},{2,3},{3,2},{4,5},{5,4},{6,7},{7,6},{8,9},{9,8},{10,11... | collective-permute-start | bytes 786440 | tf_op jit(solution)/shard_map/ppermute | solution.py:65
  132.4 5.5 %collective-permute-start.59 = (bf16[272,512]{1,0:T(8,128)(2,1)S(1)}, bf16[272,512]{1,0:T(8,128)(2,1)S(1)}, u32[]{:S(2)}, u32[]{:S(2)}) collective-permute-start(bf16[272,512]{1,0:T(8,128)(2,1)S(1)} %shard_map.83._.refs_5_.refs_3_), channel_id=1, source_target_pairs={{0,1},{1,0},{2,3},{3,2},{4,5},{5,4},{6,7},{7,6},{8,9},{9,8},{10,11... | collective-permute-start | bytes 835592 | tf_op jit(solution)/shard_map/ppermute | solution.py:65
  137.9 1.6 %collective-permute-start.60 = (bf16[272,512]{1,0:T(8,128)(2,1)S(1)}, bf16[272,512]{1,0:T(8,128)(2,1)S(1)}, u32[]{:S(2)}, u32[]{:S(2)}) collective-permute-start(bf16[272,512]{1,0:T(8,128)(2,1)S(1)} %collective-permute-done.58.refs_6_.refs_4_), channel_id=1, source_target_pairs={{0,1},{1,0},{2,3},{3,2},{4,5},{5,4},{6,7},{7,6},{8,9},{9,8},{10,11... | collective-permute-start | bytes 835592 | tf_op jit(solution)/shard_map/ppermute | solution.py:65
  139.5 3.6 %collective-permute-start.61 = (f32[1,512]{1,0:T(1,128)S(1)}, f32[1,512]{1,0:T(1,128)S(1)}, u32[]{:S(2)}, u32[]{:S(2)}) collective-permute-start(f32[1,512]{1,0:T(1,128)S(1)} %get-tuple-element.105._), channel_id=1, source_target_pairs={{0,16},{16,0},{1,17},{17,1},{2,18},{18,2},{3,19},{19,3},{4,20},{20... | collective-permute-start | bytes 6152 | tf_op jit(solution)/shard_map/ppermute | solution.py:65
  (3 other events, 4.0 us)
